TPU v7x, 256 devices: a whole 4x4x8 slice. The times are simulated.
256 devices in a mesh: seq: 64 (over y, x_hi, z), grp: 4 (over x_lo, core).
Axes of the slice: x: 4 (x_hi: 2, x_lo: 2; x = x_hi * 2 + x_lo), y: 4, z: 8, core: 2. Of those that a mesh axis runs over, the one named last changes fastest.
Arguments:
- tokens: bfloat16 [768, 65536], P('grp', 'seq'), may hold values from -6 to 6
- in_weight: bfloat16 [3, 768, 768], P(None, 'grp'), may hold values from -0.21875 to 0.21875
- short_weight: float32 [3, 3, 768], P(None, None, 'grp'), may hold values from -3.5 to 3.5
- filter_bias: float32 [768], P('grp'), may hold values from -1 to 1
- spectra: float32 [2, 768, 512, 256], P(None, 'grp', 'seq'), may hold values from -12 to 12
- out_weight: bfloat16 [768, 768], P('grp'), may hold values from -0.21875 to 0.21875
Outputs:
- mixed: bfloat16 [768, 65536], P('grp', 'seq')
All inputs are finite; a program needn't handle non-finite values.
Results may differ from a plain program's by a relative error of at most 0.019.
Values may be sent and summed in bfloat16 or wider, within the bound.
No kernel may reach another device: no remote copies, remote signals or barrier semaphores. Data moves between devices by JAX's collectives and lax.ppermute only.
A program may use at most 64 MiB of HBM per device.

v0:
```python
import math

import jax
import jax.numpy as jnp
from jax import lax
from jax.sharding import PartitionSpec as P

QCOLS = 256


def passed_along(block, axis, distance):
    devices = range(lax.axis_size(axis))
    route = [(i - distance, i) for i in devices if i - distance in devices]
    return lax.ppermute(block, axis, route)


def phase_table(row_ids, col_ids, period):
    product = row_ids[:, None] * col_ids[None, :] % period
    angles = product.astype(jnp.float32) * (2.0 * math.pi / period)
    return (jnp.cos(angles), jnp.sin(angles))


def exact_mix(tables, values):
    return jnp.einsum(
        "kb,cjb->cjk",
        tables,
        values,
        precision=lax.Precision.HIGHEST,
        preferred_element_type=jnp.float32,
    )


def exact_rows(tables, values):
    return jnp.einsum(
        "kp,cpq->ckq",
        tables,
        values,
        precision=lax.Precision.HIGHEST,
        preferred_element_type=jnp.float32,
    )


def rotate(real_part, imag_part, row_ids, col_ids, period, direction):
    cosine, sine_table = phase_table(row_ids, col_ids, period)
    sine_table = direction * sine_table
    return (
        real_part * cosine - imag_part * sine_table,
        imag_part * cosine + real_part * sine_table,
    )


def forward_rows(values, freq_rows):
    half_rows = values.shape[1]
    cosine, sine_table = phase_table(
        jnp.arange(freq_rows, dtype=jnp.int32), jnp.arange(half_rows, dtype=jnp.int32), freq_rows
    )
    return (exact_rows(cosine, values), -exact_rows(sine_table, values))


def filter_middle(real_part, imag_part, filter_real, filter_imag):
    col_count = real_part.shape[2]
    positions = jnp.arange(col_count, dtype=jnp.int32)
    cosine, sine_table = phase_table(positions, positions, col_count)
    freq_real = exact_mix(cosine, real_part) + exact_mix(sine_table, imag_part)
    freq_imag = exact_mix(cosine, imag_part) - exact_mix(sine_table, real_part)
    prod_real = freq_real * filter_real - freq_imag * filter_imag
    prod_imag = freq_real * filter_imag + freq_imag * filter_real
    out_real = exact_mix(cosine, prod_real) - exact_mix(sine_table, prod_imag)
    out_imag = exact_mix(cosine, prod_imag) + exact_mix(sine_table, prod_real)
    return (out_real, out_imag)


def inverse_rows(real_part, imag_part, half_rows, padded_len):
    freq_rows = real_part.shape[1]
    cosine, sine_table = phase_table(
        jnp.arange(half_rows, dtype=jnp.int32), jnp.arange(freq_rows, dtype=jnp.int32), freq_rows
    )
    return (exact_rows(cosine, real_part) - exact_rows(sine_table, imag_part)) * (1.0 / padded_len)


def shards(tokens, in_weight, short_weight, filter_bias, spectra, out_weight):
    seq_index = lax.axis_index("seq")
    tok_rows = tokens.shape[1]
    channels = in_weight.shape[1]
    col_count = QCOLS
    rows_dev = tok_rows // col_count
    contract_first = (((0,), (0,)), ((), ()))
    shard_part = lax.all_gather(tokens, "grp", axis=0, tiled=True)
    weight_rows = in_weight
    weight_rows = weight_rows.reshape(3 * channels, shard_part.shape[0])
    projected = jnp.dot(weight_rows, shard_part, preferred_element_type=jnp.float32)
    streams = lax.optimization_barrier(projected.astype(jnp.bfloat16)).reshape(
        3, channels, tok_rows
    )
    earlier = passed_along(streams[:, :, -2:], "seq", 1)
    extended = jnp.concatenate([earlier, streams], 2).astype(jnp.float32)
    taps = short_weight[:, :, :, None]
    smooth = (
        taps[0] * extended[:, :, 2:]
        + taps[1] * extended[:, :, 1:-1]
        + taps[2] * extended[:, :, :-2]
    )
    gate_out = smooth[0].astype(jnp.bfloat16)
    signal = (smooth[2] * smooth[1]).astype(jnp.bfloat16)
    blocks = signal.reshape(channels, rows_dev, col_count)
    all_cols = jnp.arange(col_count, dtype=jnp.int32)
    columns = lax.all_to_all(blocks, "seq", split_axis=2, concat_axis=1, tiled=True)
    half_rows = columns.shape[1]
    col_block = columns.shape[2]
    freq_rows = 2 * half_rows
    padded_len = freq_rows * col_count
    wave_real, wave_imag = forward_rows(columns.astype(jnp.float32), freq_rows)
    col_ids = seq_index * col_block + jnp.arange(col_block, dtype=jnp.int32)
    twisted = rotate(
        wave_real, wave_imag, jnp.arange(freq_rows, dtype=jnp.int32), col_ids, padded_len, -1.0
    )
    spread = lax.all_to_all(jnp.stack(twisted), "seq", split_axis=2, concat_axis=3, tiled=True)
    row_block = spread.shape[2]
    mid_real, mid_imag = filter_middle(spread[0], spread[1], spectra[0], spectra[1])
    row_ids = seq_index * row_block + jnp.arange(row_block, dtype=jnp.int32)
    rotated_back = rotate(mid_real, mid_imag, row_ids, all_cols, padded_len, 1.0)
    regrouped = lax.all_to_all(
        jnp.stack(rotated_back), "seq", split_axis=3, concat_axis=2, tiled=True
    )
    real_out = inverse_rows(regrouped[0], regrouped[1], half_rows, padded_len)
    convolved = lax.all_to_all(real_out, "seq", split_axis=1, concat_axis=2, tiled=True)
    convolved = convolved.reshape(channels, tok_rows)
    weighted = (
        gate_out.astype(jnp.float32)
        * (convolved + filter_bias[:, None] * signal.astype(jnp.float32))
    ).astype(jnp.bfloat16)
    partial_value = lax.dot_general(
        out_weight, weighted, contract_first, preferred_element_type=jnp.float32
    )
    return lax.psum_scatter(
        partial_value.astype(jnp.bfloat16), "grp", scatter_dimension=0, tiled=True
    )


def solution(mesh):
    in_specs = (
        P("grp", "seq"),
        P(None, "grp", None),
        P(None, None, "grp"),
        P("grp"),
        P(None, "grp", "seq", None),
        P("grp", None),
    )
    out_specs = P("grp", "seq")
    return jax.shard_map(shards, mesh=mesh, in_specs=in_specs, out_specs=out_specs, check_vma=False)
```

profile of v0, /device:TPU:1, one launch (start us, length us, event | category | flops | bytes accessed | tf_op | source)
XLA Modules:
  0.0 429.9 jit_solution(13519051917725174815)
XLA Ops:
  7.3 33.5 %all-gather.2.cloned.1.call-done = bf16[768,1024]{1,0:T(8,128)(2,1)} async-done(((bf16[192,1024]{1,0:T(8,128)(2,1)}), bf16[768,1024]{1,0:T(8,128)(2,1)}) %all-gather.2.cloned.1.call-update) | async-done | bytes 1572880 | tf_op jit(solution)/shard_map/all_gather | solution.py:88
  40.8 3.5 convolution_convert_fusion.1
  46.0 3.2 collective-permute-start
  54.2 14.0 %all-to-all-start = ((bf16[192,4,256]{0,1,2:T(4,128)(2,1)}), bf16[192,4,256]{0,1,2:T(4,128)(2,1)S(1)}, u32[]{:S(2)}, u32[]{:S(2)}) async-start(bf16[192,4,256]{0,1,2:T(4,128)(2,1)} %copy.59), calls=%async_computation | async-start | bytes 1048576 | tf_op jit(solution)/shard_map/all_to_all | solution.py:107
  68.3 16.6 %all-to-all-done = bf16[192,4,256]{0,1,2:T(4,128)(2,1)S(1)} async-done(((bf16[192,4,256]{0,1,2:T(4,128)(2,1)}), bf16[192,4,256]{0,1,2:T(4,128)(2,1)S(1)}, u32[]{:S(2)}, u32[]{:S(2)}) %all-to-all-start) | async-done | bytes 393248 | tf_op jit(solution)/shard_map/all_to_all | solution.py:107
  85.5 3.2 convolution_negate_fusion
  88.6 3.3 fusion.11
  91.9 2.0 pad_maximum_fusion
  93.9 5.1 %copy.63 = f32[2,192,512,4]{1,3,0,2:T(4,128)} copy(f32[2,192,512,4]{2,1,3,0:T(8,128)} %pad_maximum_fusion) | data formatting | bytes 6291456 | tf_op jit(solution)/shard_map/stack | solution.py:117
  99.0 7.6 %all-to-all-start.1 = ((f32[2,192,512,4]{1,3,0,2:T(4,128)}), f32[2,192,512,4]{1,3,0,2:T(4,128)}, u32[]{:S(2)}, u32[]{:S(2)}) async-start(f32[2,192,512,4]{1,3,0,2:T(4,128)} %copy.63), calls=%async_computation.1 | async-start | bytes 8388608 | tf_op jit(solution)/shard_map/all_to_all | solution.py:117
  106.6 12.3 %reduce-scatter.4.cloned.1.call-start = ((), (), s32[]{:S(2)}) async-start(), calls=%async_computation.6 | async-start | bytes 1966080 | tf_op jit(solution)/shard_map/reduce_scatter | solution.py:135
  119.1 80.2 %all-to-all-done.1 = f32[2,192,512,4]{1,3,0,2:T(4,128)} async-done(((f32[2,192,512,4]{1,3,0,2:T(4,128)}), f32[2,192,512,4]{1,3,0,2:T(4,128)}, u32[]{:S(2)}, u32[]{:S(2)}) %all-to-all-start.1) | async-done | bytes 3145760 | tf_op jit(solution)/shard_map/all_to_all | solution.py:117
  199.3 3.5 copy.99
  202.8 1.7 fusion.147
  206.2 2.3 copy.68
  208.5 3.5 fusion.65
  213.5 3.0 copy.66
  216.6 4.0 fusion.67
  220.6 2.4 convolution_subtract_fusion.1
  223.0 2.8 fusion.9
  225.8 2.4 fusion.61
  228.2 2.8 fusion.63
  231.0 2.5 convolution_add_fusion
  233.5 2.7 subtract_bitcast_fusion
  236.2 1.9 pad_maximum_fusion.1
  238.1 5.2 %copy.71 = f32[2,192,8,256]{1,2,0,3:T(8,128)} copy(f32[2,192,8,256]{3,2,1,0:T(8,128)} %pad_maximum_fusion.1) | data formatting | bytes 6291456 | tf_op jit(solution)/shard_map/stack | solution.py:123
  243.3 102.4 %all_to_all.63 = f32[2,192,8,256]{1,2,0,3:T(8,128)S(1)} all-to-all(f32[2,192,8,256]{1,2,0,3:T(8,128)} %copy.71), channel_id=1, replica_groups=mesh['seq'=64,'grp'=4] {'seq'}, dimensions={3} | all-to-all | bytes 6291456 | tf_op jit(solution)/shard_map/all_to_all | solution.py:122
  346.6 5.1 %fusion.2 = f32[192,4,256]{2,0,1:T(8,128)S(1)} fusion(f32[1,192,64,8,4]{1,3,4,2,0:T(8,128)S(1)} %get-tuple-element.8), kind=kOutput, calls=%fused_computation.8 | convolution fusion | flops 1209794560 | bytes 2359296 | tf_op jit(solution)/shard_map/kp,cpq->ckq/dot_general | solution.py:34
  351.7 5.1 %fusion.21 = f32[192,256,4]{1,0,2:T(8,128)S(1)} fusion(f32[192,4,256]{2,0,1:T(8,128)S(1)} %fusion.2, f32[1,192,64,8,4]{1,3,4,2,0:T(8,128)S(1)} %get-tuple-element.7), kind=kOutput, calls=%fused_computation.41 | convolution fusion | flops 1210187776 | bytes 3145728 | tf_op jit(solution)/shard_map/kp,cpq->ckq/dot_general | solution.py:34
  357.2 33.9 %all_to_all.64 = f32[192,256,4]{0,2,1:T(4,128)S(1)} all-to-all(f32[192,256,4]{0,2,1:T(4,128)S(1)} %copy.77), channel_id=1, replica_groups=mesh['seq'=64,'grp'=4] {'seq'}, dimensions={1} | all-to-all | bytes 1572864 | tf_op jit(solution)/shard_map/all_to_all | solution.py:126
  392.3 1.8 fusion.14
  395.9 26.9 %reduce-scatter.4.cloned.1.call-done = bf16[192,1024]{1,0:T(8,128)(2,1)} async-done(((bf16[768,1024]{1,0:T(8,128)(2,1)}), bf16[192,1024]{1,0:T(8,128)(2,1)}) %reduce-scatter.4.cloned.1.call-update) | async-done | bytes 393232 | tf_op jit(solution)/shard_map/reduce_scatter | solution.py:135
  (45 shorter events, 15.5 us)
Async XLA Ops:
  6.5 34.2 %copy-start = (bf16[3,192,768]{2,1,0:T(8,128)(2,1)S(1)}, bf16[3,192,768]{2,1,0:T(8,128)(2,1)}, u32[]{:S(2)}) copy-start(bf16[3,192,768]{2,1,0:T(8,128)(2,1)} %param.7) | copy-start | bytes 2654212
  6.5 34.2 %all-gather.2.cloned.1.call-start = ((), (), s32[]{:S(2)}) async-start(), calls=%async_computation.5 | async-start | bytes 1966080 | tf_op jit(solution)/shard_map/all_gather | solution.py:88
  44.3 4.9 %copy-start.8 = (f32[3,3,192]{2,1,0:T(4,128)S(1)}, f32[3,3,192]{2,1,0:T(4,128)}, u32[]{:S(2)}) copy-start(f32[3,3,192]{2,1,0:T(4,128)} %param.8) | copy-start | bytes 20740
  46.0 3.9 collective-permute-start
  51.2 1.7 copy-start.3
  54.2 30.8 %all-to-all-start = ((bf16[192,4,256]{0,1,2:T(4,128)(2,1)}), bf16[192,4,256]{0,1,2:T(4,128)(2,1)S(1)}, u32[]{:S(2)}, u32[]{:S(2)}) async-start(bf16[192,4,256]{0,1,2:T(4,128)(2,1)} %copy.59), calls=%async_computation | async-start | bytes 1048576 | tf_op jit(solution)/shard_map/all_to_all | solution.py:107
  99.0 100.3 %all-to-all-start.1 = ((f32[2,192,512,4]{1,3,0,2:T(4,128)}), f32[2,192,512,4]{1,3,0,2:T(4,128)}, u32[]{:S(2)}, u32[]{:S(2)}) async-start(f32[2,192,512,4]{1,3,0,2:T(4,128)} %copy.63), calls=%async_computation.1 | async-start | bytes 8388608 | tf_op jit(solution)/shard_map/all_to_all | solution.py:117
  106.6 316.2 %reduce-scatter.4.cloned.1.call-start = ((), (), s32[]{:S(2)}) async-start(), calls=%async_computation.6 | async-start | bytes 1966080 | tf_op jit(solution)/shard_map/reduce_scatter | solution.py:135
  208.4 3.5 copy-start.4
  216.6 4.0 copy-start.2
  216.6 4.0 copy-start.5
  220.6 2.5 copy-start.6
  391.4 1.0 copy-start.7
  391.4 1.0 copy-start.9
  394.2 28.7 %copy-start.1 = (bf16[3,192,768]{2,1,0:T(8,128)(2,1)S(1)}, bf16[3,192,768]{2,1,0:T(8,128)(2,1)}, u32[]{:S(2)}) copy-start(bf16[3,192,768]{2,1,0:T(8,128)(2,1)} %param.7) | copy-start | bytes 2654212
Sparse Core Ops, SparseCore 0:
  9.2 31.5 all-gather.1
  396.0 26.7 reduce-scatter.3
where the time goes:
time: 438 us; the launch traced here: 430 us
  waiting for transfers between devices  159 us (36%)
  blocking collectives  136 us (31%)
  matrix products  45.1 us (10%)
  starting transfers between devices  37.1 us (8%)
  local copies, waits for them, and re-layouts  33.3 us (8%)
  between operations  13.9 us (3%)
  other arithmetic  5.52 us (1%)
    all_to_all x1, blocking collectives, shards(): lax.all_to_all(jnp.stack(rotated_back), 'seq', split_axis=3, concat_axis=...  102 us
    all_to_all x1, waiting for transfers between devices, shards(): lax.all_to_all(jnp.stack(twisted), 'seq', split_axis=2, concat_axis=3, ti...  80.2 us
    all_to_all x1, blocking collectives, shards(): lax.all_to_all(real_out, 'seq', split_axis=1, concat_axis=2, tiled=True)  33.9 us
    all_gather x1, waiting for transfers between devices, shards(): shard_part = lax.all_gather(tokens, 'grp', axis=0, tiled=True)  33.5 us
    reduce_scatter x1, waiting for transfers between devices, shards(): lax.psum_scatter(partial_value.astype(jnp.bfloat16), 'grp', scatter_dimen...  26.9 us
    dot_general x8, matrix products, exact_mix(): jnp.einsum('kb,cjb->cjk', tables, values, precision=lax.Precision.HIGHEST...  23 us
    dot_general x4, matrix products, exact_rows(): jnp.einsum('kp,cpq->ckq', tables, values, precision=lax.Precision.HIGHEST...  16.7 us
    all_to_all x1, waiting for transfers between devices, shards(): lax.all_to_all(blocks, 'seq', split_axis=2, concat_axis=1, tiled=True)  16.6 us
  transfers between devices with their start and end apart: 5, of which 5 were waited for; matrix products, arithmetic and copies ran while one was open for 0% of the time, Pallas kernels for 0%

commit v1 on v0

v1 whole, which is shorter than its diff:
```python
import math

import jax
import jax.numpy as jnp
import numpy as np
from jax import lax
from jax.experimental import pallas as pl
from jax.experimental.pallas import tpu as pltpu
from jax.sharding import PartitionSpec as P

COLS = 256
FREQS = 512
LANES = 128
BF16 = jnp.bfloat16
F32 = jnp.float32


def unit_circle(rows, cols, period):
    angle = (np.outer(rows, cols) % period) * (2.0 * math.pi / period)
    return np.cos(angle), np.sin(angle)


def transform_tables(shard_count, rows_dev):
    half = shard_count * rows_dev
    order = (np.arange(shard_count)[None, :] * rows_dev + np.arange(rows_dev)[:, None]).reshape(-1)
    freqs = np.arange(2 * half)
    cols = np.arange(COLS)
    padded = 2 * half * COLS
    cos1, sin1 = unit_circle(freqs, order, 2 * half)
    cos2, sin2 = unit_circle(cols, cols, COLS)
    cost, sint = unit_circle(freqs, cols, padded)
    first = np.concatenate([cos1, -sin1], 0)
    forward = np.block([[cos2, -sin2], [sin2, cos2]])
    backward = np.block([[cos2, sin2], [-sin2, cos2]])
    last = np.concatenate([cos1.T, -sin1.T], 1) / padded
    as_bf16 = [jnp.asarray(t, BF16) for t in (first, forward, backward, last)]
    return as_bf16 + [jnp.asarray(t, F32) for t in (cost, sint)]


def pack_spectra_body(spec_ref, out_ref):
    joined = jnp.concatenate([spec_ref[0], spec_ref[1]], axis=1)
    out_ref[...] = joined.reshape(out_ref.shape).astype(BF16)


def pack_spectra(spectra, shard_count):
    _, channels, rows, cols = spectra.shape
    per_dest = channels // shard_count
    steps = 8
    return pl.pallas_call(
        pack_spectra_body,
        grid=(steps,),
        in_specs=[pl.BlockSpec((2, channels // steps, rows, cols), lambda i: (0, i, 0, 0))],
        out_specs=pl.BlockSpec((shard_count // steps, per_dest, 2 * rows, cols), lambda i: (i, 0, 0, 0)),
        out_shape=jax.ShapeDtypeStruct((shard_count, per_dest, 2 * rows, cols), BF16),
        cost_estimate=pl.CostEstimate(flops=0, bytes_accessed=6 * spectra.size, transcendentals=0),
        name="pack_spectra",
    )(spectra)


def project_body(grp_ref, own_ref, far_ref, near_ref, diag_ref, weight_ref, taps_ref,
                 message_ref, signal_ref, gate_ref, token_ref, stream_ref, spread_ref):
    channels = own_ref.shape[0]
    width = own_ref.shape[1]
    grp = grp_ref[0]
    for mask, ref in ((0, own_ref), (2, far_ref), (1, near_ref), (3, diag_ref)):
        start = pl.multiple_of((grp ^ mask) * channels, 64)
        token_ref[pl.ds(start, channels), :] = ref[...]
    step = 384
    for col in range(0, width, step):
        stream_ref[:, col:col + step] = jnp.dot(
            weight_ref[...], token_ref[:, col:col + step], preferred_element_type=F32
        )
    rows = 16

    def chunk(index, carry):
        row = pl.multiple_of(index * rows, rows)
        smooth = []
        for s in range(3):
            x = stream_ref[pl.ds(s * channels + row, rows), :].astype(BF16).astype(F32)
            w = [taps_ref[pl.ds(row, rows), 3 * tap + s:3 * tap + s + 1] for tap in range(3)]
            y = w[0] * x + w[1] * pltpu.roll(x, 1, 1) + w[2] * pltpu.roll(x, 2, 1)
            smooth.append(y[:, LANES:])
        gate_ref[pl.ds(row, rows), :] = smooth[0].astype(BF16)
        signal = smooth[2] * smooth[1]
        signal_ref[pl.ds(row, rows), :] = signal.astype(BF16)
        for part in range(8):
            spread_ref[pl.ds(row * 8 + part, rows, stride=8), :] = signal[:, part * LANES:(part + 1) * LANES]
        return carry

    lax.fori_loop(0, channels // rows, chunk, 0)
    message_ref[...] = spread_ref[...].astype(BF16)


def project(grp, own, far, near, diag, weight, taps):
    channels, width = own.shape
    tok = width - LANES
    vmem = pl.BlockSpec(memory_space=pltpu.VMEM)
    return pl.pallas_call(
        project_body,
        in_specs=[pl.BlockSpec(memory_space=pltpu.SMEM)] + [vmem] * 6,
        out_specs=[vmem] * 3,
        out_shape=[
            jax.ShapeDtypeStruct((channels * 8, LANES), BF16),
            jax.ShapeDtypeStruct((channels, tok), BF16),
            jax.ShapeDtypeStruct((channels, tok), BF16),
        ],
        scratch_shapes=[
            pltpu.VMEM((4 * channels, width), BF16),
            pltpu.VMEM((3 * channels, width), F32),
            pltpu.VMEM((channels * 8, LANES), F32),
        ],
        compiler_params=pltpu.CompilerParams(vmem_limit_bytes=40 << 20),
        cost_estimate=pl.CostEstimate(flops=2 * 3 * channels * 4 * channels * width,
                                      bytes_accessed=6 << 20, transcendentals=0),
        name="project",
    )(grp, own, far, near, diag, weight, taps)


def convolve_body(x_ref, h_ref, first_ref, forward_ref, backward_ref, last_ref, cos_ref, sin_ref,
                  out_ref, spread_ref, grid_ref, mid_ref, tall_ref):
    shards, _, pieces, lanes = x_ref.shape
    rows_dev = pieces // 2
    freqs = cos_ref.shape[0]
    spread_ref[...] = x_ref[...].astype(F32).reshape(shards * pieces, lanes)
    for a in range(rows_dev):
        for h in range(2):
            grid_ref[a * shards:(a + 1) * shards, h * lanes:(h + 1) * lanes] = spread_ref[
                pl.ds(2 * a + h, shards, stride=pieces), :].astype(BF16)
    wave = jnp.dot(first_ref[...], grid_ref[...], preferred_element_type=F32)
    real, imag = wave[:freqs], wave[freqs:]
    cosine, sine = cos_ref[...], sin_ref[...]
    mid_ref[:, :COLS] = (real * cosine + imag * sine).astype(BF16)
    mid_ref[:, COLS:] = (imag * cosine - real * sine).astype(BF16)
    freq = jnp.dot(mid_ref[...], forward_ref[...], preferred_element_type=F32)
    real, imag = freq[:, :COLS], freq[:, COLS:]
    response = h_ref[...].astype(F32)
    half = h_ref.shape[2] // 2
    h_real = response[:, 0, :half].reshape(freqs, COLS)
    h_imag = response[:, 0, half:].reshape(freqs, COLS)
    mid_ref[:, :COLS] = (real * h_real - imag * h_imag).astype(BF16)
    mid_ref[:, COLS:] = (real * h_imag + imag * h_real).astype(BF16)
    back = jnp.dot(mid_ref[...], backward_ref[...], preferred_element_type=F32)
    real, imag = back[:, :COLS], back[:, COLS:]
    tall_ref[:freqs, :] = (real * cosine - imag * sine).astype(BF16)
    tall_ref[freqs:, :] = (imag * cosine + real * sine).astype(BF16)
    out = jnp.dot(last_ref[...], tall_ref[...], preferred_element_type=F32)
    for a in range(rows_dev):
        for h in range(2):
            spread_ref[pl.ds(2 * a + h, shards, stride=pieces), :] = out[
                a * shards:(a + 1) * shards, h * lanes:(h + 1) * lanes]
    out_ref[...] = spread_ref[...].reshape(out_ref.shape).astype(BF16)


def convolve(x, response):
    shards, channels, pieces, lanes = x.shape
    tables = transform_tables(shards, pieces // 2)
    freqs = shards * pieces
    block = pl.BlockSpec((shards, 1, pieces, lanes), lambda c: (0, c, 0, 0))
    whole = [pl.BlockSpec(t.shape, lambda c: (0, 0)) for t in tables]
    return pl.pallas_call(
        convolve_body,
        grid=(channels,),
        in_specs=[block, pl.BlockSpec((shards, 1, *response.shape[2:]), lambda c: (0, c, 0, 0)), *whole],
        out_specs=block,
        out_shape=jax.ShapeDtypeStruct(x.shape, BF16),
        scratch_shapes=[
            pltpu.VMEM((shards * pieces, lanes), F32),
            pltpu.VMEM((freqs // 2, COLS), BF16),
            pltpu.VMEM((freqs, 2 * COLS), BF16),
            pltpu.VMEM((2 * freqs, COLS), BF16),
        ],
        compiler_params=pltpu.CompilerParams(vmem_limit_bytes=40 << 20),
        cost_estimate=pl.CostEstimate(flops=3 << 30, bytes_accessed=6 << 20, transcendentals=0),
        name="convolve",
    )(x, response, *tables)


def gated_body(y_ref, signal_ref, gate_ref, bias_ref, out_ref, spread_ref):
    channels = out_ref.shape[0]
    spread_ref[...] = y_ref[...].astype(F32)
    bias = bias_ref[...]
    for part in range(8):
        cols = slice(part * LANES, (part + 1) * LANES)
        y = spread_ref[pl.ds(part, channels, stride=8), :]
        direct = bias * signal_ref[:, cols].astype(F32)
        out_ref[:, cols] = (gate_ref[:, cols].astype(F32) * (y + direct)).astype(BF16)


def gated(y, signal, gate, bias):
    vmem = pl.BlockSpec(memory_space=pltpu.VMEM)
    return pl.pallas_call(
        gated_body,
        in_specs=[vmem] * 4,
        out_specs=vmem,
        out_shape=jax.ShapeDtypeStruct(signal.shape, BF16),
        scratch_shapes=[pltpu.VMEM(y.shape, F32)],
        cost_estimate=pl.CostEstimate(flops=4 * y.size, bytes_accessed=8 * y.size, transcendentals=0),
        name="gated",
    )(y, signal, gate, bias)


def mixed_body(*refs):
    values, weights, out_ref = refs[:4], refs[4:8], refs[8]
    total = jnp.dot(weights[0][...], values[0][...], preferred_element_type=F32)
    for w, v in zip(weights[1:], values[1:]):
        total = total + jnp.dot(w[...], v[...], preferred_element_type=F32)
    out_ref[...] = total.astype(BF16)


def mixed(values, weights):
    vmem = pl.BlockSpec(memory_space=pltpu.VMEM)
    channels, tok = values[0].shape
    return pl.pallas_call(
        mixed_body,
        in_specs=[vmem] * 8,
        out_specs=vmem,
        out_shape=jax.ShapeDtypeStruct((weights[0].shape[0], tok), BF16),
        compiler_params=pltpu.CompilerParams(vmem_limit_bytes=32 << 20),
        cost_estimate=pl.CostEstimate(flops=8 * channels * channels * tok, bytes_accessed=3 << 20, transcendentals=0),
        name="mixed",
    )(*values, *weights)


def swapped(block, mask):
    return lax.ppermute(block, "grp", [(i, i ^ mask) for i in range(4)])


def gathered(block):
    far = swapped(block, 2)
    near = swapped(block, 1)
    return block, far, near, swapped(far, 1)


def shards(tokens, in_weight, short_weight, filter_bias, spectra, out_weight):
    shard_count = lax.axis_size("seq")
    grp = lax.axis_index("grp")
    channels, tok = tokens.shape
    per_dest = channels // shard_count

    packed = pack_spectra(spectra, shard_count)
    packed, tokens = lax.optimization_barrier((packed, tokens))
    response = lax.all_to_all(packed, "seq", 0, 0, tiled=True)

    route = [(i, i + 1) for i in range(shard_count - 1)]
    halo = lax.ppermute(tokens[:, -LANES:], "seq", route)
    extended = gathered(jnp.concatenate([halo, tokens], 1))
    taps = jnp.transpose(short_weight, (2, 0, 1)).reshape(channels, 9)
    message, signal, gate = project(
        grp.reshape(1).astype(jnp.int32), *extended, in_weight.reshape(3 * channels, -1), taps
    )
    turned = out_weight.T
    parts = [
        lax.dynamic_slice_in_dim(turned, (grp ^ mask) * channels, channels, 0) for mask in range(4)
    ]
    weights = [parts[0]] + [swapped(parts[m], m) for m in (2, 1, 3)]
    message, response, *weights = lax.optimization_barrier((message, response, *weights))
    columns = lax.all_to_all(
        message.reshape(shard_count, per_dest, 8, LANES), "seq", 0, 0, tiled=True
    )
    result = convolve(columns, response)
    back = lax.all_to_all(result, "seq", 0, 0, tiled=True).reshape(channels * 8, LANES)

    weighted = gated(back, signal, gate, filter_bias[:, None])
    return mixed(gathered(weighted), weights)


def solution(mesh):
    in_specs = (
        P("grp", "seq"),
        P(None, "grp", None),
        P(None, None, "grp"),
        P("grp"),
        P(None, "grp", "seq", None),
        P("grp", None),
    )
    out_specs = P("grp", "seq")
    return jax.shard_map(shards, mesh=mesh, in_specs=in_specs, out_specs=out_specs, check_vma=False)
```

time: 438 us -> 160 us (0.37); the launches traced: 430 us -> 159 us
  blocking collectives: 136 us -> 29.9 us
  waiting for transfers between devices: 159 us -> 54.6 us
  matrix products: 45.1 us -> 0 us
  local copies, waits for them, and re-layouts: 33.3 us -> 12.9 us
  Pallas kernels: 0 us -> 19.5 us
  between operations: 13.9 us -> 0.17 us
  other arithmetic: 5.52 us -> 0 us
  starting transfers between devices: 37.1 us -> 41.7 us
    all_to_all x2 -> x1, blocking collectives: 136 us -> 29.9 us  [shards(): lax.all_to_all(message.reshape(shard_count, per_dest, 8, LANES), 'seq', 0...]
    all_to_all x2, waiting for transfers between devices: 96.8 us -> 13.8 us  [the longest x1 13.8 us: shards(): lax.all_to_all(result, 'seq', 0, 0, tiled=True).reshape(channels * 8, LANES)]
    dot_general x14 -> x0, matrix products: 45.1 us -> none  [the longest x8 23 us: exact_mix(): jnp.einsum('kb,cjb->cjk', tables, values, precision=lax.Precision.HIGHEST...]
    ppermute x1 -> x10, waiting for transfers between devices: 0.7 us -> 40.8 us  [the longest x1 28.7 us: shards(): halo = lax.ppermute(tokens[:, -LANES:], 'seq', route)]
    all_gather x1 -> x0, waiting for transfers between devices: 33.5 us -> none  [shards(): shard_part = lax.all_gather(tokens, 'grp', axis=0, tiled=True)]
    reduce_scatter x1 -> x0, waiting for transfers between devices: 26.9 us -> none  [shards(): lax.psum_scatter(partial_value.astype(jnp.bfloat16), 'grp', scatter_dimen...]
    pallas_call x0 -> x5, Pallas kernels: none -> 19.5 us  [the longest x1 5.76 us: pack_spectra(): pl.pallas_call(pack_spectra_body, grid=(steps,), in_specs=[pl.BlockSpec((...]
    ppermute x1 -> x10, starting transfers between devices: 3.18 us -> 20.5 us  [the longest x9 17.6 us: swapped(): return lax.ppermute(block, 'grp', [(i, i ^ mask) for i in range(4)])]
  transfers between devices with their start and end apart: 5 -> 12, of which waited for: 5 -> 5; matrix products, arithmetic and copies ran while one was open for 0% -> 1% of each run, Pallas kernels for 0% -> 3%
where the time goes in v1:
time: 160 us; the launch traced here: 159 us
  waiting for transfers between devices  54.6 us (34%)
  starting transfers between devices  41.7 us (26%)
  blocking collectives  29.9 us (19%)
  Pallas kernels  19.5 us (12%)
  local copies, waits for them, and re-layouts  12.9 us (8%)
    all_to_all x1, blocking collectives, shards(): lax.all_to_all(message.reshape(shard_count, per_dest, 8, LANES), 'seq', 0...  29.9 us
    ppermute x1, waiting for transfers between devices, shards(): halo = lax.ppermute(tokens[:, -LANES:], 'seq', route)  28.7 us
    ppermute x9, starting transfers between devices, swapped(): return lax.ppermute(block, 'grp', [(i, i ^ mask) for i in range(4)])  17.6 us
    all_to_all x1, starting transfers between devices, shards(): response = lax.all_to_all(packed, 'seq', 0, 0, tiled=True)  15.2 us
    all_to_all x1, waiting for transfers between devices, shards(): lax.all_to_all(result, 'seq', 0, 0, tiled=True).reshape(channels * 8, LANES)  13.8 us
    ppermute x9, waiting for transfers between devices, swapped(): return lax.ppermute(block, 'grp', [(i, i ^ mask) for i in range(4)])  12.1 us
    unnamed x35, local copies, waits for them, and re-layouts  11.7 us
    all_to_all x1, starting transfers between devices, shards(): lax.all_to_all(result, 'seq', 0, 0, tiled=True).reshape(channels * 8, LANES)  6.03 us
  transfers between devices with their start and end apart: 12, of which 5 were waited for; matrix products, arithmetic and copies ran while one was open for 1% of the time, Pallas kernels for 3%

profile of v1, /device:TPU:1, one launch (start us, length us, event | category | flops | bytes accessed | tf_op | source)
XLA Modules:
  0.0 158.8 jit_solution(3684379544393075696)
XLA Ops:
  0.0 5.8 %pack_spectra.1 = bf16[64,3,16,256]{3,2,1,0:T(8,128)(2,1)} custom-call(f32[2,192,8,256]{3,2,1,0:T(8,128)} %spec_ref.1), custom_call_target="tpu_custom_call" | custom-call | bytes 4718592 | tf_op jit(solution)/shard_map/pack_spectra/pallas_call | solution.py:49
  5.8 15.2 %all-to-all-start = ((bf16[64,3,16,256]{3,2,1,0:T(8,128)(2,1)}), bf16[64,3,16,256]{3,2,1,0:T(8,128)(2,1)S(1)}, u32[]{:S(2)}, u32[]{:S(2)}) async-start(bf16[64,3,16,256]{3,2,1,0:T(8,128)(2,1)} %pack_spectra.1), calls=%async_computation | async-start | bytes 3145728 | tf_op jit(solution)/shard_map/all_to_all | solution.py:242
  21.1 2.9 %collective-permute-start = (bf16[192,128]{1,0:T(8,128)(2,1)S(1)}, bf16[192,128]{1,0:T(8,128)(2,1)S(1)}, u32[]{:S(2)}, u32[]{:S(2)}) collective-permute-start(bf16[192,128]{1,0:T(8,128)(2,1)S(1)} %slice.3), channel_id=1, source_target_pairs={{0,4},{4,8},{8,12},{12,16},{16,20},{20,24},{24,28},{28,32},{32,36}... | collective-permute-start | bytes 147464 | tf_op jit(solution)/shard_map/ppermute | solution.py:245
  24.0 28.7 %collective-permute-done = bf16[192,128]{1,0:T(8,128)(2,1)S(1)} collective-permute-done((bf16[192,128]{1,0:T(8,128)(2,1)S(1)}, bf16[192,128]{1,0:T(8,128)(2,1)S(1)}, u32[]{:S(2)}, u32[]{:S(2)}) %collective-permute-start) | collective-permute-done | bytes 49184 | tf_op jit(solution)/shard_map/ppermute | solution.py:245
  53.2 3.0 %collective-permute-start.2 = (bf16[192,1152]{1,0:T(8,128)(2,1)S(1)}, bf16[192,1152]{1,0:T(8,128)(2,1)}, u32[]{:S(2)}, u32[]{:S(2)}) collective-permute-start(bf16[192,1152]{1,0:T(8,128)(2,1)S(1)} %constant_dynamic-update-slice_fusion.own_ref), channel_id=1, source_target_pairs={{0,1},{1,0},{2,3},{3,2},{4,5},{5,4},{6,7},{7,6},{8,9},{9,8},{10,11... | collective-permute-start | bytes 1327112 | tf_op jit(solution)/shard_map/ppermute | solution.py:225
  56.1 8.6 %collective-permute-done.1.far_ref = bf16[192,1152]{1,0:T(8,128)(2,1)S(1)} collective-permute-done((bf16[192,1152]{1,0:T(8,128)(2,1)S(1)}, bf16[192,1152]{1,0:T(8,128)(2,1)S(1)}, u32[]{:S(2)}, u32[]{:S(2)}) %collective-permute-start.1) | collective-permute-done | bytes 442400 | tf_op jit(solution)/shard_map/ppermute | solution.py:225
  64.7 2.3 %collective-permute-start.3 = (bf16[192,1152]{1,0:T(8,128)(2,1)S(1)}, bf16[192,1152]{1,0:T(8,128)(2,1)}, u32[]{:S(2)}, u32[]{:S(2)}) collective-permute-start(bf16[192,1152]{1,0:T(8,128)(2,1)S(1)} %collective-permute-done.1.far_ref), channel_id=1, source_target_pairs={{0,1},{1,0},{2,3},{3,2},{4,5},{5,4},{6,7},{7,6},{8,9},{9,8},{10,11... | collective-permute-start | bytes 1327112 | tf_op jit(solution)/shard_map/ppermute | solution.py:225
  67.3 1.0 collective-permute-start.4
  68.8 0.7 copy.27
  70.5 1.2 copy-done.3
  71.6 5.0 %project.1 = (bf16[1536,128]{1,0:T(8,128)(2,1)S(1)}, bf16[192,1024]{1,0:T(8,128)(2,1)S(1)}, bf16[192,1024]{1,0:T(8,128)(2,1)S(1)}) custom-call(s32[1]{0:T(128)} %bitcast.grp_ref, bf16[192,1152]{1,0:T(8,128)(2,1)S(1)} %constant_dynamic-update-slice_fusion.own_ref, bf16[192,1152]{1,0:T(8,128)(2,1)S(1)} %collective-permute-done.1.far_ref, ...), custom_call_target="tpu_custom_call" | custom-call | flops 1019215872 | bytes 6291456 | tf_op jit(solution)/shard_map/project/pallas_call | solution.py:98
  76.6 0.8 copy-done.1
  77.4 0.7 copy-done.2
  78.1 29.9 %all_to_all.15.x_ref = bf16[64,3,8,128]{3,2,1,0:T(8,128)(2,1)S(1)} all-to-all(bf16[64,3,8,128]{3,2,1,0:T(8,128)(2,1)S(1)} %bitcast.13), channel_id=1, replica_groups=mesh['seq'=64,'grp'=4] {'seq'}, dimensions={0} | all-to-all | bytes 786432 | tf_op jit(solution)/shard_map/all_to_all | solution.py:257
  108.0 1.0 copy-done.4
  109.1 1.0 copy-done.5
  110.1 1.0 copy-done.6
  111.2 1.0 copy-done.7
  112.2 1.0 copy-done.8
  113.3 1.0 copy-done.9
  114.3 5.1 %convolve.1 = bf16[64,3,8,128]{3,2,1,0:T(8,128)(2,1)} custom-call(bf16[64,3,8,128]{3,2,1,0:T(8,128)(2,1)S(1)} %all_to_all.15.x_ref, bf16[64,3,16,256]{3,2,1,0:T(8,128)(2,1)S(1)} %all-to-all-done.h_ref, bf16[1024,256]{1,0:T(8,128)(2,1)S(1)} %copy-done.4, bf16[512,512]{1,0:T(8,128)(2,1)S(1)} %copy-done.5, bf16[512,512]{1,0:T(8,128)(2,1)S(1)} %copy-done.6, ...), custom_call_target="tpu_custom_call" | custom-call | flops 3221225472 | bytes 6291456 | tf_op jit(solution)/shard_map/convolve/pallas_call | solution.py:160
  119.4 6.0 %all-to-all-start.2 = ((bf16[64,3,8,128]{3,2,1,0:T(8,128)(2,1)}), bf16[64,3,8,128]{3,2,1,0:T(8,128)(2,1)S(1)}, u32[]{:S(2)}, u32[]{:S(2)}) async-start(bf16[64,3,8,128]{3,2,1,0:T(8,128)(2,1)} %convolve.1), calls=%async_computation.2 | async-start | bytes 786432 | tf_op jit(solution)/shard_map/all_to_all | solution.py:261
  125.5 0.8 copy.23.bias_ref
  126.2 13.8 %all-to-all-done.2 = bf16[64,3,8,128]{3,2,1,0:T(8,128)(2,1)S(1)} async-done(((bf16[64,3,8,128]{3,2,1,0:T(8,128)(2,1)}), bf16[64,3,8,128]{3,2,1,0:T(8,128)(2,1)S(1)}, u32[]{:S(2)}, u32[]{:S(2)}) %all-to-all-start.2) | async-done | bytes 393248 | tf_op jit(solution)/shard_map/all_to_all | solution.py:261
  140.0 0.7 copy-done.10
  140.8 2.3 %gated.1.refs_0_ = bf16[192,1024]{1,0:T(8,128)(2,1)} custom-call(bf16[1536,128]{1,0:T(8,128)(2,1)} %bitcast.15, bf16[192,1024]{1,0:T(8,128)(2,1)} %copy-done.1, bf16[192,1024]{1,0:T(8,128)(2,1)} %copy-done.2, f32[192,1]{1,0:T(8,128)} %copy.23.bias_ref), custom_call_target="tpu_custom_call" | custom-call | flops 786432 | bytes 1572864 | tf_op jit(solution)/shard_map/gated/pallas_call | solution.py:191
  143.6 4.2 %collective-permute-start.8 = (bf16[192,1024]{1,0:T(8,128)(2,1)}, bf16[192,1024]{1,0:T(8,128)(2,1)S(1)}, u32[]{:S(2)}, u32[]{:S(2)}) collective-permute-start(bf16[192,1024]{1,0:T(8,128)(2,1)} %gated.1.refs_0_), channel_id=1, source_target_pairs={{0,1},{1,0},{2,3},{3,2},{4,5},{5,4},{6,7},{7,6},{8,9},{9,8},{10,11... | collective-permute-start | bytes 1179656 | tf_op jit(solution)/shard_map/ppermute | solution.py:225
  147.8 2.1 %collective-permute-done.7.refs_1_ = bf16[192,1024]{1,0:T(8,128)(2,1)S(1)} collective-permute-done((bf16[192,1024]{1,0:T(8,128)(2,1)}, bf16[192,1024]{1,0:T(8,128)(2,1)S(1)}, u32[]{:S(2)}, u32[]{:S(2)}) %collective-permute-start.7) | collective-permute-done | bytes 393248 | tf_op jit(solution)/shard_map/ppermute | solution.py:225
  149.9 5.2 %collective-permute-start.9 = (bf16[192,1024]{1,0:T(8,128)(2,1)S(1)}, bf16[192,1024]{1,0:T(8,128)(2,1)S(1)}, u32[]{:S(2)}, u32[]{:S(2)}) collective-permute-start(bf16[192,1024]{1,0:T(8,128)(2,1)S(1)} %collective-permute-done.7.refs_1_), channel_id=1, source_target_pairs={{0,1},{1,0},{2,3},{3,2},{4,5},{5,4},{6,7},{7,6},{8,9},{9,8},{10,11... | collective-permute-start | bytes 1179656 | tf_op jit(solution)/shard_map/ppermute | solution.py:225
  155.1 1.3 collective-permute-done.9.refs_3_
  156.5 1.0 copy-done
  157.4 1.3 mixed.1
  (39 shorter events, 2.7 us)
Async XLA Ops:
  5.8 15.3 %copy-start.12 = (bf16[192,1024]{1,0:T(8,128)(2,1)S(1)}, bf16[192,1024]{1,0:T(8,128)(2,1)}, u32[]{:S(2)}) copy-start(bf16[192,1024]{1,0:T(8,128)(2,1)} %param.12) | copy-start | bytes 1179652
  5.8 61.2 %copy-start.11 = (bf16[192,768]{1,0:T(8,128)(2,1)S(1)}, bf16[192,768]{1,0:T(8,128)(2,1)}, u32[]{:S(2)}) copy-start(bf16[192,768]{1,0:T(8,128)(2,1)} %param.17) | copy-start | bytes 884740
  5.8 72.4 %all-to-all-start = ((bf16[64,3,16,256]{3,2,1,0:T(8,128)(2,1)}), bf16[64,3,16,256]{3,2,1,0:T(8,128)(2,1)S(1)}, u32[]{:S(2)}, u32[]{:S(2)}) async-start(bf16[64,3,16,256]{3,2,1,0:T(8,128)(2,1)} %pack_spectra.1), calls=%async_computation | async-start | bytes 3145728 | tf_op jit(solution)/shard_map/all_to_all | solution.py:242
  21.0 49.2 %copy-start.13 = (f32[3,3,192]{2,1,0:T(4,128)S(1)}, f32[3,3,192]{2,1,0:T(4,128)}, u32[]{:S(2)}) copy-start(f32[3,3,192]{2,1,0:T(4,128)} %param.14) | copy-start | bytes 20740
  21.1 31.7 %collective-permute-start = (bf16[192,128]{1,0:T(8,128)(2,1)S(1)}, bf16[192,128]{1,0:T(8,128)(2,1)S(1)}, u32[]{:S(2)}, u32[]{:S(2)}) collective-permute-start(bf16[192,128]{1,0:T(8,128)(2,1)S(1)} %slice.3), channel_id=1, source_target_pairs={{0,4},{4,8},{8,12},{12,16},{16,20},{20,24},{24,28},{28,32},{32,36}... | collective-permute-start | bytes 147464 | tf_op jit(solution)/shard_map/ppermute | solution.py:245
  52.8 12.0 %collective-permute-start.1 = (bf16[192,1152]{1,0:T(8,128)(2,1)S(1)}, bf16[192,1152]{1,0:T(8,128)(2,1)S(1)}, u32[]{:S(2)}, u32[]{:S(2)}) collective-permute-start(bf16[192,1152]{1,0:T(8,128)(2,1)S(1)} %constant_dynamic-update-slice_fusion.own_ref), channel_id=1, source_target_pairs={{0,2},{1,3},{2,0},{3,1},{4,6},{5,7},{6,4},{7,5},{8,10},{9,11},{10,... | collective-permute-start | bytes 1327112 | tf_op jit(solution)/shard_map/ppermute | solution.py:225
  53.2 17.2 %collective-permute-start.2 = (bf16[192,1152]{1,0:T(8,128)(2,1)S(1)}, bf16[192,1152]{1,0:T(8,128)(2,1)}, u32[]{:S(2)}, u32[]{:S(2)}) collective-permute-start(bf16[192,1152]{1,0:T(8,128)(2,1)S(1)} %constant_dynamic-update-slice_fusion.own_ref), channel_id=1, source_target_pairs={{0,1},{1,0},{2,3},{3,2},{4,5},{5,4},{6,7},{7,6},{8,9},{9,8},{10,11... | collective-permute-start | bytes 1327112 | tf_op jit(solution)/shard_map/ppermute | solution.py:225
  64.7 5.7 %collective-permute-start.3 = (bf16[192,1152]{1,0:T(8,128)(2,1)S(1)}, bf16[192,1152]{1,0:T(8,128)(2,1)}, u32[]{:S(2)}, u32[]{:S(2)}) collective-permute-start(bf16[192,1152]{1,0:T(8,128)(2,1)S(1)} %collective-permute-done.1.far_ref), channel_id=1, source_target_pairs={{0,1},{1,0},{2,3},{3,2},{4,5},{5,4},{6,7},{7,6},{8,9},{9,8},{10,11... | collective-permute-start | bytes 1327112 | tf_op jit(solution)/shard_map/ppermute | solution.py:225
  67.3 10.8 %collective-permute-start.4 = (bf16[192,192]{1,0:T(8,128)(2,1)S(1)}, bf16[192,192]{1,0:T(8,128)(2,1)S(1)}, u32[]{:S(2)}, u32[]{:S(2)}) collective-permute-start(bf16[192,192]{1,0:T(8,128)(2,1)S(1)} %bitcast.16), channel_id=1, source_target_pairs={{0,2},{1,3},{2,0},{3,1},{4,6},{5,7},{6,4},{7,5},{8,10},{9,11},{10,... | collective-permute-start | bytes 221192 | tf_op jit(solution)/shard_map/ppermute | solution.py:225
  68.4 9.7 %collective-permute-start.5 = (bf16[192,192]{1,0:T(8,128)(2,1)S(1)}, bf16[192,192]{1,0:T(8,128)(2,1)S(1)}, u32[]{:S(2)}, u32[]{:S(2)}) collective-permute-start(bf16[192,192]{1,0:T(8,128)(2,1)S(1)} %bitcast.17), channel_id=1, source_target_pairs={{0,1},{1,0},{2,3},{3,2},{4,5},{5,4},{6,7},{7,6},{8,9},{9,8},{10,11... | collective-permute-start | bytes 221192 | tf_op jit(solution)/shard_map/ppermute | solution.py:225
  69.5 8.6 %collective-permute-start.6 = (bf16[192,192]{1,0:T(8,128)(2,1)}, bf16[192,192]{1,0:T(8,128)(2,1)S(1)}, u32[]{:S(2)}, u32[]{:S(2)}) collective-permute-start(bf16[192,192]{1,0:T(8,128)(2,1)} %bitcast.6), channel_id=1, source_target_pairs={{0,3},{1,2},{2,1},{3,0},{4,7},{5,6},{6,5},{7,4},{8,11},{9,10},{10,... | collective-permute-start | bytes 221192 | tf_op jit(solution)/shard_map/ppermute | solution.py:225
  70.4 1.2 copy-start.3
  76.6 0.8 copy-start.1
  77.4 0.7 copy-start.2
  108.0 1.0 copy-start.4
  109.1 1.0 copy-start.5
  110.1 1.0 copy-start.6
  111.2 1.0 copy-start.7
  112.2 1.0 copy-start.8
  113.3 1.0 copy-start.9
  114.3 11.2 %copy-start.14 = (f32[192]{0:T(256)S(1)}, f32[192]{0:T(256)}, u32[]{:S(2)}) copy-start(f32[192]{0:T(256)} %param.15) | copy-start | bytes 2308
  119.4 20.6 %all-to-all-start.2 = ((bf16[64,3,8,128]{3,2,1,0:T(8,128)(2,1)}), bf16[64,3,8,128]{3,2,1,0:T(8,128)(2,1)S(1)}, u32[]{:S(2)}, u32[]{:S(2)}) async-start(bf16[64,3,8,128]{3,2,1,0:T(8,128)(2,1)} %convolve.1), calls=%async_computation.2 | async-start | bytes 786432 | tf_op jit(solution)/shard_map/all_to_all | solution.py:261
  140.0 0.7 copy-start.10
  143.1 6.8 %collective-permute-start.7 = (bf16[192,1024]{1,0:T(8,128)(2,1)}, bf16[192,1024]{1,0:T(8,128)(2,1)S(1)}, u32[]{:S(2)}, u32[]{:S(2)}) collective-permute-start(bf16[192,1024]{1,0:T(8,128)(2,1)} %gated.1.refs_0_), channel_id=1, source_target_pairs={{0,2},{1,3},{2,0},{3,1},{4,6},{5,7},{6,4},{7,5},{8,10},{9,11},{10,... | collective-permute-start | bytes 1179656 | tf_op jit(solution)/shard_map/ppermute | solution.py:225
  143.6 11.5 %collective-permute-start.8 = (bf16[192,1024]{1,0:T(8,128)(2,1)}, bf16[192,1024]{1,0:T(8,128)(2,1)S(1)}, u32[]{:S(2)}, u32[]{:S(2)}) collective-permute-start(bf16[192,1024]{1,0:T(8,128)(2,1)} %gated.1.refs_0_), channel_id=1, source_target_pairs={{0,1},{1,0},{2,3},{3,2},{4,5},{5,4},{6,7},{7,6},{8,9},{9,8},{10,11... | collective-permute-start | bytes 1179656 | tf_op jit(solution)/shard_map/ppermute | solution.py:225
  149.9 6.5 %collective-permute-start.9 = (bf16[192,1024]{1,0:T(8,128)(2,1)S(1)}, bf16[192,1024]{1,0:T(8,128)(2,1)S(1)}, u32[]{:S(2)}, u32[]{:S(2)}) collective-permute-start(bf16[192,1024]{1,0:T(8,128)(2,1)S(1)} %collective-permute-done.7.refs_1_), channel_id=1, source_target_pairs={{0,1},{1,0},{2,3},{3,2},{4,5},{5,4},{6,7},{7,6},{8,9},{9,8},{10,11... | collective-permute-start | bytes 1179656 | tf_op jit(solution)/shard_map/ppermute | solution.py:225
  156.5 1.0 copy-start

commit v2 on v1

--- a/solution.py
+++ b/solution.py
@@ -29,32 +29,19 @@
     cos1, sin1 = unit_circle(freqs, order, 2 * half)
     cos2, sin2 = unit_circle(cols, cols, COLS)
     cost, sint = unit_circle(freqs, cols, padded)
-    first = np.concatenate([cos1, -sin1], 0)
+    first = np.concatenate([cos1, -sin1], 1)
     forward = np.block([[cos2, -sin2], [sin2, cos2]])
     backward = np.block([[cos2, sin2], [-sin2, cos2]])
-    last = np.concatenate([cos1.T, -sin1.T], 1) / padded
-    as_bf16 = [jnp.asarray(t, BF16) for t in (first, forward, backward, last)]
-    return as_bf16 + [jnp.asarray(t, F32) for t in (cost, sint)]
-
-
-def pack_spectra_body(spec_ref, out_ref):
-    joined = jnp.concatenate([spec_ref[0], spec_ref[1]], axis=1)
-    out_ref[...] = joined.reshape(out_ref.shape).astype(BF16)
+    last = np.concatenate([cos1.T, -sin1.T], 0) / padded
+    waves = np.concatenate([first, forward, backward, last], 0)
+    return jnp.asarray(waves, BF16), jnp.asarray(np.concatenate([cost, sint], 1), F32)
 
 
 def pack_spectra(spectra, shard_count):
     _, channels, rows, cols = spectra.shape
-    per_dest = channels // shard_count
-    steps = 8
-    return pl.pallas_call(
-        pack_spectra_body,
-        grid=(steps,),
-        in_specs=[pl.BlockSpec((2, channels // steps, rows, cols), lambda i: (0, i, 0, 0))],
-        out_specs=pl.BlockSpec((shard_count // steps, per_dest, 2 * rows, cols), lambda i: (i, 0, 0, 0)),
-        out_shape=jax.ShapeDtypeStruct((shard_count, per_dest, 2 * rows, cols), BF16),
-        cost_estimate=pl.CostEstimate(flops=0, bytes_accessed=6 * spectra.size, transcendentals=0),
-        name="pack_spectra",
-    )(spectra)
+    grouped = spectra.reshape(2, shard_count, channels // shard_count, rows, cols)
+    by_dest = jnp.transpose(grouped, (1, 2, 0, 3, 4)).astype(BF16)
+    return by_dest.reshape(shard_count, channels // shard_count, 2 * rows, cols)
 
 
 def project_body(grp_ref, own_ref, far_ref, near_ref, diag_ref, weight_ref, taps_ref,
@@ -109,67 +96,73 @@
             pltpu.VMEM((3 * channels, width), F32),
             pltpu.VMEM((channels * 8, LANES), F32),
         ],
-        compiler_params=pltpu.CompilerParams(vmem_limit_bytes=40 << 20),
+        compiler_params=pltpu.CompilerParams(vmem_limit_bytes=20 << 20),
         cost_estimate=pl.CostEstimate(flops=2 * 3 * channels * 4 * channels * width,
                                       bytes_accessed=6 << 20, transcendentals=0),
         name="project",
     )(grp, own, far, near, diag, weight, taps)
 
 
-def convolve_body(x_ref, h_ref, first_ref, forward_ref, backward_ref, last_ref, cos_ref, sin_ref,
-                  out_ref, spread_ref, grid_ref, mid_ref, tall_ref):
-    shards, _, pieces, lanes = x_ref.shape
+def convolve_body(x_ref, h_ref, wave_ref, twist_ref, out_ref,
+                  spread_ref, grid_ref, mid_ref, tall_ref, done_ref, sems):
+    shards, channels, pieces, lanes = x_ref.shape
     rows_dev = pieces // 2
-    freqs = cos_ref.shape[0]
-    spread_ref[...] = x_ref[...].astype(F32).reshape(shards * pieces, lanes)
-    for a in range(rows_dev):
-        for h in range(2):
-            grid_ref[a * shards:(a + 1) * shards, h * lanes:(h + 1) * lanes] = spread_ref[
-                pl.ds(2 * a + h, shards, stride=pieces), :].astype(BF16)
-    wave = jnp.dot(first_ref[...], grid_ref[...], preferred_element_type=F32)
-    real, imag = wave[:freqs], wave[freqs:]
-    cosine, sine = cos_ref[...], sin_ref[...]
-    mid_ref[:, :COLS] = (real * cosine + imag * sine).astype(BF16)
-    mid_ref[:, COLS:] = (imag * cosine - real * sine).astype(BF16)
-    freq = jnp.dot(mid_ref[...], forward_ref[...], preferred_element_type=F32)
-    real, imag = freq[:, :COLS], freq[:, COLS:]
-    response = h_ref[...].astype(F32)
+    freqs = twist_ref.shape[0]
     half = h_ref.shape[2] // 2
-    h_real = response[:, 0, :half].reshape(freqs, COLS)
-    h_imag = response[:, 0, half:].reshape(freqs, COLS)
-    mid_ref[:, :COLS] = (real * h_real - imag * h_imag).astype(BF16)
-    mid_ref[:, COLS:] = (real * h_imag + imag * h_real).astype(BF16)
-    back = jnp.dot(mid_ref[...], backward_ref[...], preferred_element_type=F32)
-    real, imag = back[:, :COLS], back[:, COLS:]
-    tall_ref[:freqs, :] = (real * cosine - imag * sine).astype(BF16)
-    tall_ref[freqs:, :] = (imag * cosine + real * sine).astype(BF16)
-    out = jnp.dot(last_ref[...], tall_ref[...], preferred_element_type=F32)
-    for a in range(rows_dev):
-        for h in range(2):
-            spread_ref[pl.ds(2 * a + h, shards, stride=pieces), :] = out[
-                a * shards:(a + 1) * shards, h * lanes:(h + 1) * lanes]
-    out_ref[...] = spread_ref[...].reshape(out_ref.shape).astype(BF16)
-
-
-def convolve(x, response):
+    first_ref, forward_ref, backward_ref = (wave_ref.at[pl.ds(i * freqs, freqs)] for i in range(3))
+    last = 3 * freqs
+    for c in range(channels):
+        spread_ref[...] = x_ref[:, c].astype(F32).reshape(shards * pieces, lanes)
+        for a in range(rows_dev):
+            for h in range(2):
+                grid_ref[a * shards:(a + 1) * shards, h * lanes:(h + 1) * lanes] = spread_ref[
+                    pl.ds(2 * a + h, shards, stride=pieces), :].astype(BF16)
+        real = jnp.dot(first_ref[:, :COLS], grid_ref[...], preferred_element_type=F32)
+        imag = jnp.dot(first_ref[:, COLS:], grid_ref[...], preferred_element_type=F32)
+        cosine, sine = twist_ref[:, :COLS], twist_ref[:, COLS:]
+        mid_ref[:, :COLS] = (real * cosine + imag * sine).astype(BF16)
+        mid_ref[:, COLS:] = (imag * cosine - real * sine).astype(BF16)
+        freq = jnp.dot(mid_ref[...], forward_ref[...], preferred_element_type=F32)
+        real, imag = freq[:, :COLS], freq[:, COLS:]
+        response = h_ref[:, c].astype(F32)
+        h_real = response[:, :half].reshape(freqs, COLS)
+        h_imag = response[:, half:].reshape(freqs, COLS)
+        mid_ref[:, :COLS] = (real * h_real - imag * h_imag).astype(BF16)
+        mid_ref[:, COLS:] = (real * h_imag + imag * h_real).astype(BF16)
+        back = jnp.dot(mid_ref[...], backward_ref[...], preferred_element_type=F32)
+        real, imag = back[:, :COLS], back[:, COLS:]
+        tall_ref[:freqs, :] = (real * cosine - imag * sine).astype(BF16)
+        tall_ref[freqs:, :] = (imag * cosine + real * sine).astype(BF16)
+        out = jnp.dot(wave_ref[last:last + COLS, :], tall_ref[:freqs], preferred_element_type=F32)
+        out += jnp.dot(wave_ref[last + COLS:, :], tall_ref[freqs:], preferred_element_type=F32)
+        for a in range(rows_dev):
+            for h in range(2):
+                spread_ref[pl.ds(2 * a + h, shards, stride=pieces), :] = out[
+                    a * shards:(a + 1) * shards, h * lanes:(h + 1) * lanes]
+        done_ref[c] = spread_ref[...].reshape(shards, pieces, lanes).astype(BF16)
+        pltpu.make_async_copy(done_ref.at[c], out_ref.at[:, c], sems.at[c]).start()
+    for c in range(channels):
+        pltpu.make_async_copy(done_ref.at[c], out_ref.at[:, c], sems.at[c]).wait()
+
+
+def convolve(x, response, tables):
     shards, channels, pieces, lanes = x.shape
-    tables = transform_tables(shards, pieces // 2)
     freqs = shards * pieces
-    block = pl.BlockSpec((shards, 1, pieces, lanes), lambda c: (0, c, 0, 0))
-    whole = [pl.BlockSpec(t.shape, lambda c: (0, 0)) for t in tables]
+    vmem = pl.BlockSpec(memory_space=pltpu.VMEM)
     return pl.pallas_call(
         convolve_body,
-        grid=(channels,),
-        in_specs=[block, pl.BlockSpec((shards, 1, *response.shape[2:]), lambda c: (0, c, 0, 0)), *whole],
-        out_specs=block,
+        in_specs=[vmem] * (2 + len(tables)),
+        out_specs=pl.BlockSpec(memory_space=pl.ANY),
         out_shape=jax.ShapeDtypeStruct(x.shape, BF16),
         scratch_shapes=[
             pltpu.VMEM((shards * pieces, lanes), F32),
             pltpu.VMEM((freqs // 2, COLS), BF16),
             pltpu.VMEM((freqs, 2 * COLS), BF16),
             pltpu.VMEM((2 * freqs, COLS), BF16),
+            pltpu.VMEM((channels, shards, pieces, lanes), BF16),
+            pltpu.SemaphoreType.DMA((channels,)),
         ],
-        compiler_params=pltpu.CompilerParams(vmem_limit_bytes=40 << 20),
+        compiler_params=pltpu.CompilerParams(vmem_limit_bytes=24 << 20),
         cost_estimate=pl.CostEstimate(flops=3 << 30, bytes_accessed=6 << 20, transcendentals=0),
         name="convolve",
     )(x, response, *tables)
@@ -194,6 +187,7 @@
         out_specs=vmem,
         out_shape=jax.ShapeDtypeStruct(signal.shape, BF16),
         scratch_shapes=[pltpu.VMEM(y.shape, F32)],
+        compiler_params=pltpu.CompilerParams(vmem_limit_bytes=8 << 20),
         cost_estimate=pl.CostEstimate(flops=4 * y.size, bytes_accessed=8 * y.size, transcendentals=0),
         name="gated",
     )(y, signal, gate, bias)
@@ -215,7 +209,7 @@
         in_specs=[vmem] * 8,
         out_specs=vmem,
         out_shape=jax.ShapeDtypeStruct((weights[0].shape[0], tok), BF16),
-        compiler_params=pltpu.CompilerParams(vmem_limit_bytes=32 << 20),
+        compiler_params=pltpu.CompilerParams(vmem_limit_bytes=12 << 20),
         cost_estimate=pl.CostEstimate(flops=8 * channels * channels * tok, bytes_accessed=3 << 20, transcendentals=0),
         name="mixed",
     )(*values, *weights)
@@ -237,12 +231,12 @@
     channels, tok = tokens.shape
     per_dest = channels // shard_count
 
-    packed = pack_spectra(spectra, shard_count)
-    packed, tokens = lax.optimization_barrier((packed, tokens))
-    response = lax.all_to_all(packed, "seq", 0, 0, tiled=True)
-
     route = [(i, i + 1) for i in range(shard_count - 1)]
     halo = lax.ppermute(tokens[:, -LANES:], "seq", route)
+    packed = pack_spectra(spectra, shard_count)
+    packed, halo = lax.optimization_barrier((packed, halo))
+    response = lax.all_to_all(packed, "seq", 0, 0, tiled=True)
+
     extended = gathered(jnp.concatenate([halo, tokens], 1))
     taps = jnp.transpose(short_weight, (2, 0, 1)).reshape(channels, 9)
     message, signal, gate = project(
@@ -253,14 +247,19 @@
         lax.dynamic_slice_in_dim(turned, (grp ^ mask) * channels, channels, 0) for mask in range(4)
     ]
     weights = [parts[0]] + [swapped(parts[m], m) for m in (2, 1, 3)]
-    message, response, *weights = lax.optimization_barrier((message, response, *weights))
+    zero = jnp.minimum(grp, 0)
+    tables = [t + zero.astype(t.dtype) for t in transform_tables(shard_count, tok // COLS)]
+    bias = filter_bias[:, None] + zero.astype(F32)
+    message, response, weights, tables, bias = lax.optimization_barrier(
+        (message, response, weights, tables, bias)
+    )
     columns = lax.all_to_all(
         message.reshape(shard_count, per_dest, 8, LANES), "seq", 0, 0, tiled=True
     )
-    result = convolve(columns, response)
+    result = convolve(columns, response, tables)
     back = lax.all_to_all(result, "seq", 0, 0, tiled=True).reshape(channels * 8, LANES)
 
-    weighted = gated(back, signal, gate, filter_bias[:, None])
+    weighted = gated(back, signal, gate, bias)
     return mixed(gathered(weighted), weights)
 
 

time: 160 us -> 133 us (0.83)
  waiting for transfers between devices: 54.6 us -> 37.8 us
  Pallas kernels: 19.5 us -> 11.2 us
  other arithmetic: 0 us -> 3.87 us
  local copies, waits for them, and re-layouts: 12.9 us -> 10.5 us
    ppermute x1, waiting for transfers between devices: 28.7 us -> 0.01 us  [shards(): halo = lax.ppermute(tokens[:, -LANES:], 'seq', route)]
    ppermute x9, waiting for transfers between devices: 12.1 us -> 23.5 us  [swapped(): return lax.ppermute(block, 'grp', [(i, i ^ mask) for i in range(4)])]
    pallas_call x2 -> x1, Pallas kernels: 10.9 us -> 5.76 us  [convolve(): pl.pallas_call(convolve_body, in_specs=[vmem] * (2 + len(tables)), out_sp...]
    unnamed x35 -> x31, local copies, waits for them, and re-layouts: 11.7 us -> 7.32 us
    convert_element_type x0 -> x1, other arithmetic: none -> 2.05 us  [pack_spectra(): by_dest = jnp.transpose(grouped, (1, 2, 0, 3, 4)).astype(BF16)]
    pallas_call x1, Pallas kernels: 2.33 us -> 0.32 us  [gated(): pl.pallas_call(gated_body, in_specs=[vmem] * 4, out_specs=vmem, out_shape...]
    add x0 -> x3, other arithmetic: none -> 1.82 us  [the longest x2 1.82 us: shards(): t + zero.astype(t.dtype)]
  transfers between devices with their start and end apart: 12 -> 12, of which waited for: 5 -> 4; matrix products, arithmetic and copies ran while one was open for 1% -> 6% of each run, Pallas kernels for 3% -> 3%
where the time goes in v2:
time: 133 us; the launch traced here: 132 us
  starting transfers between devices  40.2 us (30%)
  waiting for transfers between devices  37.8 us (28%)
  blocking collectives  28.7 us (22%)
  Pallas kernels  11.2 us (8%)
  local copies, waits for them, and re-layouts  10.5 us (8%)
  other arithmetic  3.87 us (3%)
    all_to_all x1, blocking collectives, shards(): lax.all_to_all(message.reshape(shard_count, per_dest, 8, LANES), 'seq', 0...  28.7 us
    ppermute x9, waiting for transfers between devices, swapped(): return lax.ppermute(block, 'grp', [(i, i ^ mask) for i in range(4)])  23.5 us
    ppermute x9, starting transfers between devices, swapped(): return lax.ppermute(block, 'grp', [(i, i ^ mask) for i in range(4)])  16 us
    all_to_all x1, waiting for transfers between devices, shards(): lax.all_to_all(result, 'seq', 0, 0, tiled=True).reshape(channels * 8, LANES)  14.3 us
    all_to_all x1, starting transfers between devices, shards(): response = lax.all_to_all(packed, 'seq', 0, 0, tiled=True)  13.8 us
    unnamed x31, local copies, waits for them, and re-layouts  7.32 us
    all_to_all x1, starting transfers between devices, shards(): lax.all_to_all(result, 'seq', 0, 0, tiled=True).reshape(channels * 8, LANES)  6.01 us
    pallas_call x1, Pallas kernels, convolve(): pl.pallas_call(convolve_body, in_specs=[vmem] * (2 + len(tables)), out_sp...  5.76 us
  transfers between devices with their start and end apart: 12, of which 4 were waited for; matrix products, arithmetic and copies ran while one was open for 6% of the time, Pallas kernels for 3%

profile of v2, /device:TPU:1, one launch (start us, length us, event | category | flops | bytes accessed | tf_op | source)
XLA Modules:
  0.0 132.5 jit_solution(10541509746980020662)
XLA Ops:
  0.0 0.8 slice.3
  0.8 4.4 %collective-permute-start = (bf16[192,128]{1,0:T(8,128)(2,1)S(1)}, bf16[192,128]{1,0:T(8,128)(2,1)S(1)}, u32[]{:S(2)}, u32[]{:S(2)}) collective-permute-start(bf16[192,128]{1,0:T(8,128)(2,1)S(1)} %slice.3), channel_id=1, source_target_pairs={{0,4},{4,8},{8,12},{12,16},{16,20},{20,24},{24,28},{28,32},{32,36}... | collective-permute-start | bytes 147464 | tf_op jit(solution)/shard_map/ppermute | solution.py:235
  5.2 2.0 %convert_element_type.16 = bf16[2,192,8,256]{3,2,1,0:T(8,128)(2,1)S(1)} convert(f32[2,192,8,256]{3,2,1,0:T(8,128)} %param.12) | non-fusion elementwise | flops 786432 | bytes 4718592 | tf_op jit(solution)/shard_map/convert_element_type | solution.py:43
  7.2 1.3 copy.27
  8.5 13.8 %all-to-all-start = ((bf16[64,3,16,256]{3,2,1,0:T(8,128)(2,1)}), bf16[64,3,16,256]{3,2,1,0:T(8,128)(2,1)}, u32[]{:S(2)}, u32[]{:S(2)}) async-start(bf16[64,3,16,256]{3,2,1,0:T(8,128)(2,1)} %bitcast.17), calls=%async_computation | async-start | bytes 3145728 | tf_op jit(solution)/shard_map/all_to_all | solution.py:238
  22.6 0.7 copy.23
  23.6 0.7 copy.24
  24.4 2.4 %collective-permute-start.5 = (bf16[192,192]{1,0:T(8,128)(2,1)}, bf16[192,192]{1,0:T(8,128)(2,1)S(1)}, u32[]{:S(2)}, u32[]{:S(2)}) collective-permute-start(bf16[192,192]{1,0:T(8,128)(2,1)} %bitcast.8), channel_id=1, source_target_pairs={{0,1},{1,0},{2,3},{3,2},{4,5},{5,4},{6,7},{7,6},{8,9},{9,8},{10,11... | collective-permute-start | bytes 221192 | tf_op jit(solution)/shard_map/ppermute | solution.py:219
  26.8 0.7 copy.25
  27.5 1.0 collective-permute-start.6
  28.6 0.8 copy.16.taps_ref
  30.0 0.9 collective-permute-start.2
  30.9 19.9 %collective-permute-done.1.far_ref = bf16[192,1152]{1,0:T(8,128)(2,1)S(1)} collective-permute-done((bf16[192,1152]{1,0:T(8,128)(2,1)S(1)}, bf16[192,1152]{1,0:T(8,128)(2,1)S(1)}, u32[]{:S(2)}, u32[]{:S(2)}) %collective-permute-start.1) | collective-permute-done | bytes 442400 | tf_op jit(solution)/shard_map/ppermute | solution.py:219
  50.8 1.4 %collective-permute-start.3 = (bf16[192,1152]{1,0:T(8,128)(2,1)S(1)}, bf16[192,1152]{1,0:T(8,128)(2,1)S(1)}, u32[]{:S(2)}, u32[]{:S(2)}) collective-permute-start(bf16[192,1152]{1,0:T(8,128)(2,1)S(1)} %collective-permute-done.1.far_ref), channel_id=1, source_target_pairs={{0,1},{1,0},{2,3},{3,2},{4,5},{5,4},{6,7},{7,6},{8,9},{9,8},{10,11... | collective-permute-start | bytes 1327112 | tf_op jit(solution)/shard_map/ppermute | solution.py:219
  52.2 1.7 %broadcast_add_fusion.wave_ref = bf16[2048,512]{1,0:T(8,128)(2,1)S(1)} fusion(bf16[2048,512]{1,0:T(8,128)(2,1)} %constant.20.clone, bf16[]{:T(256)S(6)} %convert_element_type.19), kind=kLoop, calls=%fused_computation.1 | loop fusion | flops 1048576 | bytes 4194306 | tf_op jit(solution)/shard_map/add | solution.py:251
  53.9 3.8 %project.1 = (bf16[1536,128]{1,0:T(8,128)(2,1)S(1)}, bf16[192,1024]{1,0:T(8,128)(2,1)S(1)}, bf16[192,1024]{1,0:T(8,128)(2,1)S(1)}) custom-call(s32[1]{0:T(128)} %bitcast.grp_ref, bf16[192,1152]{1,0:T(8,128)(2,1)S(1)} %constant_dynamic-update-slice_fusion.own_ref, bf16[192,1152]{1,0:T(8,128)(2,1)S(1)} %collective-permute-done.1.far_ref, ...), custom_call_target="tpu_custom_call" | custom-call | flops 1019215872 | bytes 6291456 | tf_op jit(solution)/shard_map/project/pallas_call | solution.py:85
  57.8 0.7 copy-done
  58.5 0.7 copy-done.2
  59.3 0.7 copy-done.4
  60.0 28.7 %all_to_all.15.x_ref = bf16[64,3,8,128]{3,2,1,0:T(8,128)(2,1)S(1)} all-to-all(bf16[64,3,8,128]{3,2,1,0:T(8,128)(2,1)} %bitcast.20), channel_id=1, replica_groups=mesh['seq'=64,'grp'=4] {'seq'}, dimensions={0} | all-to-all | bytes 786432 | tf_op jit(solution)/shard_map/all_to_all | solution.py:256
  88.7 5.8 %convolve.1 = bf16[64,3,8,128]{3,2,1,0:T(8,128)(2,1)S(1)} custom-call(bf16[64,3,8,128]{3,2,1,0:T(8,128)(2,1)S(1)} %all_to_all.15.x_ref, bf16[64,3,16,256]{3,2,1,0:T(8,128)(2,1)} %all-to-all-done.h_ref, bf16[2048,512]{1,0:T(8,128)(2,1)S(1)} %broadcast_add_fusion.wave_ref, f32[512,512]{1,0:T(8,128)S(1)} %broadcast_add_fusion.1.twist_ref), custom_call_target="tpu_custom_call" | custom-call | flops 3221225472 | bytes 6291456 | tf_op jit(solution)/shard_map/convolve/pallas_call | solution.py:152
  94.5 0.7 copy-done.1
  95.2 6.0 %all-to-all-start.2 = ((bf16[64,3,8,128]{3,2,1,0:T(8,128)(2,1)}), bf16[64,3,8,128]{3,2,1,0:T(8,128)(2,1)S(1)}, u32[]{:S(2)}, u32[]{:S(2)}) async-start(bf16[64,3,8,128]{3,2,1,0:T(8,128)(2,1)} %copy-done.1), calls=%async_computation.2 | async-start | bytes 786432 | tf_op jit(solution)/shard_map/all_to_all | solution.py:260
  101.4 14.3 %all-to-all-done.2 = bf16[64,3,8,128]{3,2,1,0:T(8,128)(2,1)S(1)} async-done(((bf16[64,3,8,128]{3,2,1,0:T(8,128)(2,1)}), bf16[64,3,8,128]{3,2,1,0:T(8,128)(2,1)S(1)}, u32[]{:S(2)}, u32[]{:S(2)}) %all-to-all-start.2) | async-done | bytes 393248 | tf_op jit(solution)/shard_map/all_to_all | solution.py:260
  115.7 1.0 copy-done.3
  116.7 1.0 copy-done.5
  118.0 0.5 collective-permute-start.7
  118.5 4.0 %collective-permute-start.8 = (bf16[192,1024]{1,0:T(8,128)(2,1)S(1)}, bf16[192,1024]{1,0:T(8,128)(2,1)S(1)}, u32[]{:S(2)}, u32[]{:S(2)}) collective-permute-start(bf16[192,1024]{1,0:T(8,128)(2,1)S(1)} %gated.1.refs_0_), channel_id=1, source_target_pairs={{0,1},{1,0},{2,3},{3,2},{4,5},{5,4},{6,7},{7,6},{8,9},{9,8},{10,11... | collective-permute-start | bytes 1179656 | tf_op jit(solution)/shard_map/ppermute | solution.py:219
  122.5 2.2 %collective-permute-done.7.refs_1_ = bf16[192,1024]{1,0:T(8,128)(2,1)S(1)} collective-permute-done((bf16[192,1024]{1,0:T(8,128)(2,1)S(1)}, bf16[192,1024]{1,0:T(8,128)(2,1)S(1)}, u32[]{:S(2)}, u32[]{:S(2)}) %collective-permute-start.7) | collective-permute-done | bytes 393248 | tf_op jit(solution)/shard_map/ppermute | solution.py:219
  124.7 5.1 %collective-permute-start.9 = (bf16[192,1024]{1,0:T(8,128)(2,1)S(1)}, bf16[192,1024]{1,0:T(8,128)(2,1)S(1)}, u32[]{:S(2)}, u32[]{:S(2)}) collective-permute-start(bf16[192,1024]{1,0:T(8,128)(2,1)S(1)} %collective-permute-done.7.refs_1_), channel_id=1, source_target_pairs={{0,1},{1,0},{2,3},{3,2},{4,5},{5,4},{6,7},{7,6},{8,9},{9,8},{10,11... | collective-permute-start | bytes 1179656 | tf_op jit(solution)/shard_map/ppermute | solution.py:219
  129.8 1.3 %collective-permute-done.9.refs_3_ = bf16[192,1024]{1,0:T(8,128)(2,1)S(1)} collective-permute-done((bf16[192,1024]{1,0:T(8,128)(2,1)S(1)}, bf16[192,1024]{1,0:T(8,128)(2,1)S(1)}, u32[]{:S(2)}, u32[]{:S(2)}) %collective-permute-start.9) | collective-permute-done | bytes 393248 | tf_op jit(solution)/shard_map/ppermute | solution.py:219
  131.2 1.3 mixed.1
  (39 shorter events, 1.7 us)
Async XLA Ops:
  0.8 7.7 %collective-permute-start = (bf16[192,128]{1,0:T(8,128)(2,1)S(1)}, bf16[192,128]{1,0:T(8,128)(2,1)S(1)}, u32[]{:S(2)}, u32[]{:S(2)}) collective-permute-start(bf16[192,128]{1,0:T(8,128)(2,1)S(1)} %slice.3), channel_id=1, source_target_pairs={{0,4},{4,8},{8,12},{12,16},{16,20},{20,24},{24,28},{28,32},{32,36}... | collective-permute-start | bytes 147464 | tf_op jit(solution)/shard_map/ppermute | solution.py:235
  8.5 13.9 %copy-start.9 = (bf16[192,768]{1,0:T(8,128)(2,1)S(1)}, bf16[192,768]{1,0:T(8,128)(2,1)}, u32[]{:S(2)}) copy-start(bf16[192,768]{1,0:T(8,128)(2,1)} %param.13) | copy-start | bytes 884740
  8.5 20.1 %copy-start.11 = (f32[3,3,192]{2,1,0:T(4,128)S(1)}, f32[3,3,192]{2,1,0:T(4,128)}, u32[]{:S(2)}) copy-start(f32[3,3,192]{2,1,0:T(4,128)} %param.10) | copy-start | bytes 20740
  8.5 20.9 %copy-start.10 = (bf16[192,1024]{1,0:T(8,128)(2,1)S(1)}, bf16[192,1024]{1,0:T(8,128)(2,1)}, u32[]{:S(2)}) copy-start(bf16[192,1024]{1,0:T(8,128)(2,1)} %param.8) | copy-start | bytes 1179652
  8.5 51.5 %all-to-all-start = ((bf16[64,3,16,256]{3,2,1,0:T(8,128)(2,1)}), bf16[64,3,16,256]{3,2,1,0:T(8,128)(2,1)}, u32[]{:S(2)}, u32[]{:S(2)}) async-start(bf16[64,3,16,256]{3,2,1,0:T(8,128)(2,1)} %bitcast.17), calls=%async_computation | async-start | bytes 3145728 | tf_op jit(solution)/shard_map/all_to_all | solution.py:238
  22.3 7.6 %copy-start.12 = (f32[192]{0:T(256)S(1)}, f32[192]{0:T(256)}, u32[]{:S(2)}) copy-start(f32[192]{0:T(256)} %param.11) | copy-start | bytes 2308
  22.3 7.6 %copy-start.8 = (f32[512,512]{1,0:T(8,128)S(1)}, f32[512,512]{1,0:T(8,128)}, u32[]{:S(2)}) copy-start(f32[512,512]{1,0:T(8,128)} %constant.21.clone) | copy-start | bytes 3145732
  23.3 36.7 %collective-permute-start.4 = (bf16[192,192]{1,0:T(8,128)(2,1)}, bf16[192,192]{1,0:T(8,128)(2,1)S(1)}, u32[]{:S(2)}, u32[]{:S(2)}) collective-permute-start(bf16[192,192]{1,0:T(8,128)(2,1)} %bitcast.7), channel_id=1, source_target_pairs={{0,2},{1,3},{2,0},{3,1},{4,6},{5,7},{6,4},{7,5},{8,10},{9,11},{10,... | collective-permute-start | bytes 221192 | tf_op jit(solution)/shard_map/ppermute | solution.py:219
  24.4 35.6 %collective-permute-start.5 = (bf16[192,192]{1,0:T(8,128)(2,1)}, bf16[192,192]{1,0:T(8,128)(2,1)S(1)}, u32[]{:S(2)}, u32[]{:S(2)}) collective-permute-start(bf16[192,192]{1,0:T(8,128)(2,1)} %bitcast.8), channel_id=1, source_target_pairs={{0,1},{1,0},{2,3},{3,2},{4,5},{5,4},{6,7},{7,6},{8,9},{9,8},{10,11... | collective-permute-start | bytes 221192 | tf_op jit(solution)/shard_map/ppermute | solution.py:219
  27.5 32.5 %collective-permute-start.6 = (bf16[192,192]{1,0:T(8,128)(2,1)}, bf16[192,192]{1,0:T(8,128)(2,1)S(1)}, u32[]{:S(2)}, u32[]{:S(2)}) collective-permute-start(bf16[192,192]{1,0:T(8,128)(2,1)} %bitcast.9), channel_id=1, source_target_pairs={{0,3},{1,2},{2,1},{3,0},{4,7},{5,6},{6,5},{7,4},{8,11},{9,10},{10,... | collective-permute-start | bytes 221192 | tf_op jit(solution)/shard_map/ppermute | solution.py:219
  29.5 21.3 %collective-permute-start.1 = (bf16[192,1152]{1,0:T(8,128)(2,1)S(1)}, bf16[192,1152]{1,0:T(8,128)(2,1)S(1)}, u32[]{:S(2)}, u32[]{:S(2)}) collective-permute-start(bf16[192,1152]{1,0:T(8,128)(2,1)S(1)} %constant_dynamic-update-slice_fusion.own_ref), channel_id=1, source_target_pairs={{0,2},{1,3},{2,0},{3,1},{4,6},{5,7},{6,4},{7,5},{8,10},{9,11},{10,... | collective-permute-start | bytes 1327112 | tf_op jit(solution)/shard_map/ppermute | solution.py:219
  30.0 23.9 %copy-start.6 = (f32[192,9]{1,0:T(8,128)S(1)}, f32[192,9]{1,0:T(8,128)}, u32[]{:S(2)}) copy-start(f32[192,9]{1,0:T(8,128)} %copy.16.taps_ref) | copy-start | bytes 20740
  30.0 23.9 %copy-start.7 = (bf16[3,192,768]{2,1,0:T(8,128)(2,1)S(1)}, bf16[3,192,768]{2,1,0:T(8,128)(2,1)}, u32[]{:S(2)}) copy-start(bf16[3,192,768]{2,1,0:T(8,128)(2,1)} %param.9) | copy-start | bytes 2654212
  30.0 23.9 %collective-permute-start.2 = (bf16[192,1152]{1,0:T(8,128)(2,1)S(1)}, bf16[192,1152]{1,0:T(8,128)(2,1)S(1)}, u32[]{:S(2)}, u32[]{:S(2)}) collective-permute-start(bf16[192,1152]{1,0:T(8,128)(2,1)S(1)} %constant_dynamic-update-slice_fusion.own_ref), channel_id=1, source_target_pairs={{0,1},{1,0},{2,3},{3,2},{4,5},{5,4},{6,7},{7,6},{8,9},{9,8},{10,11... | collective-permute-start | bytes 1327112 | tf_op jit(solution)/shard_map/ppermute | solution.py:219
  50.8 3.1 %collective-permute-start.3 = (bf16[192,1152]{1,0:T(8,128)(2,1)S(1)}, bf16[192,1152]{1,0:T(8,128)(2,1)S(1)}, u32[]{:S(2)}, u32[]{:S(2)}) collective-permute-start(bf16[192,1152]{1,0:T(8,128)(2,1)S(1)} %collective-permute-done.1.far_ref), channel_id=1, source_target_pairs={{0,1},{1,0},{2,3},{3,2},{4,5},{5,4},{6,7},{7,6},{8,9},{9,8},{10,11... | collective-permute-start | bytes 1327112 | tf_op jit(solution)/shard_map/ppermute | solution.py:219
  57.8 0.7 copy-start
  58.5 0.7 copy-start.2
  59.3 0.7 copy-start.4
  94.5 0.7 copy-start.1
  95.2 20.5 %all-to-all-start.2 = ((bf16[64,3,8,128]{3,2,1,0:T(8,128)(2,1)}), bf16[64,3,8,128]{3,2,1,0:T(8,128)(2,1)S(1)}, u32[]{:S(2)}, u32[]{:S(2)}) async-start(bf16[64,3,8,128]{3,2,1,0:T(8,128)(2,1)} %copy-done.1), calls=%async_computation.2 | async-start | bytes 786432 | tf_op jit(solution)/shard_map/all_to_all | solution.py:260
  115.7 1.0 copy-start.3
  116.7 1.0 copy-start.5
  118.0 6.7 %collective-permute-start.7 = (bf16[192,1024]{1,0:T(8,128)(2,1)S(1)}, bf16[192,1024]{1,0:T(8,128)(2,1)S(1)}, u32[]{:S(2)}, u32[]{:S(2)}) collective-permute-start(bf16[192,1024]{1,0:T(8,128)(2,1)S(1)} %gated.1.refs_0_), channel_id=1, source_target_pairs={{0,2},{1,3},{2,0},{3,1},{4,6},{5,7},{6,4},{7,5},{8,10},{9,11},{10,... | collective-permute-start | bytes 1179656 | tf_op jit(solution)/shard_map/ppermute | solution.py:219
  118.5 11.3 %collective-permute-start.8 = (bf16[192,1024]{1,0:T(8,128)(2,1)S(1)}, bf16[192,1024]{1,0:T(8,128)(2,1)S(1)}, u32[]{:S(2)}, u32[]{:S(2)}) collective-permute-start(bf16[192,1024]{1,0:T(8,128)(2,1)S(1)} %gated.1.refs_0_), channel_id=1, source_target_pairs={{0,1},{1,0},{2,3},{3,2},{4,5},{5,4},{6,7},{7,6},{8,9},{9,8},{10,11... | collective-permute-start | bytes 1179656 | tf_op jit(solution)/shard_map/ppermute | solution.py:219
  124.7 6.4 %collective-permute-start.9 = (bf16[192,1024]{1,0:T(8,128)(2,1)S(1)}, bf16[192,1024]{1,0:T(8,128)(2,1)S(1)}, u32[]{:S(2)}, u32[]{:S(2)}) collective-permute-start(bf16[192,1024]{1,0:T(8,128)(2,1)S(1)} %collective-permute-done.7.refs_1_), channel_id=1, source_target_pairs={{0,1},{1,0},{2,3},{3,2},{4,5},{5,4},{6,7},{7,6},{8,9},{9,8},{10,11... | collective-permute-start | bytes 1179656 | tf_op jit(solution)/shard_map/ppermute | solution.py:219

commit v3 on v2

v3 whole, which is shorter than its diff:
```python
import math

import jax
import jax.numpy as jnp
import numpy as np
from jax import lax
from jax.experimental import pallas as pl
from jax.experimental.pallas import tpu as pltpu
from jax.sharding import PartitionSpec as P

COLS = 256
FREQS = 512
LANES = 128
PROJECT_VMEM = 54000 << 10
CONVOLVE_VMEM = 50000 << 10
MASKS = (0, 2, 1, 3)
BF16 = jnp.bfloat16
F32 = jnp.float32


def unit_circle(rows, cols, period):
    angle = (np.outer(rows, cols) % period) * (2.0 * math.pi / period)
    return np.cos(angle), np.sin(angle)


def transform_tables(shard_count, rows_dev):
    half = shard_count * rows_dev
    order = (np.arange(shard_count)[None, :] * rows_dev + np.arange(rows_dev)[:, None]).reshape(-1)
    freqs = np.arange(2 * half)
    cols = np.arange(COLS)
    padded = 2 * half * COLS
    cos1, sin1 = unit_circle(freqs, order, 2 * half)
    cos2, sin2 = unit_circle(cols, cols, COLS)
    cost, sint = unit_circle(freqs, cols, padded)
    first = np.concatenate([cos1, -sin1], 1)
    forward = np.block([[cos2, -sin2], [sin2, cos2]])
    backward = np.block([[cos2, sin2], [-sin2, cos2]])
    last = np.concatenate([cos1.T, -sin1.T], 0) / padded
    waves = np.concatenate([first, forward, backward, last], 0)
    return jnp.asarray(waves, BF16), jnp.asarray(np.concatenate([cost, sint], 1), F32)


def pack_spectra_body(spec_ref, out_ref):
    dests = out_ref.shape[0]
    per_dest = spec_ref.shape[1] // dests
    for part in range(2):
        for h in range(2):
            piece = spec_ref[part, :, :, h * LANES:(h + 1) * LANES]
            piece = piece.reshape(dests, per_dest, *piece.shape[1:]).astype(BF16)
            for c in range(per_dest):
                out_ref[:, 4 * c + 2 * part + h] = piece[:, c]


def pack_spectra(spectra, shard_count):
    _, channels, rows, cols = spectra.shape
    per_dest = channels // shard_count
    steps = 2
    return pl.pallas_call(
        pack_spectra_body,
        grid=(steps,),
        in_specs=[pl.BlockSpec((2, channels // steps, rows, cols), lambda i: (0, i, 0, 0))],
        out_specs=pl.BlockSpec((shard_count // steps, 4 * per_dest, rows, LANES), lambda i: (i, 0, 0, 0)),
        out_shape=jax.ShapeDtypeStruct((shard_count, 5 * per_dest, rows, LANES), BF16),
        cost_estimate=pl.CostEstimate(flops=0, bytes_accessed=6 * spectra.size, transcendentals=0),
        name="pack_spectra",
    )(spectra)


def project_body(*refs):
    grp_ref, mains, halos, weight_ref, taps_ref = refs[0], refs[1:5], refs[5:9], refs[9], refs[10]
    message_ref, kept_ref, token_ref, stream_ref, spread_ref, part_ref, sem = refs[12:]
    channels, tok = mains[0].shape
    width = tok + LANES
    grp = grp_ref[0]
    for mask, main, halo in zip(MASKS, mains, halos):
        rows = pl.ds(pl.multiple_of((grp ^ mask) * channels, 64), channels)
        token_ref[rows, :LANES] = halo[...]
        token_ref[rows, LANES:] = main[...]
    step = 384
    for col in range(0, width, step):
        stream_ref[:, col:col + step] = jnp.dot(
            weight_ref[...], token_ref[:, col:col + step], preferred_element_type=F32
        )
    rows = 16

    def chunk(index, carry):
        row = pl.multiple_of(index * rows, rows)
        smooth = []
        for s in range(3):
            x = stream_ref[pl.ds(s * channels + row, rows), :].astype(BF16).astype(F32)
            w = [taps_ref[pl.ds(row, rows), 3 * tap + s:3 * tap + s + 1] for tap in range(3)]
            y = w[0] * x + w[1] * pltpu.roll(x, 1, 1) + w[2] * pltpu.roll(x, 2, 1)
            smooth.append(y[:, LANES:])
        kept_ref[0, pl.ds(row, rows), :] = smooth[0].astype(BF16)
        signal = smooth[2] * smooth[1]
        kept_ref[1, pl.ds(row, rows), :] = signal.astype(BF16)
        for part in range(8):
            spread_ref[pl.ds(row * 8 + part, rows, stride=8), :] = signal[:, part * LANES:(part + 1) * LANES]
        return carry

    lax.fori_loop(0, channels // rows, chunk, 0)
    part_ref[...] = spread_ref[...].reshape(part_ref.shape).astype(BF16)
    per_dest = part_ref.shape[1]
    copy = pltpu.make_async_copy(part_ref, message_ref.at[:, pl.ds(4 * per_dest, per_dest)], sem)
    copy.start()
    copy.wait()


def project(grp, mains, halos, weight, taps, packed):
    channels, tok = mains[0].shape
    width = tok + LANES
    vmem = pl.BlockSpec(memory_space=pltpu.VMEM)
    anywhere = pl.BlockSpec(memory_space=pltpu.HBM)
    shards, pieces = packed.shape[:2]
    return pl.pallas_call(
        project_body,
        in_specs=[pl.BlockSpec(memory_space=pltpu.SMEM)] + [vmem] * 10 + [anywhere],
        out_specs=[anywhere, vmem],
        out_shape=[
            jax.ShapeDtypeStruct(packed.shape, BF16),
            jax.ShapeDtypeStruct((2, channels, tok), BF16),
        ],
        scratch_shapes=[
            pltpu.VMEM((4 * channels, width), BF16),
            pltpu.VMEM((3 * channels, width), F32),
            pltpu.VMEM((channels * 8, LANES), F32),
            pltpu.VMEM((shards, pieces // 5, 8, LANES), BF16),
            pltpu.SemaphoreType.DMA,
        ],
        input_output_aliases={11: 0},
        compiler_params=pltpu.CompilerParams(vmem_limit_bytes=PROJECT_VMEM),
        cost_estimate=pl.CostEstimate(flops=2 * 3 * channels * 4 * channels * width,
                                      bytes_accessed=6 << 20, transcendentals=0),
        name="project",
    )(grp, *mains, *halos, weight, taps, packed)


def convolve_body(m_ref, wave_hbm, twist_ref, out_ref,
                  spread_ref, grid_ref, mid_ref, tall_ref, done_ref, wave_ref, sems, wave_sems):
    channels, shards, pieces, lanes = done_ref.shape
    rows_dev = pieces // 2
    freqs = twist_ref.shape[0]
    first_ref, forward_ref, backward_ref, last_ref = (wave_ref.at[i] for i in range(4))
    loads = [
        pltpu.make_async_copy(wave_hbm.at[pl.ds(i * freqs, freqs)], wave_ref.at[i], wave_sems.at[i]) for i in range(4)
    ]
    for load in loads:
        load.start()
    for c in range(channels):
        spread_ref[c] = m_ref[:, 4 * channels + c].astype(F32).reshape(shards * pieces, lanes)
        for a in range(rows_dev):
            for h in range(2):
                grid_ref[c, a * shards:(a + 1) * shards, h * lanes:(h + 1) * lanes] = spread_ref[
                    c, pl.ds(2 * a + h, shards, stride=pieces), :].astype(BF16)
        if c == 0:
            loads[0].wait()
        real = jnp.dot(first_ref[:, :COLS], grid_ref[c], preferred_element_type=F32)
        imag = jnp.dot(first_ref[:, COLS:], grid_ref[c], preferred_element_type=F32)
        cosine, sine = twist_ref[:, :COLS], twist_ref[:, COLS:]
        mid_ref[c, :, :COLS] = (real * cosine + imag * sine).astype(BF16)
        mid_ref[c, :, COLS:] = (imag * cosine - real * sine).astype(BF16)
        if c == 0:
            loads[1].wait()
        freq = jnp.dot(mid_ref[c], forward_ref[...], preferred_element_type=F32)
        for h in range(2):
            low, high = h * lanes, COLS + h * lanes
            real, imag = freq[:, low:low + lanes], freq[:, high:high + lanes]
            h_real, h_imag = (
                m_ref[:, 4 * c + 2 * part + h].astype(F32).reshape(freqs, lanes) for part in range(2)
            )
            mid_ref[c, :, low:low + lanes] = (real * h_real - imag * h_imag).astype(BF16)
            mid_ref[c, :, high:high + lanes] = (real * h_imag + imag * h_real).astype(BF16)
        if c == 0:
            loads[2].wait()
        back = jnp.dot(mid_ref[c], backward_ref[...], preferred_element_type=F32)
        real, imag = back[:, :COLS], back[:, COLS:]
        tall_ref[c, :freqs, :] = (real * cosine - imag * sine).astype(BF16)
        tall_ref[c, freqs:, :] = (imag * cosine + real * sine).astype(BF16)
        if c == 0:
            loads[3].wait()
        out = jnp.dot(last_ref[:COLS, :], tall_ref[c, :freqs], preferred_element_type=F32)
        out += jnp.dot(last_ref[COLS:, :], tall_ref[c, freqs:], preferred_element_type=F32)
        for a in range(rows_dev):
            for h in range(2):
                spread_ref[c, pl.ds(2 * a + h, shards, stride=pieces), :] = out[
                    a * shards:(a + 1) * shards, h * lanes:(h + 1) * lanes]
        done_ref[c] = spread_ref[c].reshape(shards, pieces, lanes).astype(BF16)
        pltpu.make_async_copy(done_ref.at[c], out_ref.at[:, c], sems.at[c]).start()
    for c in range(channels):
        pltpu.make_async_copy(done_ref.at[c], out_ref.at[:, c], sems.at[c]).wait()


def convolve(received, tables):
    shards, kinds, pieces, lanes = received.shape
    channels = kinds // 5
    freqs = shards * pieces
    vmem = pl.BlockSpec(memory_space=pltpu.VMEM)
    return pl.pallas_call(
        convolve_body,
        in_specs=[vmem, pl.BlockSpec(memory_space=pltpu.HBM), vmem],
        out_specs=pl.BlockSpec(memory_space=pltpu.HBM),
        out_shape=jax.ShapeDtypeStruct((shards, channels, pieces, lanes), BF16),
        scratch_shapes=[
            pltpu.VMEM((channels, shards * pieces, lanes), F32),
            pltpu.VMEM((channels, freqs // 2, COLS), BF16),
            pltpu.VMEM((channels, freqs, 2 * COLS), BF16),
            pltpu.VMEM((channels, 2 * freqs, COLS), BF16),
            pltpu.VMEM((channels, shards, pieces, lanes), BF16),
            pltpu.VMEM((4, freqs, 2 * COLS), BF16),
            pltpu.SemaphoreType.DMA((channels,)),
            pltpu.SemaphoreType.DMA((4,)),
        ],
        compiler_params=pltpu.CompilerParams(vmem_limit_bytes=CONVOLVE_VMEM),
        cost_estimate=pl.CostEstimate(flops=3 << 30, bytes_accessed=6 << 20, transcendentals=0),
        name="convolve",
    )(received, *tables)


def gated_body(y_ref, kept_ref, bias_ref, out_ref, spread_ref):
    channels = out_ref.shape[0]
    spread_ref[...] = y_ref[...].astype(F32)
    bias = bias_ref[...]
    for part in range(8):
        cols = slice(part * LANES, (part + 1) * LANES)
        y = spread_ref[pl.ds(part, channels, stride=8), :]
        direct = bias * kept_ref[1, :, cols].astype(F32)
        out_ref[:, cols] = (kept_ref[0, :, cols].astype(F32) * (y + direct)).astype(BF16)


def gated(y, kept, bias):
    vmem = pl.BlockSpec(memory_space=pltpu.VMEM)
    return pl.pallas_call(
        gated_body,
        in_specs=[vmem] * 3,
        out_specs=vmem,
        out_shape=jax.ShapeDtypeStruct(kept.shape[1:], BF16),
        scratch_shapes=[pltpu.VMEM(y.shape, F32)],
        compiler_params=pltpu.CompilerParams(vmem_limit_bytes=8 << 20),
        cost_estimate=pl.CostEstimate(flops=4 * y.size, bytes_accessed=8 * y.size, transcendentals=0),
        name="gated",
    )(y, kept, bias)


def mixed_body(*refs):
    values, weights, out_ref = refs[:4], refs[4:8], refs[8]
    total = jnp.dot(weights[0][...], values[0][...], preferred_element_type=F32)
    for w, v in zip(weights[1:], values[1:]):
        total = total + jnp.dot(w[...], v[...], preferred_element_type=F32)
    out_ref[...] = total.astype(BF16)


def mixed(values, weights):
    vmem = pl.BlockSpec(memory_space=pltpu.VMEM)
    channels, tok = values[0].shape
    return pl.pallas_call(
        mixed_body,
        in_specs=[vmem] * 8,
        out_specs=vmem,
        out_shape=jax.ShapeDtypeStruct((weights[0].shape[0], tok), BF16),
        compiler_params=pltpu.CompilerParams(vmem_limit_bytes=12 << 20),
        cost_estimate=pl.CostEstimate(flops=8 * channels * channels * tok, bytes_accessed=3 << 20, transcendentals=0),
        name="mixed",
    )(*values, *weights)


def swapped(block, mask):
    return lax.ppermute(block, "grp", [(i, i ^ mask) for i in range(4)])


def gathered(block):
    far = swapped(block, 2)
    near = swapped(block, 1)
    return block, far, near, swapped(far, 1)


def previous_tail(tail, mask, shard_count):
    route = [
        ((s - 1) * 4 + (g ^ mask), s * 4 + g) for s in range(1, shard_count) for g in range(4)
    ]
    return lax.ppermute(tail, ("seq", "grp"), route)


def shards(tokens, in_weight, short_weight, filter_bias, spectra, out_weight):
    shard_count = lax.axis_size("seq")
    grp = lax.axis_index("grp")
    channels, tok = tokens.shape
    per_dest = channels // shard_count

    far = swapped(tokens, 2)
    near = swapped(tokens, 1)
    tail = tokens[:, -LANES:]
    halos = [previous_tail(tail, mask, shard_count) for mask in MASKS]
    packed = pack_spectra(spectra, shard_count)
    far, halos, packed = lax.optimization_barrier((far, halos, packed))
    mains = [tokens, far, near, swapped(far, 1)]
    taps = jnp.transpose(short_weight, (2, 0, 1)).reshape(channels, 9)
    message, kept = project(
        grp.reshape(1).astype(jnp.int32), mains, halos, in_weight.reshape(3 * channels, -1), taps, packed
    )
    message, out_weight, filter_bias, later = lax.optimization_barrier(
        (message, out_weight, filter_bias, grp)
    )
    received = lax.all_to_all(message, "seq", 0, 0, tiled=True)

    turned = out_weight.T
    parts = [
        lax.dynamic_slice_in_dim(turned, (later ^ mask) * channels, channels, 0) for mask in MASKS
    ]
    weights = [parts[0]] + [swapped(part, mask) for part, mask in zip(parts[1:], MASKS[1:])]
    zero = jnp.minimum(later, 0)
    tables = [t + zero.astype(t.dtype) for t in transform_tables(shard_count, tok // COLS)]
    bias = filter_bias[:, None] + zero.astype(F32)
    received, weights, tables, bias = lax.optimization_barrier((received, weights, tables, bias))

    result = convolve(received, tables)
    back = lax.all_to_all(result, "seq", 0, 0, tiled=True).reshape(channels * 8, LANES)
    weighted = gated(back, kept, bias)
    return mixed(gathered(weighted), weights)


def solution(mesh):
    in_specs = (
        P("grp", "seq"),
        P(None, "grp", None),
        P(None, None, "grp"),
        P("grp"),
        P(None, "grp", "seq", None),
        P("grp", None),
    )
    out_specs = P("grp", "seq")
    return jax.shard_map(shards, mesh=mesh, in_specs=in_specs, out_specs=out_specs, check_vma=False)
```

time: 133 us -> 136 us (1.023)
  blocking collectives: 28.7 us -> 0 us
  waiting for transfers between devices: 37.8 us -> 61.3 us
  starting transfers between devices: 40.2 us -> 50.8 us
  local copies, waits for them, and re-layouts: 10.5 us -> 3.19 us
  Pallas kernels: 11.2 us -> 17.1 us
    all_to_all x1, waiting for transfers between devices: 0.01 us -> 35.3 us  [shards(): received = lax.all_to_all(message, 'seq', 0, 0, tiled=True)]
    all_to_all x1 -> x0, blocking collectives: 28.7 us -> none  [shards(): lax.all_to_all(message.reshape(shard_count, per_dest, 8, LANES), 'seq', 0...]
    ppermute x1 -> x4, starting transfers between devices: 4.36 us -> 16.7 us  [previous_tail(): return lax.ppermute(tail, ('seq', 'grp'), route)]
    ppermute x9, waiting for transfers between devices: 23.5 us -> 11.6 us  [swapped(): return lax.ppermute(block, 'grp', [(i, i ^ mask) for i in range(4)])]
    unnamed x31 -> x16, local copies, waits for them, and re-layouts: 7.32 us -> 1.91 us
    all_to_all x1, starting transfers between devices: 13.8 us -> 10.1 us  [shards(): received = lax.all_to_all(message, 'seq', 0, 0, tiled=True)]
    pallas_call x1, Pallas kernels: 3.84 us -> 6.93 us  [project(): pl.pallas_call(project_body, in_specs=[pl.BlockSpec(memory_space=pltpu.SM...]
    pallas_call x2 -> x3, Pallas kernels: 6.08 us -> 8.84 us  [the longest x1 5.63 us: convolve(): pl.pallas_call(convolve_body, in_specs=[vmem, pl.BlockSpec(memory_space=p...]
  transfers between devices with their start and end apart: 12 -> 15, of which waited for: 4 -> 8; matrix products, arithmetic and copies ran while one was open for 6% -> 3% of each run, Pallas kernels for 3% -> 2%
where the time goes in v3:
time: 136 us; the launch traced here: 135 us
  waiting for transfers between devices  61.3 us (45%)
  starting transfers between devices  50.8 us (37%)
  Pallas kernels  17.1 us (13%)
  local copies, waits for them, and re-layouts  3.19 us (2%)
  other arithmetic  2.78 us (2%)
    all_to_all x1, waiting for transfers between devices, shards(): received = lax.all_to_all(message, 'seq', 0, 0, tiled=True)  35.3 us
    ppermute x4, starting transfers between devices, previous_tail(): return lax.ppermute(tail, ('seq', 'grp'), route)  16.7 us
    ppermute x9, starting transfers between devices, swapped(): return lax.ppermute(block, 'grp', [(i, i ^ mask) for i in range(4)])  15.3 us
    all_to_all x1, waiting for transfers between devices, shards(): lax.all_to_all(result, 'seq', 0, 0, tiled=True).reshape(channels * 8, LANES)  14.4 us
    ppermute x9, waiting for transfers between devices, swapped(): return lax.ppermute(block, 'grp', [(i, i ^ mask) for i in range(4)])  11.6 us
    all_to_all x1, starting transfers between devices, shards(): received = lax.all_to_all(message, 'seq', 0, 0, tiled=True)  10.1 us
    all_to_all x1, starting transfers between devices, shards(): lax.all_to_all(result, 'seq', 0, 0, tiled=True).reshape(channels * 8, LANES)  8.67 us
    pallas_call x1, Pallas kernels, project(): pl.pallas_call(project_body, in_specs=[pl.BlockSpec(memory_space=pltpu.SM...  6.93 us
  transfers between devices with their start and end apart: 15, of which 8 were waited for; matrix products, arithmetic and copies ran while one was open for 3% of the time, Pallas kernels for 2%

profile of v3, /device:TPU:1, one launch (start us, length us, event | category | flops | bytes accessed | tf_op | source)
XLA Modules:
  0.0 135.4 jit_solution(8677170349803964089)
XLA Ops:
  0.0 2.0 %collective-permute-start = (bf16[192,1024]{1,0:T(8,128)(2,1)}, bf16[192,1024]{1,0:T(8,128)(2,1)S(1)}, u32[]{:S(2)}, u32[]{:S(2)}) collective-permute-start(bf16[192,1024]{1,0:T(8,128)(2,1)} %refs_1_.1), channel_id=1, source_target_pairs={{0,2},{1,3},{2,0},{3,1},{4,6},{5,7},{6,4},{7,5},{8,10},{9,11},{10,... | collective-permute-start | bytes 1179656 | tf_op jit(solution)/shard_map/ppermute | solution.py:267
  2.0 0.8 slice.3
  2.9 4.5 %collective-permute-start.4 = (bf16[192,128]{1,0:T(8,128)(2,1)S(1)}, bf16[192,128]{1,0:T(8,128)(2,1)S(1)}, u32[]{:S(2)}, u32[]{:S(2)}) collective-permute-start(bf16[192,128]{1,0:T(8,128)(2,1)S(1)} %slice.3), channel_id=1, source_target_pairs={{3,4},{2,5},{1,6},{0,7},{7,8},{6,9},{5,10},{4,11},{11,12},{10,13},... | collective-permute-start | bytes 147464 | tf_op jit(solution)/shard_map/ppermute | solution.py:280
  7.4 3.0 %collective-permute-start.3 = (bf16[192,128]{1,0:T(8,128)(2,1)S(1)}, bf16[192,128]{1,0:T(8,128)(2,1)S(1)}, u32[]{:S(2)}, u32[]{:S(2)}) collective-permute-start(bf16[192,128]{1,0:T(8,128)(2,1)S(1)} %slice.3), channel_id=1, source_target_pairs={{1,4},{0,5},{3,6},{2,7},{5,8},{4,9},{7,10},{6,11},{9,12},{8,13},{1... | collective-permute-start | bytes 147464 | tf_op jit(solution)/shard_map/ppermute | solution.py:280
  10.4 4.5 %collective-permute-start.2 = (bf16[192,128]{1,0:T(8,128)(2,1)S(1)}, bf16[192,128]{1,0:T(8,128)(2,1)S(1)}, u32[]{:S(2)}, u32[]{:S(2)}) collective-permute-start(bf16[192,128]{1,0:T(8,128)(2,1)S(1)} %slice.3), channel_id=1, source_target_pairs={{2,4},{3,5},{0,6},{1,7},{6,8},{7,9},{4,10},{5,11},{10,12},{11,13},... | collective-permute-start | bytes 147464 | tf_op jit(solution)/shard_map/ppermute | solution.py:280
  14.8 4.8 %collective-permute-start.1 = (bf16[192,128]{1,0:T(8,128)(2,1)S(1)}, bf16[192,128]{1,0:T(8,128)(2,1)S(1)}, u32[]{:S(2)}, u32[]{:S(2)}) collective-permute-start(bf16[192,128]{1,0:T(8,128)(2,1)S(1)} %slice.3), channel_id=1, source_target_pairs={{0,4},{1,5},{2,6},{3,7},{4,8},{5,9},{6,10},{7,11},{8,12},{9,13},{1... | collective-permute-start | bytes 147464 | tf_op jit(solution)/shard_map/ppermute | solution.py:280
  19.6 2.9 %pack_spectra.1.refs_11_ = bf16[64,15,8,128]{3,2,1,0:T(8,128)(2,1)} custom-call(f32[2,192,8,256]{3,2,1,0:T(8,128)} %spec_ref.1), custom_call_target="tpu_custom_call" | custom-call | bytes 4718592 | tf_op jit(solution)/shard_map/pack_spectra/pallas_call | solution.py:58
  22.5 1.5 %collective-permute-start.5 = (bf16[192,1024]{1,0:T(8,128)(2,1)S(1)}, bf16[192,1024]{1,0:T(8,128)(2,1)S(1)}, u32[]{:S(2)}, u32[]{:S(2)}) collective-permute-start(bf16[192,1024]{1,0:T(8,128)(2,1)S(1)} %copy-done.1), channel_id=1, source_target_pairs={{0,1},{1,0},{2,3},{3,2},{4,5},{5,4},{6,7},{7,6},{8,9},{9,8},{10,11... | collective-permute-start | bytes 1179656 | tf_op jit(solution)/shard_map/ppermute | solution.py:267
  24.3 1.1 collective-permute-done.5.refs_3_
  25.4 0.6 collective-permute-done.6.refs_4_
  25.9 0.2 copy-done.3
  26.1 0.6 copy-done.4
  26.7 6.9 %project.1 = (bf16[64,15,8,128]{3,2,1,0:T(8,128)(2,1)}, bf16[2,192,1024]{2,1,0:T(8,128)(2,1)}) custom-call(s32[1]{0:T(128)} %bitcast.refs_0_, bf16[192,1024]{1,0:T(8,128)(2,1)S(1)} %copy-done.1, bf16[192,1024]{1,0:T(8,128)(2,1)S(1)} %collective-permute-done.refs_2_, bf16[192,1024]{1,0:T(8,128)(2,1)} %copy-done.3, ...), custom_call_target="tpu_custom_call", output_to_operand_aliasing={{0}: (11, {})} | custom-call | flops 1019215872 | bytes 6291456 | tf_op jit(solution)/shard_map/project/pallas_call | solution.py:115
  33.6 10.1 %all-to-all-start = ((bf16[64,15,8,128]{3,2,1,0:T(8,128)(2,1)}), bf16[64,15,8,128]{3,2,1,0:T(8,128)(2,1)S(1)}, u32[]{:S(2)}, u32[]{:S(2)}) async-start(bf16[64,15,8,128]{3,2,1,0:T(8,128)(2,1)} %get-tuple-element.32), calls=%async_computation | async-start | bytes 3932160 | tf_op jit(solution)/shard_map/all_to_all | solution.py:303
  44.1 0.6 collective-permute-start.9
  44.6 0.3 collective-permute-start.8
  44.9 1.3 collective-permute-start.7
  46.1 1.3 broadcast_add_fusion.1.twist_ref
  47.5 1.5 %broadcast_add_fusion.wave_hbm = bf16[2048,512]{1,0:T(8,128)(2,1)} fusion(bf16[2048,512]{1,0:T(8,128)(2,1)S(1)} %copy-done.2, bf16[]{:T(256)S(6)} %convert_element_type.7), kind=kLoop, calls=%fused_computation | loop fusion | flops 1048576 | bytes 4194306 | tf_op jit(solution)/shard_map/add | solution.py:311
  49.0 4.0 %collective-permute-done.9.refs_7_ = bf16[192,192]{1,0:T(8,128)(2,1)S(1)} collective-permute-done((bf16[192,192]{1,0:T(8,128)(2,1)S(1)}, bf16[192,192]{1,0:T(8,128)(2,1)S(1)}, u32[]{:S(2)}, u32[]{:S(2)}) %collective-permute-start.9) | collective-permute-done | bytes 73760 | tf_op jit(solution)/shard_map/ppermute | solution.py:267
  53.0 2.3 %collective-permute-done.7.refs_5_ = bf16[192,192]{1,0:T(8,128)(2,1)S(1)} collective-permute-done((bf16[192,192]{1,0:T(8,128)(2,1)S(1)}, bf16[192,192]{1,0:T(8,128)(2,1)S(1)}, u32[]{:S(2)}, u32[]{:S(2)}) %collective-permute-start.7) | collective-permute-done | bytes 73760 | tf_op jit(solution)/shard_map/ppermute | solution.py:267
  55.2 35.3 %all-to-all-done.m_ref = bf16[64,15,8,128]{3,2,1,0:T(8,128)(2,1)S(1)} async-done(((bf16[64,15,8,128]{3,2,1,0:T(8,128)(2,1)}), bf16[64,15,8,128]{3,2,1,0:T(8,128)(2,1)S(1)}, u32[]{:S(2)}, u32[]{:S(2)}) %all-to-all-start) | async-done | bytes 1966112 | tf_op jit(solution)/shard_map/all_to_all | solution.py:303
  90.5 5.6 %convolve.1 = bf16[64,3,8,128]{3,2,1,0:T(8,128)(2,1)} custom-call(bf16[64,15,8,128]{3,2,1,0:T(8,128)(2,1)S(1)} %all-to-all-done.m_ref, bf16[2048,512]{1,0:T(8,128)(2,1)} %broadcast_add_fusion.wave_hbm, f32[512,512]{1,0:T(8,128)S(1)} %broadcast_add_fusion.1.twist_ref), custom_call_target="tpu_custom_call" | custom-call | flops 3221225472 | bytes 6291456 | tf_op jit(solution)/shard_map/convolve/pallas_call | solution.py:198
  96.2 8.7 %all-to-all-start.1 = ((bf16[64,3,8,128]{3,2,1,0:T(8,128)(2,1)}), bf16[64,3,8,128]{3,2,1,0:T(8,128)(2,1)S(1)}, u32[]{:S(2)}, u32[]{:S(2)}) async-start(bf16[64,3,8,128]{3,2,1,0:T(8,128)(2,1)} %convolve.1), calls=%async_computation.1 | async-start | bytes 786432 | tf_op jit(solution)/shard_map/all_to_all | solution.py:316
  105.0 14.4 %all-to-all-done.1 = bf16[64,3,8,128]{3,2,1,0:T(8,128)(2,1)S(1)} async-done(((bf16[64,3,8,128]{3,2,1,0:T(8,128)(2,1)}), bf16[64,3,8,128]{3,2,1,0:T(8,128)(2,1)S(1)}, u32[]{:S(2)}, u32[]{:S(2)}) %all-to-all-start.1) | async-done | bytes 393248 | tf_op jit(solution)/shard_map/all_to_all | solution.py:316
  119.4 1.1 copy-done
  120.5 0.3 gated.1.refs_0_
  120.9 4.3 %collective-permute-start.11 = (bf16[192,1024]{1,0:T(8,128)(2,1)S(1)}, bf16[192,1024]{1,0:T(8,128)(2,1)S(1)}, u32[]{:S(2)}, u32[]{:S(2)}) collective-permute-start(bf16[192,1024]{1,0:T(8,128)(2,1)S(1)} %gated.1.refs_0_), channel_id=1, source_target_pairs={{0,1},{1,0},{2,3},{3,2},{4,5},{5,4},{6,7},{7,6},{8,9},{9,8},{10,11... | collective-permute-start | bytes 1179656 | tf_op jit(solution)/shard_map/ppermute | solution.py:267
  125.2 2.3 %collective-permute-done.10.refs_1_ = bf16[192,1024]{1,0:T(8,128)(2,1)S(1)} collective-permute-done((bf16[192,1024]{1,0:T(8,128)(2,1)S(1)}, bf16[192,1024]{1,0:T(8,128)(2,1)S(1)}, u32[]{:S(2)}, u32[]{:S(2)}) %collective-permute-start.10) | collective-permute-done | bytes 393248 | tf_op jit(solution)/shard_map/ppermute | solution.py:267
  127.5 5.2 %collective-permute-start.12 = (bf16[192,1024]{1,0:T(8,128)(2,1)S(1)}, bf16[192,1024]{1,0:T(8,128)(2,1)S(1)}, u32[]{:S(2)}, u32[]{:S(2)}) collective-permute-start(bf16[192,1024]{1,0:T(8,128)(2,1)S(1)} %collective-permute-done.10.refs_1_), channel_id=1, source_target_pairs={{0,1},{1,0},{2,3},{3,2},{4,5},{5,4},{6,7},{7,6},{8,9},{9,8},{10,11... | collective-permute-start | bytes 1179656 | tf_op jit(solution)/shard_map/ppermute | solution.py:267
  132.7 1.3 collective-permute-done.12.refs_3_
  134.1 1.3 mixed.1
  (28 shorter events, 0.7 us)
Async XLA Ops:
  0.0 24.0 %collective-permute-start = (bf16[192,1024]{1,0:T(8,128)(2,1)}, bf16[192,1024]{1,0:T(8,128)(2,1)S(1)}, u32[]{:S(2)}, u32[]{:S(2)}) collective-permute-start(bf16[192,1024]{1,0:T(8,128)(2,1)} %refs_1_.1), channel_id=1, source_target_pairs={{0,2},{1,3},{2,0},{3,1},{4,6},{5,7},{6,4},{7,5},{8,10},{9,11},{10,... | collective-permute-start | bytes 1179656 | tf_op jit(solution)/shard_map/ppermute | solution.py:267
  2.9 19.6 %copy-start.1 = (bf16[192,1024]{1,0:T(8,128)(2,1)S(1)}, bf16[192,1024]{1,0:T(8,128)(2,1)}, u32[]{:S(2)}) copy-start(bf16[192,1024]{1,0:T(8,128)(2,1)} %refs_1_.1) | copy-start | bytes 1179652
  2.9 21.3 %copy-start.6 = (f32[3,3,192]{2,1,0:T(4,128)S(1)}, f32[3,3,192]{2,1,0:T(4,128)}, u32[]{:S(2)}) copy-start(f32[3,3,192]{2,1,0:T(4,128)} %param.10) | copy-start | bytes 20740
  2.9 19.6 %collective-permute-start.4 = (bf16[192,128]{1,0:T(8,128)(2,1)S(1)}, bf16[192,128]{1,0:T(8,128)(2,1)S(1)}, u32[]{:S(2)}, u32[]{:S(2)}) collective-permute-start(bf16[192,128]{1,0:T(8,128)(2,1)S(1)} %slice.3), channel_id=1, source_target_pairs={{3,4},{2,5},{1,6},{0,7},{7,8},{6,9},{5,10},{4,11},{11,12},{10,13},... | collective-permute-start | bytes 147464 | tf_op jit(solution)/shard_map/ppermute | solution.py:280
  7.4 16.7 %collective-permute-start.3 = (bf16[192,128]{1,0:T(8,128)(2,1)S(1)}, bf16[192,128]{1,0:T(8,128)(2,1)S(1)}, u32[]{:S(2)}, u32[]{:S(2)}) collective-permute-start(bf16[192,128]{1,0:T(8,128)(2,1)S(1)} %slice.3), channel_id=1, source_target_pairs={{1,4},{0,5},{3,6},{2,7},{5,8},{4,9},{7,10},{6,11},{9,12},{8,13},{1... | collective-permute-start | bytes 147464 | tf_op jit(solution)/shard_map/ppermute | solution.py:280
  10.4 13.7 %collective-permute-start.2 = (bf16[192,128]{1,0:T(8,128)(2,1)S(1)}, bf16[192,128]{1,0:T(8,128)(2,1)S(1)}, u32[]{:S(2)}, u32[]{:S(2)}) collective-permute-start(bf16[192,128]{1,0:T(8,128)(2,1)S(1)} %slice.3), channel_id=1, source_target_pairs={{2,4},{3,5},{0,6},{1,7},{6,8},{7,9},{4,10},{5,11},{10,12},{11,13},... | collective-permute-start | bytes 147464 | tf_op jit(solution)/shard_map/ppermute | solution.py:280
  14.8 9.2 %collective-permute-start.1 = (bf16[192,128]{1,0:T(8,128)(2,1)S(1)}, bf16[192,128]{1,0:T(8,128)(2,1)S(1)}, u32[]{:S(2)}, u32[]{:S(2)}) collective-permute-start(bf16[192,128]{1,0:T(8,128)(2,1)S(1)} %slice.3), channel_id=1, source_target_pairs={{0,4},{1,5},{2,6},{3,7},{4,8},{5,9},{6,10},{7,11},{8,12},{9,13},{1... | collective-permute-start | bytes 147464 | tf_op jit(solution)/shard_map/ppermute | solution.py:280
  22.5 2.9 %collective-permute-start.5 = (bf16[192,1024]{1,0:T(8,128)(2,1)S(1)}, bf16[192,1024]{1,0:T(8,128)(2,1)S(1)}, u32[]{:S(2)}, u32[]{:S(2)}) collective-permute-start(bf16[192,1024]{1,0:T(8,128)(2,1)S(1)} %copy-done.1), channel_id=1, source_target_pairs={{0,1},{1,0},{2,3},{3,2},{4,5},{5,4},{6,7},{7,6},{8,9},{9,8},{10,11... | collective-permute-start | bytes 1179656 | tf_op jit(solution)/shard_map/ppermute | solution.py:267
  24.0 1.9 %collective-permute-start.6 = (bf16[192,1024]{1,0:T(8,128)(2,1)S(1)}, bf16[192,1024]{1,0:T(8,128)(2,1)S(1)}, u32[]{:S(2)}, u32[]{:S(2)}) collective-permute-start(bf16[192,1024]{1,0:T(8,128)(2,1)S(1)} %collective-permute-done.refs_2_), channel_id=1, source_target_pairs={{0,1},{1,0},{2,3},{3,2},{4,5},{5,4},{6,7},{7,6},{8,9},{9,8},{10,11... | collective-permute-start | bytes 1179656 | tf_op jit(solution)/shard_map/ppermute | solution.py:267
  25.4 0.7 copy-start.3
  25.9 0.7 copy-start.4
  33.6 10.2 %copy-start.5 = (bf16[192,768]{1,0:T(8,128)(2,1)S(1)}, bf16[192,768]{1,0:T(8,128)(2,1)}, u32[]{:S(2)}) copy-start(bf16[192,768]{1,0:T(8,128)(2,1)} %param.13) | copy-start | bytes 884740
  33.6 56.9 %all-to-all-start = ((bf16[64,15,8,128]{3,2,1,0:T(8,128)(2,1)}), bf16[64,15,8,128]{3,2,1,0:T(8,128)(2,1)S(1)}, u32[]{:S(2)}, u32[]{:S(2)}) async-start(bf16[64,15,8,128]{3,2,1,0:T(8,128)(2,1)} %get-tuple-element.32), calls=%async_computation | async-start | bytes 3932160 | tf_op jit(solution)/shard_map/all_to_all | solution.py:303
  44.0 3.5 %copy-start.2 = (bf16[2048,512]{1,0:T(8,128)(2,1)S(1)}, bf16[2048,512]{1,0:T(8,128)(2,1)}, u32[]{:S(2)}) copy-start(bf16[2048,512]{1,0:T(8,128)(2,1)} %constant.20.clone) | copy-start | bytes 6291460
  44.1 8.9 %collective-permute-start.9 = (bf16[192,192]{1,0:T(8,128)(2,1)S(1)}, bf16[192,192]{1,0:T(8,128)(2,1)S(1)}, u32[]{:S(2)}, u32[]{:S(2)}) collective-permute-start(bf16[192,192]{1,0:T(8,128)(2,1)S(1)} %get-tuple-element.45), channel_id=1, source_target_pairs={{0,3},{1,2},{2,1},{3,0},{4,7},{5,6},{6,5},{7,4},{8,11},{9,10},{10,... | collective-permute-start | bytes 221192 | tf_op jit(solution)/shard_map/ppermute | solution.py:267
  44.6 8.3 %collective-permute-start.8 = (bf16[192,192]{1,0:T(8,128)(2,1)S(1)}, bf16[192,192]{1,0:T(8,128)(2,1)S(1)}, u32[]{:S(2)}, u32[]{:S(2)}) collective-permute-start(bf16[192,192]{1,0:T(8,128)(2,1)S(1)} %get-tuple-element.46), channel_id=1, source_target_pairs={{0,1},{1,0},{2,3},{3,2},{4,5},{5,4},{6,7},{7,6},{8,9},{9,8},{10,11... | collective-permute-start | bytes 221192 | tf_op jit(solution)/shard_map/ppermute | solution.py:267
  44.9 10.4 %collective-permute-start.7 = (bf16[192,192]{1,0:T(8,128)(2,1)S(1)}, bf16[192,192]{1,0:T(8,128)(2,1)S(1)}, u32[]{:S(2)}, u32[]{:S(2)}) collective-permute-start(bf16[192,192]{1,0:T(8,128)(2,1)S(1)} %get-tuple-element.47), channel_id=1, source_target_pairs={{0,2},{1,3},{2,0},{3,1},{4,6},{5,7},{6,4},{7,5},{8,10},{9,11},{10,... | collective-permute-start | bytes 221192 | tf_op jit(solution)/shard_map/ppermute | solution.py:267
  47.5 1.5 %copy-start.7 = (f32[192]{0:T(256)S(1)}, f32[192]{0:T(256)}, u32[]{:S(2)}) copy-start(f32[192]{0:T(256)} %param.11) | copy-start | bytes 2308
  96.2 23.2 %all-to-all-start.1 = ((bf16[64,3,8,128]{3,2,1,0:T(8,128)(2,1)}), bf16[64,3,8,128]{3,2,1,0:T(8,128)(2,1)S(1)}, u32[]{:S(2)}, u32[]{:S(2)}) async-start(bf16[64,3,8,128]{3,2,1,0:T(8,128)(2,1)} %convolve.1), calls=%async_computation.1 | async-start | bytes 786432 | tf_op jit(solution)/shard_map/all_to_all | solution.py:316
  119.4 1.1 copy-start
  120.8 6.7 %collective-permute-start.10 = (bf16[192,1024]{1,0:T(8,128)(2,1)S(1)}, bf16[192,1024]{1,0:T(8,128)(2,1)S(1)}, u32[]{:S(2)}, u32[]{:S(2)}) collective-permute-start(bf16[192,1024]{1,0:T(8,128)(2,1)S(1)} %gated.1.refs_0_), channel_id=1, source_target_pairs={{0,2},{1,3},{2,0},{3,1},{4,6},{5,7},{6,4},{7,5},{8,10},{9,11},{10,... | collective-permute-start | bytes 1179656 | tf_op jit(solution)/shard_map/ppermute | solution.py:267
  120.9 11.8 %collective-permute-start.11 = (bf16[192,1024]{1,0:T(8,128)(2,1)S(1)}, bf16[192,1024]{1,0:T(8,128)(2,1)S(1)}, u32[]{:S(2)}, u32[]{:S(2)}) collective-permute-start(bf16[192,1024]{1,0:T(8,128)(2,1)S(1)} %gated.1.refs_0_), channel_id=1, source_target_pairs={{0,1},{1,0},{2,3},{3,2},{4,5},{5,4},{6,7},{7,6},{8,9},{9,8},{10,11... | collective-permute-start | bytes 1179656 | tf_op jit(solution)/shard_map/ppermute | solution.py:267
  127.5 6.6 %collective-permute-start.12 = (bf16[192,1024]{1,0:T(8,128)(2,1)S(1)}, bf16[192,1024]{1,0:T(8,128)(2,1)S(1)}, u32[]{:S(2)}, u32[]{:S(2)}) collective-permute-start(bf16[192,1024]{1,0:T(8,128)(2,1)S(1)} %collective-permute-done.10.refs_1_), channel_id=1, source_target_pairs={{0,1},{1,0},{2,3},{3,2},{4,5},{5,4},{6,7},{7,6},{8,9},{9,8},{10,11... | collective-permute-start | bytes 1179656 | tf_op jit(solution)/shard_map/ppermute | solution.py:267

commit v4 on v3

--- a/solution.py
+++ b/solution.py
@@ -11,7 +11,7 @@
 COLS = 256
 FREQS = 512
 LANES = 128
-PROJECT_VMEM = 54000 << 10
+PROJECT_VMEM = 50000 << 10
 CONVOLVE_VMEM = 50000 << 10
 MASKS = (0, 2, 1, 3)
 BF16 = jnp.bfloat16
@@ -98,12 +98,21 @@
             spread_ref[pl.ds(row * 8 + part, rows, stride=8), :] = signal[:, part * LANES:(part + 1) * LANES]
         return carry
 
-    lax.fori_loop(0, channels // rows, chunk, 0)
-    part_ref[...] = spread_ref[...].reshape(part_ref.shape).astype(BF16)
-    per_dest = part_ref.shape[1]
-    copy = pltpu.make_async_copy(part_ref, message_ref.at[:, pl.ds(4 * per_dest, per_dest)], sem)
-    copy.start()
-    copy.wait()
+    shards, per_dest = part_ref.shape[:2]
+    groups = 4
+    each = channels // groups
+    copies = []
+    for group in range(groups):
+        lax.fori_loop(group * each // rows, (group + 1) * each // rows, chunk, 0)
+        dests = pl.ds(group * shards // groups, shards // groups)
+        ready = spread_ref[pl.ds(group * each * 8, each * 8), :].astype(BF16)
+        part_ref[dests] = ready.reshape(shards // groups, *part_ref.shape[1:])
+        copies.append(pltpu.make_async_copy(
+            part_ref.at[dests], message_ref.at[dests, pl.ds(4 * per_dest, per_dest)], sem.at[group]
+        ))
+        copies[-1].start()
+    for copy in copies:
+        copy.wait()
 
 
 def project(grp, mains, halos, weight, taps, packed):
@@ -125,7 +134,7 @@
             pltpu.VMEM((3 * channels, width), F32),
             pltpu.VMEM((channels * 8, LANES), F32),
             pltpu.VMEM((shards, pieces // 5, 8, LANES), BF16),
-            pltpu.SemaphoreType.DMA,
+            pltpu.SemaphoreType.DMA((4,)),
         ],
         input_output_aliases={11: 0},
         compiler_params=pltpu.CompilerParams(vmem_limit_bytes=PROJECT_VMEM),
@@ -273,13 +282,6 @@
     return block, far, near, swapped(far, 1)
 
 
-def previous_tail(tail, mask, shard_count):
-    route = [
-        ((s - 1) * 4 + (g ^ mask), s * 4 + g) for s in range(1, shard_count) for g in range(4)
-    ]
-    return lax.ppermute(tail, ("seq", "grp"), route)
-
-
 def shards(tokens, in_weight, short_weight, filter_bias, spectra, out_weight):
     shard_count = lax.axis_size("seq")
     grp = lax.axis_index("grp")
@@ -288,11 +290,15 @@
 
     far = swapped(tokens, 2)
     near = swapped(tokens, 1)
-    tail = tokens[:, -LANES:]
-    halos = [previous_tail(tail, mask, shard_count) for mask in MASKS]
+    route = [(i, i + 1) for i in range(shard_count - 1)]
+    halo = lax.ppermute(tokens[:, -LANES:], "seq", route)
     packed = pack_spectra(spectra, shard_count)
-    far, halos, packed = lax.optimization_barrier((far, halos, packed))
+    halo, packed = lax.optimization_barrier((halo, packed))
+    halo_far = swapped(halo, 2)
+    halo_near = swapped(halo, 1)
+    far, halo_far = lax.optimization_barrier((far, halo_far))
     mains = [tokens, far, near, swapped(far, 1)]
+    halos = [halo, halo_far, halo_near, swapped(halo_far, 1)]
     taps = jnp.transpose(short_weight, (2, 0, 1)).reshape(channels, 9)
     message, kept = project(
         grp.reshape(1).astype(jnp.int32), mains, halos, in_weight.reshape(3 * channels, -1), taps, packed

time: 136 us -> 128 us (0.941)
  starting transfers between devices: 50.8 us -> 44.5 us
  Pallas kernels: 17.1 us -> 14.7 us
    ppermute x4 -> x1, starting transfers between devices: 16.7 us -> 3.68 us  [shards(): halo = lax.ppermute(tokens[:, -LANES:], 'seq', route)]
    all_to_all x1, starting transfers between devices: 10.1 us -> 14.6 us  [shards(): received = lax.all_to_all(message, 'seq', 0, 0, tiled=True)]
    pallas_call x1, Pallas kernels: 6.93 us -> 4.51 us  [project(): pl.pallas_call(project_body, in_specs=[pl.BlockSpec(memory_space=pltpu.SM...]
    ppermute x9 -> x12, starting transfers between devices: 15.3 us -> 17.6 us  [swapped(): return lax.ppermute(block, 'grp', [(i, i ^ mask) for i in range(4)])]
    ppermute x9 -> x12, waiting for transfers between devices: 11.6 us -> 12.8 us  [swapped(): return lax.ppermute(block, 'grp', [(i, i ^ mask) for i in range(4)])]
  transfers between devices with their start and end apart: 15 -> 15, of which waited for: 8 -> 9; matrix products, arithmetic and copies ran while one was open for 3% -> 3% of each run, Pallas kernels for 2% -> 2%
where the time goes in v4:
time: 128 us
  waiting for transfers between devices  62.5 us (49%)
  starting transfers between devices  44.5 us (35%)
  Pallas kernels  14.7 us (11%)
  local copies, waits for them, and re-layouts  3.34 us (3%)
  other arithmetic  2.78 us (2%)
    all_to_all x1, waiting for transfers between devices, shards(): received = lax.all_to_all(message, 'seq', 0, 0, tiled=True)  35.3 us
    ppermute x12, starting transfers between devices, swapped(): return lax.ppermute(block, 'grp', [(i, i ^ mask) for i in range(4)])  17.6 us
    all_to_all x1, starting transfers between devices, shards(): received = lax.all_to_all(message, 'seq', 0, 0, tiled=True)  14.6 us
    all_to_all x1, waiting for transfers between devices, shards(): lax.all_to_all(result, 'seq', 0, 0, tiled=True).reshape(channels * 8, LANES)  14.4 us
    ppermute x12, waiting for transfers between devices, swapped(): return lax.ppermute(block, 'grp', [(i, i ^ mask) for i in range(4)])  12.8 us
    all_to_all x1, starting transfers between devices, shards(): lax.all_to_all(result, 'seq', 0, 0, tiled=True).reshape(channels * 8, LANES)  8.67 us
    pallas_call x1, Pallas kernels, convolve(): pl.pallas_call(convolve_body, in_specs=[vmem, pl.BlockSpec(memory_space=p...  5.63 us
    pallas_call x1, Pallas kernels, project(): pl.pallas_call(project_body, in_specs=[pl.BlockSpec(memory_space=pltpu.SM...  4.51 us
  transfers between devices with their start and end apart: 15, of which 9 were waited for; matrix products, arithmetic and copies ran while one was open for 3% of the time, Pallas kernels for 2%

profile of v4, /device:TPU:1, one launch (start us, length us, event | category | flops | bytes accessed | tf_op | source)
XLA Modules:
  0.0 127.9 jit_solution(4185812653557303548)
XLA Ops:
  0.0 2.0 %collective-permute-start = (bf16[192,1024]{1,0:T(8,128)(2,1)}, bf16[192,1024]{1,0:T(8,128)(2,1)S(1)}, u32[]{:S(2)}, u32[]{:S(2)}) collective-permute-start(bf16[192,1024]{1,0:T(8,128)(2,1)} %refs_1_.1), channel_id=1, source_target_pairs={{0,2},{1,3},{2,0},{3,1},{4,6},{5,7},{6,4},{7,5},{8,10},{9,11},{10,... | collective-permute-start | bytes 1179656 | tf_op jit(solution)/shard_map/ppermute | solution.py:276
  2.0 0.8 slice.3
  2.9 3.7 %collective-permute-start.1 = (bf16[192,128]{1,0:T(8,128)(2,1)S(1)}, bf16[192,128]{1,0:T(8,128)(2,1)S(1)}, u32[]{:S(2)}, u32[]{:S(2)}) collective-permute-start(bf16[192,128]{1,0:T(8,128)(2,1)S(1)} %slice.3), channel_id=1, source_target_pairs={{0,4},{4,8},{8,12},{12,16},{16,20},{20,24},{24,28},{28,32},{32,36}... | collective-permute-start | bytes 147464 | tf_op jit(solution)/shard_map/ppermute | solution.py:294
  6.6 2.9 %pack_spectra.1.refs_11_ = bf16[64,15,8,128]{3,2,1,0:T(8,128)(2,1)} custom-call(f32[2,192,8,256]{3,2,1,0:T(8,128)} %spec_ref.1), custom_call_target="tpu_custom_call" | custom-call | bytes 4718592 | tf_op jit(solution)/shard_map/pack_spectra/pallas_call | solution.py:58
  9.5 0.3 collective-permute-start.2
  9.7 1.5 %collective-permute-start.3 = (bf16[192,1024]{1,0:T(8,128)(2,1)S(1)}, bf16[192,1024]{1,0:T(8,128)(2,1)S(1)}, u32[]{:S(2)}, u32[]{:S(2)}) collective-permute-start(bf16[192,1024]{1,0:T(8,128)(2,1)S(1)} %copy-done.3), channel_id=1, source_target_pairs={{0,1},{1,0},{2,3},{3,2},{4,5},{5,4},{6,7},{7,6},{8,9},{9,8},{10,11... | collective-permute-start | bytes 1179656 | tf_op jit(solution)/shard_map/ppermute | solution.py:276
  11.2 2.0 %collective-permute-done.2.refs_6_ = bf16[192,128]{1,0:T(8,128)(2,1)S(1)} collective-permute-done((bf16[192,128]{1,0:T(8,128)(2,1)S(1)}, bf16[192,128]{1,0:T(8,128)(2,1)S(1)}, u32[]{:S(2)}, u32[]{:S(2)}) %collective-permute-start.2) | collective-permute-done | bytes 49184 | tf_op jit(solution)/shard_map/ppermute | solution.py:276
  13.2 1.6 %collective-permute-start.4 = (bf16[192,1024]{1,0:T(8,128)(2,1)S(1)}, bf16[192,1024]{1,0:T(8,128)(2,1)S(1)}, u32[]{:S(2)}, u32[]{:S(2)}) collective-permute-start(bf16[192,1024]{1,0:T(8,128)(2,1)S(1)} %collective-permute-done.refs_2_), channel_id=1, source_target_pairs={{0,1},{1,0},{2,3},{3,2},{4,5},{5,4},{6,7},{7,6},{8,9},{9,8},{10,11... | collective-permute-start | bytes 1179656 | tf_op jit(solution)/shard_map/ppermute | solution.py:276
  14.8 0.5 collective-permute-start.6
  15.4 0.8 collective-permute-done.5.refs_7_
  16.3 4.5 %project.1 = (bf16[64,15,8,128]{3,2,1,0:T(8,128)(2,1)}, bf16[2,192,1024]{2,1,0:T(8,128)(2,1)S(1)}) custom-call(s32[1]{0:T(128)} %bitcast.refs_0_, bf16[192,1024]{1,0:T(8,128)(2,1)S(1)} %copy-done.3, bf16[192,1024]{1,0:T(8,128)(2,1)S(1)} %collective-permute-done.refs_2_, ...), custom_call_target="tpu_custom_call", output_to_operand_aliasing={{0}: (11, {})} | custom-call | flops 1019215872 | bytes 6291456 | tf_op jit(solution)/shard_map/project/pallas_call | solution.py:124
  20.8 0.9 copy-done.1
  21.7 14.6 %all-to-all-start = ((bf16[64,15,8,128]{3,2,1,0:T(8,128)(2,1)}), bf16[64,15,8,128]{3,2,1,0:T(8,128)(2,1)S(1)}, u32[]{:S(2)}, u32[]{:S(2)}) async-start(bf16[64,15,8,128]{3,2,1,0:T(8,128)(2,1)} %get-tuple-element.28), calls=%async_computation | async-start | bytes 3932160 | tf_op jit(solution)/shard_map/all_to_all | solution.py:309
  36.3 0.2 copy.16
  36.6 0.6 collective-permute-start.9
  37.2 0.3 collective-permute-start.8
  37.4 1.3 collective-permute-start.7
  38.7 1.3 %broadcast_add_fusion.1.twist_ref = f32[512,512]{1,0:T(8,128)S(1)} fusion(f32[512,512]{1,0:T(8,128)} %constant.21.clone, f32[]{:T(128)S(6)} %convert_element_type.8), kind=kLoop, calls=%fused_computation.1 | loop fusion | flops 262144 | bytes 2097156 | tf_op jit(solution)/shard_map/add | solution.py:317
  40.0 1.5 %broadcast_add_fusion.wave_hbm = bf16[2048,512]{1,0:T(8,128)(2,1)} fusion(bf16[2048,512]{1,0:T(8,128)(2,1)S(1)} %copy-done.4, bf16[]{:T(256)S(6)} %convert_element_type.7), kind=kLoop, calls=%fused_computation | loop fusion | flops 1048576 | bytes 4194306 | tf_op jit(solution)/shard_map/add | solution.py:317
  41.5 4.0 %collective-permute-done.9.refs_7_ = bf16[192,192]{1,0:T(8,128)(2,1)S(1)} collective-permute-done((bf16[192,192]{1,0:T(8,128)(2,1)S(1)}, bf16[192,192]{1,0:T(8,128)(2,1)S(1)}, u32[]{:S(2)}, u32[]{:S(2)}) %collective-permute-start.9) | collective-permute-done | bytes 73760 | tf_op jit(solution)/shard_map/ppermute | solution.py:276
  45.5 2.3 %collective-permute-done.7.refs_5_ = bf16[192,192]{1,0:T(8,128)(2,1)S(1)} collective-permute-done((bf16[192,192]{1,0:T(8,128)(2,1)S(1)}, bf16[192,192]{1,0:T(8,128)(2,1)S(1)}, u32[]{:S(2)}, u32[]{:S(2)}) %collective-permute-start.7) | collective-permute-done | bytes 73760 | tf_op jit(solution)/shard_map/ppermute | solution.py:276
  47.8 35.3 %all-to-all-done.m_ref = bf16[64,15,8,128]{3,2,1,0:T(8,128)(2,1)S(1)} async-done(((bf16[64,15,8,128]{3,2,1,0:T(8,128)(2,1)}), bf16[64,15,8,128]{3,2,1,0:T(8,128)(2,1)S(1)}, u32[]{:S(2)}, u32[]{:S(2)}) %all-to-all-start) | async-done | bytes 1966112 | tf_op jit(solution)/shard_map/all_to_all | solution.py:309
  83.1 5.6 %convolve.1 = bf16[64,3,8,128]{3,2,1,0:T(8,128)(2,1)} custom-call(bf16[64,15,8,128]{3,2,1,0:T(8,128)(2,1)S(1)} %all-to-all-done.m_ref, bf16[2048,512]{1,0:T(8,128)(2,1)} %broadcast_add_fusion.wave_hbm, f32[512,512]{1,0:T(8,128)S(1)} %broadcast_add_fusion.1.twist_ref), custom_call_target="tpu_custom_call" | custom-call | flops 3221225472 | bytes 6291456 | tf_op jit(solution)/shard_map/convolve/pallas_call | solution.py:207
  88.7 8.7 %all-to-all-start.1 = ((bf16[64,3,8,128]{3,2,1,0:T(8,128)(2,1)}), bf16[64,3,8,128]{3,2,1,0:T(8,128)(2,1)S(1)}, u32[]{:S(2)}, u32[]{:S(2)}) async-start(bf16[64,3,8,128]{3,2,1,0:T(8,128)(2,1)} %convolve.1), calls=%async_computation.1 | async-start | bytes 786432 | tf_op jit(solution)/shard_map/all_to_all | solution.py:322
  97.5 14.4 %all-to-all-done.1 = bf16[64,3,8,128]{3,2,1,0:T(8,128)(2,1)S(1)} async-done(((bf16[64,3,8,128]{3,2,1,0:T(8,128)(2,1)}), bf16[64,3,8,128]{3,2,1,0:T(8,128)(2,1)S(1)}, u32[]{:S(2)}, u32[]{:S(2)}) %all-to-all-start.1) | async-done | bytes 393248 | tf_op jit(solution)/shard_map/all_to_all | solution.py:322
  111.9 1.1 copy-done.2
  113.0 0.3 gated.1.refs_0_
  113.5 4.3 %collective-permute-start.11 = (bf16[192,1024]{1,0:T(8,128)(2,1)S(1)}, bf16[192,1024]{1,0:T(8,128)(2,1)S(1)}, u32[]{:S(2)}, u32[]{:S(2)}) collective-permute-start(bf16[192,1024]{1,0:T(8,128)(2,1)S(1)} %gated.1.refs_0_), channel_id=1, source_target_pairs={{0,1},{1,0},{2,3},{3,2},{4,5},{5,4},{6,7},{7,6},{8,9},{9,8},{10,11... | collective-permute-start | bytes 1179656 | tf_op jit(solution)/shard_map/ppermute | solution.py:276
  117.7 2.3 %collective-permute-done.10.refs_1_ = bf16[192,1024]{1,0:T(8,128)(2,1)S(1)} collective-permute-done((bf16[192,1024]{1,0:T(8,128)(2,1)S(1)}, bf16[192,1024]{1,0:T(8,128)(2,1)S(1)}, u32[]{:S(2)}, u32[]{:S(2)}) %collective-permute-start.10) | collective-permute-done | bytes 393248 | tf_op jit(solution)/shard_map/ppermute | solution.py:276
  120.1 5.2 %collective-permute-start.12 = (bf16[192,1024]{1,0:T(8,128)(2,1)S(1)}, bf16[192,1024]{1,0:T(8,128)(2,1)S(1)}, u32[]{:S(2)}, u32[]{:S(2)}) collective-permute-start(bf16[192,1024]{1,0:T(8,128)(2,1)S(1)} %collective-permute-done.10.refs_1_), channel_id=1, source_target_pairs={{0,1},{1,0},{2,3},{3,2},{4,5},{5,4},{6,7},{7,6},{8,9},{9,8},{10,11... | collective-permute-start | bytes 1179656 | tf_op jit(solution)/shard_map/ppermute | solution.py:276
  125.3 1.3 %collective-permute-done.12.refs_3_ = bf16[192,1024]{1,0:T(8,128)(2,1)S(1)} collective-permute-done((bf16[192,1024]{1,0:T(8,128)(2,1)S(1)}, bf16[192,1024]{1,0:T(8,128)(2,1)S(1)}, u32[]{:S(2)}, u32[]{:S(2)}) %collective-permute-start.12) | collective-permute-done | bytes 393248 | tf_op jit(solution)/shard_map/ppermute | solution.py:276
  126.6 1.3 %mixed.1 = bf16[192,1024]{1,0:T(8,128)(2,1)} custom-call(bf16[192,1024]{1,0:T(8,128)(2,1)S(1)} %gated.1.refs_0_, bf16[192,1024]{1,0:T(8,128)(2,1)S(1)} %collective-permute-done.10.refs_1_, bf16[192,1024]{1,0:T(8,128)(2,1)S(1)} %collective-permute-done.11.refs_2_, bf16[192,1024]{1,0:T(8,128)(2,1)S(1)} %collective-permute-done.12.refs_3_, ...), custom_call_target="tpu_custom_call" | custom-call | flops 301989888 | bytes 3145728 | tf_op jit(solution)/shard_map/mixed/pallas_call | solution.py:264
  (28 shorter events, 0.5 us)
Async XLA Ops:
  0.0 13.2 %collective-permute-start = (bf16[192,1024]{1,0:T(8,128)(2,1)}, bf16[192,1024]{1,0:T(8,128)(2,1)S(1)}, u32[]{:S(2)}, u32[]{:S(2)}) collective-permute-start(bf16[192,1024]{1,0:T(8,128)(2,1)} %refs_1_.1), channel_id=1, source_target_pairs={{0,2},{1,3},{2,0},{3,1},{4,6},{5,7},{6,4},{7,5},{8,10},{9,11},{10,... | collective-permute-start | bytes 1179656 | tf_op jit(solution)/shard_map/ppermute | solution.py:276
  2.9 6.8 %copy-start.3 = (bf16[192,1024]{1,0:T(8,128)(2,1)S(1)}, bf16[192,1024]{1,0:T(8,128)(2,1)}, u32[]{:S(2)}) copy-start(bf16[192,1024]{1,0:T(8,128)(2,1)} %refs_1_.1) | copy-start | bytes 1179652
  2.9 12.4 %copy-start.6 = (f32[3,3,192]{2,1,0:T(4,128)S(1)}, f32[3,3,192]{2,1,0:T(4,128)}, u32[]{:S(2)}) copy-start(f32[3,3,192]{2,1,0:T(4,128)} %param.10) | copy-start | bytes 20740
  2.9 13.4 %copy-start = (bf16[3,192,768]{2,1,0:T(8,128)(2,1)S(1)}, bf16[3,192,768]{2,1,0:T(8,128)(2,1)}, u32[]{:S(2)}) copy-start(bf16[3,192,768]{2,1,0:T(8,128)(2,1)} %param.9) | copy-start | bytes 2654212
  2.9 6.6 %collective-permute-start.1 = (bf16[192,128]{1,0:T(8,128)(2,1)S(1)}, bf16[192,128]{1,0:T(8,128)(2,1)S(1)}, u32[]{:S(2)}, u32[]{:S(2)}) collective-permute-start(bf16[192,128]{1,0:T(8,128)(2,1)S(1)} %slice.3), channel_id=1, source_target_pairs={{0,4},{4,8},{8,12},{12,16},{16,20},{20,24},{24,28},{28,32},{32,36}... | collective-permute-start | bytes 147464 | tf_op jit(solution)/shard_map/ppermute | solution.py:294
  9.5 3.7 %collective-permute-start.2 = (bf16[192,128]{1,0:T(8,128)(2,1)S(1)}, bf16[192,128]{1,0:T(8,128)(2,1)S(1)}, u32[]{:S(2)}, u32[]{:S(2)}) collective-permute-start(bf16[192,128]{1,0:T(8,128)(2,1)S(1)} %collective-permute-done.1.refs_5_), channel_id=1, source_target_pairs={{0,2},{1,3},{2,0},{3,1},{4,6},{5,7},{6,4},{7,5},{8,10},{9,11},{10,... | collective-permute-start | bytes 147464 | tf_op jit(solution)/shard_map/ppermute | solution.py:276
  9.7 6.5 %collective-permute-start.3 = (bf16[192,1024]{1,0:T(8,128)(2,1)S(1)}, bf16[192,1024]{1,0:T(8,128)(2,1)S(1)}, u32[]{:S(2)}, u32[]{:S(2)}) collective-permute-start(bf16[192,1024]{1,0:T(8,128)(2,1)S(1)} %copy-done.3), channel_id=1, source_target_pairs={{0,1},{1,0},{2,3},{3,2},{4,5},{5,4},{6,7},{7,6},{8,9},{9,8},{10,11... | collective-permute-start | bytes 1179656 | tf_op jit(solution)/shard_map/ppermute | solution.py:276
  13.2 3.1 %collective-permute-start.4 = (bf16[192,1024]{1,0:T(8,128)(2,1)S(1)}, bf16[192,1024]{1,0:T(8,128)(2,1)S(1)}, u32[]{:S(2)}, u32[]{:S(2)}) collective-permute-start(bf16[192,1024]{1,0:T(8,128)(2,1)S(1)} %collective-permute-done.refs_2_), channel_id=1, source_target_pairs={{0,1},{1,0},{2,3},{3,2},{4,5},{5,4},{6,7},{7,6},{8,9},{9,8},{10,11... | collective-permute-start | bytes 1179656 | tf_op jit(solution)/shard_map/ppermute | solution.py:276
  14.8 1.4 %collective-permute-start.5 = (bf16[192,128]{1,0:T(8,128)(2,1)S(1)}, bf16[192,128]{1,0:T(8,128)(2,1)S(1)}, u32[]{:S(2)}, u32[]{:S(2)}) collective-permute-start(bf16[192,128]{1,0:T(8,128)(2,1)S(1)} %collective-permute-done.1.refs_5_), channel_id=1, source_target_pairs={{0,1},{1,0},{2,3},{3,2},{4,5},{5,4},{6,7},{7,6},{8,9},{9,8},{10,11... | collective-permute-start | bytes 147464 | tf_op jit(solution)/shard_map/ppermute | solution.py:276
  14.8 1.5 %collective-permute-start.6 = (bf16[192,128]{1,0:T(8,128)(2,1)S(1)}, bf16[192,128]{1,0:T(8,128)(2,1)S(1)}, u32[]{:S(2)}, u32[]{:S(2)}) collective-permute-start(bf16[192,128]{1,0:T(8,128)(2,1)S(1)} %collective-permute-done.2.refs_6_), channel_id=1, source_target_pairs={{0,1},{1,0},{2,3},{3,2},{4,5},{5,4},{6,7},{7,6},{8,9},{9,8},{10,11... | collective-permute-start | bytes 147464 | tf_op jit(solution)/shard_map/ppermute | solution.py:276
  20.8 0.9 copy-start.1
  21.7 14.6 %copy-start.5 = (bf16[192,768]{1,0:T(8,128)(2,1)S(1)}, bf16[192,768]{1,0:T(8,128)(2,1)}, u32[]{:S(2)}) copy-start(bf16[192,768]{1,0:T(8,128)(2,1)} %param.13) | copy-start | bytes 884740
  21.7 61.4 %all-to-all-start = ((bf16[64,15,8,128]{3,2,1,0:T(8,128)(2,1)}), bf16[64,15,8,128]{3,2,1,0:T(8,128)(2,1)S(1)}, u32[]{:S(2)}, u32[]{:S(2)}) async-start(bf16[64,15,8,128]{3,2,1,0:T(8,128)(2,1)} %get-tuple-element.28), calls=%async_computation | async-start | bytes 3932160 | tf_op jit(solution)/shard_map/all_to_all | solution.py:309
  36.5 3.5 %copy-start.4 = (bf16[2048,512]{1,0:T(8,128)(2,1)S(1)}, bf16[2048,512]{1,0:T(8,128)(2,1)}, u32[]{:S(2)}) copy-start(bf16[2048,512]{1,0:T(8,128)(2,1)} %constant.20.clone) | copy-start | bytes 6291460
  36.6 8.9 %collective-permute-start.9 = (bf16[192,192]{1,0:T(8,128)(2,1)S(1)}, bf16[192,192]{1,0:T(8,128)(2,1)S(1)}, u32[]{:S(2)}, u32[]{:S(2)}) collective-permute-start(bf16[192,192]{1,0:T(8,128)(2,1)S(1)} %get-tuple-element.41), channel_id=1, source_target_pairs={{0,3},{1,2},{2,1},{3,0},{4,7},{5,6},{6,5},{7,4},{8,11},{9,10},{10,... | collective-permute-start | bytes 221192 | tf_op jit(solution)/shard_map/ppermute | solution.py:276
  37.2 8.3 %collective-permute-start.8 = (bf16[192,192]{1,0:T(8,128)(2,1)S(1)}, bf16[192,192]{1,0:T(8,128)(2,1)S(1)}, u32[]{:S(2)}, u32[]{:S(2)}) collective-permute-start(bf16[192,192]{1,0:T(8,128)(2,1)S(1)} %get-tuple-element.42), channel_id=1, source_target_pairs={{0,1},{1,0},{2,3},{3,2},{4,5},{5,4},{6,7},{7,6},{8,9},{9,8},{10,11... | collective-permute-start | bytes 221192 | tf_op jit(solution)/shard_map/ppermute | solution.py:276
  37.4 10.4 %collective-permute-start.7 = (bf16[192,192]{1,0:T(8,128)(2,1)S(1)}, bf16[192,192]{1,0:T(8,128)(2,1)S(1)}, u32[]{:S(2)}, u32[]{:S(2)}) collective-permute-start(bf16[192,192]{1,0:T(8,128)(2,1)S(1)} %get-tuple-element.43), channel_id=1, source_target_pairs={{0,2},{1,3},{2,0},{3,1},{4,6},{5,7},{6,4},{7,5},{8,10},{9,11},{10,... | collective-permute-start | bytes 221192 | tf_op jit(solution)/shard_map/ppermute | solution.py:276
  40.0 1.5 %copy-start.7 = (f32[192]{0:T(256)S(1)}, f32[192]{0:T(256)}, u32[]{:S(2)}) copy-start(f32[192]{0:T(256)} %param.11) | copy-start | bytes 2308
  88.7 23.2 %all-to-all-start.1 = ((bf16[64,3,8,128]{3,2,1,0:T(8,128)(2,1)}), bf16[64,3,8,128]{3,2,1,0:T(8,128)(2,1)S(1)}, u32[]{:S(2)}, u32[]{:S(2)}) async-start(bf16[64,3,8,128]{3,2,1,0:T(8,128)(2,1)} %convolve.1), calls=%async_computation.1 | async-start | bytes 786432 | tf_op jit(solution)/shard_map/all_to_all | solution.py:322
  111.9 1.1 copy-start.2
  113.4 6.7 %collective-permute-start.10 = (bf16[192,1024]{1,0:T(8,128)(2,1)S(1)}, bf16[192,1024]{1,0:T(8,128)(2,1)S(1)}, u32[]{:S(2)}, u32[]{:S(2)}) collective-permute-start(bf16[192,1024]{1,0:T(8,128)(2,1)S(1)} %gated.1.refs_0_), channel_id=1, source_target_pairs={{0,2},{1,3},{2,0},{3,1},{4,6},{5,7},{6,4},{7,5},{8,10},{9,11},{10,... | collective-permute-start | bytes 1179656 | tf_op jit(solution)/shard_map/ppermute | solution.py:276
  113.5 11.8 %collective-permute-start.11 = (bf16[192,1024]{1,0:T(8,128)(2,1)S(1)}, bf16[192,1024]{1,0:T(8,128)(2,1)S(1)}, u32[]{:S(2)}, u32[]{:S(2)}) collective-permute-start(bf16[192,1024]{1,0:T(8,128)(2,1)S(1)} %gated.1.refs_0_), channel_id=1, source_target_pairs={{0,1},{1,0},{2,3},{3,2},{4,5},{5,4},{6,7},{7,6},{8,9},{9,8},{10,11... | collective-permute-start | bytes 1179656 | tf_op jit(solution)/shard_map/ppermute | solution.py:276
  120.1 6.6 %collective-permute-start.12 = (bf16[192,1024]{1,0:T(8,128)(2,1)S(1)}, bf16[192,1024]{1,0:T(8,128)(2,1)S(1)}, u32[]{:S(2)}, u32[]{:S(2)}) collective-permute-start(bf16[192,1024]{1,0:T(8,128)(2,1)S(1)} %collective-permute-done.10.refs_1_), channel_id=1, source_target_pairs={{0,1},{1,0},{2,3},{3,2},{4,5},{5,4},{6,7},{7,6},{8,9},{9,8},{10,11... | collective-permute-start | bytes 1179656 | tf_op jit(solution)/shard_map/ppermute | solution.py:276

commit v5 on v4

--- a/solution.py
+++ b/solution.py
@@ -11,7 +11,8 @@
 COLS = 256
 FREQS = 512
 LANES = 128
-PROJECT_VMEM = 50000 << 10
+PROJECT_VMEM = 53000 << 10
+GATED_VMEM = 54000 << 10
 CONVOLVE_VMEM = 50000 << 10
 MASKS = (0, 2, 1, 3)
 BF16 = jnp.bfloat16
@@ -67,15 +68,18 @@
 
 
 def project_body(*refs):
-    grp_ref, mains, halos, weight_ref, taps_ref = refs[0], refs[1:5], refs[5:9], refs[9], refs[10]
-    message_ref, kept_ref, token_ref, stream_ref, spread_ref, part_ref, sem = refs[12:]
+    grp_ref, mains, halos, weight_hbm, taps_ref = refs[0], refs[1:5], refs[5:9], refs[9], refs[10]
+    message_ref, kept_hbm, token_ref, stream_ref, spread_ref, part_ref, kept_ref, weight_ref, sem, kept_sem, weight_sem = refs[12:]
     channels, tok = mains[0].shape
     width = tok + LANES
     grp = grp_ref[0]
+    load = pltpu.make_async_copy(weight_hbm, weight_ref, weight_sem)
+    load.start()
     for mask, main, halo in zip(MASKS, mains, halos):
         rows = pl.ds(pl.multiple_of((grp ^ mask) * channels, 64), channels)
         token_ref[rows, :LANES] = halo[...]
         token_ref[rows, LANES:] = main[...]
+    load.wait()
     step = 384
     for col in range(0, width, step):
         stream_ref[:, col:col + step] = jnp.dot(
@@ -110,7 +114,10 @@
         copies.append(pltpu.make_async_copy(
             part_ref.at[dests], message_ref.at[dests, pl.ds(4 * per_dest, per_dest)], sem.at[group]
         ))
-        copies[-1].start()
+        mine = pl.ds(group * each, each)
+        copies.append(pltpu.make_async_copy(kept_ref.at[:, mine], kept_hbm.at[:, mine], kept_sem.at[group]))
+        for copy in copies[-2:]:
+            copy.start()
     for copy in copies:
         copy.wait()
 
@@ -123,8 +130,8 @@
     shards, pieces = packed.shape[:2]
     return pl.pallas_call(
         project_body,
-        in_specs=[pl.BlockSpec(memory_space=pltpu.SMEM)] + [vmem] * 10 + [anywhere],
-        out_specs=[anywhere, vmem],
+        in_specs=[pl.BlockSpec(memory_space=pltpu.SMEM)] + [vmem] * 8 + [anywhere, vmem, anywhere],
+        out_specs=[anywhere] * 2,
         out_shape=[
             jax.ShapeDtypeStruct(packed.shape, BF16),
             jax.ShapeDtypeStruct((2, channels, tok), BF16),
@@ -134,7 +141,11 @@
             pltpu.VMEM((3 * channels, width), F32),
             pltpu.VMEM((channels * 8, LANES), F32),
             pltpu.VMEM((shards, pieces // 5, 8, LANES), BF16),
+            pltpu.VMEM((2, channels, tok), BF16),
+            pltpu.VMEM(weight.shape, BF16),
             pltpu.SemaphoreType.DMA((4,)),
+            pltpu.SemaphoreType.DMA((4,)),
+            pltpu.SemaphoreType.DMA,
         ],
         input_output_aliases={11: 0},
         compiler_params=pltpu.CompilerParams(vmem_limit_bytes=PROJECT_VMEM),
@@ -225,10 +236,13 @@
     )(received, *tables)
 
 
-def gated_body(y_ref, kept_ref, bias_ref, out_ref, spread_ref):
+def gated_body(y_ref, kept_hbm, bias_ref, out_ref, spread_ref, kept_ref, sem):
     channels = out_ref.shape[0]
+    load = pltpu.make_async_copy(kept_hbm, kept_ref, sem)
+    load.start()
     spread_ref[...] = y_ref[...].astype(F32)
     bias = bias_ref[...]
+    load.wait()
     for part in range(8):
         cols = slice(part * LANES, (part + 1) * LANES)
         y = spread_ref[pl.ds(part, channels, stride=8), :]
@@ -240,11 +254,15 @@
     vmem = pl.BlockSpec(memory_space=pltpu.VMEM)
     return pl.pallas_call(
         gated_body,
-        in_specs=[vmem] * 3,
+        in_specs=[vmem, pl.BlockSpec(memory_space=pltpu.HBM), vmem],
         out_specs=vmem,
         out_shape=jax.ShapeDtypeStruct(kept.shape[1:], BF16),
-        scratch_shapes=[pltpu.VMEM(y.shape, F32)],
-        compiler_params=pltpu.CompilerParams(vmem_limit_bytes=8 << 20),
+        scratch_shapes=[
+            pltpu.VMEM(y.shape, F32),
+            pltpu.VMEM(kept.shape, BF16),
+            pltpu.SemaphoreType.DMA,
+        ],
+        compiler_params=pltpu.CompilerParams(vmem_limit_bytes=GATED_VMEM),
         cost_estimate=pl.CostEstimate(flops=4 * y.size, bytes_accessed=8 * y.size, transcendentals=0),
         name="gated",
     )(y, kept, bias)

time: 128 us -> 129 us (level)
  Pallas kernels: 14.7 us -> 16.9 us
  local copies, waits for them, and re-layouts: 3.34 us -> 1.31 us
    unnamed x16 -> x10, local copies, waits for them, and re-layouts: 2.05 us -> 0.03 us
where the time goes in v5:
time: 129 us; the launch traced here: 128 us
  waiting for transfers between devices  62.5 us (48%)
  starting transfers between devices  44.5 us (34%)
  Pallas kernels  16.9 us (13%)
  other arithmetic  2.78 us (2%)
  local copies, waits for them, and re-layouts  1.31 us (1%)
    all_to_all x1, waiting for transfers between devices, shards(): received = lax.all_to_all(message, 'seq', 0, 0, tiled=True)  35.3 us
    ppermute x12, starting transfers between devices, swapped(): return lax.ppermute(block, 'grp', [(i, i ^ mask) for i in range(4)])  17.6 us
    all_to_all x1, starting transfers between devices, shards(): received = lax.all_to_all(message, 'seq', 0, 0, tiled=True)  14.6 us
    all_to_all x1, waiting for transfers between devices, shards(): lax.all_to_all(result, 'seq', 0, 0, tiled=True).reshape(channels * 8, LANES)  14.4 us
    ppermute x12, waiting for transfers between devices, swapped(): return lax.ppermute(block, 'grp', [(i, i ^ mask) for i in range(4)])  12.8 us
    all_to_all x1, starting transfers between devices, shards(): lax.all_to_all(result, 'seq', 0, 0, tiled=True).reshape(channels * 8, LANES)  8.67 us
    pallas_call x1, Pallas kernels, project(): pl.pallas_call(project_body, in_specs=[pl.BlockSpec(memory_space=pltpu.SM...  5.68 us
    pallas_call x1, Pallas kernels, convolve(): pl.pallas_call(convolve_body, in_specs=[vmem, pl.BlockSpec(memory_space=p...  5.63 us
  transfers between devices with their start and end apart: 15, of which 9 were waited for; matrix products, arithmetic and copies ran while one was open for 3% of the time, Pallas kernels for 2%

profile of v5, /device:TPU:1, one launch (start us, length us, event | category | flops | bytes accessed | tf_op | source)
XLA Modules:
  0.0 128.1 jit_solution(171476802942164053)
XLA Ops:
  0.0 2.0 %collective-permute-start = (bf16[192,1024]{1,0:T(8,128)(2,1)}, bf16[192,1024]{1,0:T(8,128)(2,1)S(1)}, u32[]{:S(2)}, u32[]{:S(2)}) collective-permute-start(bf16[192,1024]{1,0:T(8,128)(2,1)} %refs_1_.1), channel_id=1, source_target_pairs={{0,2},{1,3},{2,0},{3,1},{4,6},{5,7},{6,4},{7,5},{8,10},{9,11},{10,... | collective-permute-start | bytes 1179656 | tf_op jit(solution)/shard_map/ppermute | solution.py:294
  2.0 0.8 slice.3
  2.9 3.7 %collective-permute-start.1 = (bf16[192,128]{1,0:T(8,128)(2,1)S(1)}, bf16[192,128]{1,0:T(8,128)(2,1)S(1)}, u32[]{:S(2)}, u32[]{:S(2)}) collective-permute-start(bf16[192,128]{1,0:T(8,128)(2,1)S(1)} %slice.3), channel_id=1, source_target_pairs={{0,4},{4,8},{8,12},{12,16},{16,20},{20,24},{24,28},{28,32},{32,36}... | collective-permute-start | bytes 147464 | tf_op jit(solution)/shard_map/ppermute | solution.py:312
  6.6 2.9 %pack_spectra.1.refs_11_ = bf16[64,15,8,128]{3,2,1,0:T(8,128)(2,1)} custom-call(f32[2,192,8,256]{3,2,1,0:T(8,128)} %spec_ref.1), custom_call_target="tpu_custom_call" | custom-call | bytes 4718592 | tf_op jit(solution)/shard_map/pack_spectra/pallas_call | solution.py:59
  9.5 0.3 collective-permute-start.2
  9.7 1.5 %collective-permute-start.3 = (bf16[192,1024]{1,0:T(8,128)(2,1)S(1)}, bf16[192,1024]{1,0:T(8,128)(2,1)S(1)}, u32[]{:S(2)}, u32[]{:S(2)}) collective-permute-start(bf16[192,1024]{1,0:T(8,128)(2,1)S(1)} %copy-done), channel_id=1, source_target_pairs={{0,1},{1,0},{2,3},{3,2},{4,5},{5,4},{6,7},{7,6},{8,9},{9,8},{10,11... | collective-permute-start | bytes 1179656 | tf_op jit(solution)/shard_map/ppermute | solution.py:294
  11.2 2.0 %collective-permute-done.2.refs_6_ = bf16[192,128]{1,0:T(8,128)(2,1)S(1)} collective-permute-done((bf16[192,128]{1,0:T(8,128)(2,1)S(1)}, bf16[192,128]{1,0:T(8,128)(2,1)S(1)}, u32[]{:S(2)}, u32[]{:S(2)}) %collective-permute-start.2) | collective-permute-done | bytes 49184 | tf_op jit(solution)/shard_map/ppermute | solution.py:294
  13.2 1.6 %collective-permute-start.4 = (bf16[192,1024]{1,0:T(8,128)(2,1)S(1)}, bf16[192,1024]{1,0:T(8,128)(2,1)S(1)}, u32[]{:S(2)}, u32[]{:S(2)}) collective-permute-start(bf16[192,1024]{1,0:T(8,128)(2,1)S(1)} %collective-permute-done.refs_2_), channel_id=1, source_target_pairs={{0,1},{1,0},{2,3},{3,2},{4,5},{5,4},{6,7},{7,6},{8,9},{9,8},{10,11... | collective-permute-start | bytes 1179656 | tf_op jit(solution)/shard_map/ppermute | solution.py:294
  14.8 0.5 collective-permute-start.6
  15.3 0.1 copy.15.refs_10_
  15.4 0.8 collective-permute-done.5.refs_7_
  16.3 5.7 %project.1 = (bf16[64,15,8,128]{3,2,1,0:T(8,128)(2,1)}, bf16[2,192,1024]{2,1,0:T(8,128)(2,1)}) custom-call(s32[1]{0:T(128)} %bitcast.refs_0_, bf16[192,1024]{1,0:T(8,128)(2,1)S(1)} %copy-done, bf16[192,1024]{1,0:T(8,128)(2,1)S(1)} %collective-permute-done.refs_2_, ...), custom_call_target="tpu_custom_call", output_to_operand_aliasing={{0}: (11, {})} | custom-call | flops 1019215872 | bytes 6291456 | tf_op jit(solution)/shard_map/project/pallas_call | solution.py:131
  22.0 14.6 %all-to-all-start = ((bf16[64,15,8,128]{3,2,1,0:T(8,128)(2,1)}), bf16[64,15,8,128]{3,2,1,0:T(8,128)(2,1)S(1)}, u32[]{:S(2)}, u32[]{:S(2)}) async-start(bf16[64,15,8,128]{3,2,1,0:T(8,128)(2,1)} %get-tuple-element.28), calls=%async_computation | async-start | bytes 3932160 | tf_op jit(solution)/shard_map/all_to_all | solution.py:327
  36.6 0.2 copy.16
  36.9 0.6 collective-permute-start.9
  37.4 0.3 collective-permute-start.8
  37.7 1.3 collective-permute-start.7
  39.0 1.3 %broadcast_add_fusion.1.twist_ref = f32[512,512]{1,0:T(8,128)S(1)} fusion(f32[512,512]{1,0:T(8,128)} %constant.21.clone, f32[]{:T(128)S(6)} %convert_element_type.8), kind=kLoop, calls=%fused_computation.1 | loop fusion | flops 262144 | bytes 2097156 | tf_op jit(solution)/shard_map/add | solution.py:335
  40.3 1.5 %broadcast_add_fusion.wave_hbm = bf16[2048,512]{1,0:T(8,128)(2,1)} fusion(bf16[2048,512]{1,0:T(8,128)(2,1)S(1)} %copy-done.1, bf16[]{:T(256)S(6)} %convert_element_type.7), kind=kLoop, calls=%fused_computation | loop fusion | flops 1048576 | bytes 4194306 | tf_op jit(solution)/shard_map/add | solution.py:335
  41.8 4.0 %collective-permute-done.9.refs_7_ = bf16[192,192]{1,0:T(8,128)(2,1)S(1)} collective-permute-done((bf16[192,192]{1,0:T(8,128)(2,1)S(1)}, bf16[192,192]{1,0:T(8,128)(2,1)S(1)}, u32[]{:S(2)}, u32[]{:S(2)}) %collective-permute-start.9) | collective-permute-done | bytes 73760 | tf_op jit(solution)/shard_map/ppermute | solution.py:294
  45.8 2.3 %collective-permute-done.7.refs_5_ = bf16[192,192]{1,0:T(8,128)(2,1)S(1)} collective-permute-done((bf16[192,192]{1,0:T(8,128)(2,1)S(1)}, bf16[192,192]{1,0:T(8,128)(2,1)S(1)}, u32[]{:S(2)}, u32[]{:S(2)}) %collective-permute-start.7) | collective-permute-done | bytes 73760 | tf_op jit(solution)/shard_map/ppermute | solution.py:294
  48.1 35.3 %all-to-all-done.m_ref = bf16[64,15,8,128]{3,2,1,0:T(8,128)(2,1)S(1)} async-done(((bf16[64,15,8,128]{3,2,1,0:T(8,128)(2,1)}), bf16[64,15,8,128]{3,2,1,0:T(8,128)(2,1)S(1)}, u32[]{:S(2)}, u32[]{:S(2)}) %all-to-all-start) | async-done | bytes 1966112 | tf_op jit(solution)/shard_map/all_to_all | solution.py:327
  83.3 5.6 %convolve.1 = bf16[64,3,8,128]{3,2,1,0:T(8,128)(2,1)} custom-call(bf16[64,15,8,128]{3,2,1,0:T(8,128)(2,1)S(1)} %all-to-all-done.m_ref, bf16[2048,512]{1,0:T(8,128)(2,1)} %broadcast_add_fusion.wave_hbm, f32[512,512]{1,0:T(8,128)S(1)} %broadcast_add_fusion.1.twist_ref), custom_call_target="tpu_custom_call" | custom-call | flops 3221225472 | bytes 6291456 | tf_op jit(solution)/shard_map/convolve/pallas_call | solution.py:218
  89.0 8.7 %all-to-all-start.1 = ((bf16[64,3,8,128]{3,2,1,0:T(8,128)(2,1)}), bf16[64,3,8,128]{3,2,1,0:T(8,128)(2,1)S(1)}, u32[]{:S(2)}, u32[]{:S(2)}) async-start(bf16[64,3,8,128]{3,2,1,0:T(8,128)(2,1)} %convolve.1), calls=%async_computation.1 | async-start | bytes 786432 | tf_op jit(solution)/shard_map/all_to_all | solution.py:340
  97.6 0.1 copy.20.bias_ref
  97.8 14.4 %all-to-all-done.1 = bf16[64,3,8,128]{3,2,1,0:T(8,128)(2,1)S(1)} async-done(((bf16[64,3,8,128]{3,2,1,0:T(8,128)(2,1)}), bf16[64,3,8,128]{3,2,1,0:T(8,128)(2,1)S(1)}, u32[]{:S(2)}, u32[]{:S(2)}) %all-to-all-start.1) | async-done | bytes 393248 | tf_op jit(solution)/shard_map/all_to_all | solution.py:340
  112.2 1.4 %gated.1.refs_0_ = bf16[192,1024]{1,0:T(8,128)(2,1)S(1)} custom-call(bf16[1536,128]{1,0:T(8,128)(2,1)S(1)} %bitcast.15, bf16[2,192,1024]{2,1,0:T(8,128)(2,1)} %get-tuple-element.35.kept_hbm, f32[192,1]{1,0:T(8,128)S(1)} %copy.20.bias_ref), custom_call_target="tpu_custom_call" | custom-call | flops 786432 | bytes 1572864 | tf_op jit(solution)/shard_map/gated/pallas_call | solution.py:255
  113.7 4.3 %collective-permute-start.11 = (bf16[192,1024]{1,0:T(8,128)(2,1)S(1)}, bf16[192,1024]{1,0:T(8,128)(2,1)S(1)}, u32[]{:S(2)}, u32[]{:S(2)}) collective-permute-start(bf16[192,1024]{1,0:T(8,128)(2,1)S(1)} %gated.1.refs_0_), channel_id=1, source_target_pairs={{0,1},{1,0},{2,3},{3,2},{4,5},{5,4},{6,7},{7,6},{8,9},{9,8},{10,11... | collective-permute-start | bytes 1179656 | tf_op jit(solution)/shard_map/ppermute | solution.py:294
  117.9 2.3 %collective-permute-done.10.refs_1_ = bf16[192,1024]{1,0:T(8,128)(2,1)S(1)} collective-permute-done((bf16[192,1024]{1,0:T(8,128)(2,1)S(1)}, bf16[192,1024]{1,0:T(8,128)(2,1)S(1)}, u32[]{:S(2)}, u32[]{:S(2)}) %collective-permute-start.10) | collective-permute-done | bytes 393248 | tf_op jit(solution)/shard_map/ppermute | solution.py:294
  120.3 5.2 %collective-permute-start.12 = (bf16[192,1024]{1,0:T(8,128)(2,1)S(1)}, bf16[192,1024]{1,0:T(8,128)(2,1)S(1)}, u32[]{:S(2)}, u32[]{:S(2)}) collective-permute-start(bf16[192,1024]{1,0:T(8,128)(2,1)S(1)} %collective-permute-done.10.refs_1_), channel_id=1, source_target_pairs={{0,1},{1,0},{2,3},{3,2},{4,5},{5,4},{6,7},{7,6},{8,9},{9,8},{10,11... | collective-permute-start | bytes 1179656 | tf_op jit(solution)/shard_map/ppermute | solution.py:294
  125.5 1.3 %collective-permute-done.12.refs_3_ = bf16[192,1024]{1,0:T(8,128)(2,1)S(1)} collective-permute-done((bf16[192,1024]{1,0:T(8,128)(2,1)S(1)}, bf16[192,1024]{1,0:T(8,128)(2,1)S(1)}, u32[]{:S(2)}, u32[]{:S(2)}) %collective-permute-start.12) | collective-permute-done | bytes 393248 | tf_op jit(solution)/shard_map/ppermute | solution.py:294
  126.8 1.3 %mixed.1 = bf16[192,1024]{1,0:T(8,128)(2,1)} custom-call(bf16[192,1024]{1,0:T(8,128)(2,1)S(1)} %gated.1.refs_0_, bf16[192,1024]{1,0:T(8,128)(2,1)S(1)} %collective-permute-done.10.refs_1_, bf16[192,1024]{1,0:T(8,128)(2,1)S(1)} %collective-permute-done.11.refs_2_, bf16[192,1024]{1,0:T(8,128)(2,1)S(1)} %collective-permute-done.12.refs_3_, ...), custom_call_target="tpu_custom_call" | custom-call | flops 301989888 | bytes 3145728 | tf_op jit(solution)/shard_map/mixed/pallas_call | solution.py:282
  (22 shorter events, 0.3 us)
Async XLA Ops:
  0.0 13.2 %collective-permute-start = (bf16[192,1024]{1,0:T(8,128)(2,1)}, bf16[192,1024]{1,0:T(8,128)(2,1)S(1)}, u32[]{:S(2)}, u32[]{:S(2)}) collective-permute-start(bf16[192,1024]{1,0:T(8,128)(2,1)} %refs_1_.1), channel_id=1, source_target_pairs={{0,2},{1,3},{2,0},{3,1},{4,6},{5,7},{6,4},{7,5},{8,10},{9,11},{10,... | collective-permute-start | bytes 1179656 | tf_op jit(solution)/shard_map/ppermute | solution.py:294
  2.9 6.8 %copy-start = (bf16[192,1024]{1,0:T(8,128)(2,1)S(1)}, bf16[192,1024]{1,0:T(8,128)(2,1)}, u32[]{:S(2)}) copy-start(bf16[192,1024]{1,0:T(8,128)(2,1)} %refs_1_.1) | copy-start | bytes 1179652
  2.9 12.4 %copy-start.3 = (f32[3,3,192]{2,1,0:T(4,128)S(1)}, f32[3,3,192]{2,1,0:T(4,128)}, u32[]{:S(2)}) copy-start(f32[3,3,192]{2,1,0:T(4,128)} %param.10) | copy-start | bytes 20740
  2.9 6.6 %collective-permute-start.1 = (bf16[192,128]{1,0:T(8,128)(2,1)S(1)}, bf16[192,128]{1,0:T(8,128)(2,1)S(1)}, u32[]{:S(2)}, u32[]{:S(2)}) collective-permute-start(bf16[192,128]{1,0:T(8,128)(2,1)S(1)} %slice.3), channel_id=1, source_target_pairs={{0,4},{4,8},{8,12},{12,16},{16,20},{20,24},{24,28},{28,32},{32,36}... | collective-permute-start | bytes 147464 | tf_op jit(solution)/shard_map/ppermute | solution.py:312
  9.5 3.8 %collective-permute-start.2 = (bf16[192,128]{1,0:T(8,128)(2,1)S(1)}, bf16[192,128]{1,0:T(8,128)(2,1)S(1)}, u32[]{:S(2)}, u32[]{:S(2)}) collective-permute-start(bf16[192,128]{1,0:T(8,128)(2,1)S(1)} %collective-permute-done.1.refs_5_), channel_id=1, source_target_pairs={{0,2},{1,3},{2,0},{3,1},{4,6},{5,7},{6,4},{7,5},{8,10},{9,11},{10,... | collective-permute-start | bytes 147464 | tf_op jit(solution)/shard_map/ppermute | solution.py:294
  9.7 6.5 %collective-permute-start.3 = (bf16[192,1024]{1,0:T(8,128)(2,1)S(1)}, bf16[192,1024]{1,0:T(8,128)(2,1)S(1)}, u32[]{:S(2)}, u32[]{:S(2)}) collective-permute-start(bf16[192,1024]{1,0:T(8,128)(2,1)S(1)} %copy-done), channel_id=1, source_target_pairs={{0,1},{1,0},{2,3},{3,2},{4,5},{5,4},{6,7},{7,6},{8,9},{9,8},{10,11... | collective-permute-start | bytes 1179656 | tf_op jit(solution)/shard_map/ppermute | solution.py:294
  13.2 3.1 %collective-permute-start.4 = (bf16[192,1024]{1,0:T(8,128)(2,1)S(1)}, bf16[192,1024]{1,0:T(8,128)(2,1)S(1)}, u32[]{:S(2)}, u32[]{:S(2)}) collective-permute-start(bf16[192,1024]{1,0:T(8,128)(2,1)S(1)} %collective-permute-done.refs_2_), channel_id=1, source_target_pairs={{0,1},{1,0},{2,3},{3,2},{4,5},{5,4},{6,7},{7,6},{8,9},{9,8},{10,11... | collective-permute-start | bytes 1179656 | tf_op jit(solution)/shard_map/ppermute | solution.py:294
  14.8 1.4 %collective-permute-start.5 = (bf16[192,128]{1,0:T(8,128)(2,1)S(1)}, bf16[192,128]{1,0:T(8,128)(2,1)S(1)}, u32[]{:S(2)}, u32[]{:S(2)}) collective-permute-start(bf16[192,128]{1,0:T(8,128)(2,1)S(1)} %collective-permute-done.1.refs_5_), channel_id=1, source_target_pairs={{0,1},{1,0},{2,3},{3,2},{4,5},{5,4},{6,7},{7,6},{8,9},{9,8},{10,11... | collective-permute-start | bytes 147464 | tf_op jit(solution)/shard_map/ppermute | solution.py:294
  14.8 1.5 %collective-permute-start.6 = (bf16[192,128]{1,0:T(8,128)(2,1)S(1)}, bf16[192,128]{1,0:T(8,128)(2,1)S(1)}, u32[]{:S(2)}, u32[]{:S(2)}) collective-permute-start(bf16[192,128]{1,0:T(8,128)(2,1)S(1)} %collective-permute-done.2.refs_6_), channel_id=1, source_target_pairs={{0,1},{1,0},{2,3},{3,2},{4,5},{5,4},{6,7},{7,6},{8,9},{9,8},{10,11... | collective-permute-start | bytes 147464 | tf_op jit(solution)/shard_map/ppermute | solution.py:294
  22.0 14.6 %copy-start.2 = (bf16[192,768]{1,0:T(8,128)(2,1)S(1)}, bf16[192,768]{1,0:T(8,128)(2,1)}, u32[]{:S(2)}) copy-start(bf16[192,768]{1,0:T(8,128)(2,1)} %param.13) | copy-start | bytes 884740
  22.0 61.4 %all-to-all-start = ((bf16[64,15,8,128]{3,2,1,0:T(8,128)(2,1)}), bf16[64,15,8,128]{3,2,1,0:T(8,128)(2,1)S(1)}, u32[]{:S(2)}, u32[]{:S(2)}) async-start(bf16[64,15,8,128]{3,2,1,0:T(8,128)(2,1)} %get-tuple-element.28), calls=%async_computation | async-start | bytes 3932160 | tf_op jit(solution)/shard_map/all_to_all | solution.py:327
  36.8 3.5 %copy-start.1 = (bf16[2048,512]{1,0:T(8,128)(2,1)S(1)}, bf16[2048,512]{1,0:T(8,128)(2,1)}, u32[]{:S(2)}) copy-start(bf16[2048,512]{1,0:T(8,128)(2,1)} %constant.20.clone) | copy-start | bytes 6291460
  36.9 8.9 %collective-permute-start.9 = (bf16[192,192]{1,0:T(8,128)(2,1)S(1)}, bf16[192,192]{1,0:T(8,128)(2,1)S(1)}, u32[]{:S(2)}, u32[]{:S(2)}) collective-permute-start(bf16[192,192]{1,0:T(8,128)(2,1)S(1)} %get-tuple-element.41), channel_id=1, source_target_pairs={{0,3},{1,2},{2,1},{3,0},{4,7},{5,6},{6,5},{7,4},{8,11},{9,10},{10,... | collective-permute-start | bytes 221192 | tf_op jit(solution)/shard_map/ppermute | solution.py:294
  37.4 8.3 %collective-permute-start.8 = (bf16[192,192]{1,0:T(8,128)(2,1)S(1)}, bf16[192,192]{1,0:T(8,128)(2,1)S(1)}, u32[]{:S(2)}, u32[]{:S(2)}) collective-permute-start(bf16[192,192]{1,0:T(8,128)(2,1)S(1)} %get-tuple-element.42), channel_id=1, source_target_pairs={{0,1},{1,0},{2,3},{3,2},{4,5},{5,4},{6,7},{7,6},{8,9},{9,8},{10,11... | collective-permute-start | bytes 221192 | tf_op jit(solution)/shard_map/ppermute | solution.py:294
  37.7 10.4 %collective-permute-start.7 = (bf16[192,192]{1,0:T(8,128)(2,1)S(1)}, bf16[192,192]{1,0:T(8,128)(2,1)S(1)}, u32[]{:S(2)}, u32[]{:S(2)}) collective-permute-start(bf16[192,192]{1,0:T(8,128)(2,1)S(1)} %get-tuple-element.43), channel_id=1, source_target_pairs={{0,2},{1,3},{2,0},{3,1},{4,6},{5,7},{6,4},{7,5},{8,10},{9,11},{10,... | collective-permute-start | bytes 221192 | tf_op jit(solution)/shard_map/ppermute | solution.py:294
  40.3 1.5 %copy-start.4 = (f32[192]{0:T(256)S(1)}, f32[192]{0:T(256)}, u32[]{:S(2)}) copy-start(f32[192]{0:T(256)} %param.11) | copy-start | bytes 2308
  89.0 23.2 %all-to-all-start.1 = ((bf16[64,3,8,128]{3,2,1,0:T(8,128)(2,1)}), bf16[64,3,8,128]{3,2,1,0:T(8,128)(2,1)S(1)}, u32[]{:S(2)}, u32[]{:S(2)}) async-start(bf16[64,3,8,128]{3,2,1,0:T(8,128)(2,1)} %convolve.1), calls=%async_computation.1 | async-start | bytes 786432 | tf_op jit(solution)/shard_map/all_to_all | solution.py:340
  113.6 6.7 %collective-permute-start.10 = (bf16[192,1024]{1,0:T(8,128)(2,1)S(1)}, bf16[192,1024]{1,0:T(8,128)(2,1)S(1)}, u32[]{:S(2)}, u32[]{:S(2)}) collective-permute-start(bf16[192,1024]{1,0:T(8,128)(2,1)S(1)} %gated.1.refs_0_), channel_id=1, source_target_pairs={{0,2},{1,3},{2,0},{3,1},{4,6},{5,7},{6,4},{7,5},{8,10},{9,11},{10,... | collective-permute-start | bytes 1179656 | tf_op jit(solution)/shard_map/ppermute | solution.py:294
  113.7 11.8 %collective-permute-start.11 = (bf16[192,1024]{1,0:T(8,128)(2,1)S(1)}, bf16[192,1024]{1,0:T(8,128)(2,1)S(1)}, u32[]{:S(2)}, u32[]{:S(2)}) collective-permute-start(bf16[192,1024]{1,0:T(8,128)(2,1)S(1)} %gated.1.refs_0_), channel_id=1, source_target_pairs={{0,1},{1,0},{2,3},{3,2},{4,5},{5,4},{6,7},{7,6},{8,9},{9,8},{10,11... | collective-permute-start | bytes 1179656 | tf_op jit(solution)/shard_map/ppermute | solution.py:294
  120.3 6.6 %collective-permute-start.12 = (bf16[192,1024]{1,0:T(8,128)(2,1)S(1)}, bf16[192,1024]{1,0:T(8,128)(2,1)S(1)}, u32[]{:S(2)}, u32[]{:S(2)}) collective-permute-start(bf16[192,1024]{1,0:T(8,128)(2,1)S(1)} %collective-permute-done.10.refs_1_), channel_id=1, source_target_pairs={{0,1},{1,0},{2,3},{3,2},{4,5},{5,4},{6,7},{7,6},{8,9},{9,8},{10,11... | collective-permute-start | bytes 1179656 | tf_op jit(solution)/shard_map/ppermute | solution.py:294

commit v6 on v5

--- a/solution.py
+++ b/solution.py
@@ -11,7 +11,7 @@
 COLS = 256
 FREQS = 512
 LANES = 128
-PROJECT_VMEM = 53000 << 10
+PROJECT_VMEM = 44000 << 10
 GATED_VMEM = 54000 << 10
 CONVOLVE_VMEM = 50000 << 10
 MASKS = (0, 2, 1, 3)
@@ -67,23 +67,63 @@
     )(spectra)
 
 
+def near_half_body(grp_ref, own_ref, near_ref, weight_hbm, out_ref, token_ref, weight_ref, sem):
+    channels = own_ref.shape[0]
+    grp = grp_ref[0]
+    first = pl.multiple_of((grp // 2) * 2 * channels, LANES)
+    load = pltpu.make_async_copy(weight_hbm.at[:, pl.ds(first, 2 * channels)], weight_ref, sem)
+    load.start()
+    side = grp % 2
+    token_ref[pl.ds(pl.multiple_of(side * channels, 64), channels), :] = own_ref[...]
+    token_ref[pl.ds(pl.multiple_of((1 - side) * channels, 64), channels), :] = near_ref[...]
+    load.wait()
+    step = 256
+    for col in range(0, out_ref.shape[1], step):
+        out_ref[:, col:col + step] = jnp.dot(
+            weight_ref[...], token_ref[:, col:col + step], preferred_element_type=F32
+        )
+
+
+def near_half(grp, own, near, weight):
+    channels, tok = own.shape
+    vmem = pl.BlockSpec(memory_space=pltpu.VMEM)
+    return pl.pallas_call(
+        near_half_body,
+        in_specs=[pl.BlockSpec(memory_space=pltpu.SMEM), vmem, vmem, pl.BlockSpec(memory_space=pltpu.HBM)],
+        out_specs=vmem,
+        out_shape=jax.ShapeDtypeStruct((weight.shape[0], tok), F32),
+        scratch_shapes=[
+            pltpu.VMEM((2 * channels, tok), BF16),
+            pltpu.VMEM((weight.shape[0], 2 * channels), BF16),
+            pltpu.SemaphoreType.DMA,
+        ],
+        compiler_params=pltpu.CompilerParams(vmem_limit_bytes=16 << 20),
+        cost_estimate=pl.CostEstimate(flops=4 * weight.shape[0] * channels * tok,
+                                      bytes_accessed=4 << 20, transcendentals=0),
+        name="near_half",
+    )(grp, own, near, weight)
+
+
 def project_body(*refs):
-    grp_ref, mains, halos, weight_hbm, taps_ref = refs[0], refs[1:5], refs[5:9], refs[9], refs[10]
-    message_ref, kept_hbm, token_ref, stream_ref, spread_ref, part_ref, kept_ref, weight_ref, sem, kept_sem, weight_sem = refs[12:]
-    channels, tok = mains[0].shape
-    width = tok + LANES
+    grp_ref, far_ref, diag_ref, halos, half_ref, weight_hbm, taps_ref = refs[0], refs[1], refs[2], refs[3:7], *refs[7:10]
+    message_ref, kept_ref, token_ref, halo_ref, stream_ref, spread_ref, part_ref, weight_ref = refs[11:19]
+    sem, weight_sem = refs[19:]
+    channels, tok = far_ref.shape
     grp = grp_ref[0]
     load = pltpu.make_async_copy(weight_hbm, weight_ref, weight_sem)
     load.start()
-    for mask, main, halo in zip(MASKS, mains, halos):
-        rows = pl.ds(pl.multiple_of((grp ^ mask) * channels, 64), channels)
-        token_ref[rows, :LANES] = halo[...]
-        token_ref[rows, LANES:] = main[...]
+    side = grp % 2
+    token_ref[pl.ds(pl.multiple_of(side * channels, 64), channels), :] = far_ref[...]
+    token_ref[pl.ds(pl.multiple_of((1 - side) * channels, 64), channels), :] = diag_ref[...]
+    for mask, halo in zip(MASKS, halos):
+        halo_ref[pl.ds(pl.multiple_of((grp ^ mask) * channels, 64), channels), :] = halo[...]
     load.wait()
-    step = 384
-    for col in range(0, width, step):
-        stream_ref[:, col:col + step] = jnp.dot(
-            weight_ref[...], token_ref[:, col:col + step], preferred_element_type=F32
+    stream_ref[:, :LANES] = jnp.dot(weight_ref[...], halo_ref[...], preferred_element_type=F32)
+    first = pl.multiple_of((1 - grp // 2) * 2 * channels, LANES)
+    step = 256
+    for col in range(0, tok, step):
+        stream_ref[:, LANES + col:LANES + col + step] = half_ref[:, col:col + step] + jnp.dot(
+            weight_ref[:, pl.ds(first, 2 * channels)], token_ref[:, col:col + step], preferred_element_type=F32
         )
     rows = 16
 
@@ -114,45 +154,41 @@
         copies.append(pltpu.make_async_copy(
             part_ref.at[dests], message_ref.at[dests, pl.ds(4 * per_dest, per_dest)], sem.at[group]
         ))
-        mine = pl.ds(group * each, each)
-        copies.append(pltpu.make_async_copy(kept_ref.at[:, mine], kept_hbm.at[:, mine], kept_sem.at[group]))
-        for copy in copies[-2:]:
-            copy.start()
+        copies[-1].start()
     for copy in copies:
         copy.wait()
 
 
-def project(grp, mains, halos, weight, taps, packed):
-    channels, tok = mains[0].shape
+def project(grp, far, diag, halos, half, weight, taps, packed):
+    channels, tok = far.shape
     width = tok + LANES
     vmem = pl.BlockSpec(memory_space=pltpu.VMEM)
     anywhere = pl.BlockSpec(memory_space=pltpu.HBM)
     shards, pieces = packed.shape[:2]
     return pl.pallas_call(
         project_body,
-        in_specs=[pl.BlockSpec(memory_space=pltpu.SMEM)] + [vmem] * 8 + [anywhere, vmem, anywhere],
-        out_specs=[anywhere] * 2,
+        in_specs=[pl.BlockSpec(memory_space=pltpu.SMEM)] + [vmem] * 7 + [anywhere, vmem, anywhere],
+        out_specs=[anywhere, vmem],
         out_shape=[
             jax.ShapeDtypeStruct(packed.shape, BF16),
             jax.ShapeDtypeStruct((2, channels, tok), BF16),
         ],
         scratch_shapes=[
-            pltpu.VMEM((4 * channels, width), BF16),
+            pltpu.VMEM((2 * channels, tok), BF16),
+            pltpu.VMEM((4 * channels, LANES), BF16),
             pltpu.VMEM((3 * channels, width), F32),
             pltpu.VMEM((channels * 8, LANES), F32),
             pltpu.VMEM((shards, pieces // 5, 8, LANES), BF16),
-            pltpu.VMEM((2, channels, tok), BF16),
             pltpu.VMEM(weight.shape, BF16),
-            pltpu.SemaphoreType.DMA((4,)),
             pltpu.SemaphoreType.DMA((4,)),
             pltpu.SemaphoreType.DMA,
         ],
-        input_output_aliases={11: 0},
+        input_output_aliases={10: 0},
         compiler_params=pltpu.CompilerParams(vmem_limit_bytes=PROJECT_VMEM),
-        cost_estimate=pl.CostEstimate(flops=2 * 3 * channels * 4 * channels * width,
+        cost_estimate=pl.CostEstimate(flops=3 * channels * 4 * channels * width,
                                       bytes_accessed=6 << 20, transcendentals=0),
         name="project",
-    )(grp, *mains, *halos, weight, taps, packed)
+    )(grp, far, diag, *halos, half, weight, taps, packed)
 
 
 def convolve_body(m_ref, wave_hbm, twist_ref, out_ref,
@@ -166,22 +202,28 @@
     ]
     for load in loads:
         load.start()
-    for c in range(channels):
+    cosine, sine = twist_ref[:, :COLS], twist_ref[:, COLS:]
+
+    def arrange(c):
         spread_ref[c] = m_ref[:, 4 * channels + c].astype(F32).reshape(shards * pieces, lanes)
         for a in range(rows_dev):
             for h in range(2):
                 grid_ref[c, a * shards:(a + 1) * shards, h * lanes:(h + 1) * lanes] = spread_ref[
                     c, pl.ds(2 * a + h, shards, stride=pieces), :].astype(BF16)
-        if c == 0:
-            loads[0].wait()
+
+    def rows_forward(c):
         real = jnp.dot(first_ref[:, :COLS], grid_ref[c], preferred_element_type=F32)
-        imag = jnp.dot(first_ref[:, COLS:], grid_ref[c], preferred_element_type=F32)
-        cosine, sine = twist_ref[:, :COLS], twist_ref[:, COLS:]
+        return real, jnp.dot(first_ref[:, COLS:], grid_ref[c], preferred_element_type=F32)
+
+    def twist_forward(c, wave):
+        real, imag = wave
         mid_ref[c, :, :COLS] = (real * cosine + imag * sine).astype(BF16)
         mid_ref[c, :, COLS:] = (imag * cosine - real * sine).astype(BF16)
-        if c == 0:
-            loads[1].wait()
-        freq = jnp.dot(mid_ref[c], forward_ref[...], preferred_element_type=F32)
+
+    def cols_forward(c):
+        return jnp.dot(mid_ref[c], forward_ref[...], preferred_element_type=F32)
+
+    def respond(c, freq):
         for h in range(2):
             low, high = h * lanes, COLS + h * lanes
             real, imag = freq[:, low:low + lanes], freq[:, high:high + lanes]
@@ -190,22 +232,41 @@
             )
             mid_ref[c, :, low:low + lanes] = (real * h_real - imag * h_imag).astype(BF16)
             mid_ref[c, :, high:high + lanes] = (real * h_imag + imag * h_real).astype(BF16)
-        if c == 0:
-            loads[2].wait()
-        back = jnp.dot(mid_ref[c], backward_ref[...], preferred_element_type=F32)
+
+    def cols_backward(c):
+        return jnp.dot(mid_ref[c], backward_ref[...], preferred_element_type=F32)
+
+    def twist_backward(c, back):
         real, imag = back[:, :COLS], back[:, COLS:]
         tall_ref[c, :freqs, :] = (real * cosine - imag * sine).astype(BF16)
         tall_ref[c, freqs:, :] = (imag * cosine + real * sine).astype(BF16)
-        if c == 0:
-            loads[3].wait()
+
+    def rows_backward(c):
         out = jnp.dot(last_ref[:COLS, :], tall_ref[c, :freqs], preferred_element_type=F32)
-        out += jnp.dot(last_ref[COLS:, :], tall_ref[c, freqs:], preferred_element_type=F32)
+        return out + jnp.dot(last_ref[COLS:, :], tall_ref[c, freqs:], preferred_element_type=F32)
+
+    def send(c, out):
         for a in range(rows_dev):
             for h in range(2):
                 spread_ref[c, pl.ds(2 * a + h, shards, stride=pieces), :] = out[
                     a * shards:(a + 1) * shards, h * lanes:(h + 1) * lanes]
         done_ref[c] = spread_ref[c].reshape(shards, pieces, lanes).astype(BF16)
         pltpu.make_async_copy(done_ref.at[c], out_ref.at[:, c], sems.at[c]).start()
+
+    for c in range(channels):
+        arrange(c)
+    stages = (
+        (rows_forward, twist_forward), (cols_forward, respond), (cols_backward, twist_backward), (rows_backward, send)
+    )
+    waiting = None
+    for stage, (multiply, finish) in enumerate(stages):
+        loads[stage].wait()
+        for c in range(channels):
+            product = multiply(c)
+            if waiting is not None:
+                waiting[0](*waiting[1:])
+            waiting = (finish, c, product)
+    waiting[0](*waiting[1:])
     for c in range(channels):
         pltpu.make_async_copy(done_ref.at[c], out_ref.at[:, c], sems.at[c]).wait()
 
@@ -269,35 +330,29 @@
 
 
 def mixed_body(*refs):
-    values, weights, out_ref = refs[:4], refs[4:8], refs[8]
-    total = jnp.dot(weights[0][...], values[0][...], preferred_element_type=F32)
-    for w, v in zip(weights[1:], values[1:]):
+    values, weights, out_ref = refs[:2], refs[2:4], refs[-1]
+    total = refs[4][...] if len(refs) == 6 else 0.0
+    for w, v in zip(weights, values):
         total = total + jnp.dot(w[...], v[...], preferred_element_type=F32)
-    out_ref[...] = total.astype(BF16)
-
-
-def mixed(values, weights):
+    out_ref[...] = total.astype(out_ref.dtype)
+
+
+def mixed(values, weights, dtype, *earlier):
     vmem = pl.BlockSpec(memory_space=pltpu.VMEM)
     channels, tok = values[0].shape
     return pl.pallas_call(
         mixed_body,
-        in_specs=[vmem] * 8,
+        in_specs=[vmem] * (4 + len(earlier)),
         out_specs=vmem,
-        out_shape=jax.ShapeDtypeStruct((weights[0].shape[0], tok), BF16),
+        out_shape=jax.ShapeDtypeStruct((weights[0].shape[0], tok), dtype),
         compiler_params=pltpu.CompilerParams(vmem_limit_bytes=12 << 20),
-        cost_estimate=pl.CostEstimate(flops=8 * channels * channels * tok, bytes_accessed=3 << 20, transcendentals=0),
+        cost_estimate=pl.CostEstimate(flops=4 * channels * channels * tok, bytes_accessed=2 << 20, transcendentals=0),
         name="mixed",
-    )(*values, *weights)
+    )(*values, *weights, *earlier)
 
 
 def swapped(block, mask):
     return lax.ppermute(block, "grp", [(i, i ^ mask) for i in range(4)])
-
-
-def gathered(block):
-    far = swapped(block, 2)
-    near = swapped(block, 1)
-    return block, far, near, swapped(far, 1)
 
 
 def shards(tokens, in_weight, short_weight, filter_bias, spectra, out_weight):
@@ -307,20 +362,22 @@
     per_dest = channels // shard_count
 
     far = swapped(tokens, 2)
-    near = swapped(tokens, 1)
+    tail, own = lax.optimization_barrier((tokens[:, -LANES:], tokens))
+    near = swapped(own, 1)
     route = [(i, i + 1) for i in range(shard_count - 1)]
-    halo = lax.ppermute(tokens[:, -LANES:], "seq", route)
+    halo = lax.ppermute(tail, "seq", route)
     packed = pack_spectra(spectra, shard_count)
     halo, packed = lax.optimization_barrier((halo, packed))
     halo_far = swapped(halo, 2)
     halo_near = swapped(halo, 1)
-    far, halo_far = lax.optimization_barrier((far, halo_far))
-    mains = [tokens, far, near, swapped(far, 1)]
+    where = grp.reshape(1).astype(jnp.int32)
+    weight = in_weight.reshape(3 * channels, -1)
+    half = near_half(where, tokens, near, weight)
+    far, halo_far, half = lax.optimization_barrier((far, halo_far, half))
+    diag = swapped(far, 1)
     halos = [halo, halo_far, halo_near, swapped(halo_far, 1)]
     taps = jnp.transpose(short_weight, (2, 0, 1)).reshape(channels, 9)
-    message, kept = project(
-        grp.reshape(1).astype(jnp.int32), mains, halos, in_weight.reshape(3 * channels, -1), taps, packed
-    )
+    message, kept = project(where, far, diag, halos, half, weight, taps, packed)
     message, out_weight, filter_bias, later = lax.optimization_barrier(
         (message, out_weight, filter_bias, grp)
     )
@@ -339,7 +396,10 @@
     result = convolve(received, tables)
     back = lax.all_to_all(result, "seq", 0, 0, tiled=True).reshape(channels * 8, LANES)
     weighted = gated(back, kept, bias)
-    return mixed(gathered(weighted), weights)
+    far, near = swapped(weighted, 2), swapped(weighted, 1)
+    half = mixed((weighted, near), (weights[0], weights[2]), F32)
+    far, half = lax.optimization_barrier((far, half))
+    return mixed((far, swapped(far, 1)), (weights[1], weights[3]), BF16, half)
 
 
 def solution(mesh):

time: 129 us -> 133 us (1.031)
  waiting for transfers between devices: 62.5 us -> 71.6 us
  starting transfers between devices: 44.5 us -> 35.8 us
  local copies, waits for them, and re-layouts: 1.31 us -> 4.9 us
    ppermute x12, waiting for transfers between devices: 12.8 us -> 22.1 us  [swapped(): return lax.ppermute(block, 'grp', [(i, i ^ mask) for i in range(4)])]
    ppermute x12, starting transfers between devices: 17.6 us -> 12.3 us  [swapped(): return lax.ppermute(block, 'grp', [(i, i ^ mask) for i in range(4)])]
    unnamed x10 -> x18, local copies, waits for them, and re-layouts: 0.03 us -> 3.65 us
    all_to_all x1, starting transfers between devices: 14.6 us -> 11.8 us  [shards(): received = lax.all_to_all(message, 'seq', 0, 0, tiled=True)]
  transfers between devices with their start and end apart: 15 -> 15, of which waited for: 9 -> 11; matrix products, arithmetic and copies ran while one was open for 3% -> 2% of each run, Pallas kernels for 2% -> 3%
where the time goes in v6:
time: 133 us
  waiting for transfers between devices  71.6 us (54%)
  starting transfers between devices  35.8 us (27%)
  Pallas kernels  17.4 us (13%)
  local copies, waits for them, and re-layouts  4.9 us (4%)
  other arithmetic  2.79 us (2%)
    all_to_all x1, waiting for transfers between devices, shards(): received = lax.all_to_all(message, 'seq', 0, 0, tiled=True)  35.1 us
    ppermute x12, waiting for transfers between devices, swapped(): return lax.ppermute(block, 'grp', [(i, i ^ mask) for i in range(4)])  22.1 us
    all_to_all x1, waiting for transfers between devices, shards(): lax.all_to_all(result, 'seq', 0, 0, tiled=True).reshape(channels * 8, LANES)  14.4 us
    ppermute x12, starting transfers between devices, swapped(): return lax.ppermute(block, 'grp', [(i, i ^ mask) for i in range(4)])  12.3 us
    all_to_all x1, starting transfers between devices, shards(): received = lax.all_to_all(message, 'seq', 0, 0, tiled=True)  11.8 us
    all_to_all x1, starting transfers between devices, shards(): lax.all_to_all(result, 'seq', 0, 0, tiled=True).reshape(channels * 8, LANES)  8.67 us
    pallas_call x1, Pallas kernels, convolve(): pl.pallas_call(convolve_body, in_specs=[vmem, pl.BlockSpec(memory_space=p...  5.47 us
    pallas_call x1, Pallas kernels, project(): pl.pallas_call(project_body, in_specs=[pl.BlockSpec(memory_space=pltpu.SM...  5.27 us
  transfers between devices with their start and end apart: 15, of which 11 were waited for; matrix products, arithmetic and copies ran while one was open for 2% of the time, Pallas kernels for 3%

profile of v6, /device:TPU:1, one launch (start us, length us, event | category | flops | bytes accessed | tf_op | source)
XLA Modules:
  0.0 132.6 jit_solution(14373563159866164202)
XLA Ops:
  0.0 0.8 slice.3
  0.8 3.2 %collective-permute-start.3 = (bf16[192,1024]{1,0:T(8,128)(2,1)}, bf16[192,1024]{1,0:T(8,128)(2,1)S(1)}, u32[]{:S(2)}, u32[]{:S(2)}) collective-permute-start(bf16[192,1024]{1,0:T(8,128)(2,1)} %own_ref.1), channel_id=1, source_target_pairs={{0,1},{1,0},{2,3},{3,2},{4,5},{5,4},{6,7},{7,6},{8,9},{9,8},{10,11... | collective-permute-start | bytes 1179656 | tf_op jit(solution)/shard_map/ppermute | solution.py:355
  4.0 3.0 %collective-permute-start.1 = (bf16[192,128]{1,0:T(8,128)(2,1)S(1)}, bf16[192,128]{1,0:T(8,128)(2,1)S(1)}, u32[]{:S(2)}, u32[]{:S(2)}) collective-permute-start(bf16[192,128]{1,0:T(8,128)(2,1)S(1)} %slice.3), channel_id=1, source_target_pairs={{0,4},{4,8},{8,12},{12,16},{16,20},{20,24},{24,28},{28,32},{32,36}... | collective-permute-start | bytes 147464 | tf_op jit(solution)/shard_map/ppermute | solution.py:368
  7.1 2.9 %pack_spectra.1.refs_10_ = bf16[64,15,8,128]{3,2,1,0:T(8,128)(2,1)} custom-call(f32[2,192,8,256]{3,2,1,0:T(8,128)} %spec_ref.1), custom_call_target="tpu_custom_call" | custom-call | bytes 4718592 | tf_op jit(solution)/shard_map/pack_spectra/pallas_call | solution.py:59
  10.3 0.7 copy-done.3
  11.0 1.0 copy-done.2
  12.0 1.0 copy-done.4
  13.0 0.9 near_half.1.refs_7_
  13.9 3.1 %collective-permute-done.2.refs_4_ = bf16[192,128]{1,0:T(8,128)(2,1)S(1)} collective-permute-done((bf16[192,128]{1,0:T(8,128)(2,1)S(1)}, bf16[192,128]{1,0:T(8,128)(2,1)S(1)}, u32[]{:S(2)}, u32[]{:S(2)}) %collective-permute-start.2) | collective-permute-done | bytes 49184 | tf_op jit(solution)/shard_map/ppermute | solution.py:355
  17.0 0.9 collective-permute-start.4
  17.9 0.5 collective-permute-start.6
  18.6 0.6 collective-permute-done.5.refs_5_
  19.7 5.3 %project.1 = (bf16[64,15,8,128]{3,2,1,0:T(8,128)(2,1)}, bf16[2,192,1024]{2,1,0:T(8,128)(2,1)S(1)}) custom-call(s32[1]{0:T(128)} %bitcast.grp_ref.refs_0_, bf16[192,1024]{1,0:T(8,128)(2,1)} %collective-permute-done.refs_1_, bf16[192,1024]{1,0:T(8,128)(2,1)} %collective-permute-done.4.refs_2_, ...), custom_call_target="tpu_custom_call", output_to_operand_aliasing={{0}: (10, {})} | custom-call | flops 509607936 | bytes 6291456 | tf_op jit(solution)/shard_map/project/pallas_call | solution.py:168
  25.0 0.9 copy-done.1
  25.9 11.8 %all-to-all-start = ((bf16[64,15,8,128]{3,2,1,0:T(8,128)(2,1)}), bf16[64,15,8,128]{3,2,1,0:T(8,128)(2,1)S(1)}, u32[]{:S(2)}, u32[]{:S(2)}) async-start(bf16[64,15,8,128]{3,2,1,0:T(8,128)(2,1)} %get-tuple-element.36), calls=%async_computation | async-start | bytes 3932160 | tf_op jit(solution)/shard_map/all_to_all | solution.py:384
  37.9 0.9 collective-permute-start.9
  38.8 1.2 collective-permute-start.7
  40.0 1.3 broadcast_add_fusion.1.twist_ref
  41.4 1.5 %broadcast_add_fusion.wave_hbm = bf16[2048,512]{1,0:T(8,128)(2,1)} fusion(bf16[2048,512]{1,0:T(8,128)(2,1)S(1)} %copy-done.5, bf16[]{:T(256)S(6)} %convert_element_type.7), kind=kLoop, calls=%fused_computation | loop fusion | flops 1048576 | bytes 4194306 | tf_op jit(solution)/shard_map/add | solution.py:392
  42.8 4.5 %collective-permute-done.9.refs_3_ = bf16[192,192]{1,0:T(8,128)(2,1)S(1)} collective-permute-done((bf16[192,192]{1,0:T(8,128)(2,1)S(1)}, bf16[192,192]{1,0:T(8,128)(2,1)S(1)}, u32[]{:S(2)}, u32[]{:S(2)}) %collective-permute-start.9) | collective-permute-done | bytes 73760 | tf_op jit(solution)/shard_map/ppermute | solution.py:355
  47.3 2.0 %collective-permute-done.7.refs_2_ = bf16[192,192]{1,0:T(8,128)(2,1)S(1)} collective-permute-done((bf16[192,192]{1,0:T(8,128)(2,1)S(1)}, bf16[192,192]{1,0:T(8,128)(2,1)S(1)}, u32[]{:S(2)}, u32[]{:S(2)}) %collective-permute-start.7) | collective-permute-done | bytes 73760 | tf_op jit(solution)/shard_map/ppermute | solution.py:355
  49.3 35.1 %all-to-all-done.m_ref = bf16[64,15,8,128]{3,2,1,0:T(8,128)(2,1)S(1)} async-done(((bf16[64,15,8,128]{3,2,1,0:T(8,128)(2,1)}), bf16[64,15,8,128]{3,2,1,0:T(8,128)(2,1)S(1)}, u32[]{:S(2)}, u32[]{:S(2)}) %all-to-all-start) | async-done | bytes 1966112 | tf_op jit(solution)/shard_map/all_to_all | solution.py:384
  84.4 5.5 %convolve.1 = bf16[64,3,8,128]{3,2,1,0:T(8,128)(2,1)} custom-call(bf16[64,15,8,128]{3,2,1,0:T(8,128)(2,1)S(1)} %all-to-all-done.m_ref, bf16[2048,512]{1,0:T(8,128)(2,1)} %broadcast_add_fusion.wave_hbm, f32[512,512]{1,0:T(8,128)S(1)} %broadcast_add_fusion.1.twist_ref), custom_call_target="tpu_custom_call" | custom-call | flops 3221225472 | bytes 6291456 | tf_op jit(solution)/shard_map/convolve/pallas_call | solution.py:279
  89.9 8.7 %all-to-all-start.1 = ((bf16[64,3,8,128]{3,2,1,0:T(8,128)(2,1)}), bf16[64,3,8,128]{3,2,1,0:T(8,128)(2,1)S(1)}, u32[]{:S(2)}, u32[]{:S(2)}) async-start(bf16[64,3,8,128]{3,2,1,0:T(8,128)(2,1)} %convolve.1), calls=%async_computation.1 | async-start | bytes 786432 | tf_op jit(solution)/shard_map/all_to_all | solution.py:397
  98.7 14.4 %all-to-all-done.1 = bf16[64,3,8,128]{3,2,1,0:T(8,128)(2,1)S(1)} async-done(((bf16[64,3,8,128]{3,2,1,0:T(8,128)(2,1)}), bf16[64,3,8,128]{3,2,1,0:T(8,128)(2,1)S(1)}, u32[]{:S(2)}, u32[]{:S(2)}) %all-to-all-start.1) | async-done | bytes 393248 | tf_op jit(solution)/shard_map/all_to_all | solution.py:397
  113.1 1.4 %gated.1.refs_0_ = bf16[192,1024]{1,0:T(8,128)(2,1)S(1)} custom-call(bf16[1536,128]{1,0:T(8,128)(2,1)S(1)} %bitcast.17, bf16[2,192,1024]{2,1,0:T(8,128)(2,1)} %copy-done.1, f32[192,1]{1,0:T(8,128)S(1)} %copy.20.bias_ref), custom_call_target="tpu_custom_call" | custom-call | flops 786432 | bytes 1572864 | tf_op jit(solution)/shard_map/gated/pallas_call | solution.py:316
  114.5 4.1 %collective-permute-start.11 = (bf16[192,1024]{1,0:T(8,128)(2,1)S(1)}, bf16[192,1024]{1,0:T(8,128)(2,1)S(1)}, u32[]{:S(2)}, u32[]{:S(2)}) collective-permute-start(bf16[192,1024]{1,0:T(8,128)(2,1)S(1)} %gated.1.refs_0_), channel_id=1, source_target_pairs={{0,1},{1,0},{2,3},{3,2},{4,5},{5,4},{6,7},{7,6},{8,9},{9,8},{10,11... | collective-permute-start | bytes 1179656 | tf_op jit(solution)/shard_map/ppermute | solution.py:355
  118.9 1.0 collective-permute-done.11.refs_1_
  120.3 9.0 %collective-permute-done.10.refs_0_ = bf16[192,1024]{1,0:T(8,128)(2,1)S(1)} collective-permute-done((bf16[192,1024]{1,0:T(8,128)(2,1)S(1)}, bf16[192,1024]{1,0:T(8,128)(2,1)S(1)}, u32[]{:S(2)}, u32[]{:S(2)}) %collective-permute-start.10) | collective-permute-done | bytes 393248 | tf_op jit(solution)/shard_map/ppermute | solution.py:355
  129.3 0.9 collective-permute-start.12
  130.2 1.3 %collective-permute-done.12.refs_1_ = bf16[192,1024]{1,0:T(8,128)(2,1)S(1)} collective-permute-done((bf16[192,1024]{1,0:T(8,128)(2,1)S(1)}, bf16[192,1024]{1,0:T(8,128)(2,1)S(1)}, u32[]{:S(2)}, u32[]{:S(2)}) %collective-permute-start.12) | collective-permute-done | bytes 393248 | tf_op jit(solution)/shard_map/ppermute | solution.py:355
  131.5 1.1 mixed.3
  (32 shorter events, 1.9 us)
Async XLA Ops:
  0.8 10.2 %copy-start = (bf16[3,192,768]{2,1,0:T(8,128)(2,1)S(1)}, bf16[3,192,768]{2,1,0:T(8,128)(2,1)}, u32[]{:S(2)}) copy-start(bf16[3,192,768]{2,1,0:T(8,128)(2,1)} %param.9) | copy-start | bytes 2654212
  0.8 9.5 %collective-permute-start.3 = (bf16[192,1024]{1,0:T(8,128)(2,1)}, bf16[192,1024]{1,0:T(8,128)(2,1)S(1)}, u32[]{:S(2)}, u32[]{:S(2)}) collective-permute-start(bf16[192,1024]{1,0:T(8,128)(2,1)} %own_ref.1), channel_id=1, source_target_pairs={{0,1},{1,0},{2,3},{3,2},{4,5},{5,4},{6,7},{7,6},{8,9},{9,8},{10,11... | collective-permute-start | bytes 1179656 | tf_op jit(solution)/shard_map/ppermute | solution.py:355
  4.0 13.0 %collective-permute-start = (bf16[192,1024]{1,0:T(8,128)(2,1)}, bf16[192,1024]{1,0:T(8,128)(2,1)}, u32[]{:S(2)}, u32[]{:S(2)}) collective-permute-start(bf16[192,1024]{1,0:T(8,128)(2,1)} %own_ref.1), channel_id=1, source_target_pairs={{0,2},{1,3},{2,0},{3,1},{4,6},{5,7},{6,4},{7,5},{8,10},{9,11},{10,... | collective-permute-start | bytes 1179656 | tf_op jit(solution)/shard_map/ppermute | solution.py:355
  4.0 6.0 %collective-permute-start.1 = (bf16[192,128]{1,0:T(8,128)(2,1)S(1)}, bf16[192,128]{1,0:T(8,128)(2,1)S(1)}, u32[]{:S(2)}, u32[]{:S(2)}) collective-permute-start(bf16[192,128]{1,0:T(8,128)(2,1)S(1)} %slice.3), channel_id=1, source_target_pairs={{0,4},{4,8},{8,12},{12,16},{16,20},{20,24},{24,28},{28,32},{32,36}... | collective-permute-start | bytes 147464 | tf_op jit(solution)/shard_map/ppermute | solution.py:368
  7.1 11.4 %copy-start.7 = (f32[3,3,192]{2,1,0:T(4,128)S(1)}, f32[3,3,192]{2,1,0:T(4,128)}, u32[]{:S(2)}) copy-start(f32[3,3,192]{2,1,0:T(4,128)} %param.10) | copy-start | bytes 20740
  10.0 7.0 %collective-permute-start.2 = (bf16[192,128]{1,0:T(8,128)(2,1)S(1)}, bf16[192,128]{1,0:T(8,128)(2,1)S(1)}, u32[]{:S(2)}, u32[]{:S(2)}) collective-permute-start(bf16[192,128]{1,0:T(8,128)(2,1)S(1)} %collective-permute-done.1.refs_3_), channel_id=1, source_target_pairs={{0,2},{1,3},{2,0},{3,1},{4,6},{5,7},{6,4},{7,5},{8,10},{9,11},{10,... | collective-permute-start | bytes 147464 | tf_op jit(solution)/shard_map/ppermute | solution.py:355
  10.3 0.7 copy-start.3
  11.0 1.0 copy-start.2
  12.0 1.0 copy-start.4
  17.0 2.6 %collective-permute-start.4 = (bf16[192,1024]{1,0:T(8,128)(2,1)}, bf16[192,1024]{1,0:T(8,128)(2,1)}, u32[]{:S(2)}, u32[]{:S(2)}) collective-permute-start(bf16[192,1024]{1,0:T(8,128)(2,1)} %collective-permute-done.refs_1_), channel_id=1, source_target_pairs={{0,1},{1,0},{2,3},{3,2},{4,5},{5,4},{6,7},{7,6},{8,9},{9,8},{10,11... | collective-permute-start | bytes 1179656 | tf_op jit(solution)/shard_map/ppermute | solution.py:355
  17.9 1.3 collective-permute-start.5
  17.9 1.5 %collective-permute-start.6 = (bf16[192,128]{1,0:T(8,128)(2,1)S(1)}, bf16[192,128]{1,0:T(8,128)(2,1)S(1)}, u32[]{:S(2)}, u32[]{:S(2)}) collective-permute-start(bf16[192,128]{1,0:T(8,128)(2,1)S(1)} %collective-permute-done.2.refs_4_), channel_id=1, source_target_pairs={{0,1},{1,0},{2,3},{3,2},{4,5},{5,4},{6,7},{7,6},{8,9},{9,8},{10,11... | collective-permute-start | bytes 147464 | tf_op jit(solution)/shard_map/ppermute | solution.py:355
  25.0 0.9 copy-start.1
  25.9 11.8 %copy-start.6 = (bf16[192,768]{1,0:T(8,128)(2,1)S(1)}, bf16[192,768]{1,0:T(8,128)(2,1)}, u32[]{:S(2)}) copy-start(bf16[192,768]{1,0:T(8,128)(2,1)} %param.13) | copy-start | bytes 884740
  25.9 58.6 %all-to-all-start = ((bf16[64,15,8,128]{3,2,1,0:T(8,128)(2,1)}), bf16[64,15,8,128]{3,2,1,0:T(8,128)(2,1)S(1)}, u32[]{:S(2)}, u32[]{:S(2)}) async-start(bf16[64,15,8,128]{3,2,1,0:T(8,128)(2,1)} %get-tuple-element.36), calls=%async_computation | async-start | bytes 3932160 | tf_op jit(solution)/shard_map/all_to_all | solution.py:384
  37.9 3.5 %copy-start.5 = (bf16[2048,512]{1,0:T(8,128)(2,1)S(1)}, bf16[2048,512]{1,0:T(8,128)(2,1)}, u32[]{:S(2)}) copy-start(bf16[2048,512]{1,0:T(8,128)(2,1)} %constant.20.clone) | copy-start | bytes 6291460
  37.9 9.4 %collective-permute-start.9 = (bf16[192,192]{1,0:T(8,128)(2,1)S(1)}, bf16[192,192]{1,0:T(8,128)(2,1)S(1)}, u32[]{:S(2)}, u32[]{:S(2)}) collective-permute-start(bf16[192,192]{1,0:T(8,128)(2,1)S(1)} %get-tuple-element.51), channel_id=1, source_target_pairs={{0,3},{1,2},{2,1},{3,0},{4,7},{5,6},{6,5},{7,4},{8,11},{9,10},{10,... | collective-permute-start | bytes 221192 | tf_op jit(solution)/shard_map/ppermute | solution.py:355
  38.8 8.5 %collective-permute-start.8 = (bf16[192,192]{1,0:T(8,128)(2,1)S(1)}, bf16[192,192]{1,0:T(8,128)(2,1)S(1)}, u32[]{:S(2)}, u32[]{:S(2)}) collective-permute-start(bf16[192,192]{1,0:T(8,128)(2,1)S(1)} %get-tuple-element.52), channel_id=1, source_target_pairs={{0,1},{1,0},{2,3},{3,2},{4,5},{5,4},{6,7},{7,6},{8,9},{9,8},{10,11... | collective-permute-start | bytes 221192 | tf_op jit(solution)/shard_map/ppermute | solution.py:355
  38.8 10.5 %collective-permute-start.7 = (bf16[192,192]{1,0:T(8,128)(2,1)S(1)}, bf16[192,192]{1,0:T(8,128)(2,1)S(1)}, u32[]{:S(2)}, u32[]{:S(2)}) collective-permute-start(bf16[192,192]{1,0:T(8,128)(2,1)S(1)} %get-tuple-element.53), channel_id=1, source_target_pairs={{0,2},{1,3},{2,0},{3,1},{4,6},{5,7},{6,4},{7,5},{8,10},{9,11},{10,... | collective-permute-start | bytes 221192 | tf_op jit(solution)/shard_map/ppermute | solution.py:355
  41.4 1.5 %copy-start.8 = (f32[192]{0:T(256)S(1)}, f32[192]{0:T(256)}, u32[]{:S(2)}) copy-start(f32[192]{0:T(256)} %param.11) | copy-start | bytes 2308
  89.9 23.2 %all-to-all-start.1 = ((bf16[64,3,8,128]{3,2,1,0:T(8,128)(2,1)}), bf16[64,3,8,128]{3,2,1,0:T(8,128)(2,1)S(1)}, u32[]{:S(2)}, u32[]{:S(2)}) async-start(bf16[64,3,8,128]{3,2,1,0:T(8,128)(2,1)} %convolve.1), calls=%async_computation.1 | async-start | bytes 786432 | tf_op jit(solution)/shard_map/all_to_all | solution.py:397
  114.5 5.5 %collective-permute-start.11 = (bf16[192,1024]{1,0:T(8,128)(2,1)S(1)}, bf16[192,1024]{1,0:T(8,128)(2,1)S(1)}, u32[]{:S(2)}, u32[]{:S(2)}) collective-permute-start(bf16[192,1024]{1,0:T(8,128)(2,1)S(1)} %gated.1.refs_0_), channel_id=1, source_target_pairs={{0,1},{1,0},{2,3},{3,2},{4,5},{5,4},{6,7},{7,6},{8,9},{9,8},{10,11... | collective-permute-start | bytes 1179656 | tf_op jit(solution)/shard_map/ppermute | solution.py:355
  118.6 10.7 %collective-permute-start.10 = (bf16[192,1024]{1,0:T(8,128)(2,1)S(1)}, bf16[192,1024]{1,0:T(8,128)(2,1)S(1)}, u32[]{:S(2)}, u32[]{:S(2)}) collective-permute-start(bf16[192,1024]{1,0:T(8,128)(2,1)S(1)} %gated.1.refs_0_), channel_id=1, source_target_pairs={{0,2},{1,3},{2,0},{3,1},{4,6},{5,7},{6,4},{7,5},{8,10},{9,11},{10,... | collective-permute-start | bytes 1179656 | tf_op jit(solution)/shard_map/ppermute | solution.py:355
  129.3 2.2 %collective-permute-start.12 = (bf16[192,1024]{1,0:T(8,128)(2,1)S(1)}, bf16[192,1024]{1,0:T(8,128)(2,1)S(1)}, u32[]{:S(2)}, u32[]{:S(2)}) collective-permute-start(bf16[192,1024]{1,0:T(8,128)(2,1)S(1)} %collective-permute-done.10.refs_0_), channel_id=1, source_target_pairs={{0,1},{1,0},{2,3},{3,2},{4,5},{5,4},{6,7},{7,6},{8,9},{9,8},{10,11... | collective-permute-start | bytes 1179656 | tf_op jit(solution)/shard_map/ppermute | solution.py:355

commit v7 on v4

--- a/solution.py
+++ b/solution.py
@@ -11,7 +11,9 @@
 COLS = 256
 FREQS = 512
 LANES = 128
-PROJECT_VMEM = 50000 << 10
+PROJECT_VMEM = 51500 << 10
+GATED_VMEM = 54000 << 10
+MIXED_VMEM = 12 << 20
 CONVOLVE_VMEM = 50000 << 10
 MASKS = (0, 2, 1, 3)
 BF16 = jnp.bfloat16
@@ -66,9 +68,16 @@
     )(spectra)
 
 
+def filtered(stream, taps_ref, row, s):
+    x = stream.astype(F32)
+    w = [taps_ref[pl.ds(row, x.shape[0]), 3 * tap + s:3 * tap + s + 1] for tap in range(3)]
+    y = w[0] * x + w[1] * pltpu.roll(x, 1, 1) + w[2] * pltpu.roll(x, 2, 1)
+    return y[:, LANES:]
+
+
 def project_body(*refs):
     grp_ref, mains, halos, weight_ref, taps_ref = refs[0], refs[1:5], refs[5:9], refs[9], refs[10]
-    message_ref, kept_ref, token_ref, stream_ref, spread_ref, part_ref, sem = refs[12:]
+    message_ref, gate_ref, token_ref, stream_ref, spread_ref, part_ref, sem = refs[12:]
     channels, tok = mains[0].shape
     width = tok + LANES
     grp = grp_ref[0]
@@ -85,15 +94,11 @@
 
     def chunk(index, carry):
         row = pl.multiple_of(index * rows, rows)
-        smooth = []
-        for s in range(3):
-            x = stream_ref[pl.ds(s * channels + row, rows), :].astype(BF16).astype(F32)
-            w = [taps_ref[pl.ds(row, rows), 3 * tap + s:3 * tap + s + 1] for tap in range(3)]
-            y = w[0] * x + w[1] * pltpu.roll(x, 1, 1) + w[2] * pltpu.roll(x, 2, 1)
-            smooth.append(y[:, LANES:])
-        kept_ref[0, pl.ds(row, rows), :] = smooth[0].astype(BF16)
-        signal = smooth[2] * smooth[1]
-        kept_ref[1, pl.ds(row, rows), :] = signal.astype(BF16)
+        gate_ref[pl.ds(row, rows), :] = stream_ref[pl.ds(row, rows), :].astype(BF16)
+        first, second = (
+            filtered(stream_ref[pl.ds(s * channels + row, rows), :].astype(BF16), taps_ref, row, s) for s in (1, 2)
+        )
+        signal = second * first
         for part in range(8):
             spread_ref[pl.ds(row * 8 + part, rows, stride=8), :] = signal[:, part * LANES:(part + 1) * LANES]
         return carry
@@ -127,7 +132,7 @@
         out_specs=[anywhere, vmem],
         out_shape=[
             jax.ShapeDtypeStruct(packed.shape, BF16),
-            jax.ShapeDtypeStruct((2, channels, tok), BF16),
+            jax.ShapeDtypeStruct((channels, width), BF16),
         ],
         scratch_shapes=[
             pltpu.VMEM((4 * channels, width), BF16),
@@ -144,6 +149,45 @@
     )(grp, *mains, *halos, weight, taps, packed)
 
 
+def keep_body(message_hbm, gate_ref, taps_ref, kept_ref, part_ref, spread_ref, sem):
+    channels = gate_ref.shape[0]
+    per_dest = part_ref.shape[1]
+    load = pltpu.make_async_copy(message_hbm.at[:, pl.ds(4 * per_dest, per_dest)], part_ref, sem)
+    load.start()
+    rows = 16
+
+    def chunk(index, carry):
+        row = pl.multiple_of(index * rows, rows)
+        kept_ref[0, pl.ds(row, rows), :] = filtered(gate_ref[pl.ds(row, rows), :], taps_ref, row, 0).astype(BF16)
+        return carry
+
+    lax.fori_loop(0, channels // rows, chunk, 0)
+    load.wait()
+    spread_ref[...] = part_ref[...].astype(F32).reshape(spread_ref.shape)
+    for part in range(8):
+        column = spread_ref[pl.ds(part, channels, stride=8), :]
+        kept_ref[1, :, part * LANES:(part + 1) * LANES] = column.astype(BF16)
+
+
+def keep(message, gate_stream, taps):
+    channels, width = gate_stream.shape
+    shards, pieces = message.shape[:2]
+    vmem = pl.BlockSpec(memory_space=pltpu.VMEM)
+    return pl.pallas_call(
+        keep_body,
+        in_specs=[pl.BlockSpec(memory_space=pltpu.HBM), vmem, vmem],
+        out_specs=vmem,
+        out_shape=jax.ShapeDtypeStruct((2, channels, width - LANES), BF16),
+        scratch_shapes=[
+            pltpu.VMEM((shards, pieces // 5, 8, LANES), BF16),
+            pltpu.VMEM((channels * 8, LANES), F32),
+            pltpu.SemaphoreType.DMA,
+        ],
+        cost_estimate=pl.CostEstimate(flops=8 * channels * width, bytes_accessed=2 << 20, transcendentals=0),
+        name="keep",
+    )(message, gate_stream, taps)
+
+
 def convolve_body(m_ref, wave_hbm, twist_ref, out_ref,
                   spread_ref, grid_ref, mid_ref, tall_ref, done_ref, wave_ref, sems, wave_sems):
     channels, shards, pieces, lanes = done_ref.shape
@@ -155,22 +199,28 @@
     ]
     for load in loads:
         load.start()
-    for c in range(channels):
+    cosine, sine = twist_ref[:, :COLS], twist_ref[:, COLS:]
+
+    def arrange(c):
         spread_ref[c] = m_ref[:, 4 * channels + c].astype(F32).reshape(shards * pieces, lanes)
         for a in range(rows_dev):
             for h in range(2):
                 grid_ref[c, a * shards:(a + 1) * shards, h * lanes:(h + 1) * lanes] = spread_ref[
                     c, pl.ds(2 * a + h, shards, stride=pieces), :].astype(BF16)
-        if c == 0:
-            loads[0].wait()
+
+    def rows_forward(c):
         real = jnp.dot(first_ref[:, :COLS], grid_ref[c], preferred_element_type=F32)
-        imag = jnp.dot(first_ref[:, COLS:], grid_ref[c], preferred_element_type=F32)
-        cosine, sine = twist_ref[:, :COLS], twist_ref[:, COLS:]
+        return real, jnp.dot(first_ref[:, COLS:], grid_ref[c], preferred_element_type=F32)
+
+    def twist_forward(c, wave):
+        real, imag = wave
         mid_ref[c, :, :COLS] = (real * cosine + imag * sine).astype(BF16)
         mid_ref[c, :, COLS:] = (imag * cosine - real * sine).astype(BF16)
-        if c == 0:
-            loads[1].wait()
-        freq = jnp.dot(mid_ref[c], forward_ref[...], preferred_element_type=F32)
+
+    def cols_forward(c):
+        return jnp.dot(mid_ref[c], forward_ref[...], preferred_element_type=F32)
+
+    def respond(c, freq):
         for h in range(2):
             low, high = h * lanes, COLS + h * lanes
             real, imag = freq[:, low:low + lanes], freq[:, high:high + lanes]
@@ -179,22 +229,41 @@
             )
             mid_ref[c, :, low:low + lanes] = (real * h_real - imag * h_imag).astype(BF16)
             mid_ref[c, :, high:high + lanes] = (real * h_imag + imag * h_real).astype(BF16)
-        if c == 0:
-            loads[2].wait()
-        back = jnp.dot(mid_ref[c], backward_ref[...], preferred_element_type=F32)
+
+    def cols_backward(c):
+        return jnp.dot(mid_ref[c], backward_ref[...], preferred_element_type=F32)
+
+    def twist_backward(c, back):
         real, imag = back[:, :COLS], back[:, COLS:]
         tall_ref[c, :freqs, :] = (real * cosine - imag * sine).astype(BF16)
         tall_ref[c, freqs:, :] = (imag * cosine + real * sine).astype(BF16)
-        if c == 0:
-            loads[3].wait()
+
+    def rows_backward(c):
         out = jnp.dot(last_ref[:COLS, :], tall_ref[c, :freqs], preferred_element_type=F32)
-        out += jnp.dot(last_ref[COLS:, :], tall_ref[c, freqs:], preferred_element_type=F32)
+        return out + jnp.dot(last_ref[COLS:, :], tall_ref[c, freqs:], preferred_element_type=F32)
+
+    def send(c, out):
         for a in range(rows_dev):
             for h in range(2):
                 spread_ref[c, pl.ds(2 * a + h, shards, stride=pieces), :] = out[
                     a * shards:(a + 1) * shards, h * lanes:(h + 1) * lanes]
         done_ref[c] = spread_ref[c].reshape(shards, pieces, lanes).astype(BF16)
         pltpu.make_async_copy(done_ref.at[c], out_ref.at[:, c], sems.at[c]).start()
+
+    for c in range(channels):
+        arrange(c)
+    stages = (
+        (rows_forward, twist_forward), (cols_forward, respond), (cols_backward, twist_backward), (rows_backward, send)
+    )
+    waiting = None
+    for stage, (multiply, finish) in enumerate(stages):
+        loads[stage].wait()
+        for c in range(channels):
+            product = multiply(c)
+            if waiting is not None:
+                waiting[0](*waiting[1:])
+            waiting = (finish, c, product)
+    waiting[0](*waiting[1:])
     for c in range(channels):
         pltpu.make_async_copy(done_ref.at[c], out_ref.at[:, c], sems.at[c]).wait()
 
@@ -225,61 +294,66 @@
     )(received, *tables)
 
 
-def gated_body(y_ref, kept_ref, bias_ref, out_ref, spread_ref):
-    channels = out_ref.shape[0]
+def gated_body(y_ref, kept_hbm, bias_ref, early_ref, late_ref, spread_ref, kept_ref, sem):
+    channels = early_ref.shape[0]
+    load = pltpu.make_async_copy(kept_hbm, kept_ref, sem)
+    load.start()
     spread_ref[...] = y_ref[...].astype(F32)
     bias = bias_ref[...]
+    load.wait()
     for part in range(8):
         cols = slice(part * LANES, (part + 1) * LANES)
         y = spread_ref[pl.ds(part, channels, stride=8), :]
         direct = bias * kept_ref[1, :, cols].astype(F32)
-        out_ref[:, cols] = (kept_ref[0, :, cols].astype(F32) * (y + direct)).astype(BF16)
+        out_ref, at = (early_ref, part) if part < 4 else (late_ref, part - 4)
+        value = kept_ref[0, :, cols].astype(F32) * (y + direct)
+        out_ref[:, at * LANES:(at + 1) * LANES] = value.astype(BF16)
 
 
 def gated(y, kept, bias):
     vmem = pl.BlockSpec(memory_space=pltpu.VMEM)
     return pl.pallas_call(
         gated_body,
-        in_specs=[vmem] * 3,
-        out_specs=vmem,
-        out_shape=jax.ShapeDtypeStruct(kept.shape[1:], BF16),
-        scratch_shapes=[pltpu.VMEM(y.shape, F32)],
-        compiler_params=pltpu.CompilerParams(vmem_limit_bytes=8 << 20),
+        in_specs=[vmem, pl.BlockSpec(memory_space=pltpu.HBM), vmem],
+        out_specs=[vmem] * 2,
+        out_shape=[jax.ShapeDtypeStruct((kept.shape[1], kept.shape[2] // 2), BF16)] * 2,
+        scratch_shapes=[
+            pltpu.VMEM(y.shape, F32),
+            pltpu.VMEM(kept.shape, BF16),
+            pltpu.SemaphoreType.DMA,
+        ],
+        compiler_params=pltpu.CompilerParams(vmem_limit_bytes=GATED_VMEM),
         cost_estimate=pl.CostEstimate(flops=4 * y.size, bytes_accessed=8 * y.size, transcendentals=0),
         name="gated",
     )(y, kept, bias)
 
 
 def mixed_body(*refs):
-    values, weights, out_ref = refs[:4], refs[4:8], refs[8]
+    values, weights, out_ref = refs[:4], refs[4:8], refs[-1]
     total = jnp.dot(weights[0][...], values[0][...], preferred_element_type=F32)
     for w, v in zip(weights[1:], values[1:]):
         total = total + jnp.dot(w[...], v[...], preferred_element_type=F32)
     out_ref[...] = total.astype(BF16)
 
 
-def mixed(values, weights):
-    vmem = pl.BlockSpec(memory_space=pltpu.VMEM)
+def mixed(values, weights, half, *earlier):
     channels, tok = values[0].shape
+    whole = [pl.BlockSpec(memory_space=pltpu.VMEM)] * 8
     return pl.pallas_call(
         mixed_body,
-        in_specs=[vmem] * 8,
-        out_specs=vmem,
-        out_shape=jax.ShapeDtypeStruct((weights[0].shape[0], tok), BF16),
-        compiler_params=pltpu.CompilerParams(vmem_limit_bytes=12 << 20),
-        cost_estimate=pl.CostEstimate(flops=8 * channels * channels * tok, bytes_accessed=3 << 20, transcendentals=0),
+        grid=(1,),
+        in_specs=whole + [pl.BlockSpec(memory_space=pl.ANY)] * len(earlier),
+        out_specs=pl.BlockSpec((weights[0].shape[0], tok), lambda i: (0, half)),
+        out_shape=jax.ShapeDtypeStruct((weights[0].shape[0], 2 * tok), BF16),
+        input_output_aliases={8: 0} if earlier else {},
+        compiler_params=pltpu.CompilerParams(vmem_limit_bytes=MIXED_VMEM),
+        cost_estimate=pl.CostEstimate(flops=8 * channels * channels * tok, bytes_accessed=2 << 20, transcendentals=0),
         name="mixed",
-    )(*values, *weights)
+    )(*values, *weights, *earlier)
 
 
 def swapped(block, mask):
     return lax.ppermute(block, "grp", [(i, i ^ mask) for i in range(4)])
-
-
-def gathered(block):
-    far = swapped(block, 2)
-    near = swapped(block, 1)
-    return block, far, near, swapped(far, 1)
 
 
 def shards(tokens, in_weight, short_weight, filter_bias, spectra, out_weight):
@@ -300,12 +374,13 @@
     mains = [tokens, far, near, swapped(far, 1)]
     halos = [halo, halo_far, halo_near, swapped(halo_far, 1)]
     taps = jnp.transpose(short_weight, (2, 0, 1)).reshape(channels, 9)
-    message, kept = project(
+    message, gate_stream = project(
         grp.reshape(1).astype(jnp.int32), mains, halos, in_weight.reshape(3 * channels, -1), taps, packed
     )
-    message, out_weight, filter_bias, later = lax.optimization_barrier(
-        (message, out_weight, filter_bias, grp)
+    message, out_weight, filter_bias, later, gate_stream = lax.optimization_barrier(
+        (message, out_weight, filter_bias, grp, gate_stream)
     )
+    kept = keep(message, gate_stream, taps)
     received = lax.all_to_all(message, "seq", 0, 0, tiled=True)
 
     turned = out_weight.T
@@ -316,12 +391,16 @@
     zero = jnp.minimum(later, 0)
     tables = [t + zero.astype(t.dtype) for t in transform_tables(shard_count, tok // COLS)]
     bias = filter_bias[:, None] + zero.astype(F32)
-    received, weights, tables, bias = lax.optimization_barrier((received, weights, tables, bias))
+    received, weights, tables, bias, kept = lax.optimization_barrier((received, weights, tables, bias, kept))
 
     result = convolve(received, tables)
     back = lax.all_to_all(result, "seq", 0, 0, tiled=True).reshape(channels * 8, LANES)
-    weighted = gated(back, kept, bias)
-    return mixed(gathered(weighted), weights)
+    early, late = gated(back, kept, bias)
+    far_early, far_late = swapped(early, 2), swapped(late, 2)
+    far_early, early, late = lax.optimization_barrier((far_early, early, late))
+    near_early, near_late = swapped(early, 1), swapped(late, 1)
+    out = mixed((early, far_early, near_early, swapped(far_early, 1)), weights, 0)
+    return mixed((late, far_late, near_late, swapped(far_late, 1)), weights, 1, out)
 
 
 def solution(mesh):

time: 128 us -> 127 us (level)
  Pallas kernels: 14.7 us -> 19.3 us
  waiting for transfers between devices: 62.5 us -> 57.9 us
    pallas_call x2 -> x4, Pallas kernels: 1.62 us -> 6.82 us  [the longest x1 3.36 us: keep(): pl.pallas_call(keep_body, in_specs=[pl.BlockSpec(memory_space=pltpu.HBM),...]
    ppermute x12 -> x15, waiting for transfers between devices: 12.8 us -> 8.84 us  [swapped(): return lax.ppermute(block, 'grp', [(i, i ^ mask) for i in range(4)])]
    ppermute x12 -> x15, starting transfers between devices: 17.6 us -> 16.8 us  [swapped(): return lax.ppermute(block, 'grp', [(i, i ^ mask) for i in range(4)])]
  transfers between devices with their start and end apart: 15 -> 18, of which waited for: 9 -> 7; matrix products, arithmetic and copies ran while one was open for 3% -> 4% of each run, Pallas kernels for 2% -> 6%
where the time goes in v7:
time: 127 us
  waiting for transfers between devices  57.9 us (46%)
  starting transfers between devices  43.9 us (35%)
  Pallas kernels  19.3 us (15%)
  other arithmetic  2.81 us (2%)
  local copies, waits for them, and re-layouts  2.79 us (2%)
    all_to_all x1, waiting for transfers between devices, shards(): received = lax.all_to_all(message, 'seq', 0, 0, tiled=True)  34.6 us
    ppermute x15, starting transfers between devices, swapped(): return lax.ppermute(block, 'grp', [(i, i ^ mask) for i in range(4)])  16.8 us
    all_to_all x1, starting transfers between devices, shards(): received = lax.all_to_all(message, 'seq', 0, 0, tiled=True)  14.6 us
    all_to_all x1, waiting for transfers between devices, shards(): lax.all_to_all(result, 'seq', 0, 0, tiled=True).reshape(channels * 8, LANES)  14.4 us
    all_to_all x1, starting transfers between devices, shards(): lax.all_to_all(result, 'seq', 0, 0, tiled=True).reshape(channels * 8, LANES)  8.85 us
    ppermute x15, waiting for transfers between devices, swapped(): return lax.ppermute(block, 'grp', [(i, i ^ mask) for i in range(4)])  8.84 us
    pallas_call x1, Pallas kernels, convolve(): pl.pallas_call(convolve_body, in_specs=[vmem, pl.BlockSpec(memory_space=p...  5.47 us
    pallas_call x1, Pallas kernels, project(): pl.pallas_call(project_body, in_specs=[pl.BlockSpec(memory_space=pltpu.SM...  4.1 us
  transfers between devices with their start and end apart: 18, of which 7 were waited for; matrix products, arithmetic and copies ran while one was open for 4% of the time, Pallas kernels for 6%

profile of v7, /device:TPU:1, one launch (start us, length us, event | category | flops | bytes accessed | tf_op | source)
XLA Modules:
  0.0 126.8 jit_solution(422265014625624736)
XLA Ops:
  0.0 2.0 %collective-permute-start = (bf16[192,1024]{1,0:T(8,128)(2,1)}, bf16[192,1024]{1,0:T(8,128)(2,1)S(1)}, u32[]{:S(2)}, u32[]{:S(2)}) collective-permute-start(bf16[192,1024]{1,0:T(8,128)(2,1)} %refs_1_.1), channel_id=1, source_target_pairs={{0,2},{1,3},{2,0},{3,1},{4,6},{5,7},{6,4},{7,5},{8,10},{9,11},{10,... | collective-permute-start | bytes 1179656 | tf_op jit(solution)/shard_map/ppermute | solution.py:356
  2.0 0.8 slice.3
  2.9 3.7 %collective-permute-start.1 = (bf16[192,128]{1,0:T(8,128)(2,1)S(1)}, bf16[192,128]{1,0:T(8,128)(2,1)S(1)}, u32[]{:S(2)}, u32[]{:S(2)}) collective-permute-start(bf16[192,128]{1,0:T(8,128)(2,1)S(1)} %slice.3), channel_id=1, source_target_pairs={{0,4},{4,8},{8,12},{12,16},{16,20},{20,24},{24,28},{28,32},{32,36}... | collective-permute-start | bytes 147464 | tf_op jit(solution)/shard_map/ppermute | solution.py:368
  6.6 2.9 %pack_spectra.1.refs_11_ = bf16[64,15,8,128]{3,2,1,0:T(8,128)(2,1)} custom-call(f32[2,192,8,256]{3,2,1,0:T(8,128)} %spec_ref.1), custom_call_target="tpu_custom_call" | custom-call | bytes 4718592 | tf_op jit(solution)/shard_map/pack_spectra/pallas_call | solution.py:60
  9.5 0.3 collective-permute-start.2
  9.7 1.5 %collective-permute-start.3 = (bf16[192,1024]{1,0:T(8,128)(2,1)S(1)}, bf16[192,1024]{1,0:T(8,128)(2,1)S(1)}, u32[]{:S(2)}, u32[]{:S(2)}) collective-permute-start(bf16[192,1024]{1,0:T(8,128)(2,1)S(1)} %copy-done.2), channel_id=1, source_target_pairs={{0,1},{1,0},{2,3},{3,2},{4,5},{5,4},{6,7},{7,6},{8,9},{9,8},{10,11... | collective-permute-start | bytes 1179656 | tf_op jit(solution)/shard_map/ppermute | solution.py:356
  11.2 2.0 %collective-permute-done.2.refs_6_ = bf16[192,128]{1,0:T(8,128)(2,1)S(1)} collective-permute-done((bf16[192,128]{1,0:T(8,128)(2,1)S(1)}, bf16[192,128]{1,0:T(8,128)(2,1)S(1)}, u32[]{:S(2)}, u32[]{:S(2)}) %collective-permute-start.2) | collective-permute-done | bytes 49184 | tf_op jit(solution)/shard_map/ppermute | solution.py:356
  13.2 1.6 %collective-permute-start.4 = (bf16[192,1024]{1,0:T(8,128)(2,1)S(1)}, bf16[192,1024]{1,0:T(8,128)(2,1)S(1)}, u32[]{:S(2)}, u32[]{:S(2)}) collective-permute-start(bf16[192,1024]{1,0:T(8,128)(2,1)S(1)} %collective-permute-done.refs_2_), channel_id=1, source_target_pairs={{0,1},{1,0},{2,3},{3,2},{4,5},{5,4},{6,7},{7,6},{8,9},{9,8},{10,11... | collective-permute-start | bytes 1179656 | tf_op jit(solution)/shard_map/ppermute | solution.py:356
  14.8 0.5 collective-permute-start.6
  15.4 0.8 collective-permute-done.5.refs_7_
  16.3 4.1 %project.1 = (bf16[64,15,8,128]{3,2,1,0:T(8,128)(2,1)}, bf16[192,1152]{1,0:T(8,128)(2,1)S(1)}) custom-call(s32[1]{0:T(128)} %bitcast.refs_0_, bf16[192,1024]{1,0:T(8,128)(2,1)S(1)} %copy-done.2, bf16[192,1024]{1,0:T(8,128)(2,1)S(1)} %collective-permute-done.refs_2_, ...), custom_call_target="tpu_custom_call", output_to_operand_aliasing={{0}: (11, {})} | custom-call | flops 1019215872 | bytes 6291456 | tf_op jit(solution)/shard_map/project/pallas_call | solution.py:129
  20.4 0.8 copy-done.3
  21.2 14.6 %all-to-all-start = ((bf16[64,15,8,128]{3,2,1,0:T(8,128)(2,1)}), bf16[64,15,8,128]{3,2,1,0:T(8,128)(2,1)S(1)}, u32[]{:S(2)}, u32[]{:S(2)}) async-start(bf16[64,15,8,128]{3,2,1,0:T(8,128)(2,1)} %get-tuple-element.36.message_hbm), calls=%async_computation | async-start | bytes 3932160 | tf_op jit(solution)/shard_map/all_to_all | solution.py:384
  36.0 0.7 dynamic-slice_bitcast_fusion
  36.8 0.5 collective-permute-start.9
  37.4 1.4 %collective-permute-start.7 = (bf16[192,192]{1,0:T(8,128)(2,1)S(1)}, bf16[192,192]{1,0:T(8,128)(2,1)S(1)}, u32[]{:S(2)}, u32[]{:S(2)}) collective-permute-start(bf16[192,192]{1,0:T(8,128)(2,1)S(1)} %get-tuple-element.57), channel_id=1, source_target_pairs={{0,2},{1,3},{2,0},{3,1},{4,6},{5,7},{6,4},{7,5},{8,10},{9,11},{10,... | collective-permute-start | bytes 221192 | tf_op jit(solution)/shard_map/ppermute | solution.py:356
  38.8 1.3 %broadcast_add_fusion.1.twist_ref = f32[512,512]{1,0:T(8,128)S(1)} fusion(f32[512,512]{1,0:T(8,128)} %constant.21.clone, f32[]{:T(128)S(6)} %convert_element_type.8), kind=kLoop, calls=%fused_computation.1 | loop fusion | flops 262144 | bytes 2097156 | tf_op jit(solution)/shard_map/add | solution.py:392
  40.1 1.5 %broadcast_add_fusion.wave_hbm = bf16[2048,512]{1,0:T(8,128)(2,1)} fusion(bf16[2048,512]{1,0:T(8,128)(2,1)S(1)} %copy-done.4, bf16[]{:T(256)S(6)} %convert_element_type.7), kind=kLoop, calls=%fused_computation | loop fusion | flops 1048576 | bytes 4194306 | tf_op jit(solution)/shard_map/add | solution.py:392
  41.6 3.4 %keep.1.kept_hbm = bf16[2,192,1024]{2,1,0:T(8,128)(2,1)} custom-call(bf16[64,15,8,128]{3,2,1,0:T(8,128)(2,1)} %get-tuple-element.36.message_hbm, bf16[192,1152]{1,0:T(8,128)(2,1)} %copy-done.3, f32[192,9]{1,0:T(8,128)} %copy-done), custom_call_target="tpu_custom_call" | custom-call | flops 1769472 | bytes 2097152 | tf_op jit(solution)/shard_map/keep/pallas_call | solution.py:176
  45.0 2.9 %collective-permute-done.7.refs_5_ = bf16[192,192]{1,0:T(8,128)(2,1)S(1)} collective-permute-done((bf16[192,192]{1,0:T(8,128)(2,1)S(1)}, bf16[192,192]{1,0:T(8,128)(2,1)S(1)}, u32[]{:S(2)}, u32[]{:S(2)}) %collective-permute-start.7) | collective-permute-done | bytes 73760 | tf_op jit(solution)/shard_map/ppermute | solution.py:356
  47.9 34.6 %all-to-all-done.m_ref = bf16[64,15,8,128]{3,2,1,0:T(8,128)(2,1)S(1)} async-done(((bf16[64,15,8,128]{3,2,1,0:T(8,128)(2,1)}), bf16[64,15,8,128]{3,2,1,0:T(8,128)(2,1)S(1)}, u32[]{:S(2)}, u32[]{:S(2)}) %all-to-all-start) | async-done | bytes 1966112 | tf_op jit(solution)/shard_map/all_to_all | solution.py:384
  82.6 5.5 %convolve.1 = bf16[64,3,8,128]{3,2,1,0:T(8,128)(2,1)} custom-call(bf16[64,15,8,128]{3,2,1,0:T(8,128)(2,1)S(1)} %all-to-all-done.m_ref, bf16[2048,512]{1,0:T(8,128)(2,1)} %broadcast_add_fusion.wave_hbm, f32[512,512]{1,0:T(8,128)S(1)} %broadcast_add_fusion.1.twist_ref), custom_call_target="tpu_custom_call" | custom-call | flops 3221225472 | bytes 6291456 | tf_op jit(solution)/shard_map/convolve/pallas_call | solution.py:276
  88.0 8.9 %all-to-all-start.1 = ((bf16[64,3,8,128]{3,2,1,0:T(8,128)(2,1)}), bf16[64,3,8,128]{3,2,1,0:T(8,128)(2,1)S(1)}, u32[]{:S(2)}, u32[]{:S(2)}) async-start(bf16[64,3,8,128]{3,2,1,0:T(8,128)(2,1)} %convolve.1), calls=%async_computation.1 | async-start | bytes 786432 | tf_op jit(solution)/shard_map/all_to_all | solution.py:397
  97.0 14.4 %all-to-all-done.1 = bf16[64,3,8,128]{3,2,1,0:T(8,128)(2,1)S(1)} async-done(((bf16[64,3,8,128]{3,2,1,0:T(8,128)(2,1)}), bf16[64,3,8,128]{3,2,1,0:T(8,128)(2,1)S(1)}, u32[]{:S(2)}, u32[]{:S(2)}) %all-to-all-start.1) | async-done | bytes 393248 | tf_op jit(solution)/shard_map/all_to_all | solution.py:397
  111.4 1.4 %gated.1 = (bf16[192,512]{1,0:T(8,128)(2,1)S(1)}, bf16[192,512]{1,0:T(8,128)(2,1)S(1)}) custom-call(bf16[1536,128]{1,0:T(8,128)(2,1)S(1)} %bitcast.15, bf16[2,192,1024]{2,1,0:T(8,128)(2,1)} %keep.1.kept_hbm, f32[192,1]{1,0:T(8,128)S(1)} %copy.22.bias_ref), custom_call_target="tpu_custom_call" | custom-call | flops 786432 | bytes 1572864 | tf_op jit(solution)/shard_map/gated/pallas_call | solution.py:315
  112.9 1.5 %collective-permute-start.11 = (bf16[192,512]{1,0:T(8,128)(2,1)S(1)}, bf16[192,512]{1,0:T(8,128)(2,1)S(1)}, u32[]{:S(2)}, u32[]{:S(2)}) collective-permute-start(bf16[192,512]{1,0:T(8,128)(2,1)S(1)} %get-tuple-element.48.refs_0_), channel_id=1, source_target_pairs={{0,2},{1,3},{2,0},{3,1},{4,6},{5,7},{6,4},{7,5},{8,10},{9,11},{10,... | collective-permute-start | bytes 589832 | tf_op jit(solution)/shard_map/ppermute | solution.py:356
  114.4 3.1 %collective-permute-done.10.refs_1_ = bf16[192,512]{1,0:T(8,128)(2,1)S(1)} collective-permute-done((bf16[192,512]{1,0:T(8,128)(2,1)S(1)}, bf16[192,512]{1,0:T(8,128)(2,1)S(1)}, u32[]{:S(2)}, u32[]{:S(2)}) %collective-permute-start.10) | collective-permute-done | bytes 196640 | tf_op jit(solution)/shard_map/ppermute | solution.py:356
  117.4 5.2 %collective-permute-start.14 = (bf16[192,512]{1,0:T(8,128)(2,1)S(1)}, bf16[192,512]{1,0:T(8,128)(2,1)S(1)}, u32[]{:S(2)}, u32[]{:S(2)}) collective-permute-start(bf16[192,512]{1,0:T(8,128)(2,1)S(1)} %get-tuple-element.53.refs_0_), channel_id=1, source_target_pairs={{0,1},{1,0},{2,3},{3,2},{4,5},{5,4},{6,7},{7,6},{8,9},{9,8},{10,11... | collective-permute-start | bytes 589832 | tf_op jit(solution)/shard_map/ppermute | solution.py:356
  122.6 0.5 collective-permute-start.12
  123.1 1.6 %collective-permute-start.13 = (bf16[192,512]{1,0:T(8,128)(2,1)S(1)}, bf16[192,512]{1,0:T(8,128)(2,1)S(1)}, u32[]{:S(2)}, u32[]{:S(2)}) collective-permute-start(bf16[192,512]{1,0:T(8,128)(2,1)S(1)} %collective-permute-done.11.refs_1_), channel_id=1, source_target_pairs={{0,1},{1,0},{2,3},{3,2},{4,5},{5,4},{6,7},{7,6},{8,9},{9,8},{10,11... | collective-permute-start | bytes 589832 | tf_op jit(solution)/shard_map/ppermute | solution.py:356
  124.7 1.0 mixed.2.refs_8_
  125.8 1.0 mixed.3
  (36 shorter events, 0.8 us)
Async XLA Ops:
  0.0 13.2 %collective-permute-start = (bf16[192,1024]{1,0:T(8,128)(2,1)}, bf16[192,1024]{1,0:T(8,128)(2,1)S(1)}, u32[]{:S(2)}, u32[]{:S(2)}) collective-permute-start(bf16[192,1024]{1,0:T(8,128)(2,1)} %refs_1_.1), channel_id=1, source_target_pairs={{0,2},{1,3},{2,0},{3,1},{4,6},{5,7},{6,4},{7,5},{8,10},{9,11},{10,... | collective-permute-start | bytes 1179656 | tf_op jit(solution)/shard_map/ppermute | solution.py:356
  2.9 6.8 %copy-start.2 = (bf16[192,1024]{1,0:T(8,128)(2,1)S(1)}, bf16[192,1024]{1,0:T(8,128)(2,1)}, u32[]{:S(2)}) copy-start(bf16[192,1024]{1,0:T(8,128)(2,1)} %refs_1_.1) | copy-start | bytes 1179652
  2.9 12.4 %copy-start.6 = (f32[3,3,192]{2,1,0:T(4,128)S(1)}, f32[3,3,192]{2,1,0:T(4,128)}, u32[]{:S(2)}) copy-start(f32[3,3,192]{2,1,0:T(4,128)} %param.10) | copy-start | bytes 20740
  2.9 13.4 %copy-start.1 = (bf16[3,192,768]{2,1,0:T(8,128)(2,1)S(1)}, bf16[3,192,768]{2,1,0:T(8,128)(2,1)}, u32[]{:S(2)}) copy-start(bf16[3,192,768]{2,1,0:T(8,128)(2,1)} %param.9) | copy-start | bytes 2654212
  2.9 6.6 %collective-permute-start.1 = (bf16[192,128]{1,0:T(8,128)(2,1)S(1)}, bf16[192,128]{1,0:T(8,128)(2,1)S(1)}, u32[]{:S(2)}, u32[]{:S(2)}) collective-permute-start(bf16[192,128]{1,0:T(8,128)(2,1)S(1)} %slice.3), channel_id=1, source_target_pairs={{0,4},{4,8},{8,12},{12,16},{16,20},{20,24},{24,28},{28,32},{32,36}... | collective-permute-start | bytes 147464 | tf_op jit(solution)/shard_map/ppermute | solution.py:368
  9.5 3.8 %collective-permute-start.2 = (bf16[192,128]{1,0:T(8,128)(2,1)S(1)}, bf16[192,128]{1,0:T(8,128)(2,1)S(1)}, u32[]{:S(2)}, u32[]{:S(2)}) collective-permute-start(bf16[192,128]{1,0:T(8,128)(2,1)S(1)} %collective-permute-done.1.refs_5_), channel_id=1, source_target_pairs={{0,2},{1,3},{2,0},{3,1},{4,6},{5,7},{6,4},{7,5},{8,10},{9,11},{10,... | collective-permute-start | bytes 147464 | tf_op jit(solution)/shard_map/ppermute | solution.py:356
  9.7 6.5 %collective-permute-start.3 = (bf16[192,1024]{1,0:T(8,128)(2,1)S(1)}, bf16[192,1024]{1,0:T(8,128)(2,1)S(1)}, u32[]{:S(2)}, u32[]{:S(2)}) collective-permute-start(bf16[192,1024]{1,0:T(8,128)(2,1)S(1)} %copy-done.2), channel_id=1, source_target_pairs={{0,1},{1,0},{2,3},{3,2},{4,5},{5,4},{6,7},{7,6},{8,9},{9,8},{10,11... | collective-permute-start | bytes 1179656 | tf_op jit(solution)/shard_map/ppermute | solution.py:356
  13.2 3.1 %collective-permute-start.4 = (bf16[192,1024]{1,0:T(8,128)(2,1)S(1)}, bf16[192,1024]{1,0:T(8,128)(2,1)S(1)}, u32[]{:S(2)}, u32[]{:S(2)}) collective-permute-start(bf16[192,1024]{1,0:T(8,128)(2,1)S(1)} %collective-permute-done.refs_2_), channel_id=1, source_target_pairs={{0,1},{1,0},{2,3},{3,2},{4,5},{5,4},{6,7},{7,6},{8,9},{9,8},{10,11... | collective-permute-start | bytes 1179656 | tf_op jit(solution)/shard_map/ppermute | solution.py:356
  14.8 1.4 %collective-permute-start.5 = (bf16[192,128]{1,0:T(8,128)(2,1)S(1)}, bf16[192,128]{1,0:T(8,128)(2,1)S(1)}, u32[]{:S(2)}, u32[]{:S(2)}) collective-permute-start(bf16[192,128]{1,0:T(8,128)(2,1)S(1)} %collective-permute-done.1.refs_5_), channel_id=1, source_target_pairs={{0,1},{1,0},{2,3},{3,2},{4,5},{5,4},{6,7},{7,6},{8,9},{9,8},{10,11... | collective-permute-start | bytes 147464 | tf_op jit(solution)/shard_map/ppermute | solution.py:356
  14.8 1.5 %collective-permute-start.6 = (bf16[192,128]{1,0:T(8,128)(2,1)S(1)}, bf16[192,128]{1,0:T(8,128)(2,1)S(1)}, u32[]{:S(2)}, u32[]{:S(2)}) collective-permute-start(bf16[192,128]{1,0:T(8,128)(2,1)S(1)} %collective-permute-done.2.refs_6_), channel_id=1, source_target_pairs={{0,1},{1,0},{2,3},{3,2},{4,5},{5,4},{6,7},{7,6},{8,9},{9,8},{10,11... | collective-permute-start | bytes 147464 | tf_op jit(solution)/shard_map/ppermute | solution.py:356
  15.4 5.0 %copy-start = (f32[192,9]{1,0:T(8,128)}, f32[192,9]{1,0:T(8,128)S(1)}, u32[]{:S(2)}) copy-start(f32[192,9]{1,0:T(8,128)S(1)} %copy.16.refs_10_.taps_ref) | copy-start | bytes 20740
  20.4 0.8 copy-start.3
  21.2 14.6 %copy-start.5 = (bf16[192,768]{1,0:T(8,128)(2,1)S(1)}, bf16[192,768]{1,0:T(8,128)(2,1)}, u32[]{:S(2)}) copy-start(bf16[192,768]{1,0:T(8,128)(2,1)} %param.13) | copy-start | bytes 884740
  21.2 61.4 %all-to-all-start = ((bf16[64,15,8,128]{3,2,1,0:T(8,128)(2,1)}), bf16[64,15,8,128]{3,2,1,0:T(8,128)(2,1)S(1)}, u32[]{:S(2)}, u32[]{:S(2)}) async-start(bf16[64,15,8,128]{3,2,1,0:T(8,128)(2,1)} %get-tuple-element.36.message_hbm), calls=%async_computation | async-start | bytes 3932160 | tf_op jit(solution)/shard_map/all_to_all | solution.py:384
  36.0 4.1 %copy-start.4 = (bf16[2048,512]{1,0:T(8,128)(2,1)S(1)}, bf16[2048,512]{1,0:T(8,128)(2,1)}, u32[]{:S(2)}) copy-start(bf16[2048,512]{1,0:T(8,128)(2,1)} %constant.20.clone) | copy-start | bytes 6291460
  36.8 8.2 %collective-permute-start.9 = (bf16[192,192]{1,0:T(8,128)(2,1)}, bf16[192,192]{1,0:T(8,128)(2,1)S(1)}, u32[]{:S(2)}, u32[]{:S(2)}) collective-permute-start(bf16[192,192]{1,0:T(8,128)(2,1)} %get-tuple-element.55), channel_id=1, source_target_pairs={{0,3},{1,2},{2,1},{3,0},{4,7},{5,6},{6,5},{7,4},{8,11},{9,10},{10,... | collective-permute-start | bytes 221192 | tf_op jit(solution)/shard_map/ppermute | solution.py:356
  37.2 7.7 %collective-permute-start.8 = (bf16[192,192]{1,0:T(8,128)(2,1)}, bf16[192,192]{1,0:T(8,128)(2,1)S(1)}, u32[]{:S(2)}, u32[]{:S(2)}) collective-permute-start(bf16[192,192]{1,0:T(8,128)(2,1)} %get-tuple-element.56), channel_id=1, source_target_pairs={{0,1},{1,0},{2,3},{3,2},{4,5},{5,4},{6,7},{7,6},{8,9},{9,8},{10,11... | collective-permute-start | bytes 221192 | tf_op jit(solution)/shard_map/ppermute | solution.py:356
  37.4 10.5 %collective-permute-start.7 = (bf16[192,192]{1,0:T(8,128)(2,1)S(1)}, bf16[192,192]{1,0:T(8,128)(2,1)S(1)}, u32[]{:S(2)}, u32[]{:S(2)}) collective-permute-start(bf16[192,192]{1,0:T(8,128)(2,1)S(1)} %get-tuple-element.57), channel_id=1, source_target_pairs={{0,2},{1,3},{2,0},{3,1},{4,6},{5,7},{6,4},{7,5},{8,10},{9,11},{10,... | collective-permute-start | bytes 221192 | tf_op jit(solution)/shard_map/ppermute | solution.py:356
  40.1 1.5 %copy-start.7 = (f32[192]{0:T(256)S(1)}, f32[192]{0:T(256)}, u32[]{:S(2)}) copy-start(f32[192]{0:T(256)} %param.11) | copy-start | bytes 2308
  88.0 23.4 %all-to-all-start.1 = ((bf16[64,3,8,128]{3,2,1,0:T(8,128)(2,1)}), bf16[64,3,8,128]{3,2,1,0:T(8,128)(2,1)S(1)}, u32[]{:S(2)}, u32[]{:S(2)}) async-start(bf16[64,3,8,128]{3,2,1,0:T(8,128)(2,1)} %convolve.1), calls=%async_computation.1 | async-start | bytes 786432 | tf_op jit(solution)/shard_map/all_to_all | solution.py:397
  112.8 4.6 %collective-permute-start.10 = (bf16[192,512]{1,0:T(8,128)(2,1)S(1)}, bf16[192,512]{1,0:T(8,128)(2,1)S(1)}, u32[]{:S(2)}, u32[]{:S(2)}) collective-permute-start(bf16[192,512]{1,0:T(8,128)(2,1)S(1)} %get-tuple-element.53.refs_0_), channel_id=1, source_target_pairs={{0,2},{1,3},{2,0},{3,1},{4,6},{5,7},{6,4},{7,5},{8,10},{9,11},{10,... | collective-permute-start | bytes 589832 | tf_op jit(solution)/shard_map/ppermute | solution.py:356
  112.9 10.2 %collective-permute-start.11 = (bf16[192,512]{1,0:T(8,128)(2,1)S(1)}, bf16[192,512]{1,0:T(8,128)(2,1)S(1)}, u32[]{:S(2)}, u32[]{:S(2)}) collective-permute-start(bf16[192,512]{1,0:T(8,128)(2,1)S(1)} %get-tuple-element.48.refs_0_), channel_id=1, source_target_pairs={{0,2},{1,3},{2,0},{3,1},{4,6},{5,7},{6,4},{7,5},{8,10},{9,11},{10,... | collective-permute-start | bytes 589832 | tf_op jit(solution)/shard_map/ppermute | solution.py:356
  117.4 7.3 %collective-permute-start.14 = (bf16[192,512]{1,0:T(8,128)(2,1)S(1)}, bf16[192,512]{1,0:T(8,128)(2,1)S(1)}, u32[]{:S(2)}, u32[]{:S(2)}) collective-permute-start(bf16[192,512]{1,0:T(8,128)(2,1)S(1)} %get-tuple-element.53.refs_0_), channel_id=1, source_target_pairs={{0,1},{1,0},{2,3},{3,2},{4,5},{5,4},{6,7},{7,6},{8,9},{9,8},{10,11... | collective-permute-start | bytes 589832 | tf_op jit(solution)/shard_map/ppermute | solution.py:356
  122.6 2.1 %collective-permute-start.15 = (bf16[192,512]{1,0:T(8,128)(2,1)S(1)}, bf16[192,512]{1,0:T(8,128)(2,1)S(1)}, u32[]{:S(2)}, u32[]{:S(2)}) collective-permute-start(bf16[192,512]{1,0:T(8,128)(2,1)S(1)} %collective-permute-done.10.refs_1_), channel_id=1, source_target_pairs={{0,1},{1,0},{2,3},{3,2},{4,5},{5,4},{6,7},{7,6},{8,9},{9,8},{10,11... | collective-permute-start | bytes 589832 | tf_op jit(solution)/shard_map/ppermute | solution.py:356
  122.6 3.1 %collective-permute-start.12 = (bf16[192,512]{1,0:T(8,128)(2,1)S(1)}, bf16[192,512]{1,0:T(8,128)(2,1)S(1)}, u32[]{:S(2)}, u32[]{:S(2)}) collective-permute-start(bf16[192,512]{1,0:T(8,128)(2,1)S(1)} %get-tuple-element.48.refs_0_), channel_id=1, source_target_pairs={{0,1},{1,0},{2,3},{3,2},{4,5},{5,4},{6,7},{7,6},{8,9},{9,8},{10,11... | collective-permute-start | bytes 589832 | tf_op jit(solution)/shard_map/ppermute | solution.py:356
  123.1 2.7 %collective-permute-start.13 = (bf16[192,512]{1,0:T(8,128)(2,1)S(1)}, bf16[192,512]{1,0:T(8,128)(2,1)S(1)}, u32[]{:S(2)}, u32[]{:S(2)}) collective-permute-start(bf16[192,512]{1,0:T(8,128)(2,1)S(1)} %collective-permute-done.11.refs_1_), channel_id=1, source_target_pairs={{0,1},{1,0},{2,3},{3,2},{4,5},{5,4},{6,7},{7,6},{8,9},{9,8},{10,11... | collective-permute-start | bytes 589832 | tf_op jit(solution)/shard_map/ppermute | solution.py:356

commit v8 on v7

--- a/solution.py
+++ b/solution.py
@@ -11,7 +11,7 @@
 COLS = 256
 FREQS = 512
 LANES = 128
-PROJECT_VMEM = 51500 << 10
+PROJECT_VMEM = 53100 << 10
 GATED_VMEM = 54000 << 10
 MIXED_VMEM = 12 << 20
 CONVOLVE_VMEM = 50000 << 10
@@ -76,15 +76,18 @@
 
 
 def project_body(*refs):
-    grp_ref, mains, halos, weight_ref, taps_ref = refs[0], refs[1:5], refs[5:9], refs[9], refs[10]
-    message_ref, gate_ref, token_ref, stream_ref, spread_ref, part_ref, sem = refs[12:]
+    grp_ref, mains, halos, weight_hbm, taps_ref = refs[0], refs[1:5], refs[5:9], refs[9], refs[10]
+    message_ref, gate_hbm, token_ref, stream_ref, spread_ref, part_ref, gate_ref, weight_ref, sem, gate_sem, load_sem = refs[12:]
     channels, tok = mains[0].shape
     width = tok + LANES
     grp = grp_ref[0]
+    load = pltpu.make_async_copy(weight_hbm, weight_ref, load_sem)
+    load.start()
     for mask, main, halo in zip(MASKS, mains, halos):
         rows = pl.ds(pl.multiple_of((grp ^ mask) * channels, 64), channels)
         token_ref[rows, :LANES] = halo[...]
         token_ref[rows, LANES:] = main[...]
+    load.wait()
     step = 384
     for col in range(0, width, step):
         stream_ref[:, col:col + step] = jnp.dot(
@@ -115,7 +118,10 @@
         copies.append(pltpu.make_async_copy(
             part_ref.at[dests], message_ref.at[dests, pl.ds(4 * per_dest, per_dest)], sem.at[group]
         ))
-        copies[-1].start()
+        mine = pl.ds(group * each, each)
+        copies.append(pltpu.make_async_copy(gate_ref.at[mine], gate_hbm.at[mine], gate_sem.at[group]))
+        for copy in copies[-2:]:
+            copy.start()
     for copy in copies:
         copy.wait()
 
@@ -128,8 +134,8 @@
     shards, pieces = packed.shape[:2]
     return pl.pallas_call(
         project_body,
-        in_specs=[pl.BlockSpec(memory_space=pltpu.SMEM)] + [vmem] * 10 + [anywhere],
-        out_specs=[anywhere, vmem],
+        in_specs=[pl.BlockSpec(memory_space=pltpu.SMEM)] + [vmem] * 8 + [anywhere, vmem, anywhere],
+        out_specs=[anywhere] * 2,
         out_shape=[
             jax.ShapeDtypeStruct(packed.shape, BF16),
             jax.ShapeDtypeStruct((channels, width), BF16),
@@ -139,7 +145,11 @@
             pltpu.VMEM((3 * channels, width), F32),
             pltpu.VMEM((channels * 8, LANES), F32),
             pltpu.VMEM((shards, pieces // 5, 8, LANES), BF16),
+            pltpu.VMEM((channels, width), BF16),
+            pltpu.VMEM(weight.shape, BF16),
             pltpu.SemaphoreType.DMA((4,)),
+            pltpu.SemaphoreType.DMA((4,)),
+            pltpu.SemaphoreType.DMA,
         ],
         input_output_aliases={11: 0},
         compiler_params=pltpu.CompilerParams(vmem_limit_bytes=PROJECT_VMEM),
@@ -397,7 +407,6 @@
     back = lax.all_to_all(result, "seq", 0, 0, tiled=True).reshape(channels * 8, LANES)
     early, late = gated(back, kept, bias)
     far_early, far_late = swapped(early, 2), swapped(late, 2)
-    far_early, early, late = lax.optimization_barrier((far_early, early, late))
     near_early, near_late = swapped(early, 1), swapped(late, 1)
     out = mixed((early, far_early, near_early, swapped(far_early, 1)), weights, 0)
     return mixed((late, far_late, near_late, swapped(far_late, 1)), weights, 1, out)

time: 127 us -> 128 us (level)
  waiting for transfers between devices: 57.9 us -> 54.8 us
  starting transfers between devices: 43.9 us -> 46.9 us
    ppermute x15, waiting for transfers between devices: 8.84 us -> 5.78 us  [swapped(): return lax.ppermute(block, 'grp', [(i, i ^ mask) for i in range(4)])]
    ppermute x15, starting transfers between devices: 16.8 us -> 19.8 us  [swapped(): return lax.ppermute(block, 'grp', [(i, i ^ mask) for i in range(4)])]
  transfers between devices with their start and end apart: 18 -> 18, of which waited for: 7 -> 6; matrix products, arithmetic and copies ran while one was open for 4% -> 4% of each run, Pallas kernels for 6% -> 6%
where the time goes in v8:
time: 128 us; the launch traced here: 127 us
  waiting for transfers between devices  54.8 us (43%)
  starting transfers between devices  46.9 us (37%)
  Pallas kernels  20.4 us (16%)
  other arithmetic  2.8 us (2%)
  local copies, waits for them, and re-layouts  2 us (2%)
    all_to_all x1, waiting for transfers between devices, shards(): received = lax.all_to_all(message, 'seq', 0, 0, tiled=True)  34.6 us
    ppermute x15, starting transfers between devices, swapped(): return lax.ppermute(block, 'grp', [(i, i ^ mask) for i in range(4)])  19.8 us
    all_to_all x1, starting transfers between devices, shards(): received = lax.all_to_all(message, 'seq', 0, 0, tiled=True)  14.6 us
    all_to_all x1, waiting for transfers between devices, shards(): lax.all_to_all(result, 'seq', 0, 0, tiled=True).reshape(channels * 8, LANES)  14.4 us
    all_to_all x1, starting transfers between devices, shards(): lax.all_to_all(result, 'seq', 0, 0, tiled=True).reshape(channels * 8, LANES)  8.85 us
    ppermute x15, waiting for transfers between devices, swapped(): return lax.ppermute(block, 'grp', [(i, i ^ mask) for i in range(4)])  5.78 us
    pallas_call x1, Pallas kernels, convolve(): pl.pallas_call(convolve_body, in_specs=[vmem, pl.BlockSpec(memory_space=p...  5.47 us
    pallas_call x1, Pallas kernels, project(): pl.pallas_call(project_body, in_specs=[pl.BlockSpec(memory_space=pltpu.SM...  5.2 us
  transfers between devices with their start and end apart: 18, of which 6 were waited for; matrix products, arithmetic and copies ran while one was open for 4% of the time, Pallas kernels for 6%

profile of v8, /device:TPU:1, one launch (start us, length us, event | category | flops | bytes accessed | tf_op | source)
XLA Modules:
  0.0 127.2 jit_solution(9001300072536324701)
XLA Ops:
  0.0 2.0 %collective-permute-start = (bf16[192,1024]{1,0:T(8,128)(2,1)}, bf16[192,1024]{1,0:T(8,128)(2,1)S(1)}, u32[]{:S(2)}, u32[]{:S(2)}) collective-permute-start(bf16[192,1024]{1,0:T(8,128)(2,1)} %refs_1_.1), channel_id=1, source_target_pairs={{0,2},{1,3},{2,0},{3,1},{4,6},{5,7},{6,4},{7,5},{8,10},{9,11},{10,... | collective-permute-start | bytes 1179656 | tf_op jit(solution)/shard_map/ppermute | solution.py:366
  2.0 0.8 slice.3
  2.9 3.7 %collective-permute-start.1 = (bf16[192,128]{1,0:T(8,128)(2,1)S(1)}, bf16[192,128]{1,0:T(8,128)(2,1)S(1)}, u32[]{:S(2)}, u32[]{:S(2)}) collective-permute-start(bf16[192,128]{1,0:T(8,128)(2,1)S(1)} %slice.3), channel_id=1, source_target_pairs={{0,4},{4,8},{8,12},{12,16},{16,20},{20,24},{24,28},{28,32},{32,36}... | collective-permute-start | bytes 147464 | tf_op jit(solution)/shard_map/ppermute | solution.py:378
  6.6 2.9 %pack_spectra.1.refs_11_ = bf16[64,15,8,128]{3,2,1,0:T(8,128)(2,1)} custom-call(f32[2,192,8,256]{3,2,1,0:T(8,128)} %spec_ref.1), custom_call_target="tpu_custom_call" | custom-call | bytes 4718592 | tf_op jit(solution)/shard_map/pack_spectra/pallas_call | solution.py:60
  9.5 0.3 collective-permute-start.2
  9.7 1.5 %collective-permute-start.3 = (bf16[192,1024]{1,0:T(8,128)(2,1)S(1)}, bf16[192,1024]{1,0:T(8,128)(2,1)S(1)}, u32[]{:S(2)}, u32[]{:S(2)}) collective-permute-start(bf16[192,1024]{1,0:T(8,128)(2,1)S(1)} %copy-done.1), channel_id=1, source_target_pairs={{0,1},{1,0},{2,3},{3,2},{4,5},{5,4},{6,7},{7,6},{8,9},{9,8},{10,11... | collective-permute-start | bytes 1179656 | tf_op jit(solution)/shard_map/ppermute | solution.py:366
  11.2 2.0 %collective-permute-done.2.refs_6_ = bf16[192,128]{1,0:T(8,128)(2,1)S(1)} collective-permute-done((bf16[192,128]{1,0:T(8,128)(2,1)S(1)}, bf16[192,128]{1,0:T(8,128)(2,1)S(1)}, u32[]{:S(2)}, u32[]{:S(2)}) %collective-permute-start.2) | collective-permute-done | bytes 49184 | tf_op jit(solution)/shard_map/ppermute | solution.py:366
  13.2 1.6 %collective-permute-start.4 = (bf16[192,1024]{1,0:T(8,128)(2,1)S(1)}, bf16[192,1024]{1,0:T(8,128)(2,1)S(1)}, u32[]{:S(2)}, u32[]{:S(2)}) collective-permute-start(bf16[192,1024]{1,0:T(8,128)(2,1)S(1)} %collective-permute-done.refs_2_), channel_id=1, source_target_pairs={{0,1},{1,0},{2,3},{3,2},{4,5},{5,4},{6,7},{7,6},{8,9},{9,8},{10,11... | collective-permute-start | bytes 1179656 | tf_op jit(solution)/shard_map/ppermute | solution.py:366
  14.8 0.5 collective-permute-start.6
  15.4 0.8 collective-permute-done.5.refs_7_
  16.3 5.2 %project.1 = (bf16[64,15,8,128]{3,2,1,0:T(8,128)(2,1)}, bf16[192,1152]{1,0:T(8,128)(2,1)}) custom-call(s32[1]{0:T(128)} %bitcast.refs_0_, bf16[192,1024]{1,0:T(8,128)(2,1)S(1)} %copy-done.1, bf16[192,1024]{1,0:T(8,128)(2,1)S(1)} %collective-permute-done.refs_2_, ...), custom_call_target="tpu_custom_call", output_to_operand_aliasing={{0}: (11, {})} | custom-call | flops 1019215872 | bytes 6291456 | tf_op jit(solution)/shard_map/project/pallas_call | solution.py:135
  21.5 14.6 %all-to-all-start = ((bf16[64,15,8,128]{3,2,1,0:T(8,128)(2,1)}), bf16[64,15,8,128]{3,2,1,0:T(8,128)(2,1)S(1)}, u32[]{:S(2)}, u32[]{:S(2)}) async-start(bf16[64,15,8,128]{3,2,1,0:T(8,128)(2,1)} %get-tuple-element.33.message_hbm), calls=%async_computation | async-start | bytes 3932160 | tf_op jit(solution)/shard_map/all_to_all | solution.py:394
  36.1 0.2 copy.17
  36.3 0.7 dynamic-slice_bitcast_fusion
  37.1 0.5 collective-permute-start.9
  37.6 0.2 collective-permute-start.8
  37.7 1.4 %collective-permute-start.7 = (bf16[192,192]{1,0:T(8,128)(2,1)S(1)}, bf16[192,192]{1,0:T(8,128)(2,1)S(1)}, u32[]{:S(2)}, u32[]{:S(2)}) collective-permute-start(bf16[192,192]{1,0:T(8,128)(2,1)S(1)} %get-tuple-element.51), channel_id=1, source_target_pairs={{0,2},{1,3},{2,0},{3,1},{4,6},{5,7},{6,4},{7,5},{8,10},{9,11},{10,... | collective-permute-start | bytes 221192 | tf_op jit(solution)/shard_map/ppermute | solution.py:366
  39.1 1.3 %broadcast_add_fusion.1.twist_ref = f32[512,512]{1,0:T(8,128)S(1)} fusion(f32[512,512]{1,0:T(8,128)} %constant.21.clone, f32[]{:T(128)S(6)} %convert_element_type.8), kind=kLoop, calls=%fused_computation.1 | loop fusion | flops 262144 | bytes 2097156 | tf_op jit(solution)/shard_map/add | solution.py:402
  40.4 1.5 %broadcast_add_fusion.wave_hbm = bf16[2048,512]{1,0:T(8,128)(2,1)} fusion(bf16[2048,512]{1,0:T(8,128)(2,1)S(1)} %copy-done.2, bf16[]{:T(256)S(6)} %convert_element_type.7), kind=kLoop, calls=%fused_computation | loop fusion | flops 1048576 | bytes 4194306 | tf_op jit(solution)/shard_map/add | solution.py:402
  41.9 3.4 %keep.1.kept_hbm = bf16[2,192,1024]{2,1,0:T(8,128)(2,1)} custom-call(bf16[64,15,8,128]{3,2,1,0:T(8,128)(2,1)} %get-tuple-element.33.message_hbm, bf16[192,1152]{1,0:T(8,128)(2,1)} %get-tuple-element.37.gate_ref, f32[192,9]{1,0:T(8,128)} %copy-done), custom_call_target="tpu_custom_call" | custom-call | flops 1769472 | bytes 2097152 | tf_op jit(solution)/shard_map/keep/pallas_call | solution.py:186
  45.3 2.9 %collective-permute-done.7.refs_5_ = bf16[192,192]{1,0:T(8,128)(2,1)S(1)} collective-permute-done((bf16[192,192]{1,0:T(8,128)(2,1)S(1)}, bf16[192,192]{1,0:T(8,128)(2,1)S(1)}, u32[]{:S(2)}, u32[]{:S(2)}) %collective-permute-start.7) | collective-permute-done | bytes 73760 | tf_op jit(solution)/shard_map/ppermute | solution.py:366
  48.2 34.6 %all-to-all-done.m_ref = bf16[64,15,8,128]{3,2,1,0:T(8,128)(2,1)S(1)} async-done(((bf16[64,15,8,128]{3,2,1,0:T(8,128)(2,1)}), bf16[64,15,8,128]{3,2,1,0:T(8,128)(2,1)S(1)}, u32[]{:S(2)}, u32[]{:S(2)}) %all-to-all-start) | async-done | bytes 1966112 | tf_op jit(solution)/shard_map/all_to_all | solution.py:394
  82.9 5.5 %convolve.1 = bf16[64,3,8,128]{3,2,1,0:T(8,128)(2,1)} custom-call(bf16[64,15,8,128]{3,2,1,0:T(8,128)(2,1)S(1)} %all-to-all-done.m_ref, bf16[2048,512]{1,0:T(8,128)(2,1)} %broadcast_add_fusion.wave_hbm, f32[512,512]{1,0:T(8,128)S(1)} %broadcast_add_fusion.1.twist_ref), custom_call_target="tpu_custom_call" | custom-call | flops 3221225472 | bytes 6291456 | tf_op jit(solution)/shard_map/convolve/pallas_call | solution.py:286
  88.3 8.8 %all-to-all-start.1 = ((bf16[64,3,8,128]{3,2,1,0:T(8,128)(2,1)}), bf16[64,3,8,128]{3,2,1,0:T(8,128)(2,1)S(1)}, u32[]{:S(2)}, u32[]{:S(2)}) async-start(bf16[64,3,8,128]{3,2,1,0:T(8,128)(2,1)} %convolve.1), calls=%async_computation.1 | async-start | bytes 786432 | tf_op jit(solution)/shard_map/all_to_all | solution.py:407
  97.3 14.4 %all-to-all-done.1 = bf16[64,3,8,128]{3,2,1,0:T(8,128)(2,1)S(1)} async-done(((bf16[64,3,8,128]{3,2,1,0:T(8,128)(2,1)}), bf16[64,3,8,128]{3,2,1,0:T(8,128)(2,1)S(1)}, u32[]{:S(2)}, u32[]{:S(2)}) %all-to-all-start.1) | async-done | bytes 393248 | tf_op jit(solution)/shard_map/all_to_all | solution.py:407
  111.7 1.4 %gated.1 = (bf16[192,512]{1,0:T(8,128)(2,1)S(1)}, bf16[192,512]{1,0:T(8,128)(2,1)S(1)}) custom-call(bf16[1536,128]{1,0:T(8,128)(2,1)S(1)} %bitcast.15, bf16[2,192,1024]{2,1,0:T(8,128)(2,1)} %keep.1.kept_hbm, f32[192,1]{1,0:T(8,128)S(1)} %copy.22.bias_ref), custom_call_target="tpu_custom_call" | custom-call | flops 786432 | bytes 1572864 | tf_op jit(solution)/shard_map/gated/pallas_call | solution.py:325
  113.2 1.5 %collective-permute-start.10 = (bf16[192,512]{1,0:T(8,128)(2,1)S(1)}, bf16[192,512]{1,0:T(8,128)(2,1)S(1)}, u32[]{:S(2)}, u32[]{:S(2)}) collective-permute-start(bf16[192,512]{1,0:T(8,128)(2,1)S(1)} %get-tuple-element.43.refs_0_), channel_id=1, source_target_pairs={{0,2},{1,3},{2,0},{3,1},{4,6},{5,7},{6,4},{7,5},{8,10},{9,11},{10,... | collective-permute-start | bytes 589832 | tf_op jit(solution)/shard_map/ppermute | solution.py:366
  114.7 4.6 %collective-permute-start.14 = (bf16[192,512]{1,0:T(8,128)(2,1)S(1)}, bf16[192,512]{1,0:T(8,128)(2,1)S(1)}, u32[]{:S(2)}, u32[]{:S(2)}) collective-permute-start(bf16[192,512]{1,0:T(8,128)(2,1)S(1)} %get-tuple-element.48.refs_0_), channel_id=1, source_target_pairs={{0,1},{1,0},{2,3},{3,2},{4,5},{5,4},{6,7},{7,6},{8,9},{9,8},{10,11... | collective-permute-start | bytes 589832 | tf_op jit(solution)/shard_map/ppermute | solution.py:366
  119.3 3.6 %collective-permute-start.15 = (bf16[192,512]{1,0:T(8,128)(2,1)S(1)}, bf16[192,512]{1,0:T(8,128)(2,1)S(1)}, u32[]{:S(2)}, u32[]{:S(2)}) collective-permute-start(bf16[192,512]{1,0:T(8,128)(2,1)S(1)} %collective-permute-done.13.refs_1_), channel_id=1, source_target_pairs={{0,1},{1,0},{2,3},{3,2},{4,5},{5,4},{6,7},{7,6},{8,9},{9,8},{10,11... | collective-permute-start | bytes 589832 | tf_op jit(solution)/shard_map/ppermute | solution.py:366
  123.0 2.1 %collective-permute-start.12 = (bf16[192,512]{1,0:T(8,128)(2,1)S(1)}, bf16[192,512]{1,0:T(8,128)(2,1)S(1)}, u32[]{:S(2)}, u32[]{:S(2)}) collective-permute-start(bf16[192,512]{1,0:T(8,128)(2,1)S(1)} %collective-permute-done.10.refs_1_), channel_id=1, source_target_pairs={{0,1},{1,0},{2,3},{3,2},{4,5},{5,4},{6,7},{7,6},{8,9},{9,8},{10,11... | collective-permute-start | bytes 589832 | tf_op jit(solution)/shard_map/ppermute | solution.py:366
  125.1 1.0 mixed.2.refs_8_
  126.1 1.0 mixed.3
  (32 shorter events, 0.5 us)
Async XLA Ops:
  0.0 13.2 %collective-permute-start = (bf16[192,1024]{1,0:T(8,128)(2,1)}, bf16[192,1024]{1,0:T(8,128)(2,1)S(1)}, u32[]{:S(2)}, u32[]{:S(2)}) collective-permute-start(bf16[192,1024]{1,0:T(8,128)(2,1)} %refs_1_.1), channel_id=1, source_target_pairs={{0,2},{1,3},{2,0},{3,1},{4,6},{5,7},{6,4},{7,5},{8,10},{9,11},{10,... | collective-permute-start | bytes 1179656 | tf_op jit(solution)/shard_map/ppermute | solution.py:366
  2.9 6.9 %copy-start.1 = (bf16[192,1024]{1,0:T(8,128)(2,1)S(1)}, bf16[192,1024]{1,0:T(8,128)(2,1)}, u32[]{:S(2)}) copy-start(bf16[192,1024]{1,0:T(8,128)(2,1)} %refs_1_.1) | copy-start | bytes 1179652
  2.9 12.4 %copy-start.4 = (f32[3,3,192]{2,1,0:T(4,128)S(1)}, f32[3,3,192]{2,1,0:T(4,128)}, u32[]{:S(2)}) copy-start(f32[3,3,192]{2,1,0:T(4,128)} %param.10) | copy-start | bytes 20740
  2.9 6.6 %collective-permute-start.1 = (bf16[192,128]{1,0:T(8,128)(2,1)S(1)}, bf16[192,128]{1,0:T(8,128)(2,1)S(1)}, u32[]{:S(2)}, u32[]{:S(2)}) collective-permute-start(bf16[192,128]{1,0:T(8,128)(2,1)S(1)} %slice.3), channel_id=1, source_target_pairs={{0,4},{4,8},{8,12},{12,16},{16,20},{20,24},{24,28},{28,32},{32,36}... | collective-permute-start | bytes 147464 | tf_op jit(solution)/shard_map/ppermute | solution.py:378
  9.5 3.7 %collective-permute-start.2 = (bf16[192,128]{1,0:T(8,128)(2,1)S(1)}, bf16[192,128]{1,0:T(8,128)(2,1)S(1)}, u32[]{:S(2)}, u32[]{:S(2)}) collective-permute-start(bf16[192,128]{1,0:T(8,128)(2,1)S(1)} %collective-permute-done.1.refs_5_), channel_id=1, source_target_pairs={{0,2},{1,3},{2,0},{3,1},{4,6},{5,7},{6,4},{7,5},{8,10},{9,11},{10,... | collective-permute-start | bytes 147464 | tf_op jit(solution)/shard_map/ppermute | solution.py:366
  9.7 6.5 %collective-permute-start.3 = (bf16[192,1024]{1,0:T(8,128)(2,1)S(1)}, bf16[192,1024]{1,0:T(8,128)(2,1)S(1)}, u32[]{:S(2)}, u32[]{:S(2)}) collective-permute-start(bf16[192,1024]{1,0:T(8,128)(2,1)S(1)} %copy-done.1), channel_id=1, source_target_pairs={{0,1},{1,0},{2,3},{3,2},{4,5},{5,4},{6,7},{7,6},{8,9},{9,8},{10,11... | collective-permute-start | bytes 1179656 | tf_op jit(solution)/shard_map/ppermute | solution.py:366
  13.2 3.1 %collective-permute-start.4 = (bf16[192,1024]{1,0:T(8,128)(2,1)S(1)}, bf16[192,1024]{1,0:T(8,128)(2,1)S(1)}, u32[]{:S(2)}, u32[]{:S(2)}) collective-permute-start(bf16[192,1024]{1,0:T(8,128)(2,1)S(1)} %collective-permute-done.refs_2_), channel_id=1, source_target_pairs={{0,1},{1,0},{2,3},{3,2},{4,5},{5,4},{6,7},{7,6},{8,9},{9,8},{10,11... | collective-permute-start | bytes 1179656 | tf_op jit(solution)/shard_map/ppermute | solution.py:366
  14.8 1.4 %collective-permute-start.5 = (bf16[192,128]{1,0:T(8,128)(2,1)S(1)}, bf16[192,128]{1,0:T(8,128)(2,1)S(1)}, u32[]{:S(2)}, u32[]{:S(2)}) collective-permute-start(bf16[192,128]{1,0:T(8,128)(2,1)S(1)} %collective-permute-done.1.refs_5_), channel_id=1, source_target_pairs={{0,1},{1,0},{2,3},{3,2},{4,5},{5,4},{6,7},{7,6},{8,9},{9,8},{10,11... | collective-permute-start | bytes 147464 | tf_op jit(solution)/shard_map/ppermute | solution.py:366
  14.8 1.5 %collective-permute-start.6 = (bf16[192,128]{1,0:T(8,128)(2,1)S(1)}, bf16[192,128]{1,0:T(8,128)(2,1)S(1)}, u32[]{:S(2)}, u32[]{:S(2)}) collective-permute-start(bf16[192,128]{1,0:T(8,128)(2,1)S(1)} %collective-permute-done.2.refs_6_), channel_id=1, source_target_pairs={{0,1},{1,0},{2,3},{3,2},{4,5},{5,4},{6,7},{7,6},{8,9},{9,8},{10,11... | collective-permute-start | bytes 147464 | tf_op jit(solution)/shard_map/ppermute | solution.py:366
  15.4 6.1 %copy-start = (f32[192,9]{1,0:T(8,128)}, f32[192,9]{1,0:T(8,128)S(1)}, u32[]{:S(2)}) copy-start(f32[192,9]{1,0:T(8,128)S(1)} %copy.16.refs_10_.taps_ref) | copy-start | bytes 20740
  21.5 14.6 %copy-start.3 = (bf16[192,768]{1,0:T(8,128)(2,1)S(1)}, bf16[192,768]{1,0:T(8,128)(2,1)}, u32[]{:S(2)}) copy-start(bf16[192,768]{1,0:T(8,128)(2,1)} %param.13) | copy-start | bytes 884740
  21.5 61.3 %all-to-all-start = ((bf16[64,15,8,128]{3,2,1,0:T(8,128)(2,1)}), bf16[64,15,8,128]{3,2,1,0:T(8,128)(2,1)S(1)}, u32[]{:S(2)}, u32[]{:S(2)}) async-start(bf16[64,15,8,128]{3,2,1,0:T(8,128)(2,1)} %get-tuple-element.33.message_hbm), calls=%async_computation | async-start | bytes 3932160 | tf_op jit(solution)/shard_map/all_to_all | solution.py:394
  36.3 4.1 %copy-start.2 = (bf16[2048,512]{1,0:T(8,128)(2,1)S(1)}, bf16[2048,512]{1,0:T(8,128)(2,1)}, u32[]{:S(2)}) copy-start(bf16[2048,512]{1,0:T(8,128)(2,1)} %constant.20.clone) | copy-start | bytes 6291460
  37.1 8.2 %collective-permute-start.9 = (bf16[192,192]{1,0:T(8,128)(2,1)}, bf16[192,192]{1,0:T(8,128)(2,1)S(1)}, u32[]{:S(2)}, u32[]{:S(2)}) collective-permute-start(bf16[192,192]{1,0:T(8,128)(2,1)} %get-tuple-element.49), channel_id=1, source_target_pairs={{0,3},{1,2},{2,1},{3,0},{4,7},{5,6},{6,5},{7,4},{8,11},{9,10},{10,... | collective-permute-start | bytes 221192 | tf_op jit(solution)/shard_map/ppermute | solution.py:366
  37.6 7.7 %collective-permute-start.8 = (bf16[192,192]{1,0:T(8,128)(2,1)}, bf16[192,192]{1,0:T(8,128)(2,1)S(1)}, u32[]{:S(2)}, u32[]{:S(2)}) collective-permute-start(bf16[192,192]{1,0:T(8,128)(2,1)} %get-tuple-element.50), channel_id=1, source_target_pairs={{0,1},{1,0},{2,3},{3,2},{4,5},{5,4},{6,7},{7,6},{8,9},{9,8},{10,11... | collective-permute-start | bytes 221192 | tf_op jit(solution)/shard_map/ppermute | solution.py:366
  37.7 10.5 %collective-permute-start.7 = (bf16[192,192]{1,0:T(8,128)(2,1)S(1)}, bf16[192,192]{1,0:T(8,128)(2,1)S(1)}, u32[]{:S(2)}, u32[]{:S(2)}) collective-permute-start(bf16[192,192]{1,0:T(8,128)(2,1)S(1)} %get-tuple-element.51), channel_id=1, source_target_pairs={{0,2},{1,3},{2,0},{3,1},{4,6},{5,7},{6,4},{7,5},{8,10},{9,11},{10,... | collective-permute-start | bytes 221192 | tf_op jit(solution)/shard_map/ppermute | solution.py:366
  40.4 1.5 %copy-start.5 = (f32[192]{0:T(256)S(1)}, f32[192]{0:T(256)}, u32[]{:S(2)}) copy-start(f32[192]{0:T(256)} %param.11) | copy-start | bytes 2308
  88.3 23.4 %all-to-all-start.1 = ((bf16[64,3,8,128]{3,2,1,0:T(8,128)(2,1)}), bf16[64,3,8,128]{3,2,1,0:T(8,128)(2,1)S(1)}, u32[]{:S(2)}, u32[]{:S(2)}) async-start(bf16[64,3,8,128]{3,2,1,0:T(8,128)(2,1)} %convolve.1), calls=%async_computation.1 | async-start | bytes 786432 | tf_op jit(solution)/shard_map/all_to_all | solution.py:407
  113.1 6.2 %collective-permute-start.13 = (bf16[192,512]{1,0:T(8,128)(2,1)S(1)}, bf16[192,512]{1,0:T(8,128)(2,1)S(1)}, u32[]{:S(2)}, u32[]{:S(2)}) collective-permute-start(bf16[192,512]{1,0:T(8,128)(2,1)S(1)} %get-tuple-element.48.refs_0_), channel_id=1, source_target_pairs={{0,2},{1,3},{2,0},{3,1},{4,6},{5,7},{6,4},{7,5},{8,10},{9,11},{10,... | collective-permute-start | bytes 589832 | tf_op jit(solution)/shard_map/ppermute | solution.py:366
  113.2 9.7 %collective-permute-start.10 = (bf16[192,512]{1,0:T(8,128)(2,1)S(1)}, bf16[192,512]{1,0:T(8,128)(2,1)S(1)}, u32[]{:S(2)}, u32[]{:S(2)}) collective-permute-start(bf16[192,512]{1,0:T(8,128)(2,1)S(1)} %get-tuple-element.43.refs_0_), channel_id=1, source_target_pairs={{0,2},{1,3},{2,0},{3,1},{4,6},{5,7},{6,4},{7,5},{8,10},{9,11},{10,... | collective-permute-start | bytes 589832 | tf_op jit(solution)/shard_map/ppermute | solution.py:366
  114.7 10.4 %collective-permute-start.14 = (bf16[192,512]{1,0:T(8,128)(2,1)S(1)}, bf16[192,512]{1,0:T(8,128)(2,1)S(1)}, u32[]{:S(2)}, u32[]{:S(2)}) collective-permute-start(bf16[192,512]{1,0:T(8,128)(2,1)S(1)} %get-tuple-element.48.refs_0_), channel_id=1, source_target_pairs={{0,1},{1,0},{2,3},{3,2},{4,5},{5,4},{6,7},{7,6},{8,9},{9,8},{10,11... | collective-permute-start | bytes 589832 | tf_op jit(solution)/shard_map/ppermute | solution.py:366
  119.3 5.8 %collective-permute-start.15 = (bf16[192,512]{1,0:T(8,128)(2,1)S(1)}, bf16[192,512]{1,0:T(8,128)(2,1)S(1)}, u32[]{:S(2)}, u32[]{:S(2)}) collective-permute-start(bf16[192,512]{1,0:T(8,128)(2,1)S(1)} %collective-permute-done.13.refs_1_), channel_id=1, source_target_pairs={{0,1},{1,0},{2,3},{3,2},{4,5},{5,4},{6,7},{7,6},{8,9},{9,8},{10,11... | collective-permute-start | bytes 589832 | tf_op jit(solution)/shard_map/ppermute | solution.py:366
  122.9 3.1 %collective-permute-start.11 = (bf16[192,512]{1,0:T(8,128)(2,1)S(1)}, bf16[192,512]{1,0:T(8,128)(2,1)S(1)}, u32[]{:S(2)}, u32[]{:S(2)}) collective-permute-start(bf16[192,512]{1,0:T(8,128)(2,1)S(1)} %get-tuple-element.43.refs_0_), channel_id=1, source_target_pairs={{0,1},{1,0},{2,3},{3,2},{4,5},{5,4},{6,7},{7,6},{8,9},{9,8},{10,11... | collective-permute-start | bytes 589832 | tf_op jit(solution)/shard_map/ppermute | solution.py:366
  123.0 3.2 %collective-permute-start.12 = (bf16[192,512]{1,0:T(8,128)(2,1)S(1)}, bf16[192,512]{1,0:T(8,128)(2,1)S(1)}, u32[]{:S(2)}, u32[]{:S(2)}) collective-permute-start(bf16[192,512]{1,0:T(8,128)(2,1)S(1)} %collective-permute-done.10.refs_1_), channel_id=1, source_target_pairs={{0,1},{1,0},{2,3},{3,2},{4,5},{5,4},{6,7},{7,6},{8,9},{9,8},{10,11... | collective-permute-start | bytes 589832 | tf_op jit(solution)/shard_map/ppermute | solution.py:366

commit v9 on v8

--- a/solution.py
+++ b/solution.py
@@ -12,9 +12,10 @@
 FREQS = 512
 LANES = 128
 PROJECT_VMEM = 53100 << 10
-GATED_VMEM = 54000 << 10
+GATED_VMEM = 8 << 20
+KEEP_VMEM = 52500 << 10
 MIXED_VMEM = 12 << 20
-CONVOLVE_VMEM = 50000 << 10
+CONVOLVE_VMEM = 52000 << 10
 MASKS = (0, 2, 1, 3)
 BF16 = jnp.bfloat16
 F32 = jnp.float32
@@ -159,7 +160,8 @@
     )(grp, *mains, *halos, weight, taps, packed)
 
 
-def keep_body(message_hbm, gate_ref, taps_ref, kept_ref, part_ref, spread_ref, sem):
+def keep_body(message_hbm, gate_ref, taps_ref, *refs):
+    weights, kept_ref, stacked_ref, part_ref, spread_ref, sem = refs[:4], *refs[4:]
     channels = gate_ref.shape[0]
     per_dest = part_ref.shape[1]
     load = pltpu.make_async_copy(message_hbm.at[:, pl.ds(4 * per_dest, per_dest)], part_ref, sem)
@@ -172,6 +174,9 @@
         return carry
 
     lax.fori_loop(0, channels // rows, chunk, 0)
+    feats = weights[0].shape[0]
+    for i, weight in enumerate(weights):
+        stacked_ref[i * feats:(i + 1) * feats] = weight[...]
     load.wait()
     spread_ref[...] = part_ref[...].astype(F32).reshape(spread_ref.shape)
     for part in range(8):
@@ -179,27 +184,31 @@
         kept_ref[1, :, part * LANES:(part + 1) * LANES] = column.astype(BF16)
 
 
-def keep(message, gate_stream, taps):
+def keep(message, gate_stream, taps, weights):
     channels, width = gate_stream.shape
     shards, pieces = message.shape[:2]
     vmem = pl.BlockSpec(memory_space=pltpu.VMEM)
     return pl.pallas_call(
         keep_body,
-        in_specs=[pl.BlockSpec(memory_space=pltpu.HBM), vmem, vmem],
-        out_specs=vmem,
-        out_shape=jax.ShapeDtypeStruct((2, channels, width - LANES), BF16),
+        in_specs=[pl.BlockSpec(memory_space=pltpu.HBM)] + [vmem] * 6,
+        out_specs=[vmem] * 2,
+        out_shape=[
+            jax.ShapeDtypeStruct((2, channels, width - LANES), BF16),
+            jax.ShapeDtypeStruct((4 * weights[0].shape[0], channels), BF16),
+        ],
         scratch_shapes=[
             pltpu.VMEM((shards, pieces // 5, 8, LANES), BF16),
             pltpu.VMEM((channels * 8, LANES), F32),
             pltpu.SemaphoreType.DMA,
         ],
+        compiler_params=pltpu.CompilerParams(vmem_limit_bytes=KEEP_VMEM),
         cost_estimate=pl.CostEstimate(flops=8 * channels * width, bytes_accessed=2 << 20, transcendentals=0),
         name="keep",
-    )(message, gate_stream, taps)
-
-
-def convolve_body(m_ref, wave_hbm, twist_ref, out_ref,
-                  spread_ref, grid_ref, mid_ref, tall_ref, done_ref, wave_ref, sems, wave_sems):
+    )(message, gate_stream, taps, *weights)
+
+
+def convolve_body(m_hbm, wave_hbm, twist_ref, out_ref,
+                  spread_ref, grid_ref, mid_ref, tall_ref, done_ref, wave_ref, m_ref, sems, wave_sems, m_sems):
     channels, shards, pieces, lanes = done_ref.shape
     rows_dev = pieces // 2
     freqs = twist_ref.shape[0]
@@ -207,7 +216,13 @@
     loads = [
         pltpu.make_async_copy(wave_hbm.at[pl.ds(i * freqs, freqs)], wave_ref.at[i], wave_sems.at[i]) for i in range(4)
     ]
-    for load in loads:
+    signals = pl.ds(4 * channels, channels)
+    arrival = pltpu.make_async_copy(m_hbm.at[:, signals], m_ref.at[:, signals], m_sems.at[channels])
+    responses = [
+        pltpu.make_async_copy(m_hbm.at[:, pl.ds(4 * c, 4)], m_ref.at[:, pl.ds(4 * c, 4)], m_sems.at[c])
+        for c in range(channels)
+    ]
+    for load in (arrival, *loads[:2], *responses, *loads[2:]):
         load.start()
     cosine, sine = twist_ref[:, :COLS], twist_ref[:, COLS:]
 
@@ -231,6 +246,7 @@
         return jnp.dot(mid_ref[c], forward_ref[...], preferred_element_type=F32)
 
     def respond(c, freq):
+        responses[c].wait()
         for h in range(2):
             low, high = h * lanes, COLS + h * lanes
             real, imag = freq[:, low:low + lanes], freq[:, high:high + lanes]
@@ -260,6 +276,7 @@
         done_ref[c] = spread_ref[c].reshape(shards, pieces, lanes).astype(BF16)
         pltpu.make_async_copy(done_ref.at[c], out_ref.at[:, c], sems.at[c]).start()
 
+    arrival.wait()
     for c in range(channels):
         arrange(c)
     stages = (
@@ -285,7 +302,7 @@
     vmem = pl.BlockSpec(memory_space=pltpu.VMEM)
     return pl.pallas_call(
         convolve_body,
-        in_specs=[vmem, pl.BlockSpec(memory_space=pltpu.HBM), vmem],
+        in_specs=[vmem] * 3,
         out_specs=pl.BlockSpec(memory_space=pltpu.HBM),
         out_shape=jax.ShapeDtypeStruct((shards, channels, pieces, lanes), BF16),
         scratch_shapes=[
@@ -295,8 +312,10 @@
             pltpu.VMEM((channels, 2 * freqs, COLS), BF16),
             pltpu.VMEM((channels, shards, pieces, lanes), BF16),
             pltpu.VMEM((4, freqs, 2 * COLS), BF16),
+            pltpu.VMEM(received.shape, BF16),
             pltpu.SemaphoreType.DMA((channels,)),
             pltpu.SemaphoreType.DMA((4,)),
+            pltpu.SemaphoreType.DMA((channels + 1,)),
         ],
         compiler_params=pltpu.CompilerParams(vmem_limit_bytes=CONVOLVE_VMEM),
         cost_estimate=pl.CostEstimate(flops=3 << 30, bytes_accessed=6 << 20, transcendentals=0),
@@ -304,13 +323,10 @@
     )(received, *tables)
 
 
-def gated_body(y_ref, kept_hbm, bias_ref, early_ref, late_ref, spread_ref, kept_ref, sem):
+def gated_body(y_ref, kept_ref, bias_ref, early_ref, late_ref, spread_ref):
     channels = early_ref.shape[0]
-    load = pltpu.make_async_copy(kept_hbm, kept_ref, sem)
-    load.start()
     spread_ref[...] = y_ref[...].astype(F32)
     bias = bias_ref[...]
-    load.wait()
     for part in range(8):
         cols = slice(part * LANES, (part + 1) * LANES)
         y = spread_ref[pl.ds(part, channels, stride=8), :]
@@ -324,13 +340,11 @@
     vmem = pl.BlockSpec(memory_space=pltpu.VMEM)
     return pl.pallas_call(
         gated_body,
-        in_specs=[vmem, pl.BlockSpec(memory_space=pltpu.HBM), vmem],
+        in_specs=[vmem] * 3,
         out_specs=[vmem] * 2,
         out_shape=[jax.ShapeDtypeStruct((kept.shape[1], kept.shape[2] // 2), BF16)] * 2,
         scratch_shapes=[
             pltpu.VMEM(y.shape, F32),
-            pltpu.VMEM(kept.shape, BF16),
-            pltpu.SemaphoreType.DMA,
         ],
         compiler_params=pltpu.CompilerParams(vmem_limit_bytes=GATED_VMEM),
         cost_estimate=pl.CostEstimate(flops=4 * y.size, bytes_accessed=8 * y.size, transcendentals=0),
@@ -339,27 +353,28 @@
 
 
 def mixed_body(*refs):
-    values, weights, out_ref = refs[:4], refs[4:8], refs[-1]
-    total = jnp.dot(weights[0][...], values[0][...], preferred_element_type=F32)
-    for w, v in zip(weights[1:], values[1:]):
-        total = total + jnp.dot(w[...], v[...], preferred_element_type=F32)
+    values, weights_ref, out_ref = refs[:4], refs[4], refs[-1]
+    rows = values[0].shape[0]
+    total = jnp.dot(weights_ref[:rows], values[0][...], preferred_element_type=F32)
+    for i in range(1, 4):
+        total = total + jnp.dot(weights_ref[i * rows:(i + 1) * rows], values[i][...], preferred_element_type=F32)
     out_ref[...] = total.astype(BF16)
 
 
 def mixed(values, weights, half, *earlier):
     channels, tok = values[0].shape
-    whole = [pl.BlockSpec(memory_space=pltpu.VMEM)] * 8
+    feats = weights.shape[0] // 4
     return pl.pallas_call(
         mixed_body,
         grid=(1,),
-        in_specs=whole + [pl.BlockSpec(memory_space=pl.ANY)] * len(earlier),
-        out_specs=pl.BlockSpec((weights[0].shape[0], tok), lambda i: (0, half)),
-        out_shape=jax.ShapeDtypeStruct((weights[0].shape[0], 2 * tok), BF16),
-        input_output_aliases={8: 0} if earlier else {},
+        in_specs=[pl.BlockSpec(memory_space=pltpu.VMEM)] * 5 + [pl.BlockSpec(memory_space=pl.ANY)] * len(earlier),
+        out_specs=pl.BlockSpec((feats, tok), lambda i: (0, half)),
+        out_shape=jax.ShapeDtypeStruct((feats, 2 * tok), BF16),
+        input_output_aliases={5: 0} if earlier else {},
         compiler_params=pltpu.CompilerParams(vmem_limit_bytes=MIXED_VMEM),
-        cost_estimate=pl.CostEstimate(flops=8 * channels * channels * tok, bytes_accessed=2 << 20, transcendentals=0),
+        cost_estimate=pl.CostEstimate(flops=8 * channels * feats * tok, bytes_accessed=2 << 20, transcendentals=0),
         name="mixed",
-    )(*values, *weights, *earlier)
+    )(*values, weights, *earlier)
 
 
 def swapped(block, mask):
@@ -390,7 +405,6 @@
     message, out_weight, filter_bias, later, gate_stream = lax.optimization_barrier(
         (message, out_weight, filter_bias, grp, gate_stream)
     )
-    kept = keep(message, gate_stream, taps)
     received = lax.all_to_all(message, "seq", 0, 0, tiled=True)
 
     turned = out_weight.T
@@ -401,9 +415,13 @@
     zero = jnp.minimum(later, 0)
     tables = [t + zero.astype(t.dtype) for t in transform_tables(shard_count, tok // COLS)]
     bias = filter_bias[:, None] + zero.astype(F32)
-    received, weights, tables, bias, kept = lax.optimization_barrier((received, weights, tables, bias, kept))
+    received, weights, tables, bias = lax.optimization_barrier((received, weights, tables, bias))
 
     result = convolve(received, tables)
+    result, message, gate_stream, weights, taps = lax.optimization_barrier(
+        (result, message, gate_stream, weights, taps)
+    )
+    kept, weights = keep(message, gate_stream, taps, weights)
     back = lax.all_to_all(result, "seq", 0, 0, tiled=True).reshape(channels * 8, LANES)
     early, late = gated(back, kept, bias)
     far_early, far_late = swapped(early, 2), swapped(late, 2)

time: 128 us -> 129 us (level)
  waiting for transfers between devices: 54.8 us -> 56.7 us
    ppermute x15, waiting for transfers between devices: 5.78 us -> 8.74 us  [swapped(): return lax.ppermute(block, 'grp', [(i, i ^ mask) for i in range(4)])]
    all_to_all x1, waiting for transfers between devices: 14.4 us -> 12.8 us  [shards(): lax.all_to_all(result, 'seq', 0, 0, tiled=True).reshape(channels * 8, LANES)]
  transfers between devices with their start and end apart: 18 -> 18, of which waited for: 6 -> 7; matrix products, arithmetic and copies ran while one was open for 4% -> 4% of each run, Pallas kernels for 6% -> 4%
where the time goes in v9:
time: 129 us
  waiting for transfers between devices  56.7 us (44%)
  starting transfers between devices  47.1 us (37%)
  Pallas kernels  20.3 us (16%)
  other arithmetic  3.16 us (2%)
  local copies, waits for them, and re-layouts  1.43 us (1%)
    all_to_all x1, waiting for transfers between devices, shards(): received = lax.all_to_all(message, 'seq', 0, 0, tiled=True)  35.2 us
    ppermute x15, starting transfers between devices, swapped(): return lax.ppermute(block, 'grp', [(i, i ^ mask) for i in range(4)])  19.9 us
    all_to_all x1, starting transfers between devices, shards(): received = lax.all_to_all(message, 'seq', 0, 0, tiled=True)  14.8 us
    all_to_all x1, waiting for transfers between devices, shards(): lax.all_to_all(result, 'seq', 0, 0, tiled=True).reshape(channels * 8, LANES)  12.8 us
    ppermute x15, waiting for transfers between devices, swapped(): return lax.ppermute(block, 'grp', [(i, i ^ mask) for i in range(4)])  8.74 us
    all_to_all x1, starting transfers between devices, shards(): lax.all_to_all(result, 'seq', 0, 0, tiled=True).reshape(channels * 8, LANES)  8.67 us
    pallas_call x1, Pallas kernels, convolve(): pl.pallas_call(convolve_body, in_specs=[vmem] * 3, out_specs=pl.BlockSpec...  8.31 us
    pallas_call x1, Pallas kernels, project(): pl.pallas_call(project_body, in_specs=[pl.BlockSpec(memory_space=pltpu.SM...  5.19 us
  transfers between devices with their start and end apart: 18, of which 7 were waited for; matrix products, arithmetic and copies ran while one was open for 4% of the time, Pallas kernels for 4%

profile of v9, /device:TPU:1, one launch (start us, length us, event | category | flops | bytes accessed | tf_op | source)
XLA Modules:
  0.0 128.8 jit_solution(6621429709507088980)
XLA Ops:
  0.0 2.0 %collective-permute-start = (bf16[192,1024]{1,0:T(8,128)(2,1)}, bf16[192,1024]{1,0:T(8,128)(2,1)S(1)}, u32[]{:S(2)}, u32[]{:S(2)}) collective-permute-start(bf16[192,1024]{1,0:T(8,128)(2,1)} %refs_1_.1), channel_id=1, source_target_pairs={{0,2},{1,3},{2,0},{3,1},{4,6},{5,7},{6,4},{7,5},{8,10},{9,11},{10,... | collective-permute-start | bytes 1179656 | tf_op jit(solution)/shard_map/ppermute | solution.py:381
  2.0 0.8 slice.3
  2.9 3.7 %collective-permute-start.1 = (bf16[192,128]{1,0:T(8,128)(2,1)S(1)}, bf16[192,128]{1,0:T(8,128)(2,1)S(1)}, u32[]{:S(2)}, u32[]{:S(2)}) collective-permute-start(bf16[192,128]{1,0:T(8,128)(2,1)S(1)} %slice.3), channel_id=1, source_target_pairs={{0,4},{4,8},{8,12},{12,16},{16,20},{20,24},{24,28},{28,32},{32,36}... | collective-permute-start | bytes 147464 | tf_op jit(solution)/shard_map/ppermute | solution.py:393
  6.6 2.9 %pack_spectra.1.refs_11_ = bf16[64,15,8,128]{3,2,1,0:T(8,128)(2,1)} custom-call(f32[2,192,8,256]{3,2,1,0:T(8,128)} %spec_ref.1), custom_call_target="tpu_custom_call" | custom-call | bytes 4718592 | tf_op jit(solution)/shard_map/pack_spectra/pallas_call | solution.py:61
  9.5 0.3 collective-permute-start.2
  9.7 1.5 %collective-permute-start.3 = (bf16[192,1024]{1,0:T(8,128)(2,1)S(1)}, bf16[192,1024]{1,0:T(8,128)(2,1)S(1)}, u32[]{:S(2)}, u32[]{:S(2)}) collective-permute-start(bf16[192,1024]{1,0:T(8,128)(2,1)S(1)} %copy-done), channel_id=1, source_target_pairs={{0,1},{1,0},{2,3},{3,2},{4,5},{5,4},{6,7},{7,6},{8,9},{9,8},{10,11... | collective-permute-start | bytes 1179656 | tf_op jit(solution)/shard_map/ppermute | solution.py:381
  11.3 1.9 %collective-permute-done.2.refs_6_ = bf16[192,128]{1,0:T(8,128)(2,1)S(1)} collective-permute-done((bf16[192,128]{1,0:T(8,128)(2,1)S(1)}, bf16[192,128]{1,0:T(8,128)(2,1)S(1)}, u32[]{:S(2)}, u32[]{:S(2)}) %collective-permute-start.2) | collective-permute-done | bytes 49184 | tf_op jit(solution)/shard_map/ppermute | solution.py:381
  13.2 1.6 %collective-permute-start.4 = (bf16[192,1024]{1,0:T(8,128)(2,1)S(1)}, bf16[192,1024]{1,0:T(8,128)(2,1)S(1)}, u32[]{:S(2)}, u32[]{:S(2)}) collective-permute-start(bf16[192,1024]{1,0:T(8,128)(2,1)S(1)} %collective-permute-done.refs_2_), channel_id=1, source_target_pairs={{0,1},{1,0},{2,3},{3,2},{4,5},{5,4},{6,7},{7,6},{8,9},{9,8},{10,11... | collective-permute-start | bytes 1179656 | tf_op jit(solution)/shard_map/ppermute | solution.py:381
  14.8 0.5 collective-permute-start.6
  15.3 0.1 copy.16.refs_10_
  15.5 0.8 collective-permute-done.5.refs_7_
  16.3 5.2 %project.1 = (bf16[64,15,8,128]{3,2,1,0:T(8,128)(2,1)}, bf16[192,1152]{1,0:T(8,128)(2,1)}) custom-call(s32[1]{0:T(128)} %bitcast.refs_0_, bf16[192,1024]{1,0:T(8,128)(2,1)S(1)} %copy-done, bf16[192,1024]{1,0:T(8,128)(2,1)S(1)} %collective-permute-done.refs_2_, ...), custom_call_target="tpu_custom_call", output_to_operand_aliasing={{0}: (11, {})} | custom-call | flops 1019215872 | bytes 6291456 | tf_op jit(solution)/shard_map/project/pallas_call | solution.py:136
  21.5 14.8 %all-to-all-start = ((bf16[64,15,8,128]{3,2,1,0:T(8,128)(2,1)}), bf16[64,15,8,128]{3,2,1,0:T(8,128)(2,1)}, u32[]{:S(2)}, u32[]{:S(2)}) async-start(bf16[64,15,8,128]{3,2,1,0:T(8,128)(2,1)} %get-tuple-element.55.message_hbm), calls=%async_computation | async-start | bytes 3932160 | tf_op jit(solution)/shard_map/all_to_all | solution.py:408
  36.4 0.2 copy.17
  36.6 0.6 collective-permute-start.9
  37.2 0.3 collective-permute-start.8
  37.4 1.3 collective-permute-start.7
  38.8 3.1 %broadcast_add_fusion.wave_hbm = bf16[2048,512]{1,0:T(8,128)(2,1)} fusion(bf16[2048,512]{1,0:T(8,128)(2,1)} %constant.20.clone, bf16[]{:T(256)S(6)} %convert_element_type.7), kind=kLoop, calls=%fused_computation | loop fusion | flops 1048576 | bytes 4194306 | tf_op jit(solution)/shard_map/add | solution.py:416
  41.9 3.4 %collective-permute-done.9.refs_3_ = bf16[192,192]{1,0:T(8,128)(2,1)S(1)} collective-permute-done((bf16[192,192]{1,0:T(8,128)(2,1)S(1)}, bf16[192,192]{1,0:T(8,128)(2,1)S(1)}, u32[]{:S(2)}, u32[]{:S(2)}) %collective-permute-start.9) | collective-permute-done | bytes 73760 | tf_op jit(solution)/shard_map/ppermute | solution.py:381
  45.3 2.5 %collective-permute-done.7.refs_1_ = bf16[192,192]{1,0:T(8,128)(2,1)S(1)} collective-permute-done((bf16[192,192]{1,0:T(8,128)(2,1)S(1)}, bf16[192,192]{1,0:T(8,128)(2,1)S(1)}, u32[]{:S(2)}, u32[]{:S(2)}) %collective-permute-start.7) | collective-permute-done | bytes 73760 | tf_op jit(solution)/shard_map/ppermute | solution.py:381
  47.8 35.2 %all-to-all-done.m_hbm = bf16[64,15,8,128]{3,2,1,0:T(8,128)(2,1)} async-done(((bf16[64,15,8,128]{3,2,1,0:T(8,128)(2,1)}), bf16[64,15,8,128]{3,2,1,0:T(8,128)(2,1)}, u32[]{:S(2)}, u32[]{:S(2)}) %all-to-all-start) | async-done | bytes 1966112 | tf_op jit(solution)/shard_map/all_to_all | solution.py:408
  83.0 8.3 %convolve.1 = bf16[64,3,8,128]{3,2,1,0:T(8,128)(2,1)} custom-call(bf16[64,15,8,128]{3,2,1,0:T(8,128)(2,1)} %all-to-all-done.m_hbm, bf16[2048,512]{1,0:T(8,128)(2,1)} %broadcast_add_fusion.wave_hbm, f32[512,512]{1,0:T(8,128)S(1)} %broadcast_add_fusion.1.twist_ref), custom_call_target="tpu_custom_call" | custom-call | flops 3221225472 | bytes 6291456 | tf_op jit(solution)/shard_map/convolve/pallas_call | solution.py:303
  91.3 8.7 %all-to-all-start.1 = ((bf16[64,3,8,128]{3,2,1,0:T(8,128)(2,1)}), bf16[64,3,8,128]{3,2,1,0:T(8,128)(2,1)S(1)}, u32[]{:S(2)}, u32[]{:S(2)}) async-start(bf16[64,3,8,128]{3,2,1,0:T(8,128)(2,1)} %convolve.1), calls=%async_computation.1 | async-start | bytes 786432 | tf_op jit(solution)/shard_map/all_to_all | solution.py:425
  100.2 1.5 %keep.1 = (bf16[2,192,1024]{2,1,0:T(8,128)(2,1)S(1)}, bf16[768,192]{1,0:T(8,128)(2,1)S(1)}) custom-call(bf16[64,15,8,128]{3,2,1,0:T(8,128)(2,1)} %get-tuple-element.55.message_hbm, bf16[192,1152]{1,0:T(8,128)(2,1)S(1)} %copy-done.1, f32[192,9]{1,0:T(8,128)S(1)} %copy.21.taps_ref, bf16[192,192]{1,0:T(8,128)(2,1)S(1)} %get-tuple-element.58.refs_0_, ...), custom_call_target="tpu_custom_call" | custom-call | flops 1769472 | bytes 2097152 | tf_op jit(solution)/shard_map/keep/pallas_call | solution.py:191
  101.7 12.8 %all-to-all-done.1 = bf16[64,3,8,128]{3,2,1,0:T(8,128)(2,1)S(1)} async-done(((bf16[64,3,8,128]{3,2,1,0:T(8,128)(2,1)}), bf16[64,3,8,128]{3,2,1,0:T(8,128)(2,1)S(1)}, u32[]{:S(2)}, u32[]{:S(2)}) %all-to-all-start.1) | async-done | bytes 393248 | tf_op jit(solution)/shard_map/all_to_all | solution.py:425
  114.5 0.3 gated.1
  114.9 1.5 %collective-permute-start.10 = (bf16[192,512]{1,0:T(8,128)(2,1)S(1)}, bf16[192,512]{1,0:T(8,128)(2,1)S(1)}, u32[]{:S(2)}, u32[]{:S(2)}) collective-permute-start(bf16[192,512]{1,0:T(8,128)(2,1)S(1)} %get-tuple-element.64.refs_0_), channel_id=1, source_target_pairs={{0,2},{1,3},{2,0},{3,1},{4,6},{5,7},{6,4},{7,5},{8,10},{9,11},{10,... | collective-permute-start | bytes 589832 | tf_op jit(solution)/shard_map/ppermute | solution.py:381
  116.4 4.6 %collective-permute-start.14 = (bf16[192,512]{1,0:T(8,128)(2,1)S(1)}, bf16[192,512]{1,0:T(8,128)(2,1)S(1)}, u32[]{:S(2)}, u32[]{:S(2)}) collective-permute-start(bf16[192,512]{1,0:T(8,128)(2,1)S(1)} %get-tuple-element.66.refs_0_), channel_id=1, source_target_pairs={{0,1},{1,0},{2,3},{3,2},{4,5},{5,4},{6,7},{7,6},{8,9},{9,8},{10,11... | collective-permute-start | bytes 589832 | tf_op jit(solution)/shard_map/ppermute | solution.py:381
  121.0 3.6 %collective-permute-start.15 = (bf16[192,512]{1,0:T(8,128)(2,1)S(1)}, bf16[192,512]{1,0:T(8,128)(2,1)S(1)}, u32[]{:S(2)}, u32[]{:S(2)}) collective-permute-start(bf16[192,512]{1,0:T(8,128)(2,1)S(1)} %collective-permute-done.13.refs_1_), channel_id=1, source_target_pairs={{0,1},{1,0},{2,3},{3,2},{4,5},{5,4},{6,7},{7,6},{8,9},{9,8},{10,11... | collective-permute-start | bytes 589832 | tf_op jit(solution)/shard_map/ppermute | solution.py:381
  124.6 2.1 %collective-permute-start.12 = (bf16[192,512]{1,0:T(8,128)(2,1)S(1)}, bf16[192,512]{1,0:T(8,128)(2,1)S(1)}, u32[]{:S(2)}, u32[]{:S(2)}) collective-permute-start(bf16[192,512]{1,0:T(8,128)(2,1)S(1)} %collective-permute-done.10.refs_1_), channel_id=1, source_target_pairs={{0,1},{1,0},{2,3},{3,2},{4,5},{5,4},{6,7},{7,6},{8,9},{9,8},{10,11... | collective-permute-start | bytes 589832 | tf_op jit(solution)/shard_map/ppermute | solution.py:381
  126.7 1.0 mixed.2.refs_5_
  127.8 1.0 mixed.3
  (33 shorter events, 0.6 us)
Async XLA Ops:
  0.0 13.2 %collective-permute-start = (bf16[192,1024]{1,0:T(8,128)(2,1)}, bf16[192,1024]{1,0:T(8,128)(2,1)S(1)}, u32[]{:S(2)}, u32[]{:S(2)}) collective-permute-start(bf16[192,1024]{1,0:T(8,128)(2,1)} %refs_1_.1), channel_id=1, source_target_pairs={{0,2},{1,3},{2,0},{3,1},{4,6},{5,7},{6,4},{7,5},{8,10},{9,11},{10,... | collective-permute-start | bytes 1179656 | tf_op jit(solution)/shard_map/ppermute | solution.py:381
  2.9 6.9 %copy-start = (bf16[192,1024]{1,0:T(8,128)(2,1)S(1)}, bf16[192,1024]{1,0:T(8,128)(2,1)}, u32[]{:S(2)}) copy-start(bf16[192,1024]{1,0:T(8,128)(2,1)} %refs_1_.1) | copy-start | bytes 1179652
  2.9 12.5 %copy-start.4 = (f32[3,3,192]{2,1,0:T(4,128)S(1)}, f32[3,3,192]{2,1,0:T(4,128)}, u32[]{:S(2)}) copy-start(f32[3,3,192]{2,1,0:T(4,128)} %param.10) | copy-start | bytes 20740
  2.9 6.6 %collective-permute-start.1 = (bf16[192,128]{1,0:T(8,128)(2,1)S(1)}, bf16[192,128]{1,0:T(8,128)(2,1)S(1)}, u32[]{:S(2)}, u32[]{:S(2)}) collective-permute-start(bf16[192,128]{1,0:T(8,128)(2,1)S(1)} %slice.3), channel_id=1, source_target_pairs={{0,4},{4,8},{8,12},{12,16},{16,20},{20,24},{24,28},{28,32},{32,36}... | collective-permute-start | bytes 147464 | tf_op jit(solution)/shard_map/ppermute | solution.py:393
  9.5 3.7 %collective-permute-start.2 = (bf16[192,128]{1,0:T(8,128)(2,1)S(1)}, bf16[192,128]{1,0:T(8,128)(2,1)S(1)}, u32[]{:S(2)}, u32[]{:S(2)}) collective-permute-start(bf16[192,128]{1,0:T(8,128)(2,1)S(1)} %collective-permute-done.1.refs_5_), channel_id=1, source_target_pairs={{0,2},{1,3},{2,0},{3,1},{4,6},{5,7},{6,4},{7,5},{8,10},{9,11},{10,... | collective-permute-start | bytes 147464 | tf_op jit(solution)/shard_map/ppermute | solution.py:381
  9.7 6.5 %collective-permute-start.3 = (bf16[192,1024]{1,0:T(8,128)(2,1)S(1)}, bf16[192,1024]{1,0:T(8,128)(2,1)S(1)}, u32[]{:S(2)}, u32[]{:S(2)}) collective-permute-start(bf16[192,1024]{1,0:T(8,128)(2,1)S(1)} %copy-done), channel_id=1, source_target_pairs={{0,1},{1,0},{2,3},{3,2},{4,5},{5,4},{6,7},{7,6},{8,9},{9,8},{10,11... | collective-permute-start | bytes 1179656 | tf_op jit(solution)/shard_map/ppermute | solution.py:381
  13.2 3.1 %collective-permute-start.4 = (bf16[192,1024]{1,0:T(8,128)(2,1)S(1)}, bf16[192,1024]{1,0:T(8,128)(2,1)S(1)}, u32[]{:S(2)}, u32[]{:S(2)}) collective-permute-start(bf16[192,1024]{1,0:T(8,128)(2,1)S(1)} %collective-permute-done.refs_2_), channel_id=1, source_target_pairs={{0,1},{1,0},{2,3},{3,2},{4,5},{5,4},{6,7},{7,6},{8,9},{9,8},{10,11... | collective-permute-start | bytes 1179656 | tf_op jit(solution)/shard_map/ppermute | solution.py:381
  14.8 1.4 %collective-permute-start.5 = (bf16[192,128]{1,0:T(8,128)(2,1)S(1)}, bf16[192,128]{1,0:T(8,128)(2,1)S(1)}, u32[]{:S(2)}, u32[]{:S(2)}) collective-permute-start(bf16[192,128]{1,0:T(8,128)(2,1)S(1)} %collective-permute-done.1.refs_5_), channel_id=1, source_target_pairs={{0,1},{1,0},{2,3},{3,2},{4,5},{5,4},{6,7},{7,6},{8,9},{9,8},{10,11... | collective-permute-start | bytes 147464 | tf_op jit(solution)/shard_map/ppermute | solution.py:381
  14.8 1.5 %collective-permute-start.6 = (bf16[192,128]{1,0:T(8,128)(2,1)S(1)}, bf16[192,128]{1,0:T(8,128)(2,1)S(1)}, u32[]{:S(2)}, u32[]{:S(2)}) collective-permute-start(bf16[192,128]{1,0:T(8,128)(2,1)S(1)} %collective-permute-done.2.refs_6_), channel_id=1, source_target_pairs={{0,1},{1,0},{2,3},{3,2},{4,5},{5,4},{6,7},{7,6},{8,9},{9,8},{10,11... | collective-permute-start | bytes 147464 | tf_op jit(solution)/shard_map/ppermute | solution.py:381
  21.5 14.8 %copy-start.3 = (bf16[192,768]{1,0:T(8,128)(2,1)S(1)}, bf16[192,768]{1,0:T(8,128)(2,1)}, u32[]{:S(2)}) copy-start(bf16[192,768]{1,0:T(8,128)(2,1)} %param.13) | copy-start | bytes 884740
  21.5 17.2 %copy-start.2 = (f32[512,512]{1,0:T(8,128)S(1)}, f32[512,512]{1,0:T(8,128)}, u32[]{:S(2)}) copy-start(f32[512,512]{1,0:T(8,128)} %constant.21.clone) | copy-start | bytes 3145732
  21.5 61.4 %all-to-all-start = ((bf16[64,15,8,128]{3,2,1,0:T(8,128)(2,1)}), bf16[64,15,8,128]{3,2,1,0:T(8,128)(2,1)}, u32[]{:S(2)}, u32[]{:S(2)}) async-start(bf16[64,15,8,128]{3,2,1,0:T(8,128)(2,1)} %get-tuple-element.55.message_hbm), calls=%async_computation | async-start | bytes 3932160 | tf_op jit(solution)/shard_map/all_to_all | solution.py:408
  36.6 8.7 %collective-permute-start.9 = (bf16[192,192]{1,0:T(8,128)(2,1)S(1)}, bf16[192,192]{1,0:T(8,128)(2,1)S(1)}, u32[]{:S(2)}, u32[]{:S(2)}) collective-permute-start(bf16[192,192]{1,0:T(8,128)(2,1)S(1)} %get-tuple-element.67), channel_id=1, source_target_pairs={{0,3},{1,2},{2,1},{3,0},{4,7},{5,6},{6,5},{7,4},{8,11},{9,10},{10,... | collective-permute-start | bytes 221192 | tf_op jit(solution)/shard_map/ppermute | solution.py:381
  37.2 8.2 %collective-permute-start.8 = (bf16[192,192]{1,0:T(8,128)(2,1)S(1)}, bf16[192,192]{1,0:T(8,128)(2,1)S(1)}, u32[]{:S(2)}, u32[]{:S(2)}) collective-permute-start(bf16[192,192]{1,0:T(8,128)(2,1)S(1)} %get-tuple-element.68), channel_id=1, source_target_pairs={{0,1},{1,0},{2,3},{3,2},{4,5},{5,4},{6,7},{7,6},{8,9},{9,8},{10,11... | collective-permute-start | bytes 221192 | tf_op jit(solution)/shard_map/ppermute | solution.py:381
  37.4 10.3 %collective-permute-start.7 = (bf16[192,192]{1,0:T(8,128)(2,1)S(1)}, bf16[192,192]{1,0:T(8,128)(2,1)S(1)}, u32[]{:S(2)}, u32[]{:S(2)}) collective-permute-start(bf16[192,192]{1,0:T(8,128)(2,1)S(1)} %get-tuple-element.69), channel_id=1, source_target_pairs={{0,2},{1,3},{2,0},{3,1},{4,6},{5,7},{6,4},{7,5},{8,10},{9,11},{10,... | collective-permute-start | bytes 221192 | tf_op jit(solution)/shard_map/ppermute | solution.py:381
  38.8 3.1 %copy-start.5 = (f32[192]{0:T(256)S(1)}, f32[192]{0:T(256)}, u32[]{:S(2)}) copy-start(f32[192]{0:T(256)} %param.11) | copy-start | bytes 2308
  83.0 17.2 %copy-start.1 = (bf16[192,1152]{1,0:T(8,128)(2,1)S(1)}, bf16[192,1152]{1,0:T(8,128)(2,1)}, u32[]{:S(2)}) copy-start(bf16[192,1152]{1,0:T(8,128)(2,1)} %get-tuple-element.56.gate_ref) | copy-start | bytes 1327108
  91.3 23.2 %all-to-all-start.1 = ((bf16[64,3,8,128]{3,2,1,0:T(8,128)(2,1)}), bf16[64,3,8,128]{3,2,1,0:T(8,128)(2,1)S(1)}, u32[]{:S(2)}, u32[]{:S(2)}) async-start(bf16[64,3,8,128]{3,2,1,0:T(8,128)(2,1)} %convolve.1), calls=%async_computation.1 | async-start | bytes 786432 | tf_op jit(solution)/shard_map/all_to_all | solution.py:425
  114.8 6.2 %collective-permute-start.13 = (bf16[192,512]{1,0:T(8,128)(2,1)S(1)}, bf16[192,512]{1,0:T(8,128)(2,1)S(1)}, u32[]{:S(2)}, u32[]{:S(2)}) collective-permute-start(bf16[192,512]{1,0:T(8,128)(2,1)S(1)} %get-tuple-element.66.refs_0_), channel_id=1, source_target_pairs={{0,2},{1,3},{2,0},{3,1},{4,6},{5,7},{6,4},{7,5},{8,10},{9,11},{10,... | collective-permute-start | bytes 589832 | tf_op jit(solution)/shard_map/ppermute | solution.py:381
  114.9 9.7 %collective-permute-start.10 = (bf16[192,512]{1,0:T(8,128)(2,1)S(1)}, bf16[192,512]{1,0:T(8,128)(2,1)S(1)}, u32[]{:S(2)}, u32[]{:S(2)}) collective-permute-start(bf16[192,512]{1,0:T(8,128)(2,1)S(1)} %get-tuple-element.64.refs_0_), channel_id=1, source_target_pairs={{0,2},{1,3},{2,0},{3,1},{4,6},{5,7},{6,4},{7,5},{8,10},{9,11},{10,... | collective-permute-start | bytes 589832 | tf_op jit(solution)/shard_map/ppermute | solution.py:381
  116.4 10.4 %collective-permute-start.14 = (bf16[192,512]{1,0:T(8,128)(2,1)S(1)}, bf16[192,512]{1,0:T(8,128)(2,1)S(1)}, u32[]{:S(2)}, u32[]{:S(2)}) collective-permute-start(bf16[192,512]{1,0:T(8,128)(2,1)S(1)} %get-tuple-element.66.refs_0_), channel_id=1, source_target_pairs={{0,1},{1,0},{2,3},{3,2},{4,5},{5,4},{6,7},{7,6},{8,9},{9,8},{10,11... | collective-permute-start | bytes 589832 | tf_op jit(solution)/shard_map/ppermute | solution.py:381
  121.0 5.8 %collective-permute-start.15 = (bf16[192,512]{1,0:T(8,128)(2,1)S(1)}, bf16[192,512]{1,0:T(8,128)(2,1)S(1)}, u32[]{:S(2)}, u32[]{:S(2)}) collective-permute-start(bf16[192,512]{1,0:T(8,128)(2,1)S(1)} %collective-permute-done.13.refs_1_), channel_id=1, source_target_pairs={{0,1},{1,0},{2,3},{3,2},{4,5},{5,4},{6,7},{7,6},{8,9},{9,8},{10,11... | collective-permute-start | bytes 589832 | tf_op jit(solution)/shard_map/ppermute | solution.py:381
  124.6 3.1 %collective-permute-start.11 = (bf16[192,512]{1,0:T(8,128)(2,1)S(1)}, bf16[192,512]{1,0:T(8,128)(2,1)S(1)}, u32[]{:S(2)}, u32[]{:S(2)}) collective-permute-start(bf16[192,512]{1,0:T(8,128)(2,1)S(1)} %get-tuple-element.64.refs_0_), channel_id=1, source_target_pairs={{0,1},{1,0},{2,3},{3,2},{4,5},{5,4},{6,7},{7,6},{8,9},{9,8},{10,11... | collective-permute-start | bytes 589832 | tf_op jit(solution)/shard_map/ppermute | solution.py:381
  124.6 3.2 %collective-permute-start.12 = (bf16[192,512]{1,0:T(8,128)(2,1)S(1)}, bf16[192,512]{1,0:T(8,128)(2,1)S(1)}, u32[]{:S(2)}, u32[]{:S(2)}) collective-permute-start(bf16[192,512]{1,0:T(8,128)(2,1)S(1)} %collective-permute-done.10.refs_1_), channel_id=1, source_target_pairs={{0,1},{1,0},{2,3},{3,2},{4,5},{5,4},{6,7},{7,6},{8,9},{9,8},{10,11... | collective-permute-start | bytes 589832 | tf_op jit(solution)/shard_map/ppermute | solution.py:381

commit v10 on v9

--- a/solution.py
+++ b/solution.py
@@ -15,7 +15,7 @@
 GATED_VMEM = 8 << 20
 KEEP_VMEM = 52500 << 10
 MIXED_VMEM = 12 << 20
-CONVOLVE_VMEM = 52000 << 10
+CONVOLVE_VMEM = 50600 << 10
 MASKS = (0, 2, 1, 3)
 BF16 = jnp.bfloat16
 F32 = jnp.float32
@@ -37,9 +37,8 @@
     cost, sint = unit_circle(freqs, cols, padded)
     first = np.concatenate([cos1, -sin1], 1)
     forward = np.block([[cos2, -sin2], [sin2, cos2]])
-    backward = np.block([[cos2, sin2], [-sin2, cos2]])
     last = np.concatenate([cos1.T, -sin1.T], 0) / padded
-    waves = np.concatenate([first, forward, backward, last], 0)
+    waves = np.concatenate([first, forward, last], 0)
     return jnp.asarray(waves, BF16), jnp.asarray(np.concatenate([cost, sint], 1), F32)
 
 
@@ -207,22 +206,19 @@
     )(message, gate_stream, taps, *weights)
 
 
-def convolve_body(m_hbm, wave_hbm, twist_ref, out_ref,
-                  spread_ref, grid_ref, mid_ref, tall_ref, done_ref, wave_ref, m_ref, sems, wave_sems, m_sems):
+def convolve_body(m_hbm, wave_ref, twist_ref, out_ref,
+                  spread_ref, grid_ref, mid_ref, tall_ref, done_ref, m_ref, sems, m_sems):
     channels, shards, pieces, lanes = done_ref.shape
     rows_dev = pieces // 2
     freqs = twist_ref.shape[0]
-    first_ref, forward_ref, backward_ref, last_ref = (wave_ref.at[i] for i in range(4))
-    loads = [
-        pltpu.make_async_copy(wave_hbm.at[pl.ds(i * freqs, freqs)], wave_ref.at[i], wave_sems.at[i]) for i in range(4)
-    ]
+    first_ref, forward_ref, last_ref = (wave_ref.at[pl.ds(i * freqs, freqs)] for i in range(3))
     signals = pl.ds(4 * channels, channels)
     arrival = pltpu.make_async_copy(m_hbm.at[:, signals], m_ref.at[:, signals], m_sems.at[channels])
     responses = [
         pltpu.make_async_copy(m_hbm.at[:, pl.ds(4 * c, 4)], m_ref.at[:, pl.ds(4 * c, 4)], m_sems.at[c])
         for c in range(channels)
     ]
-    for load in (arrival, *loads[:2], *responses, *loads[2:]):
+    for load in (arrival, *responses):
         load.start()
     cosine, sine = twist_ref[:, :COLS], twist_ref[:, COLS:]
 
@@ -254,15 +250,15 @@
                 m_ref[:, 4 * c + 2 * part + h].astype(F32).reshape(freqs, lanes) for part in range(2)
             )
             mid_ref[c, :, low:low + lanes] = (real * h_real - imag * h_imag).astype(BF16)
-            mid_ref[c, :, high:high + lanes] = (real * h_imag + imag * h_real).astype(BF16)
+            mid_ref[c, :, high:high + lanes] = (-(real * h_imag) - imag * h_real).astype(BF16)
 
     def cols_backward(c):
-        return jnp.dot(mid_ref[c], backward_ref[...], preferred_element_type=F32)
+        return jnp.dot(mid_ref[c], forward_ref[...], preferred_element_type=F32)
 
     def twist_backward(c, back):
-        real, imag = back[:, :COLS], back[:, COLS:]
-        tall_ref[c, :freqs, :] = (real * cosine - imag * sine).astype(BF16)
-        tall_ref[c, freqs:, :] = (imag * cosine + real * sine).astype(BF16)
+        real, minus = back[:, :COLS], back[:, COLS:]
+        tall_ref[c, :freqs, :] = (real * cosine + minus * sine).astype(BF16)
+        tall_ref[c, freqs:, :] = (real * sine - minus * cosine).astype(BF16)
 
     def rows_backward(c):
         out = jnp.dot(last_ref[:COLS, :], tall_ref[c, :freqs], preferred_element_type=F32)
@@ -283,8 +279,7 @@
         (rows_forward, twist_forward), (cols_forward, respond), (cols_backward, twist_backward), (rows_backward, send)
     )
     waiting = None
-    for stage, (multiply, finish) in enumerate(stages):
-        loads[stage].wait()
+    for multiply, finish in stages:
         for c in range(channels):
             product = multiply(c)
             if waiting is not None:
@@ -311,10 +306,8 @@
             pltpu.VMEM((channels, freqs, 2 * COLS), BF16),
             pltpu.VMEM((channels, 2 * freqs, COLS), BF16),
             pltpu.VMEM((channels, shards, pieces, lanes), BF16),
-            pltpu.VMEM((4, freqs, 2 * COLS), BF16),
             pltpu.VMEM(received.shape, BF16),
             pltpu.SemaphoreType.DMA((channels,)),
-            pltpu.SemaphoreType.DMA((4,)),
             pltpu.SemaphoreType.DMA((channels + 1,)),
         ],
         compiler_params=pltpu.CompilerParams(vmem_limit_bytes=CONVOLVE_VMEM),

time: 129 us -> 128 us (level)
  other arithmetic: 3.16 us -> 1.61 us
  waiting for transfers between devices: 56.7 us -> 58.2 us
  Pallas kernels: 20.3 us -> 18.9 us
    add x2, other arithmetic: 3.16 us -> 1.61 us  [shards(): t + zero.astype(t.dtype)]
    ppermute x15, waiting for transfers between devices: 8.74 us -> 10.3 us  [swapped(): return lax.ppermute(block, 'grp', [(i, i ^ mask) for i in range(4)])]
    pallas_call x1, Pallas kernels: 8.31 us -> 6.88 us  [convolve(): pl.pallas_call(convolve_body, in_specs=[vmem] * 3, out_specs=pl.BlockSpec...]
  transfers between devices with their start and end apart: 18 -> 18, of which waited for: 7 -> 7; matrix products, arithmetic and copies ran while one was open for 4% -> 2% of each run, Pallas kernels for 4% -> 4%
where the time goes in v10:
time: 128 us; the launch traced here: 127 us
  waiting for transfers between devices  58.2 us (45%)
  starting transfers between devices  47.1 us (37%)
  Pallas kernels  18.9 us (15%)
  other arithmetic  1.61 us (1%)
  local copies, waits for them, and re-layouts  1.43 us (1%)
    all_to_all x1, waiting for transfers between devices, shards(): received = lax.all_to_all(message, 'seq', 0, 0, tiled=True)  35.2 us
    ppermute x15, starting transfers between devices, swapped(): return lax.ppermute(block, 'grp', [(i, i ^ mask) for i in range(4)])  19.9 us
    all_to_all x1, starting transfers between devices, shards(): received = lax.all_to_all(message, 'seq', 0, 0, tiled=True)  14.8 us
    all_to_all x1, waiting for transfers between devices, shards(): lax.all_to_all(result, 'seq', 0, 0, tiled=True).reshape(channels * 8, LANES)  12.8 us
    ppermute x15, waiting for transfers between devices, swapped(): return lax.ppermute(block, 'grp', [(i, i ^ mask) for i in range(4)])  10.3 us
    all_to_all x1, starting transfers between devices, shards(): lax.all_to_all(result, 'seq', 0, 0, tiled=True).reshape(channels * 8, LANES)  8.67 us
    pallas_call x1, Pallas kernels, convolve(): pl.pallas_call(convolve_body, in_specs=[vmem] * 3, out_specs=pl.BlockSpec...  6.88 us
    pallas_call x1, Pallas kernels, project(): pl.pallas_call(project_body, in_specs=[pl.BlockSpec(memory_space=pltpu.SM...  5.22 us
  transfers between devices with their start and end apart: 18, of which 7 were waited for; matrix products, arithmetic and copies ran while one was open for 2% of the time, Pallas kernels for 4%

profile of v10, /device:TPU:1, one launch (start us, length us, event | category | flops | bytes accessed | tf_op | source)
XLA Modules:
  0.0 127.4 jit_solution(488798442180202298)
XLA Ops:
  0.0 2.0 %collective-permute-start = (bf16[192,1024]{1,0:T(8,128)(2,1)}, bf16[192,1024]{1,0:T(8,128)(2,1)S(1)}, u32[]{:S(2)}, u32[]{:S(2)}) collective-permute-start(bf16[192,1024]{1,0:T(8,128)(2,1)} %refs_1_.1), channel_id=1, source_target_pairs={{0,2},{1,3},{2,0},{3,1},{4,6},{5,7},{6,4},{7,5},{8,10},{9,11},{10,... | collective-permute-start | bytes 1179656 | tf_op jit(solution)/shard_map/ppermute | solution.py:374
  2.0 0.8 slice.3
  2.9 3.7 %collective-permute-start.1 = (bf16[192,128]{1,0:T(8,128)(2,1)S(1)}, bf16[192,128]{1,0:T(8,128)(2,1)S(1)}, u32[]{:S(2)}, u32[]{:S(2)}) collective-permute-start(bf16[192,128]{1,0:T(8,128)(2,1)S(1)} %slice.3), channel_id=1, source_target_pairs={{0,4},{4,8},{8,12},{12,16},{16,20},{20,24},{24,28},{28,32},{32,36}... | collective-permute-start | bytes 147464 | tf_op jit(solution)/shard_map/ppermute | solution.py:386
  6.6 2.9 %pack_spectra.1.refs_11_ = bf16[64,15,8,128]{3,2,1,0:T(8,128)(2,1)} custom-call(f32[2,192,8,256]{3,2,1,0:T(8,128)} %spec_ref.1), custom_call_target="tpu_custom_call" | custom-call | bytes 4718592 | tf_op jit(solution)/shard_map/pack_spectra/pallas_call | solution.py:60
  9.5 0.3 collective-permute-start.2
  9.7 1.5 %collective-permute-start.3 = (bf16[192,1024]{1,0:T(8,128)(2,1)S(1)}, bf16[192,1024]{1,0:T(8,128)(2,1)S(1)}, u32[]{:S(2)}, u32[]{:S(2)}) collective-permute-start(bf16[192,1024]{1,0:T(8,128)(2,1)S(1)} %copy-done), channel_id=1, source_target_pairs={{0,1},{1,0},{2,3},{3,2},{4,5},{5,4},{6,7},{7,6},{8,9},{9,8},{10,11... | collective-permute-start | bytes 1179656 | tf_op jit(solution)/shard_map/ppermute | solution.py:374
  11.2 2.0 %collective-permute-done.2.refs_6_ = bf16[192,128]{1,0:T(8,128)(2,1)S(1)} collective-permute-done((bf16[192,128]{1,0:T(8,128)(2,1)S(1)}, bf16[192,128]{1,0:T(8,128)(2,1)S(1)}, u32[]{:S(2)}, u32[]{:S(2)}) %collective-permute-start.2) | collective-permute-done | bytes 49184 | tf_op jit(solution)/shard_map/ppermute | solution.py:374
  13.2 1.6 %collective-permute-start.4 = (bf16[192,1024]{1,0:T(8,128)(2,1)S(1)}, bf16[192,1024]{1,0:T(8,128)(2,1)S(1)}, u32[]{:S(2)}, u32[]{:S(2)}) collective-permute-start(bf16[192,1024]{1,0:T(8,128)(2,1)S(1)} %collective-permute-done.refs_2_), channel_id=1, source_target_pairs={{0,1},{1,0},{2,3},{3,2},{4,5},{5,4},{6,7},{7,6},{8,9},{9,8},{10,11... | collective-permute-start | bytes 1179656 | tf_op jit(solution)/shard_map/ppermute | solution.py:374
  14.8 0.5 collective-permute-start.6
  15.3 0.1 copy.16.refs_10_
  15.4 0.8 collective-permute-done.5.refs_7_
  16.3 5.2 %project.1 = (bf16[64,15,8,128]{3,2,1,0:T(8,128)(2,1)}, bf16[192,1152]{1,0:T(8,128)(2,1)}) custom-call(s32[1]{0:T(128)} %bitcast.refs_0_, bf16[192,1024]{1,0:T(8,128)(2,1)S(1)} %copy-done, bf16[192,1024]{1,0:T(8,128)(2,1)S(1)} %collective-permute-done.refs_2_, ...), custom_call_target="tpu_custom_call", output_to_operand_aliasing={{0}: (11, {})} | custom-call | flops 1019215872 | bytes 6291456 | tf_op jit(solution)/shard_map/project/pallas_call | solution.py:135
  21.5 14.8 %all-to-all-start = ((bf16[64,15,8,128]{3,2,1,0:T(8,128)(2,1)}), bf16[64,15,8,128]{3,2,1,0:T(8,128)(2,1)}, u32[]{:S(2)}, u32[]{:S(2)}) async-start(bf16[64,15,8,128]{3,2,1,0:T(8,128)(2,1)} %get-tuple-element.55.message_hbm), calls=%async_computation | async-start | bytes 3932160 | tf_op jit(solution)/shard_map/all_to_all | solution.py:401
  36.4 0.2 copy.17
  36.6 0.6 collective-permute-start.9
  37.2 0.3 collective-permute-start.8
  37.5 1.3 collective-permute-start.7
  38.8 1.5 %broadcast_add_fusion.wave_ref = bf16[1536,512]{1,0:T(8,128)(2,1)S(1)} fusion(bf16[1536,512]{1,0:T(8,128)(2,1)} %constant.20.clone, bf16[]{:T(256)S(6)} %convert_element_type.7), kind=kLoop, calls=%fused_computation | loop fusion | flops 786432 | bytes 3145730 | tf_op jit(solution)/shard_map/add | solution.py:409
  40.4 5.0 %collective-permute-done.9.refs_3_ = bf16[192,192]{1,0:T(8,128)(2,1)S(1)} collective-permute-done((bf16[192,192]{1,0:T(8,128)(2,1)S(1)}, bf16[192,192]{1,0:T(8,128)(2,1)S(1)}, u32[]{:S(2)}, u32[]{:S(2)}) %collective-permute-start.9) | collective-permute-done | bytes 73760 | tf_op jit(solution)/shard_map/ppermute | solution.py:374
  45.3 2.5 %collective-permute-done.7.refs_1_ = bf16[192,192]{1,0:T(8,128)(2,1)S(1)} collective-permute-done((bf16[192,192]{1,0:T(8,128)(2,1)S(1)}, bf16[192,192]{1,0:T(8,128)(2,1)S(1)}, u32[]{:S(2)}, u32[]{:S(2)}) %collective-permute-start.7) | collective-permute-done | bytes 73760 | tf_op jit(solution)/shard_map/ppermute | solution.py:374
  47.8 35.2 %all-to-all-done.m_hbm = bf16[64,15,8,128]{3,2,1,0:T(8,128)(2,1)} async-done(((bf16[64,15,8,128]{3,2,1,0:T(8,128)(2,1)}), bf16[64,15,8,128]{3,2,1,0:T(8,128)(2,1)}, u32[]{:S(2)}, u32[]{:S(2)}) %all-to-all-start) | async-done | bytes 1966112 | tf_op jit(solution)/shard_map/all_to_all | solution.py:401
  83.0 6.9 %convolve.1 = bf16[64,3,8,128]{3,2,1,0:T(8,128)(2,1)} custom-call(bf16[64,15,8,128]{3,2,1,0:T(8,128)(2,1)} %all-to-all-done.m_hbm, bf16[1536,512]{1,0:T(8,128)(2,1)S(1)} %broadcast_add_fusion.wave_ref, f32[512,512]{1,0:T(8,128)S(1)} %broadcast_add_fusion.1.twist_ref), custom_call_target="tpu_custom_call" | custom-call | flops 3221225472 | bytes 6291456 | tf_op jit(solution)/shard_map/convolve/pallas_call | solution.py:298
  89.9 8.7 %all-to-all-start.1 = ((bf16[64,3,8,128]{3,2,1,0:T(8,128)(2,1)}), bf16[64,3,8,128]{3,2,1,0:T(8,128)(2,1)S(1)}, u32[]{:S(2)}, u32[]{:S(2)}) async-start(bf16[64,3,8,128]{3,2,1,0:T(8,128)(2,1)} %convolve.1), calls=%async_computation.1 | async-start | bytes 786432 | tf_op jit(solution)/shard_map/all_to_all | solution.py:418
  98.8 1.5 %keep.1 = (bf16[2,192,1024]{2,1,0:T(8,128)(2,1)S(1)}, bf16[768,192]{1,0:T(8,128)(2,1)S(1)}) custom-call(bf16[64,15,8,128]{3,2,1,0:T(8,128)(2,1)} %get-tuple-element.55.message_hbm, bf16[192,1152]{1,0:T(8,128)(2,1)S(1)} %copy-done.1, f32[192,9]{1,0:T(8,128)S(1)} %copy.21.taps_ref, bf16[192,192]{1,0:T(8,128)(2,1)S(1)} %get-tuple-element.58.refs_0_, ...), custom_call_target="tpu_custom_call" | custom-call | flops 1769472 | bytes 2097152 | tf_op jit(solution)/shard_map/keep/pallas_call | solution.py:190
  100.3 12.8 %all-to-all-done.1 = bf16[64,3,8,128]{3,2,1,0:T(8,128)(2,1)S(1)} async-done(((bf16[64,3,8,128]{3,2,1,0:T(8,128)(2,1)}), bf16[64,3,8,128]{3,2,1,0:T(8,128)(2,1)S(1)}, u32[]{:S(2)}, u32[]{:S(2)}) %all-to-all-start.1) | async-done | bytes 393248 | tf_op jit(solution)/shard_map/all_to_all | solution.py:418
  113.1 0.3 gated.1
  113.5 1.5 %collective-permute-start.10 = (bf16[192,512]{1,0:T(8,128)(2,1)S(1)}, bf16[192,512]{1,0:T(8,128)(2,1)S(1)}, u32[]{:S(2)}, u32[]{:S(2)}) collective-permute-start(bf16[192,512]{1,0:T(8,128)(2,1)S(1)} %get-tuple-element.64.refs_0_), channel_id=1, source_target_pairs={{0,2},{1,3},{2,0},{3,1},{4,6},{5,7},{6,4},{7,5},{8,10},{9,11},{10,... | collective-permute-start | bytes 589832 | tf_op jit(solution)/shard_map/ppermute | solution.py:374
  114.9 4.6 %collective-permute-start.14 = (bf16[192,512]{1,0:T(8,128)(2,1)S(1)}, bf16[192,512]{1,0:T(8,128)(2,1)S(1)}, u32[]{:S(2)}, u32[]{:S(2)}) collective-permute-start(bf16[192,512]{1,0:T(8,128)(2,1)S(1)} %get-tuple-element.66.refs_0_), channel_id=1, source_target_pairs={{0,1},{1,0},{2,3},{3,2},{4,5},{5,4},{6,7},{7,6},{8,9},{9,8},{10,11... | collective-permute-start | bytes 589832 | tf_op jit(solution)/shard_map/ppermute | solution.py:374
  119.6 3.6 %collective-permute-start.15 = (bf16[192,512]{1,0:T(8,128)(2,1)S(1)}, bf16[192,512]{1,0:T(8,128)(2,1)S(1)}, u32[]{:S(2)}, u32[]{:S(2)}) collective-permute-start(bf16[192,512]{1,0:T(8,128)(2,1)S(1)} %collective-permute-done.13.refs_1_), channel_id=1, source_target_pairs={{0,1},{1,0},{2,3},{3,2},{4,5},{5,4},{6,7},{7,6},{8,9},{9,8},{10,11... | collective-permute-start | bytes 589832 | tf_op jit(solution)/shard_map/ppermute | solution.py:374
  123.2 2.1 %collective-permute-start.12 = (bf16[192,512]{1,0:T(8,128)(2,1)S(1)}, bf16[192,512]{1,0:T(8,128)(2,1)S(1)}, u32[]{:S(2)}, u32[]{:S(2)}) collective-permute-start(bf16[192,512]{1,0:T(8,128)(2,1)S(1)} %collective-permute-done.10.refs_1_), channel_id=1, source_target_pairs={{0,1},{1,0},{2,3},{3,2},{4,5},{5,4},{6,7},{7,6},{8,9},{9,8},{10,11... | collective-permute-start | bytes 589832 | tf_op jit(solution)/shard_map/ppermute | solution.py:374
  125.3 1.0 mixed.2.refs_5_
  126.4 1.0 mixed.3
  (33 shorter events, 0.6 us)
Async XLA Ops:
  0.0 13.2 %collective-permute-start = (bf16[192,1024]{1,0:T(8,128)(2,1)}, bf16[192,1024]{1,0:T(8,128)(2,1)S(1)}, u32[]{:S(2)}, u32[]{:S(2)}) collective-permute-start(bf16[192,1024]{1,0:T(8,128)(2,1)} %refs_1_.1), channel_id=1, source_target_pairs={{0,2},{1,3},{2,0},{3,1},{4,6},{5,7},{6,4},{7,5},{8,10},{9,11},{10,... | collective-permute-start | bytes 1179656 | tf_op jit(solution)/shard_map/ppermute | solution.py:374
  2.9 6.8 %copy-start = (bf16[192,1024]{1,0:T(8,128)(2,1)S(1)}, bf16[192,1024]{1,0:T(8,128)(2,1)}, u32[]{:S(2)}) copy-start(bf16[192,1024]{1,0:T(8,128)(2,1)} %refs_1_.1) | copy-start | bytes 1179652
  2.9 12.4 %copy-start.4 = (f32[3,3,192]{2,1,0:T(4,128)S(1)}, f32[3,3,192]{2,1,0:T(4,128)}, u32[]{:S(2)}) copy-start(f32[3,3,192]{2,1,0:T(4,128)} %param.10) | copy-start | bytes 20740
  2.9 6.6 %collective-permute-start.1 = (bf16[192,128]{1,0:T(8,128)(2,1)S(1)}, bf16[192,128]{1,0:T(8,128)(2,1)S(1)}, u32[]{:S(2)}, u32[]{:S(2)}) collective-permute-start(bf16[192,128]{1,0:T(8,128)(2,1)S(1)} %slice.3), channel_id=1, source_target_pairs={{0,4},{4,8},{8,12},{12,16},{16,20},{20,24},{24,28},{28,32},{32,36}... | collective-permute-start | bytes 147464 | tf_op jit(solution)/shard_map/ppermute | solution.py:386
  9.5 3.7 %collective-permute-start.2 = (bf16[192,128]{1,0:T(8,128)(2,1)S(1)}, bf16[192,128]{1,0:T(8,128)(2,1)S(1)}, u32[]{:S(2)}, u32[]{:S(2)}) collective-permute-start(bf16[192,128]{1,0:T(8,128)(2,1)S(1)} %collective-permute-done.1.refs_5_), channel_id=1, source_target_pairs={{0,2},{1,3},{2,0},{3,1},{4,6},{5,7},{6,4},{7,5},{8,10},{9,11},{10,... | collective-permute-start | bytes 147464 | tf_op jit(solution)/shard_map/ppermute | solution.py:374
  9.7 6.5 %collective-permute-start.3 = (bf16[192,1024]{1,0:T(8,128)(2,1)S(1)}, bf16[192,1024]{1,0:T(8,128)(2,1)S(1)}, u32[]{:S(2)}, u32[]{:S(2)}) collective-permute-start(bf16[192,1024]{1,0:T(8,128)(2,1)S(1)} %copy-done), channel_id=1, source_target_pairs={{0,1},{1,0},{2,3},{3,2},{4,5},{5,4},{6,7},{7,6},{8,9},{9,8},{10,11... | collective-permute-start | bytes 1179656 | tf_op jit(solution)/shard_map/ppermute | solution.py:374
  13.2 3.1 %collective-permute-start.4 = (bf16[192,1024]{1,0:T(8,128)(2,1)S(1)}, bf16[192,1024]{1,0:T(8,128)(2,1)S(1)}, u32[]{:S(2)}, u32[]{:S(2)}) collective-permute-start(bf16[192,1024]{1,0:T(8,128)(2,1)S(1)} %collective-permute-done.refs_2_), channel_id=1, source_target_pairs={{0,1},{1,0},{2,3},{3,2},{4,5},{5,4},{6,7},{7,6},{8,9},{9,8},{10,11... | collective-permute-start | bytes 1179656 | tf_op jit(solution)/shard_map/ppermute | solution.py:374
  14.8 1.4 %collective-permute-start.5 = (bf16[192,128]{1,0:T(8,128)(2,1)S(1)}, bf16[192,128]{1,0:T(8,128)(2,1)S(1)}, u32[]{:S(2)}, u32[]{:S(2)}) collective-permute-start(bf16[192,128]{1,0:T(8,128)(2,1)S(1)} %collective-permute-done.1.refs_5_), channel_id=1, source_target_pairs={{0,1},{1,0},{2,3},{3,2},{4,5},{5,4},{6,7},{7,6},{8,9},{9,8},{10,11... | collective-permute-start | bytes 147464 | tf_op jit(solution)/shard_map/ppermute | solution.py:374
  14.8 1.5 %collective-permute-start.6 = (bf16[192,128]{1,0:T(8,128)(2,1)S(1)}, bf16[192,128]{1,0:T(8,128)(2,1)S(1)}, u32[]{:S(2)}, u32[]{:S(2)}) collective-permute-start(bf16[192,128]{1,0:T(8,128)(2,1)S(1)} %collective-permute-done.2.refs_6_), channel_id=1, source_target_pairs={{0,1},{1,0},{2,3},{3,2},{4,5},{5,4},{6,7},{7,6},{8,9},{9,8},{10,11... | collective-permute-start | bytes 147464 | tf_op jit(solution)/shard_map/ppermute | solution.py:374
  21.5 14.9 %copy-start.3 = (bf16[192,768]{1,0:T(8,128)(2,1)S(1)}, bf16[192,768]{1,0:T(8,128)(2,1)}, u32[]{:S(2)}) copy-start(bf16[192,768]{1,0:T(8,128)(2,1)} %param.13) | copy-start | bytes 884740
  21.5 61.5 %all-to-all-start = ((bf16[64,15,8,128]{3,2,1,0:T(8,128)(2,1)}), bf16[64,15,8,128]{3,2,1,0:T(8,128)(2,1)}, u32[]{:S(2)}, u32[]{:S(2)}) async-start(bf16[64,15,8,128]{3,2,1,0:T(8,128)(2,1)} %get-tuple-element.55.message_hbm), calls=%async_computation | async-start | bytes 3932160 | tf_op jit(solution)/shard_map/all_to_all | solution.py:401
  36.4 2.4 %copy-start.2 = (f32[512,512]{1,0:T(8,128)S(1)}, f32[512,512]{1,0:T(8,128)}, u32[]{:S(2)}) copy-start(f32[512,512]{1,0:T(8,128)} %constant.21.clone) | copy-start | bytes 3145732
  36.6 8.7 %collective-permute-start.9 = (bf16[192,192]{1,0:T(8,128)(2,1)S(1)}, bf16[192,192]{1,0:T(8,128)(2,1)S(1)}, u32[]{:S(2)}, u32[]{:S(2)}) collective-permute-start(bf16[192,192]{1,0:T(8,128)(2,1)S(1)} %get-tuple-element.67), channel_id=1, source_target_pairs={{0,3},{1,2},{2,1},{3,0},{4,7},{5,6},{6,5},{7,4},{8,11},{9,10},{10,... | collective-permute-start | bytes 221192 | tf_op jit(solution)/shard_map/ppermute | solution.py:374
  37.2 8.1 %collective-permute-start.8 = (bf16[192,192]{1,0:T(8,128)(2,1)S(1)}, bf16[192,192]{1,0:T(8,128)(2,1)S(1)}, u32[]{:S(2)}, u32[]{:S(2)}) collective-permute-start(bf16[192,192]{1,0:T(8,128)(2,1)S(1)} %get-tuple-element.68), channel_id=1, source_target_pairs={{0,1},{1,0},{2,3},{3,2},{4,5},{5,4},{6,7},{7,6},{8,9},{9,8},{10,11... | collective-permute-start | bytes 221192 | tf_op jit(solution)/shard_map/ppermute | solution.py:374
  37.5 10.3 %collective-permute-start.7 = (bf16[192,192]{1,0:T(8,128)(2,1)S(1)}, bf16[192,192]{1,0:T(8,128)(2,1)S(1)}, u32[]{:S(2)}, u32[]{:S(2)}) collective-permute-start(bf16[192,192]{1,0:T(8,128)(2,1)S(1)} %get-tuple-element.69), channel_id=1, source_target_pairs={{0,2},{1,3},{2,0},{3,1},{4,6},{5,7},{6,4},{7,5},{8,10},{9,11},{10,... | collective-permute-start | bytes 221192 | tf_op jit(solution)/shard_map/ppermute | solution.py:374
  38.8 1.5 %copy-start.5 = (f32[192]{0:T(256)S(1)}, f32[192]{0:T(256)}, u32[]{:S(2)}) copy-start(f32[192]{0:T(256)} %param.11) | copy-start | bytes 2308
  83.0 15.8 %copy-start.1 = (bf16[192,1152]{1,0:T(8,128)(2,1)S(1)}, bf16[192,1152]{1,0:T(8,128)(2,1)}, u32[]{:S(2)}) copy-start(bf16[192,1152]{1,0:T(8,128)(2,1)} %get-tuple-element.56.gate_ref) | copy-start | bytes 1327108
  89.9 23.2 %all-to-all-start.1 = ((bf16[64,3,8,128]{3,2,1,0:T(8,128)(2,1)}), bf16[64,3,8,128]{3,2,1,0:T(8,128)(2,1)S(1)}, u32[]{:S(2)}, u32[]{:S(2)}) async-start(bf16[64,3,8,128]{3,2,1,0:T(8,128)(2,1)} %convolve.1), calls=%async_computation.1 | async-start | bytes 786432 | tf_op jit(solution)/shard_map/all_to_all | solution.py:418
  113.4 6.2 %collective-permute-start.13 = (bf16[192,512]{1,0:T(8,128)(2,1)S(1)}, bf16[192,512]{1,0:T(8,128)(2,1)S(1)}, u32[]{:S(2)}, u32[]{:S(2)}) collective-permute-start(bf16[192,512]{1,0:T(8,128)(2,1)S(1)} %get-tuple-element.66.refs_0_), channel_id=1, source_target_pairs={{0,2},{1,3},{2,0},{3,1},{4,6},{5,7},{6,4},{7,5},{8,10},{9,11},{10,... | collective-permute-start | bytes 589832 | tf_op jit(solution)/shard_map/ppermute | solution.py:374
  113.5 9.7 %collective-permute-start.10 = (bf16[192,512]{1,0:T(8,128)(2,1)S(1)}, bf16[192,512]{1,0:T(8,128)(2,1)S(1)}, u32[]{:S(2)}, u32[]{:S(2)}) collective-permute-start(bf16[192,512]{1,0:T(8,128)(2,1)S(1)} %get-tuple-element.64.refs_0_), channel_id=1, source_target_pairs={{0,2},{1,3},{2,0},{3,1},{4,6},{5,7},{6,4},{7,5},{8,10},{9,11},{10,... | collective-permute-start | bytes 589832 | tf_op jit(solution)/shard_map/ppermute | solution.py:374
  114.9 10.4 %collective-permute-start.14 = (bf16[192,512]{1,0:T(8,128)(2,1)S(1)}, bf16[192,512]{1,0:T(8,128)(2,1)S(1)}, u32[]{:S(2)}, u32[]{:S(2)}) collective-permute-start(bf16[192,512]{1,0:T(8,128)(2,1)S(1)} %get-tuple-element.66.refs_0_), channel_id=1, source_target_pairs={{0,1},{1,0},{2,3},{3,2},{4,5},{5,4},{6,7},{7,6},{8,9},{9,8},{10,11... | collective-permute-start | bytes 589832 | tf_op jit(solution)/shard_map/ppermute | solution.py:374
  119.6 5.8 %collective-permute-start.15 = (bf16[192,512]{1,0:T(8,128)(2,1)S(1)}, bf16[192,512]{1,0:T(8,128)(2,1)S(1)}, u32[]{:S(2)}, u32[]{:S(2)}) collective-permute-start(bf16[192,512]{1,0:T(8,128)(2,1)S(1)} %collective-permute-done.13.refs_1_), channel_id=1, source_target_pairs={{0,1},{1,0},{2,3},{3,2},{4,5},{5,4},{6,7},{7,6},{8,9},{9,8},{10,11... | collective-permute-start | bytes 589832 | tf_op jit(solution)/shard_map/ppermute | solution.py:374
  123.2 3.2 %collective-permute-start.11 = (bf16[192,512]{1,0:T(8,128)(2,1)S(1)}, bf16[192,512]{1,0:T(8,128)(2,1)S(1)}, u32[]{:S(2)}, u32[]{:S(2)}) collective-permute-start(bf16[192,512]{1,0:T(8,128)(2,1)S(1)} %get-tuple-element.64.refs_0_), channel_id=1, source_target_pairs={{0,1},{1,0},{2,3},{3,2},{4,5},{5,4},{6,7},{7,6},{8,9},{9,8},{10,11... | collective-permute-start | bytes 589832 | tf_op jit(solution)/shard_map/ppermute | solution.py:374
  123.2 3.2 %collective-permute-start.12 = (bf16[192,512]{1,0:T(8,128)(2,1)S(1)}, bf16[192,512]{1,0:T(8,128)(2,1)S(1)}, u32[]{:S(2)}, u32[]{:S(2)}) collective-permute-start(bf16[192,512]{1,0:T(8,128)(2,1)S(1)} %collective-permute-done.10.refs_1_), channel_id=1, source_target_pairs={{0,1},{1,0},{2,3},{3,2},{4,5},{5,4},{6,7},{7,6},{8,9},{9,8},{10,11... | collective-permute-start | bytes 589832 | tf_op jit(solution)/shard_map/ppermute | solution.py:374

commit v11 on v7

--- a/solution.py
+++ b/solution.py
@@ -370,10 +370,10 @@
     halo, packed = lax.optimization_barrier((halo, packed))
     halo_far = swapped(halo, 2)
     halo_near = swapped(halo, 1)
-    far, halo_far = lax.optimization_barrier((far, halo_far))
+    taps = jnp.transpose(short_weight, (2, 0, 1)).reshape(channels, 9)
+    far, halo_far, halo_near, near, taps = lax.optimization_barrier((far, halo_far, halo_near, near, taps))
     mains = [tokens, far, near, swapped(far, 1)]
     halos = [halo, halo_far, halo_near, swapped(halo_far, 1)]
-    taps = jnp.transpose(short_weight, (2, 0, 1)).reshape(channels, 9)
     message, gate_stream = project(
         grp.reshape(1).astype(jnp.int32), mains, halos, in_weight.reshape(3 * channels, -1), taps, packed
     )
@@ -397,7 +397,6 @@
     back = lax.all_to_all(result, "seq", 0, 0, tiled=True).reshape(channels * 8, LANES)
     early, late = gated(back, kept, bias)
     far_early, far_late = swapped(early, 2), swapped(late, 2)
-    far_early, early, late = lax.optimization_barrier((far_early, early, late))
     near_early, near_late = swapped(early, 1), swapped(late, 1)
     out = mixed((early, far_early, near_early, swapped(far_early, 1)), weights, 0)
     return mixed((late, far_late, near_late, swapped(far_late, 1)), weights, 1, out)

time: 127 us -> 127 us (level)
  starting transfers between devices: 43.9 us -> 45.2 us
  waiting for transfers between devices: 57.9 us -> 56.6 us
    ppermute x15, starting transfers between devices: 16.8 us -> 18.5 us  [swapped(): return lax.ppermute(block, 'grp', [(i, i ^ mask) for i in range(4)])]
  transfers between devices with their start and end apart: 18 -> 18, of which waited for: 7 -> 6; matrix products, arithmetic and copies ran while one was open for 4% -> 4% of each run, Pallas kernels for 6% -> 6%
where the time goes in v11:
time: 127 us
  waiting for transfers between devices  56.6 us (45%)
  starting transfers between devices  45.2 us (36%)
  Pallas kernels  19.3 us (15%)
  other arithmetic  2.81 us (2%)
  local copies, waits for them, and re-layouts  2.75 us (2%)
    all_to_all x1, waiting for transfers between devices, shards(): received = lax.all_to_all(message, 'seq', 0, 0, tiled=True)  34.6 us
    ppermute x15, starting transfers between devices, swapped(): return lax.ppermute(block, 'grp', [(i, i ^ mask) for i in range(4)])  18.5 us
    all_to_all x1, waiting for transfers between devices, shards(): lax.all_to_all(result, 'seq', 0, 0, tiled=True).reshape(channels * 8, LANES)  14.4 us
    all_to_all x1, starting transfers between devices, shards(): received = lax.all_to_all(message, 'seq', 0, 0, tiled=True)  14.3 us
    all_to_all x1, starting transfers between devices, shards(): lax.all_to_all(result, 'seq', 0, 0, tiled=True).reshape(channels * 8, LANES)  8.88 us
    ppermute x15, waiting for transfers between devices, swapped(): return lax.ppermute(block, 'grp', [(i, i ^ mask) for i in range(4)])  7.64 us
    pallas_call x1, Pallas kernels, convolve(): pl.pallas_call(convolve_body, in_specs=[vmem, pl.BlockSpec(memory_space=p...  5.46 us
    pallas_call x1, Pallas kernels, project(): pl.pallas_call(project_body, in_specs=[pl.BlockSpec(memory_space=pltpu.SM...  4.1 us
  transfers between devices with their start and end apart: 18, of which 6 were waited for; matrix products, arithmetic and copies ran while one was open for 4% of the time, Pallas kernels for 6%

profile of v11, /device:TPU:1, one launch (start us, length us, event | category | flops | bytes accessed | tf_op | source)
XLA Modules:
  0.0 126.9 jit_solution(15348220262028278032)
XLA Ops:
  0.0 2.0 %collective-permute-start = (bf16[192,1024]{1,0:T(8,128)(2,1)}, bf16[192,1024]{1,0:T(8,128)(2,1)S(1)}, u32[]{:S(2)}, u32[]{:S(2)}) collective-permute-start(bf16[192,1024]{1,0:T(8,128)(2,1)} %refs_1_.1), channel_id=1, source_target_pairs={{0,2},{1,3},{2,0},{3,1},{4,6},{5,7},{6,4},{7,5},{8,10},{9,11},{10,... | collective-permute-start | bytes 1179656 | tf_op jit(solution)/shard_map/ppermute | solution.py:356
  2.0 1.2 collective-permute-start.4
  3.2 0.8 slice.3
  4.1 3.4 %collective-permute-start.1 = (bf16[192,128]{1,0:T(8,128)(2,1)S(1)}, bf16[192,128]{1,0:T(8,128)(2,1)S(1)}, u32[]{:S(2)}, u32[]{:S(2)}) collective-permute-start(bf16[192,128]{1,0:T(8,128)(2,1)S(1)} %slice.3), channel_id=1, source_target_pairs={{0,4},{4,8},{8,12},{12,16},{16,20},{20,24},{24,28},{28,32},{32,36}... | collective-permute-start | bytes 147464 | tf_op jit(solution)/shard_map/ppermute | solution.py:368
  7.5 2.9 %pack_spectra.1.refs_11_ = bf16[64,15,8,128]{3,2,1,0:T(8,128)(2,1)} custom-call(f32[2,192,8,256]{3,2,1,0:T(8,128)} %spec_ref.1), custom_call_target="tpu_custom_call" | custom-call | bytes 4718592 | tf_op jit(solution)/shard_map/pack_spectra/pallas_call | solution.py:60
  10.4 0.3 collective-permute-start.3
  10.7 0.3 collective-permute-start.2
  11.0 0.6 collective-permute-done.3.refs_7_
  11.6 2.8 %collective-permute-done.2.refs_6_ = bf16[192,128]{1,0:T(8,128)(2,1)S(1)} collective-permute-done((bf16[192,128]{1,0:T(8,128)(2,1)S(1)}, bf16[192,128]{1,0:T(8,128)(2,1)S(1)}, u32[]{:S(2)}, u32[]{:S(2)}) %collective-permute-start.2) | collective-permute-done | bytes 49184 | tf_op jit(solution)/shard_map/ppermute | solution.py:356
  14.4 0.7 collective-permute-start.5
  15.4 1.2 collective-permute-done.6.refs_8_
  16.6 4.1 %project.1 = (bf16[64,15,8,128]{3,2,1,0:T(8,128)(2,1)}, bf16[192,1152]{1,0:T(8,128)(2,1)S(1)}) custom-call(s32[1]{0:T(128)} %bitcast.refs_0_, bf16[192,1024]{1,0:T(8,128)(2,1)S(1)} %copy-done.2, bf16[192,1024]{1,0:T(8,128)(2,1)S(1)} %collective-permute-done.refs_2_, ...), custom_call_target="tpu_custom_call", output_to_operand_aliasing={{0}: (11, {})} | custom-call | flops 1019215872 | bytes 6291456 | tf_op jit(solution)/shard_map/project/pallas_call | solution.py:129
  20.7 0.8 copy-done.3
  21.5 14.3 %all-to-all-start = ((bf16[64,15,8,128]{3,2,1,0:T(8,128)(2,1)}), bf16[64,15,8,128]{3,2,1,0:T(8,128)(2,1)S(1)}, u32[]{:S(2)}, u32[]{:S(2)}) async-start(bf16[64,15,8,128]{3,2,1,0:T(8,128)(2,1)} %get-tuple-element.39.message_hbm), calls=%async_computation | async-start | bytes 3932160 | tf_op jit(solution)/shard_map/all_to_all | solution.py:384
  36.1 0.7 dynamic-slice_bitcast_fusion
  36.8 0.5 collective-permute-start.9
  37.5 1.4 %collective-permute-start.7 = (bf16[192,192]{1,0:T(8,128)(2,1)S(1)}, bf16[192,192]{1,0:T(8,128)(2,1)S(1)}, u32[]{:S(2)}, u32[]{:S(2)}) collective-permute-start(bf16[192,192]{1,0:T(8,128)(2,1)S(1)} %get-tuple-element.57), channel_id=1, source_target_pairs={{0,2},{1,3},{2,0},{3,1},{4,6},{5,7},{6,4},{7,5},{8,10},{9,11},{10,... | collective-permute-start | bytes 221192 | tf_op jit(solution)/shard_map/ppermute | solution.py:356
  38.8 1.3 %broadcast_add_fusion.1.twist_ref = f32[512,512]{1,0:T(8,128)S(1)} fusion(f32[512,512]{1,0:T(8,128)} %constant.21.clone, f32[]{:T(128)S(6)} %convert_element_type.8), kind=kLoop, calls=%fused_computation.1 | loop fusion | flops 262144 | bytes 2097156 | tf_op jit(solution)/shard_map/add | solution.py:392
  40.2 1.5 %broadcast_add_fusion.wave_hbm = bf16[2048,512]{1,0:T(8,128)(2,1)} fusion(bf16[2048,512]{1,0:T(8,128)(2,1)S(1)} %copy-done.4, bf16[]{:T(256)S(6)} %convert_element_type.7), kind=kLoop, calls=%fused_computation | loop fusion | flops 1048576 | bytes 4194306 | tf_op jit(solution)/shard_map/add | solution.py:392
  41.7 3.4 %keep.1.kept_hbm = bf16[2,192,1024]{2,1,0:T(8,128)(2,1)} custom-call(bf16[64,15,8,128]{3,2,1,0:T(8,128)(2,1)} %get-tuple-element.39.message_hbm, bf16[192,1152]{1,0:T(8,128)(2,1)} %copy-done.3, f32[192,9]{1,0:T(8,128)} %copy-done), custom_call_target="tpu_custom_call" | custom-call | flops 1769472 | bytes 2097152 | tf_op jit(solution)/shard_map/keep/pallas_call | solution.py:176
  45.0 2.9 %collective-permute-done.7.refs_5_ = bf16[192,192]{1,0:T(8,128)(2,1)S(1)} collective-permute-done((bf16[192,192]{1,0:T(8,128)(2,1)S(1)}, bf16[192,192]{1,0:T(8,128)(2,1)S(1)}, u32[]{:S(2)}, u32[]{:S(2)}) %collective-permute-start.7) | collective-permute-done | bytes 73760 | tf_op jit(solution)/shard_map/ppermute | solution.py:356
  48.0 34.6 %all-to-all-done.m_ref = bf16[64,15,8,128]{3,2,1,0:T(8,128)(2,1)S(1)} async-done(((bf16[64,15,8,128]{3,2,1,0:T(8,128)(2,1)}), bf16[64,15,8,128]{3,2,1,0:T(8,128)(2,1)S(1)}, u32[]{:S(2)}, u32[]{:S(2)}) %all-to-all-start) | async-done | bytes 1966112 | tf_op jit(solution)/shard_map/all_to_all | solution.py:384
  82.6 5.5 %convolve.1 = bf16[64,3,8,128]{3,2,1,0:T(8,128)(2,1)} custom-call(bf16[64,15,8,128]{3,2,1,0:T(8,128)(2,1)S(1)} %all-to-all-done.m_ref, bf16[2048,512]{1,0:T(8,128)(2,1)} %broadcast_add_fusion.wave_hbm, f32[512,512]{1,0:T(8,128)S(1)} %broadcast_add_fusion.1.twist_ref), custom_call_target="tpu_custom_call" | custom-call | flops 3221225472 | bytes 6291456 | tf_op jit(solution)/shard_map/convolve/pallas_call | solution.py:276
  88.0 8.9 %all-to-all-start.1 = ((bf16[64,3,8,128]{3,2,1,0:T(8,128)(2,1)}), bf16[64,3,8,128]{3,2,1,0:T(8,128)(2,1)S(1)}, u32[]{:S(2)}, u32[]{:S(2)}) async-start(bf16[64,3,8,128]{3,2,1,0:T(8,128)(2,1)} %convolve.1), calls=%async_computation.1 | async-start | bytes 786432 | tf_op jit(solution)/shard_map/all_to_all | solution.py:397
  97.0 14.4 %all-to-all-done.1 = bf16[64,3,8,128]{3,2,1,0:T(8,128)(2,1)S(1)} async-done(((bf16[64,3,8,128]{3,2,1,0:T(8,128)(2,1)}), bf16[64,3,8,128]{3,2,1,0:T(8,128)(2,1)S(1)}, u32[]{:S(2)}, u32[]{:S(2)}) %all-to-all-start.1) | async-done | bytes 393248 | tf_op jit(solution)/shard_map/all_to_all | solution.py:397
  111.4 1.4 %gated.1 = (bf16[192,512]{1,0:T(8,128)(2,1)S(1)}, bf16[192,512]{1,0:T(8,128)(2,1)S(1)}) custom-call(bf16[1536,128]{1,0:T(8,128)(2,1)S(1)} %bitcast.15, bf16[2,192,1024]{2,1,0:T(8,128)(2,1)} %keep.1.kept_hbm, f32[192,1]{1,0:T(8,128)S(1)} %copy.22.bias_ref), custom_call_target="tpu_custom_call" | custom-call | flops 786432 | bytes 1572864 | tf_op jit(solution)/shard_map/gated/pallas_call | solution.py:315
  112.9 1.5 %collective-permute-start.10 = (bf16[192,512]{1,0:T(8,128)(2,1)S(1)}, bf16[192,512]{1,0:T(8,128)(2,1)S(1)}, u32[]{:S(2)}, u32[]{:S(2)}) collective-permute-start(bf16[192,512]{1,0:T(8,128)(2,1)S(1)} %get-tuple-element.49.refs_0_), channel_id=1, source_target_pairs={{0,2},{1,3},{2,0},{3,1},{4,6},{5,7},{6,4},{7,5},{8,10},{9,11},{10,... | collective-permute-start | bytes 589832 | tf_op jit(solution)/shard_map/ppermute | solution.py:356
  114.4 4.6 %collective-permute-start.14 = (bf16[192,512]{1,0:T(8,128)(2,1)S(1)}, bf16[192,512]{1,0:T(8,128)(2,1)S(1)}, u32[]{:S(2)}, u32[]{:S(2)}) collective-permute-start(bf16[192,512]{1,0:T(8,128)(2,1)S(1)} %get-tuple-element.54.refs_0_), channel_id=1, source_target_pairs={{0,1},{1,0},{2,3},{3,2},{4,5},{5,4},{6,7},{7,6},{8,9},{9,8},{10,11... | collective-permute-start | bytes 589832 | tf_op jit(solution)/shard_map/ppermute | solution.py:356
  119.0 3.6 %collective-permute-start.15 = (bf16[192,512]{1,0:T(8,128)(2,1)S(1)}, bf16[192,512]{1,0:T(8,128)(2,1)S(1)}, u32[]{:S(2)}, u32[]{:S(2)}) collective-permute-start(bf16[192,512]{1,0:T(8,128)(2,1)S(1)} %collective-permute-done.13.refs_1_), channel_id=1, source_target_pairs={{0,1},{1,0},{2,3},{3,2},{4,5},{5,4},{6,7},{7,6},{8,9},{9,8},{10,11... | collective-permute-start | bytes 589832 | tf_op jit(solution)/shard_map/ppermute | solution.py:356
  122.7 2.1 %collective-permute-start.12 = (bf16[192,512]{1,0:T(8,128)(2,1)S(1)}, bf16[192,512]{1,0:T(8,128)(2,1)S(1)}, u32[]{:S(2)}, u32[]{:S(2)}) collective-permute-start(bf16[192,512]{1,0:T(8,128)(2,1)S(1)} %collective-permute-done.10.refs_1_), channel_id=1, source_target_pairs={{0,1},{1,0},{2,3},{3,2},{4,5},{5,4},{6,7},{7,6},{8,9},{9,8},{10,11... | collective-permute-start | bytes 589832 | tf_op jit(solution)/shard_map/ppermute | solution.py:356
  124.8 1.0 mixed.2.refs_8_
  125.8 1.0 mixed.3
  (36 shorter events, 0.9 us)
Async XLA Ops:
  0.0 14.4 %collective-permute-start = (bf16[192,1024]{1,0:T(8,128)(2,1)}, bf16[192,1024]{1,0:T(8,128)(2,1)S(1)}, u32[]{:S(2)}, u32[]{:S(2)}) collective-permute-start(bf16[192,1024]{1,0:T(8,128)(2,1)} %refs_1_.1), channel_id=1, source_target_pairs={{0,2},{1,3},{2,0},{3,1},{4,6},{5,7},{6,4},{7,5},{8,10},{9,11},{10,... | collective-permute-start | bytes 1179656 | tf_op jit(solution)/shard_map/ppermute | solution.py:356
  2.0 12.4 %collective-permute-start.4 = (bf16[192,1024]{1,0:T(8,128)(2,1)}, bf16[192,1024]{1,0:T(8,128)(2,1)S(1)}, u32[]{:S(2)}, u32[]{:S(2)}) collective-permute-start(bf16[192,1024]{1,0:T(8,128)(2,1)} %refs_1_.1), channel_id=1, source_target_pairs={{0,1},{1,0},{2,3},{3,2},{4,5},{5,4},{6,7},{7,6},{8,9},{9,8},{10,11... | collective-permute-start | bytes 1179656 | tf_op jit(solution)/shard_map/ppermute | solution.py:356
  4.0 6.9 %copy-start.6 = (f32[3,3,192]{2,1,0:T(4,128)S(1)}, f32[3,3,192]{2,1,0:T(4,128)}, u32[]{:S(2)}) copy-start(f32[3,3,192]{2,1,0:T(4,128)} %param.10) | copy-start | bytes 20740
  4.0 12.5 %copy-start.1 = (bf16[3,192,768]{2,1,0:T(8,128)(2,1)S(1)}, bf16[3,192,768]{2,1,0:T(8,128)(2,1)}, u32[]{:S(2)}) copy-start(bf16[3,192,768]{2,1,0:T(8,128)(2,1)} %param.9) | copy-start | bytes 2654212
  4.1 12.5 %copy-start.2 = (bf16[192,1024]{1,0:T(8,128)(2,1)S(1)}, bf16[192,1024]{1,0:T(8,128)(2,1)}, u32[]{:S(2)}) copy-start(bf16[192,1024]{1,0:T(8,128)(2,1)} %refs_1_.1) | copy-start | bytes 1179652
  4.1 6.3 %collective-permute-start.1 = (bf16[192,128]{1,0:T(8,128)(2,1)S(1)}, bf16[192,128]{1,0:T(8,128)(2,1)S(1)}, u32[]{:S(2)}, u32[]{:S(2)}) collective-permute-start(bf16[192,128]{1,0:T(8,128)(2,1)S(1)} %slice.3), channel_id=1, source_target_pairs={{0,4},{4,8},{8,12},{12,16},{16,20},{20,24},{24,28},{28,32},{32,36}... | collective-permute-start | bytes 147464 | tf_op jit(solution)/shard_map/ppermute | solution.py:368
  10.4 1.2 collective-permute-start.3
  10.7 3.7 %collective-permute-start.2 = (bf16[192,128]{1,0:T(8,128)(2,1)S(1)}, bf16[192,128]{1,0:T(8,128)(2,1)S(1)}, u32[]{:S(2)}, u32[]{:S(2)}) collective-permute-start(bf16[192,128]{1,0:T(8,128)(2,1)S(1)} %collective-permute-done.1.refs_5_), channel_id=1, source_target_pairs={{0,2},{1,3},{2,0},{3,1},{4,6},{5,7},{6,4},{7,5},{8,10},{9,11},{10,... | collective-permute-start | bytes 147464 | tf_op jit(solution)/shard_map/ppermute | solution.py:356
  14.4 2.1 %collective-permute-start.5 = (bf16[192,1024]{1,0:T(8,128)(2,1)S(1)}, bf16[192,1024]{1,0:T(8,128)(2,1)S(1)}, u32[]{:S(2)}, u32[]{:S(2)}) collective-permute-start(bf16[192,1024]{1,0:T(8,128)(2,1)S(1)} %collective-permute-done.refs_2_), channel_id=1, source_target_pairs={{0,1},{1,0},{2,3},{3,2},{4,5},{5,4},{6,7},{7,6},{8,9},{9,8},{10,11... | collective-permute-start | bytes 1179656 | tf_op jit(solution)/shard_map/ppermute | solution.py:356
  15.1 1.4 %collective-permute-start.6 = (bf16[192,128]{1,0:T(8,128)(2,1)S(1)}, bf16[192,128]{1,0:T(8,128)(2,1)S(1)}, u32[]{:S(2)}, u32[]{:S(2)}) collective-permute-start(bf16[192,128]{1,0:T(8,128)(2,1)S(1)} %collective-permute-done.2.refs_6_), channel_id=1, source_target_pairs={{0,1},{1,0},{2,3},{3,2},{4,5},{5,4},{6,7},{7,6},{8,9},{9,8},{10,11... | collective-permute-start | bytes 147464 | tf_op jit(solution)/shard_map/ppermute | solution.py:356
  15.4 5.3 %copy-start = (f32[192,9]{1,0:T(8,128)}, f32[192,9]{1,0:T(8,128)S(1)}, u32[]{:S(2)}) copy-start(f32[192,9]{1,0:T(8,128)S(1)} %copy.16.refs_10_.taps_ref) | copy-start | bytes 20740
  20.7 0.8 copy-start.3
  21.5 14.4 %copy-start.5 = (bf16[192,768]{1,0:T(8,128)(2,1)S(1)}, bf16[192,768]{1,0:T(8,128)(2,1)}, u32[]{:S(2)}) copy-start(bf16[192,768]{1,0:T(8,128)(2,1)} %param.13) | copy-start | bytes 884740
  21.5 61.1 %all-to-all-start = ((bf16[64,15,8,128]{3,2,1,0:T(8,128)(2,1)}), bf16[64,15,8,128]{3,2,1,0:T(8,128)(2,1)S(1)}, u32[]{:S(2)}, u32[]{:S(2)}) async-start(bf16[64,15,8,128]{3,2,1,0:T(8,128)(2,1)} %get-tuple-element.39.message_hbm), calls=%async_computation | async-start | bytes 3932160 | tf_op jit(solution)/shard_map/all_to_all | solution.py:384
  36.1 4.1 %copy-start.4 = (bf16[2048,512]{1,0:T(8,128)(2,1)S(1)}, bf16[2048,512]{1,0:T(8,128)(2,1)}, u32[]{:S(2)}) copy-start(bf16[2048,512]{1,0:T(8,128)(2,1)} %constant.20.clone) | copy-start | bytes 6291460
  36.8 8.2 %collective-permute-start.9 = (bf16[192,192]{1,0:T(8,128)(2,1)}, bf16[192,192]{1,0:T(8,128)(2,1)S(1)}, u32[]{:S(2)}, u32[]{:S(2)}) collective-permute-start(bf16[192,192]{1,0:T(8,128)(2,1)} %get-tuple-element.55), channel_id=1, source_target_pairs={{0,3},{1,2},{2,1},{3,0},{4,7},{5,6},{6,5},{7,4},{8,11},{9,10},{10,... | collective-permute-start | bytes 221192 | tf_op jit(solution)/shard_map/ppermute | solution.py:356
  37.3 7.7 %collective-permute-start.8 = (bf16[192,192]{1,0:T(8,128)(2,1)}, bf16[192,192]{1,0:T(8,128)(2,1)S(1)}, u32[]{:S(2)}, u32[]{:S(2)}) collective-permute-start(bf16[192,192]{1,0:T(8,128)(2,1)} %get-tuple-element.56), channel_id=1, source_target_pairs={{0,1},{1,0},{2,3},{3,2},{4,5},{5,4},{6,7},{7,6},{8,9},{9,8},{10,11... | collective-permute-start | bytes 221192 | tf_op jit(solution)/shard_map/ppermute | solution.py:356
  37.5 10.5 %collective-permute-start.7 = (bf16[192,192]{1,0:T(8,128)(2,1)S(1)}, bf16[192,192]{1,0:T(8,128)(2,1)S(1)}, u32[]{:S(2)}, u32[]{:S(2)}) collective-permute-start(bf16[192,192]{1,0:T(8,128)(2,1)S(1)} %get-tuple-element.57), channel_id=1, source_target_pairs={{0,2},{1,3},{2,0},{3,1},{4,6},{5,7},{6,4},{7,5},{8,10},{9,11},{10,... | collective-permute-start | bytes 221192 | tf_op jit(solution)/shard_map/ppermute | solution.py:356
  40.1 1.5 %copy-start.7 = (f32[192]{0:T(256)S(1)}, f32[192]{0:T(256)}, u32[]{:S(2)}) copy-start(f32[192]{0:T(256)} %param.11) | copy-start | bytes 2308
  88.0 23.4 %all-to-all-start.1 = ((bf16[64,3,8,128]{3,2,1,0:T(8,128)(2,1)}), bf16[64,3,8,128]{3,2,1,0:T(8,128)(2,1)S(1)}, u32[]{:S(2)}, u32[]{:S(2)}) async-start(bf16[64,3,8,128]{3,2,1,0:T(8,128)(2,1)} %convolve.1), calls=%async_computation.1 | async-start | bytes 786432 | tf_op jit(solution)/shard_map/all_to_all | solution.py:397
  112.8 6.2 %collective-permute-start.13 = (bf16[192,512]{1,0:T(8,128)(2,1)S(1)}, bf16[192,512]{1,0:T(8,128)(2,1)S(1)}, u32[]{:S(2)}, u32[]{:S(2)}) collective-permute-start(bf16[192,512]{1,0:T(8,128)(2,1)S(1)} %get-tuple-element.54.refs_0_), channel_id=1, source_target_pairs={{0,2},{1,3},{2,0},{3,1},{4,6},{5,7},{6,4},{7,5},{8,10},{9,11},{10,... | collective-permute-start | bytes 589832 | tf_op jit(solution)/shard_map/ppermute | solution.py:356
  112.9 9.7 %collective-permute-start.10 = (bf16[192,512]{1,0:T(8,128)(2,1)S(1)}, bf16[192,512]{1,0:T(8,128)(2,1)S(1)}, u32[]{:S(2)}, u32[]{:S(2)}) collective-permute-start(bf16[192,512]{1,0:T(8,128)(2,1)S(1)} %get-tuple-element.49.refs_0_), channel_id=1, source_target_pairs={{0,2},{1,3},{2,0},{3,1},{4,6},{5,7},{6,4},{7,5},{8,10},{9,11},{10,... | collective-permute-start | bytes 589832 | tf_op jit(solution)/shard_map/ppermute | solution.py:356
  114.4 10.4 %collective-permute-start.14 = (bf16[192,512]{1,0:T(8,128)(2,1)S(1)}, bf16[192,512]{1,0:T(8,128)(2,1)S(1)}, u32[]{:S(2)}, u32[]{:S(2)}) collective-permute-start(bf16[192,512]{1,0:T(8,128)(2,1)S(1)} %get-tuple-element.54.refs_0_), channel_id=1, source_target_pairs={{0,1},{1,0},{2,3},{3,2},{4,5},{5,4},{6,7},{7,6},{8,9},{9,8},{10,11... | collective-permute-start | bytes 589832 | tf_op jit(solution)/shard_map/ppermute | solution.py:356
  119.0 5.8 %collective-permute-start.15 = (bf16[192,512]{1,0:T(8,128)(2,1)S(1)}, bf16[192,512]{1,0:T(8,128)(2,1)S(1)}, u32[]{:S(2)}, u32[]{:S(2)}) collective-permute-start(bf16[192,512]{1,0:T(8,128)(2,1)S(1)} %collective-permute-done.13.refs_1_), channel_id=1, source_target_pairs={{0,1},{1,0},{2,3},{3,2},{4,5},{5,4},{6,7},{7,6},{8,9},{9,8},{10,11... | collective-permute-start | bytes 589832 | tf_op jit(solution)/shard_map/ppermute | solution.py:356
  122.7 3.2 %collective-permute-start.11 = (bf16[192,512]{1,0:T(8,128)(2,1)S(1)}, bf16[192,512]{1,0:T(8,128)(2,1)S(1)}, u32[]{:S(2)}, u32[]{:S(2)}) collective-permute-start(bf16[192,512]{1,0:T(8,128)(2,1)S(1)} %get-tuple-element.49.refs_0_), channel_id=1, source_target_pairs={{0,1},{1,0},{2,3},{3,2},{4,5},{5,4},{6,7},{7,6},{8,9},{9,8},{10,11... | collective-permute-start | bytes 589832 | tf_op jit(solution)/shard_map/ppermute | solution.py:356
  122.7 3.2 %collective-permute-start.12 = (bf16[192,512]{1,0:T(8,128)(2,1)S(1)}, bf16[192,512]{1,0:T(8,128)(2,1)S(1)}, u32[]{:S(2)}, u32[]{:S(2)}) collective-permute-start(bf16[192,512]{1,0:T(8,128)(2,1)S(1)} %collective-permute-done.10.refs_1_), channel_id=1, source_target_pairs={{0,1},{1,0},{2,3},{3,2},{4,5},{5,4},{6,7},{7,6},{8,9},{9,8},{10,11... | collective-permute-start | bytes 589832 | tf_op jit(solution)/shard_map/ppermute | solution.py:356

commit v12 on v11

--- a/solution.py
+++ b/solution.py
@@ -193,12 +193,12 @@
     channels, shards, pieces, lanes = done_ref.shape
     rows_dev = pieces // 2
     freqs = twist_ref.shape[0]
-    first_ref, forward_ref, backward_ref, last_ref = (wave_ref.at[i] for i in range(4))
+    first_ref, forward_ref, _, last_ref = (wave_ref.at[i] for i in range(4))
     loads = [
         pltpu.make_async_copy(wave_hbm.at[pl.ds(i * freqs, freqs)], wave_ref.at[i], wave_sems.at[i]) for i in range(4)
     ]
-    for load in loads:
-        load.start()
+    for i in (0, 1, 3):
+        loads[i].start()
     cosine, sine = twist_ref[:, :COLS], twist_ref[:, COLS:]
 
     def arrange(c):
@@ -228,15 +228,15 @@
                 m_ref[:, 4 * c + 2 * part + h].astype(F32).reshape(freqs, lanes) for part in range(2)
             )
             mid_ref[c, :, low:low + lanes] = (real * h_real - imag * h_imag).astype(BF16)
-            mid_ref[c, :, high:high + lanes] = (real * h_imag + imag * h_real).astype(BF16)
+            mid_ref[c, :, high:high + lanes] = (-(real * h_imag) - imag * h_real).astype(BF16)
 
     def cols_backward(c):
-        return jnp.dot(mid_ref[c], backward_ref[...], preferred_element_type=F32)
+        return jnp.dot(mid_ref[c], forward_ref[...], preferred_element_type=F32)
 
     def twist_backward(c, back):
-        real, imag = back[:, :COLS], back[:, COLS:]
-        tall_ref[c, :freqs, :] = (real * cosine - imag * sine).astype(BF16)
-        tall_ref[c, freqs:, :] = (imag * cosine + real * sine).astype(BF16)
+        real, minus = back[:, :COLS], back[:, COLS:]
+        tall_ref[c, :freqs, :] = (real * cosine + minus * sine).astype(BF16)
+        tall_ref[c, freqs:, :] = (real * sine - minus * cosine).astype(BF16)
 
     def rows_backward(c):
         out = jnp.dot(last_ref[:COLS, :], tall_ref[c, :freqs], preferred_element_type=F32)
@@ -257,7 +257,8 @@
     )
     waiting = None
     for stage, (multiply, finish) in enumerate(stages):
-        loads[stage].wait()
+        if stage != 2:
+            loads[stage].wait()
         for c in range(channels):
             product = multiply(c)
             if waiting is not None:

time: 127 us -> 127 us (level)
  no operation moved by 1% of the time
where the time goes in v12:
time: 127 us
  waiting for transfers between devices  56.7 us (45%)
  starting transfers between devices  45.2 us (36%)
  Pallas kernels  19.1 us (15%)
  other arithmetic  2.81 us (2%)
  local copies, waits for them, and re-layouts  2.75 us (2%)
    all_to_all x1, waiting for transfers between devices, shards(): received = lax.all_to_all(message, 'seq', 0, 0, tiled=True)  34.6 us
    ppermute x15, starting transfers between devices, swapped(): return lax.ppermute(block, 'grp', [(i, i ^ mask) for i in range(4)])  18.5 us
    all_to_all x1, waiting for transfers between devices, shards(): lax.all_to_all(result, 'seq', 0, 0, tiled=True).reshape(channels * 8, LANES)  14.4 us
    all_to_all x1, starting transfers between devices, shards(): received = lax.all_to_all(message, 'seq', 0, 0, tiled=True)  14.3 us
    all_to_all x1, starting transfers between devices, shards(): lax.all_to_all(result, 'seq', 0, 0, tiled=True).reshape(channels * 8, LANES)  8.87 us
    ppermute x15, waiting for transfers between devices, swapped(): return lax.ppermute(block, 'grp', [(i, i ^ mask) for i in range(4)])  7.65 us
    pallas_call x1, Pallas kernels, convolve(): pl.pallas_call(convolve_body, in_specs=[vmem, pl.BlockSpec(memory_space=p...  5.29 us
    pallas_call x1, Pallas kernels, project(): pl.pallas_call(project_body, in_specs=[pl.BlockSpec(memory_space=pltpu.SM...  4.1 us
  transfers between devices with their start and end apart: 18, of which 6 were waited for; matrix products, arithmetic and copies ran while one was open for 4% of the time, Pallas kernels for 6%

profile of v12, /device:TPU:1, one launch (start us, length us, event | category | flops | bytes accessed | tf_op | source)
XLA Modules:
  0.0 126.7 jit_solution(36167146366080447)
XLA Ops:
  0.0 2.0 %collective-permute-start = (bf16[192,1024]{1,0:T(8,128)(2,1)}, bf16[192,1024]{1,0:T(8,128)(2,1)S(1)}, u32[]{:S(2)}, u32[]{:S(2)}) collective-permute-start(bf16[192,1024]{1,0:T(8,128)(2,1)} %refs_1_.1), channel_id=1, source_target_pairs={{0,2},{1,3},{2,0},{3,1},{4,6},{5,7},{6,4},{7,5},{8,10},{9,11},{10,... | collective-permute-start | bytes 1179656 | tf_op jit(solution)/shard_map/ppermute | solution.py:357
  2.0 1.2 collective-permute-start.4
  3.2 0.8 slice.3
  4.1 3.4 %collective-permute-start.1 = (bf16[192,128]{1,0:T(8,128)(2,1)S(1)}, bf16[192,128]{1,0:T(8,128)(2,1)S(1)}, u32[]{:S(2)}, u32[]{:S(2)}) collective-permute-start(bf16[192,128]{1,0:T(8,128)(2,1)S(1)} %slice.3), channel_id=1, source_target_pairs={{0,4},{4,8},{8,12},{12,16},{16,20},{20,24},{24,28},{28,32},{32,36}... | collective-permute-start | bytes 147464 | tf_op jit(solution)/shard_map/ppermute | solution.py:369
  7.5 2.9 %pack_spectra.1.refs_11_ = bf16[64,15,8,128]{3,2,1,0:T(8,128)(2,1)} custom-call(f32[2,192,8,256]{3,2,1,0:T(8,128)} %spec_ref.1), custom_call_target="tpu_custom_call" | custom-call | bytes 4718592 | tf_op jit(solution)/shard_map/pack_spectra/pallas_call | solution.py:60
  10.4 0.3 collective-permute-start.3
  10.7 0.3 collective-permute-start.2
  11.0 0.6 collective-permute-done.3.refs_7_
  11.6 2.8 %collective-permute-done.2.refs_6_ = bf16[192,128]{1,0:T(8,128)(2,1)S(1)} collective-permute-done((bf16[192,128]{1,0:T(8,128)(2,1)S(1)}, bf16[192,128]{1,0:T(8,128)(2,1)S(1)}, u32[]{:S(2)}, u32[]{:S(2)}) %collective-permute-start.2) | collective-permute-done | bytes 49184 | tf_op jit(solution)/shard_map/ppermute | solution.py:357
  14.4 0.7 collective-permute-start.5
  15.4 1.2 collective-permute-done.6.refs_8_
  16.6 4.1 %project.1 = (bf16[64,15,8,128]{3,2,1,0:T(8,128)(2,1)}, bf16[192,1152]{1,0:T(8,128)(2,1)S(1)}) custom-call(s32[1]{0:T(128)} %bitcast.refs_0_, bf16[192,1024]{1,0:T(8,128)(2,1)S(1)} %copy-done.2, bf16[192,1024]{1,0:T(8,128)(2,1)S(1)} %collective-permute-done.refs_2_, ...), custom_call_target="tpu_custom_call", output_to_operand_aliasing={{0}: (11, {})} | custom-call | flops 1019215872 | bytes 6291456 | tf_op jit(solution)/shard_map/project/pallas_call | solution.py:129
  20.7 0.8 copy-done.3
  21.5 14.3 %all-to-all-start = ((bf16[64,15,8,128]{3,2,1,0:T(8,128)(2,1)}), bf16[64,15,8,128]{3,2,1,0:T(8,128)(2,1)S(1)}, u32[]{:S(2)}, u32[]{:S(2)}) async-start(bf16[64,15,8,128]{3,2,1,0:T(8,128)(2,1)} %get-tuple-element.39.message_hbm), calls=%async_computation | async-start | bytes 3932160 | tf_op jit(solution)/shard_map/all_to_all | solution.py:385
  36.1 0.7 dynamic-slice_bitcast_fusion
  36.8 0.5 collective-permute-start.9
  37.5 1.4 %collective-permute-start.7 = (bf16[192,192]{1,0:T(8,128)(2,1)S(1)}, bf16[192,192]{1,0:T(8,128)(2,1)S(1)}, u32[]{:S(2)}, u32[]{:S(2)}) collective-permute-start(bf16[192,192]{1,0:T(8,128)(2,1)S(1)} %get-tuple-element.57), channel_id=1, source_target_pairs={{0,2},{1,3},{2,0},{3,1},{4,6},{5,7},{6,4},{7,5},{8,10},{9,11},{10,... | collective-permute-start | bytes 221192 | tf_op jit(solution)/shard_map/ppermute | solution.py:357
  38.8 1.3 %broadcast_add_fusion.1.twist_ref = f32[512,512]{1,0:T(8,128)S(1)} fusion(f32[512,512]{1,0:T(8,128)} %constant.21.clone, f32[]{:T(128)S(6)} %convert_element_type.8), kind=kLoop, calls=%fused_computation.1 | loop fusion | flops 262144 | bytes 2097156 | tf_op jit(solution)/shard_map/add | solution.py:393
  40.2 1.5 %broadcast_add_fusion.wave_hbm = bf16[2048,512]{1,0:T(8,128)(2,1)} fusion(bf16[2048,512]{1,0:T(8,128)(2,1)S(1)} %copy-done.4, bf16[]{:T(256)S(6)} %convert_element_type.7), kind=kLoop, calls=%fused_computation | loop fusion | flops 1048576 | bytes 4194306 | tf_op jit(solution)/shard_map/add | solution.py:393
  41.7 3.4 %keep.1.kept_hbm = bf16[2,192,1024]{2,1,0:T(8,128)(2,1)} custom-call(bf16[64,15,8,128]{3,2,1,0:T(8,128)(2,1)} %get-tuple-element.39.message_hbm, bf16[192,1152]{1,0:T(8,128)(2,1)} %copy-done.3, f32[192,9]{1,0:T(8,128)} %copy-done), custom_call_target="tpu_custom_call" | custom-call | flops 1769472 | bytes 2097152 | tf_op jit(solution)/shard_map/keep/pallas_call | solution.py:176
  45.0 2.9 %collective-permute-done.7.refs_5_ = bf16[192,192]{1,0:T(8,128)(2,1)S(1)} collective-permute-done((bf16[192,192]{1,0:T(8,128)(2,1)S(1)}, bf16[192,192]{1,0:T(8,128)(2,1)S(1)}, u32[]{:S(2)}, u32[]{:S(2)}) %collective-permute-start.7) | collective-permute-done | bytes 73760 | tf_op jit(solution)/shard_map/ppermute | solution.py:357
  48.0 34.6 %all-to-all-done.m_ref = bf16[64,15,8,128]{3,2,1,0:T(8,128)(2,1)S(1)} async-done(((bf16[64,15,8,128]{3,2,1,0:T(8,128)(2,1)}), bf16[64,15,8,128]{3,2,1,0:T(8,128)(2,1)S(1)}, u32[]{:S(2)}, u32[]{:S(2)}) %all-to-all-start) | async-done | bytes 1966112 | tf_op jit(solution)/shard_map/all_to_all | solution.py:385
  82.6 5.3 %convolve.1 = bf16[64,3,8,128]{3,2,1,0:T(8,128)(2,1)} custom-call(bf16[64,15,8,128]{3,2,1,0:T(8,128)(2,1)S(1)} %all-to-all-done.m_ref, bf16[2048,512]{1,0:T(8,128)(2,1)} %broadcast_add_fusion.wave_hbm, f32[512,512]{1,0:T(8,128)S(1)} %broadcast_add_fusion.1.twist_ref), custom_call_target="tpu_custom_call" | custom-call | flops 3221225472 | bytes 6291456 | tf_op jit(solution)/shard_map/convolve/pallas_call | solution.py:277
  87.9 8.9 %all-to-all-start.1 = ((bf16[64,3,8,128]{3,2,1,0:T(8,128)(2,1)}), bf16[64,3,8,128]{3,2,1,0:T(8,128)(2,1)S(1)}, u32[]{:S(2)}, u32[]{:S(2)}) async-start(bf16[64,3,8,128]{3,2,1,0:T(8,128)(2,1)} %convolve.1), calls=%async_computation.1 | async-start | bytes 786432 | tf_op jit(solution)/shard_map/all_to_all | solution.py:398
  96.9 14.4 %all-to-all-done.1 = bf16[64,3,8,128]{3,2,1,0:T(8,128)(2,1)S(1)} async-done(((bf16[64,3,8,128]{3,2,1,0:T(8,128)(2,1)}), bf16[64,3,8,128]{3,2,1,0:T(8,128)(2,1)S(1)}, u32[]{:S(2)}, u32[]{:S(2)}) %all-to-all-start.1) | async-done | bytes 393248 | tf_op jit(solution)/shard_map/all_to_all | solution.py:398
  111.3 1.4 %gated.1 = (bf16[192,512]{1,0:T(8,128)(2,1)S(1)}, bf16[192,512]{1,0:T(8,128)(2,1)S(1)}) custom-call(bf16[1536,128]{1,0:T(8,128)(2,1)S(1)} %bitcast.15, bf16[2,192,1024]{2,1,0:T(8,128)(2,1)} %keep.1.kept_hbm, f32[192,1]{1,0:T(8,128)S(1)} %copy.22.bias_ref), custom_call_target="tpu_custom_call" | custom-call | flops 786432 | bytes 1572864 | tf_op jit(solution)/shard_map/gated/pallas_call | solution.py:316
  112.8 1.5 %collective-permute-start.10 = (bf16[192,512]{1,0:T(8,128)(2,1)S(1)}, bf16[192,512]{1,0:T(8,128)(2,1)S(1)}, u32[]{:S(2)}, u32[]{:S(2)}) collective-permute-start(bf16[192,512]{1,0:T(8,128)(2,1)S(1)} %get-tuple-element.49.refs_0_), channel_id=1, source_target_pairs={{0,2},{1,3},{2,0},{3,1},{4,6},{5,7},{6,4},{7,5},{8,10},{9,11},{10,... | collective-permute-start | bytes 589832 | tf_op jit(solution)/shard_map/ppermute | solution.py:357
  114.2 4.6 %collective-permute-start.14 = (bf16[192,512]{1,0:T(8,128)(2,1)S(1)}, bf16[192,512]{1,0:T(8,128)(2,1)S(1)}, u32[]{:S(2)}, u32[]{:S(2)}) collective-permute-start(bf16[192,512]{1,0:T(8,128)(2,1)S(1)} %get-tuple-element.54.refs_0_), channel_id=1, source_target_pairs={{0,1},{1,0},{2,3},{3,2},{4,5},{5,4},{6,7},{7,6},{8,9},{9,8},{10,11... | collective-permute-start | bytes 589832 | tf_op jit(solution)/shard_map/ppermute | solution.py:357
  118.8 3.6 %collective-permute-start.15 = (bf16[192,512]{1,0:T(8,128)(2,1)S(1)}, bf16[192,512]{1,0:T(8,128)(2,1)S(1)}, u32[]{:S(2)}, u32[]{:S(2)}) collective-permute-start(bf16[192,512]{1,0:T(8,128)(2,1)S(1)} %collective-permute-done.13.refs_1_), channel_id=1, source_target_pairs={{0,1},{1,0},{2,3},{3,2},{4,5},{5,4},{6,7},{7,6},{8,9},{9,8},{10,11... | collective-permute-start | bytes 589832 | tf_op jit(solution)/shard_map/ppermute | solution.py:357
  122.5 2.1 %collective-permute-start.12 = (bf16[192,512]{1,0:T(8,128)(2,1)S(1)}, bf16[192,512]{1,0:T(8,128)(2,1)S(1)}, u32[]{:S(2)}, u32[]{:S(2)}) collective-permute-start(bf16[192,512]{1,0:T(8,128)(2,1)S(1)} %collective-permute-done.10.refs_1_), channel_id=1, source_target_pairs={{0,1},{1,0},{2,3},{3,2},{4,5},{5,4},{6,7},{7,6},{8,9},{9,8},{10,11... | collective-permute-start | bytes 589832 | tf_op jit(solution)/shard_map/ppermute | solution.py:357
  124.6 1.0 mixed.2.refs_8_
  125.7 1.0 mixed.3
  (36 shorter events, 0.9 us)
Async XLA Ops:
  0.0 14.4 %collective-permute-start = (bf16[192,1024]{1,0:T(8,128)(2,1)}, bf16[192,1024]{1,0:T(8,128)(2,1)S(1)}, u32[]{:S(2)}, u32[]{:S(2)}) collective-permute-start(bf16[192,1024]{1,0:T(8,128)(2,1)} %refs_1_.1), channel_id=1, source_target_pairs={{0,2},{1,3},{2,0},{3,1},{4,6},{5,7},{6,4},{7,5},{8,10},{9,11},{10,... | collective-permute-start | bytes 1179656 | tf_op jit(solution)/shard_map/ppermute | solution.py:357
  2.0 12.4 %collective-permute-start.4 = (bf16[192,1024]{1,0:T(8,128)(2,1)}, bf16[192,1024]{1,0:T(8,128)(2,1)S(1)}, u32[]{:S(2)}, u32[]{:S(2)}) collective-permute-start(bf16[192,1024]{1,0:T(8,128)(2,1)} %refs_1_.1), channel_id=1, source_target_pairs={{0,1},{1,0},{2,3},{3,2},{4,5},{5,4},{6,7},{7,6},{8,9},{9,8},{10,11... | collective-permute-start | bytes 1179656 | tf_op jit(solution)/shard_map/ppermute | solution.py:357
  4.0 6.9 %copy-start.6 = (f32[3,3,192]{2,1,0:T(4,128)S(1)}, f32[3,3,192]{2,1,0:T(4,128)}, u32[]{:S(2)}) copy-start(f32[3,3,192]{2,1,0:T(4,128)} %param.10) | copy-start | bytes 20740
  4.0 12.5 %copy-start.1 = (bf16[3,192,768]{2,1,0:T(8,128)(2,1)S(1)}, bf16[3,192,768]{2,1,0:T(8,128)(2,1)}, u32[]{:S(2)}) copy-start(bf16[3,192,768]{2,1,0:T(8,128)(2,1)} %param.9) | copy-start | bytes 2654212
  4.1 12.5 %copy-start.2 = (bf16[192,1024]{1,0:T(8,128)(2,1)S(1)}, bf16[192,1024]{1,0:T(8,128)(2,1)}, u32[]{:S(2)}) copy-start(bf16[192,1024]{1,0:T(8,128)(2,1)} %refs_1_.1) | copy-start | bytes 1179652
  4.1 6.3 %collective-permute-start.1 = (bf16[192,128]{1,0:T(8,128)(2,1)S(1)}, bf16[192,128]{1,0:T(8,128)(2,1)S(1)}, u32[]{:S(2)}, u32[]{:S(2)}) collective-permute-start(bf16[192,128]{1,0:T(8,128)(2,1)S(1)} %slice.3), channel_id=1, source_target_pairs={{0,4},{4,8},{8,12},{12,16},{16,20},{20,24},{24,28},{28,32},{32,36}... | collective-permute-start | bytes 147464 | tf_op jit(solution)/shard_map/ppermute | solution.py:369
  10.4 1.2 collective-permute-start.3
  10.7 3.7 %collective-permute-start.2 = (bf16[192,128]{1,0:T(8,128)(2,1)S(1)}, bf16[192,128]{1,0:T(8,128)(2,1)S(1)}, u32[]{:S(2)}, u32[]{:S(2)}) collective-permute-start(bf16[192,128]{1,0:T(8,128)(2,1)S(1)} %collective-permute-done.1.refs_5_), channel_id=1, source_target_pairs={{0,2},{1,3},{2,0},{3,1},{4,6},{5,7},{6,4},{7,5},{8,10},{9,11},{10,... | collective-permute-start | bytes 147464 | tf_op jit(solution)/shard_map/ppermute | solution.py:357
  14.4 2.1 %collective-permute-start.5 = (bf16[192,1024]{1,0:T(8,128)(2,1)S(1)}, bf16[192,1024]{1,0:T(8,128)(2,1)S(1)}, u32[]{:S(2)}, u32[]{:S(2)}) collective-permute-start(bf16[192,1024]{1,0:T(8,128)(2,1)S(1)} %collective-permute-done.refs_2_), channel_id=1, source_target_pairs={{0,1},{1,0},{2,3},{3,2},{4,5},{5,4},{6,7},{7,6},{8,9},{9,8},{10,11... | collective-permute-start | bytes 1179656 | tf_op jit(solution)/shard_map/ppermute | solution.py:357
  15.1 1.4 %collective-permute-start.6 = (bf16[192,128]{1,0:T(8,128)(2,1)S(1)}, bf16[192,128]{1,0:T(8,128)(2,1)S(1)}, u32[]{:S(2)}, u32[]{:S(2)}) collective-permute-start(bf16[192,128]{1,0:T(8,128)(2,1)S(1)} %collective-permute-done.2.refs_6_), channel_id=1, source_target_pairs={{0,1},{1,0},{2,3},{3,2},{4,5},{5,4},{6,7},{7,6},{8,9},{9,8},{10,11... | collective-permute-start | bytes 147464 | tf_op jit(solution)/shard_map/ppermute | solution.py:357
  15.4 5.3 %copy-start = (f32[192,9]{1,0:T(8,128)}, f32[192,9]{1,0:T(8,128)S(1)}, u32[]{:S(2)}) copy-start(f32[192,9]{1,0:T(8,128)S(1)} %copy.16.refs_10_.taps_ref) | copy-start | bytes 20740
  20.7 0.8 copy-start.3
  21.5 14.4 %copy-start.5 = (bf16[192,768]{1,0:T(8,128)(2,1)S(1)}, bf16[192,768]{1,0:T(8,128)(2,1)}, u32[]{:S(2)}) copy-start(bf16[192,768]{1,0:T(8,128)(2,1)} %param.13) | copy-start | bytes 884740
  21.5 61.1 %all-to-all-start = ((bf16[64,15,8,128]{3,2,1,0:T(8,128)(2,1)}), bf16[64,15,8,128]{3,2,1,0:T(8,128)(2,1)S(1)}, u32[]{:S(2)}, u32[]{:S(2)}) async-start(bf16[64,15,8,128]{3,2,1,0:T(8,128)(2,1)} %get-tuple-element.39.message_hbm), calls=%async_computation | async-start | bytes 3932160 | tf_op jit(solution)/shard_map/all_to_all | solution.py:385
  36.1 4.1 %copy-start.4 = (bf16[2048,512]{1,0:T(8,128)(2,1)S(1)}, bf16[2048,512]{1,0:T(8,128)(2,1)}, u32[]{:S(2)}) copy-start(bf16[2048,512]{1,0:T(8,128)(2,1)} %constant.20.clone) | copy-start | bytes 6291460
  36.8 8.2 %collective-permute-start.9 = (bf16[192,192]{1,0:T(8,128)(2,1)}, bf16[192,192]{1,0:T(8,128)(2,1)S(1)}, u32[]{:S(2)}, u32[]{:S(2)}) collective-permute-start(bf16[192,192]{1,0:T(8,128)(2,1)} %get-tuple-element.55), channel_id=1, source_target_pairs={{0,3},{1,2},{2,1},{3,0},{4,7},{5,6},{6,5},{7,4},{8,11},{9,10},{10,... | collective-permute-start | bytes 221192 | tf_op jit(solution)/shard_map/ppermute | solution.py:357
  37.3 7.7 %collective-permute-start.8 = (bf16[192,192]{1,0:T(8,128)(2,1)}, bf16[192,192]{1,0:T(8,128)(2,1)S(1)}, u32[]{:S(2)}, u32[]{:S(2)}) collective-permute-start(bf16[192,192]{1,0:T(8,128)(2,1)} %get-tuple-element.56), channel_id=1, source_target_pairs={{0,1},{1,0},{2,3},{3,2},{4,5},{5,4},{6,7},{7,6},{8,9},{9,8},{10,11... | collective-permute-start | bytes 221192 | tf_op jit(solution)/shard_map/ppermute | solution.py:357
  37.5 10.5 %collective-permute-start.7 = (bf16[192,192]{1,0:T(8,128)(2,1)S(1)}, bf16[192,192]{1,0:T(8,128)(2,1)S(1)}, u32[]{:S(2)}, u32[]{:S(2)}) collective-permute-start(bf16[192,192]{1,0:T(8,128)(2,1)S(1)} %get-tuple-element.57), channel_id=1, source_target_pairs={{0,2},{1,3},{2,0},{3,1},{4,6},{5,7},{6,4},{7,5},{8,10},{9,11},{10,... | collective-permute-start | bytes 221192 | tf_op jit(solution)/shard_map/ppermute | solution.py:357
  40.1 1.5 %copy-start.7 = (f32[192]{0:T(256)S(1)}, f32[192]{0:T(256)}, u32[]{:S(2)}) copy-start(f32[192]{0:T(256)} %param.11) | copy-start | bytes 2308
  87.9 23.4 %all-to-all-start.1 = ((bf16[64,3,8,128]{3,2,1,0:T(8,128)(2,1)}), bf16[64,3,8,128]{3,2,1,0:T(8,128)(2,1)S(1)}, u32[]{:S(2)}, u32[]{:S(2)}) async-start(bf16[64,3,8,128]{3,2,1,0:T(8,128)(2,1)} %convolve.1), calls=%async_computation.1 | async-start | bytes 786432 | tf_op jit(solution)/shard_map/all_to_all | solution.py:398
  112.7 6.1 %collective-permute-start.13 = (bf16[192,512]{1,0:T(8,128)(2,1)S(1)}, bf16[192,512]{1,0:T(8,128)(2,1)S(1)}, u32[]{:S(2)}, u32[]{:S(2)}) collective-permute-start(bf16[192,512]{1,0:T(8,128)(2,1)S(1)} %get-tuple-element.54.refs_0_), channel_id=1, source_target_pairs={{0,2},{1,3},{2,0},{3,1},{4,6},{5,7},{6,4},{7,5},{8,10},{9,11},{10,... | collective-permute-start | bytes 589832 | tf_op jit(solution)/shard_map/ppermute | solution.py:357
  112.8 9.7 %collective-permute-start.10 = (bf16[192,512]{1,0:T(8,128)(2,1)S(1)}, bf16[192,512]{1,0:T(8,128)(2,1)S(1)}, u32[]{:S(2)}, u32[]{:S(2)}) collective-permute-start(bf16[192,512]{1,0:T(8,128)(2,1)S(1)} %get-tuple-element.49.refs_0_), channel_id=1, source_target_pairs={{0,2},{1,3},{2,0},{3,1},{4,6},{5,7},{6,4},{7,5},{8,10},{9,11},{10,... | collective-permute-start | bytes 589832 | tf_op jit(solution)/shard_map/ppermute | solution.py:357
  114.2 10.3 %collective-permute-start.14 = (bf16[192,512]{1,0:T(8,128)(2,1)S(1)}, bf16[192,512]{1,0:T(8,128)(2,1)S(1)}, u32[]{:S(2)}, u32[]{:S(2)}) collective-permute-start(bf16[192,512]{1,0:T(8,128)(2,1)S(1)} %get-tuple-element.54.refs_0_), channel_id=1, source_target_pairs={{0,1},{1,0},{2,3},{3,2},{4,5},{5,4},{6,7},{7,6},{8,9},{9,8},{10,11... | collective-permute-start | bytes 589832 | tf_op jit(solution)/shard_map/ppermute | solution.py:357
  118.8 5.8 %collective-permute-start.15 = (bf16[192,512]{1,0:T(8,128)(2,1)S(1)}, bf16[192,512]{1,0:T(8,128)(2,1)S(1)}, u32[]{:S(2)}, u32[]{:S(2)}) collective-permute-start(bf16[192,512]{1,0:T(8,128)(2,1)S(1)} %collective-permute-done.13.refs_1_), channel_id=1, source_target_pairs={{0,1},{1,0},{2,3},{3,2},{4,5},{5,4},{6,7},{7,6},{8,9},{9,8},{10,11... | collective-permute-start | bytes 589832 | tf_op jit(solution)/shard_map/ppermute | solution.py:357
  122.5 3.1 %collective-permute-start.11 = (bf16[192,512]{1,0:T(8,128)(2,1)S(1)}, bf16[192,512]{1,0:T(8,128)(2,1)S(1)}, u32[]{:S(2)}, u32[]{:S(2)}) collective-permute-start(bf16[192,512]{1,0:T(8,128)(2,1)S(1)} %get-tuple-element.49.refs_0_), channel_id=1, source_target_pairs={{0,1},{1,0},{2,3},{3,2},{4,5},{5,4},{6,7},{7,6},{8,9},{9,8},{10,11... | collective-permute-start | bytes 589832 | tf_op jit(solution)/shard_map/ppermute | solution.py:357
  122.5 3.2 %collective-permute-start.12 = (bf16[192,512]{1,0:T(8,128)(2,1)S(1)}, bf16[192,512]{1,0:T(8,128)(2,1)S(1)}, u32[]{:S(2)}, u32[]{:S(2)}) collective-permute-start(bf16[192,512]{1,0:T(8,128)(2,1)S(1)} %collective-permute-done.10.refs_1_), channel_id=1, source_target_pairs={{0,1},{1,0},{2,3},{3,2},{4,5},{5,4},{6,7},{7,6},{8,9},{9,8},{10,11... | collective-permute-start | bytes 589832 | tf_op jit(solution)/shard_map/ppermute | solution.py:357
